TPU v7x, 32 devices: a whole 2x2x4 slice. The times are simulated.
32 devices in a mesh: dp: 4 (over y, core), mp: 8 (over z, x).
Axes of the slice: x: 2, y: 2, z: 4, core: 2. Of those that a mesh axis runs over, the one named last changes fastest.
Arguments:
- grad_partials: bfloat16 [4, 16, 512, 512], P('dp', 'mp')
- owner_lists: int32 [16], replicated, may hold values from 0 to 15, as said below
- owner_offsets: int32 [9], replicated, may hold values from 0 to 16, as said below
- left_roots: bfloat16 [8, 4, 512, 512], P('mp', 'dp')
- right_roots: bfloat16 [8, 4, 512, 512], P('mp', 'dp')
Outputs:
- update: bfloat16 [16, 512, 512], P('mp', 'dp')
Inputs may be any that keep to these rules, and one draw needn't show every extreme that they name: `owner_lists`: a permutation of the block numbers; no owner column owns two blocks of one mp shard (blocks j * 2 to j * 2 + 1). `owner_offsets`: begins with 0, ends with 16, never falls; every owner column owns 1 to 4 blocks, and some column exactly 4.
All inputs are finite; a program needn't handle non-finite values.
Results may differ from a plain program's by a relative error of at most 0.025.
Values may be sent and summed in bfloat16 or wider, within the bound.
No kernel may reach another device: no remote copies, remote signals or barrier semaphores. Data moves between devices by JAX's collectives and lax.ppermute only.
A program may use at most 64 MiB of HBM per device.

v0:
```python
import jax
import jax.numpy as jnp
from jax import lax
from jax.sharding import PartitionSpec as P

epsilon = 1e-06
max_rms = 1.0


def shards(grad_partials, owner_lists, owner_offsets, left_roots, right_roots):
    dp_count = lax.axis_size("dp")
    mp_count = lax.axis_size("mp")
    mp_index = lax.axis_index("mp")
    partial_blocks = grad_partials[0]
    per_shard = partial_blocks.shape[0]
    block_width = partial_blocks.shape[2]
    blocks_all = owner_lists.shape[0]
    cells = blocks_all * block_width * block_width
    summed = lax.psum_scatter(
        partial_blocks.astype(jnp.float32).astype(jnp.bfloat16),
        "dp",
        scatter_dimension=1,
        tiled=True,
    )
    slab_f = summed.astype(jnp.float32)
    square_total = lax.psum(jnp.sum(slab_f * slab_f), ("dp", "mp"))
    positions = jnp.arange(blocks_all, dtype=jnp.int32)
    column_of_pos = jnp.sum(
        (owner_offsets[1:][None, :] <= positions[:, None]).astype(jnp.int32), axis=1
    )
    own_blocks = mp_index * per_shard + jnp.arange(per_shard, dtype=jnp.int32)
    matches = owner_lists[None, :] == own_blocks[:, None]
    home_column = jnp.sum(jnp.where(matches, column_of_pos[None, :], 0), axis=1)
    column_ids = jnp.arange(mp_count, dtype=jnp.int32)
    column_pick = (home_column[None, :] == column_ids[:, None]).astype(jnp.bfloat16)
    list_start = owner_offsets[mp_index]
    list_count = owner_offsets[mp_index + 1] - list_start
    slot_ids = jnp.arange(dp_count, dtype=jnp.int32)
    slot_match = positions[None, :] == (list_start + slot_ids)[:, None]
    slot_block = jnp.sum(jnp.where(slot_match, owner_lists[None, :], 0), axis=1)
    slot_live = slot_ids < list_count
    shard_pick = (
        ((slot_block // per_shard)[:, None] == column_ids[None, :]) & slot_live[:, None]
    ).astype(jnp.bfloat16)
    block_ids = jnp.arange(blocks_all, dtype=jnp.int32)
    block_pick = ((slot_block[:, None] == block_ids[None, :]) & slot_live[:, None]).astype(
        jnp.bfloat16
    )
    ordered = jnp.einsum(
        "kb,bsc->ksc",
        block_pick,
        lax.all_gather(summed, "mp", axis=0, tiled=True),
        preferred_element_type=jnp.float32,
    ).astype(jnp.bfloat16)
    whole_block = lax.all_to_all(ordered, "dp", split_axis=0, concat_axis=1, tiled=True)[0]
    right_prod = jnp.dot(whole_block, right_roots[0, 0], preferred_element_type=jnp.float32).astype(
        jnp.bfloat16
    )
    precond = jnp.dot(left_roots[0, 0], right_prod, preferred_element_type=jnp.float32)
    block_f = whole_block.astype(jnp.float32)
    block_sq = jnp.sum(block_f * block_f)
    area = block_width * block_width
    graft_scale = jnp.sqrt(block_sq / area + epsilon) / jnp.sqrt(
        jnp.sum(precond * precond) / area + epsilon
    )
    clip_factor = max_rms / jnp.sqrt(square_total / cells + epsilon)
    finished = (clip_factor * graft_scale * precond).astype(jnp.bfloat16)
    returned_rows = lax.all_to_all(finished[None], "dp", split_axis=1, concat_axis=0, tiled=True)
    outgoing_home = jnp.einsum(
        "km,ksc->msc", shard_pick, returned_rows, preferred_element_type=jnp.float32
    ).astype(jnp.bfloat16)
    arrived_home = lax.all_to_all(outgoing_home, "mp", split_axis=0, concat_axis=0, tiled=True)
    update = jnp.einsum(
        "mr,msc->rsc", column_pick, arrived_home, preferred_element_type=jnp.float32
    )
    return update.astype(jnp.bfloat16)


def solution(mesh):
    return jax.shard_map(
        shards,
        mesh=mesh,
        in_specs=(
            P("dp", "mp", None, None),
            P(),
            P(),
            P("mp", "dp", None, None),
            P("mp", "dp", None, None),
        ),
        out_specs=P("mp", "dp", None),
        check_vma=False,
    )
```

profile of v0, /device:TPU:0, one launch (start us, length us, event | category | flops | bytes accessed | tf_op | source)
XLA Modules:
  0.0 214.4 jit_solution(5048218598818643486)
XLA Ops:
  6.5 0.0 copy-start
  6.5 0.0 copy-start.4
  6.5 0.0 copy-start.1
  6.5 0.0 copy-start.2
  6.5 0.0 all-reduce.3.cloned.1.call-start
  6.6 3.4 %copy.47 = bf16[1,2,512,512]{3,1,2,0:T(2,128)(2,1)} copy(bf16[1,2,512,512]{3,2,1,0:T(8,128)(2,1)} %param.5) | data formatting | bytes 2097152 | tf_op args[0]
  10.0 0.0 all-reduce.3.cloned.1.call-update
  10.0 0.0 all-gather.2.cloned.1.call-start
  10.1 0.0 copy-done.4
  10.1 0.6 dynamic-slice
  11.3 37.6 %all-reduce.3.cloned.1.call-done = bf16[2,512,512]{2,0,1:T(2,128)(2,1)} async-done(((bf16[2,512,512]{2,0,1:T(2,128)(2,1)}), bf16[2,512,512]{2,0,1:T(2,128)(2,1)}) %all-reduce.3.cloned.1.call-update) | async-done | bytes 1048592
  48.9 2.1 multiply_reduce_fusion.2
  51.0 0.7 copy.29
  51.8 0.0 all-gather.2.cloned.1.call-update
  51.8 0.0 copy-done.1
  51.8 0.6 fusion.27
  53.6 0.6 iota_add_fusion
  54.3 0.0 copy-done.2
  54.3 0.2 select_reduce_fusion
  54.5 0.0 copy-start.3
  54.5 47.1 %all-gather.2.cloned.1.call-done = bf16[16,128,512]{2,1,0:T(8,128)(2,1)} async-done(((bf16[2,128,512]{2,1,0:T(8,128)(2,1)}), bf16[16,128,512]{2,1,0:T(8,128)(2,1)}) %all-gather.2.cloned.1.call-update) | async-done | bytes 2097168 | tf_op jit(solution)/shard_map/all_gather | solution.py:52
  101.6 2.9 %fusion.2 = bf16[4,128,512]{2,0,1:T(4,128)(2,1)S(1)} fusion(bf16[16,128,512]{2,1,0:T(8,128)(2,1)} %all-gather.2.cloned.1.call-done, s32[4]{0:T(128)S(1)} %select_reduce_fusion, pred[4]{0:T(512)(128)(4,1)S(1)} %iota_compare_fusion.4), kind=kOutput, calls=%fused_computation.3 | convolution fusion | flops 8650880 | bytes 2621460 | tf_op jit(solution)/shard_map/kb,bsc->ksc/dot_general | solution.py:49
  104.5 0.9 copy.31
  105.4 3.5 %all-to-all-start = ((bf16[4,128,512]{2,1,0:T(8,128)(2,1)}), bf16[4,128,512]{2,1,0:T(8,128)(2,1)S(1)}, u32[]{:S(2)}, u32[]{:S(2)}) async-start(bf16[4,128,512]{2,1,0:T(8,128)(2,1)} %copy.31), calls=%async_computation | async-start | bytes 1048576 | tf_op jit(solution)/shard_map/all_to_all | solution.py:55
  108.8 40.5 %psum.7 = f32[]{:T(128)} all-reduce(f32[]{:T(128)} %get-tuple-element.5), channel_id=1, replica_groups=mesh['dp'=4,'mp'=8] {'dp','mp'}, use_global_device_ids=true, to_apply=%region_5.6 | all-reduce | flops 1 | bytes 8 | tf_op jit(solution)/shard_map/psum | solution.py:26
  150.1 0.0 all-to-all-done
  150.1 0.0 copy-done
  150.1 0.0 copy-done.3
  150.1 1.5 multiply_reduce_fusion
  152.3 0.9 multiply_reduce_fusion.1
  153.9 0.1 fusion.7
  154.0 0.9 copy.32
  154.9 0.5 broadcast.61
  155.4 3.8 %reduce.2 = bf16[512,512]{1,0:T(8,128)(2,1)S(1)} reduce(bf16[512,1,512]{2,1,0:T(2,128)(2,1)S(1)} %bitcast.37, bf16[]{:T(256)} %broadcast.61), dimensions={1}, to_apply=%bitcast.27.reduce_sub_computation | reduce | bytes 1048578
  159.3 1.2 reshape.45
  160.4 3.7 %all-to-all-start.1 = ((bf16[4,2,32768]{2,1,0:T(2,128)(2,1)}), bf16[4,2,32768]{2,1,0:T(2,128)(2,1)S(1)}, u32[]{:S(2)}, u32[]{:S(2)}) async-start(bf16[4,2,32768]{2,1,0:T(2,128)(2,1)} %reshape.45), calls=%async_computation.1 | async-start | bytes 1048576 | tf_op jit(solution)/shard_map/all_to_all | solution.py:68
  164.2 8.8 %all-to-all-done.1 = bf16[4,2,32768]{2,1,0:T(2,128)(2,1)S(1)} async-done(((bf16[4,2,32768]{2,1,0:T(2,128)(2,1)}), bf16[4,2,32768]{2,1,0:T(2,128)(2,1)S(1)}, u32[]{:S(2)}, u32[]{:S(2)}) %all-to-all-start.1) | async-done | bytes 524320 | tf_op jit(solution)/shard_map/all_to_all | solution.py:68
  173.0 0.5 reshape.46
  173.5 0.1 copy.37
  173.7 0.6 convolution_convert_fusion
  174.3 1.3 copy.34
  175.6 4.7 %all-to-all-start.2 = ((bf16[8,128,512]{2,1,0:T(8,128)(2,1)}), bf16[8,128,512]{2,1,0:T(8,128)(2,1)S(1)}, u32[]{:S(2)}, u32[]{:S(2)}) async-start(bf16[8,128,512]{2,1,0:T(8,128)(2,1)} %copy.34), calls=%async_computation.2 | async-start | bytes 2097152 | tf_op jit(solution)/shard_map/all_to_all | solution.py:72
  180.4 0.1 slice.3
  180.4 0.1 convert_reduce_fusion
  180.5 0.2 fusion.20
  180.7 25.3 %all-to-all-done.2 = bf16[8,128,512]{2,1,0:T(8,128)(2,1)S(1)} async-done(((bf16[8,128,512]{2,1,0:T(8,128)(2,1)}), bf16[8,128,512]{2,1,0:T(8,128)(2,1)S(1)}, u32[]{:S(2)}, u32[]{:S(2)}) %all-to-all-start.2) | async-done | bytes 1048608 | tf_op jit(solution)/shard_map/all_to_all | solution.py:72
  206.0 0.8 convolution_convert_fusion.2
  206.8 0.7 copy.36
  (3 shorter events, 0.0 us)
Async XLA Ops:
  6.5 143.6 %copy-start = (bf16[1,1,512,512]{3,2,1,0:T(8,128)(2,1)S(1)}, bf16[1,1,512,512]{3,2,1,0:T(8,128)(2,1)}, u32[]{:S(2)}) copy-start(bf16[1,1,512,512]{3,2,1,0:T(8,128)(2,1)} %param.8) | copy-start | bytes 1572868
  6.5 3.5 %copy-start.4 = (u32[32]{0:T(128)S(1)}, u32[32]{0:T(128)}, u32[]{:S(2)}) copy-start(u32[32]{0:T(128)} %constant.42) | copy-start | bytes 388
  6.5 45.2 %copy-start.1 = (s32[9]{0:T(128)S(1)}, s32[9]{0:T(128)}, u32[]{:S(2)}) copy-start(s32[9]{0:T(128)} %param.7) | copy-start | bytes 112
  6.5 47.7 %copy-start.2 = (s32[16]{0:T(128)S(1)}, s32[16]{0:T(128)}, u32[]{:S(2)}) copy-start(s32[16]{0:T(128)} %param.6) | copy-start | bytes 196
  6.5 42.4 %all-reduce.3.cloned.1.call-start = ((), (), s32[]{:S(2)}) async-start(), calls=%async_computation.4 | async-start | bytes 2097152
  10.0 91.6 %all-gather.2.cloned.1.call-start = ((), (), s32[]{:S(2)}) async-start(), calls=%async_computation.3 | async-start | bytes 2359296 | tf_op jit(solution)/shard_map/all_gather | solution.py:52
  54.5 95.6 %copy-start.3 = (bf16[1,1,512,512]{3,2,1,0:T(8,128)(2,1)S(1)}, bf16[1,1,512,512]{3,2,1,0:T(8,128)(2,1)}, u32[]{:S(2)}) copy-start(bf16[1,1,512,512]{3,2,1,0:T(8,128)(2,1)} %param.9) | copy-start | bytes 1572868
  105.4 44.7 %all-to-all-start = ((bf16[4,128,512]{2,1,0:T(8,128)(2,1)}), bf16[4,128,512]{2,1,0:T(8,128)(2,1)S(1)}, u32[]{:S(2)}, u32[]{:S(2)}) async-start(bf16[4,128,512]{2,1,0:T(8,128)(2,1)} %copy.31), calls=%async_computation | async-start | bytes 1048576 | tf_op jit(solution)/shard_map/all_to_all | solution.py:55
  160.4 12.6 %all-to-all-start.1 = ((bf16[4,2,32768]{2,1,0:T(2,128)(2,1)}), bf16[4,2,32768]{2,1,0:T(2,128)(2,1)S(1)}, u32[]{:S(2)}, u32[]{:S(2)}) async-start(bf16[4,2,32768]{2,1,0:T(2,128)(2,1)} %reshape.45), calls=%async_computation.1 | async-start | bytes 1048576 | tf_op jit(solution)/shard_map/all_to_all | solution.py:68
  175.6 30.4 %all-to-all-start.2 = ((bf16[8,128,512]{2,1,0:T(8,128)(2,1)}), bf16[8,128,512]{2,1,0:T(8,128)(2,1)S(1)}, u32[]{:S(2)}, u32[]{:S(2)}) async-start(bf16[8,128,512]{2,1,0:T(8,128)(2,1)} %copy.34), calls=%async_computation.2 | async-start | bytes 2097152 | tf_op jit(solution)/shard_map/all_to_all | solution.py:72
Sparse Core Ops, SparseCore 0:
  10.1 38.7 all-reduce.2
  51.9 49.6 all-gather.1
where the time goes:
time: 215 us; the launch traced here: 214 us
  waiting for transfers between devices  119 us (55%)
  blocking collectives  40.5 us (19%)
  between operations  17.5 us (8%)
  starting transfers between devices  12 us (6%)
  local copies, waits for them, and re-layouts  11.5 us (5%)
  other arithmetic  8 us (4%)
  matrix products  5.83 us (3%)
    all_gather x1, waiting for transfers between devices, shards(): lax.all_gather(summed, 'mp', axis=0, tiled=True)  47.1 us
    psum x1, blocking collectives, shards(): square_total = lax.psum(jnp.sum(slab_f * slab_f), ('dp', 'mp'))  40.5 us
    unnamed x3, waiting for transfers between devices  37.7 us
    all_to_all x1, waiting for transfers between devices, shards(): lax.all_to_all(outgoing_home, 'mp', split_axis=0, concat_axis=0, tiled=True)  25.3 us
    all_to_all x1, waiting for transfers between devices, shards(): lax.all_to_all(finished[None], 'dp', split_axis=1, concat_axis=0, tiled=T...  8.84 us
    unnamed x16, local copies, waits for them, and re-layouts  6.31 us
    all_to_all x1, starting transfers between devices, shards(): lax.all_to_all(outgoing_home, 'mp', split_axis=0, concat_axis=0, tiled=True)  4.73 us
  transfers between devices with their start and end apart: 5, of which 4 were waited for; matrix products, arithmetic and copies ran while one was open for 1% of the time, Pallas kernels for 0%

commit v1 on v0

v1 whole, which is shorter than its diff:
```python
import functools

import jax
import jax.numpy as jnp
from jax import lax
from jax.experimental import pallas as pl
from jax.experimental.pallas import tpu as pltpu
from jax.sharding import PartitionSpec as P

epsilon = 1e-06
max_rms = 1.0

SMEM = pl.BlockSpec(memory_space=pltpu.SMEM)
VMEM = pl.BlockSpec(memory_space=pltpu.VMEM)


def swap(value, axis, distance):
    count = lax.axis_size(axis)
    return lax.ppermute(value, axis, [(i, i ^ distance) for i in range(count)])


def add_rounded(a, b):
    return (a.astype(jnp.float32) + b.astype(jnp.float32)).astype(jnp.bfloat16)


def core_sum(partial_blocks, dp_index):
    half = partial_blocks.shape[1] // 2
    core = dp_index % 2
    kept = lax.dynamic_slice_in_dim(partial_blocks, core * half, half, axis=1)
    given = lax.dynamic_slice_in_dim(partial_blocks, (1 - core) * half, half, axis=1)
    return add_rounded(kept, swap(given, "dp", 1))


def chip_sum(total, dp_count):
    distance = 2
    while distance < dp_count:
        total = add_rounded(total, swap(total, "dp", distance))
        distance *= 2
    return total


def both_halves(total, dp_index):
    core = dp_index % 2
    other = swap(total, "dp", 1)
    low = jnp.where(core == 0, total, other)
    high = jnp.where(core == 0, other, total)
    return jnp.concatenate([low, high], axis=1)


def gather_rows(rows, dp_count, dp_index):
    per_shard, _, width = rows.shape
    parts = rows[:, None]
    distance = dp_count // 2
    while distance >= 1:
        other = swap(parts, "dp", distance)
        bit = (dp_index // distance) % 2
        low = jnp.where(bit == 0, parts, other)
        high = jnp.where(bit == 0, other, parts)
        parts = jnp.stack([low, high], axis=2)
        parts = parts.reshape(per_shard, -1, *rows.shape[1:])
        distance //= 2
    return parts.reshape(per_shard, -1, width)


def plan_routes(mp_count, per_shard, lists, offsets, plan):
    column = lax.axis_index("mp")
    start = offsets[column]
    for j in range(mp_count):
        plan[j] = 0

    def note(p, carry):
        plan[lists[p] // per_shard] = p - start
        return carry

    lax.fori_loop(start, offsets[column + 1], note, 0)

    def owner(p, carry):
        block = lists[p]

        @pl.when(block // per_shard == column)
        def _():
            plan[mp_count + block % per_shard] = lax.fori_loop(
                0, mp_count, lambda c, total: total + (offsets[c + 1] <= p).astype(jnp.int32), 0
            )

        return carry

    lax.fori_loop(0, lists.shape[0], owner, 0)


def right_kernel(mp_count, per_shard, lists, offsets, slots, plan, out):
    plan_routes(mp_count, per_shard, lists, offsets, plan)
    for j in range(mp_count):
        out[j] = slots[plan[j]]


def split_kernel(dp_count, factor, *outs):
    rows = outs[0].shape[0]
    me = lax.axis_index("dp")
    for d in range(1, dp_count):
        outs[d - 1][...] = factor[0, 0, pl.ds(pl.multiple_of((me ^ d) * rows, rows), rows), :]


def left_kernel(mp_count, dp_count, plan, factor, half_sq, *refs):
    pieces, out, slots = refs[: dp_count - 1], refs[dp_count - 1], refs[dp_count]
    rows, width = slots.shape[1:]
    lanes = out.shape[2]
    me = lax.axis_index("dp")
    slots[me] = factor[0, 0, pl.ds(pl.multiple_of(me * rows, rows), rows), :]
    for d in range(1, dp_count):
        slots[me ^ d] = pieces[d - 1][...]
    total = jnp.sum(half_sq[...], axis=0, keepdims=True)
    first = total.astype(jnp.bfloat16).astype(jnp.float32)
    second = (total - first).astype(jnp.bfloat16).astype(jnp.float32)
    third = total - first - second
    row = lax.broadcasted_iota(jnp.int32, (16, lanes), 0)
    parts = jnp.where(row == 0, first, jnp.where(row == 1, second, jnp.where(row == 2, third, 0.0)))
    parts = parts.astype(jnp.bfloat16)
    for j in range(mp_count):
        slot = plan[j]
        for c in range(width // lanes):
            out[j, c * rows : (c + 1) * rows, :] = slots[slot, :, c * lanes : (c + 1) * lanes]
        out[j, out.shape[1] - 16 :, :] = parts


def pick_kernel(mp_count, per_shard, plan, arrived, out):
    for r in range(per_shard):
        out[r] = arrived[plan[mp_count + r]]


def precond_kernel(mp_count, per_shard, plan, right_prod, half_sq, arrived, precond, stats, left):
    rows, lanes = left.shape[0], arrived.shape[2]
    stats[...] = jnp.zeros_like(stats)
    stats[per_shard : 2 * per_shard, :] = half_sq[...]
    parts = jnp.sum(arrived[:, arrived.shape[1] - 16 :, :].astype(jnp.float32), axis=0)
    stats[2 * per_shard : 2 * per_shard + 1, :] = jnp.sum(parts, axis=0, keepdims=True)
    for r in range(per_shard):
        source = plan[mp_count + r]
        for c in range(left.shape[1] // lanes):
            left[:, c * lanes : (c + 1) * lanes] = arrived[source, c * rows : (c + 1) * rows, :]
        product = jnp.dot(left[...], right_prod[r], preferred_element_type=jnp.float32)
        precond[r] = product
        total = jnp.sum(jnp.sum(product * product, axis=1, keepdims=True), axis=0, keepdims=True)
        stats[r : r + 1, :] = jnp.broadcast_to(total, (1, lanes))


def finish_kernel(area, cells, precond, *refs):
    parts, update = refs[:-1], refs[-1]
    per_shard = update.shape[0]
    total = parts[0][...]
    for part in parts[1:]:
        total += part[...]
    precond_sq, block_sq = total[:per_shard], total[per_shard : 2 * per_shard]
    square_total = total[2 * per_shard : 2 * per_shard + 1]
    graft = jnp.sqrt(block_sq / area + epsilon) / jnp.sqrt(precond_sq / area + epsilon)
    scale = max_rms / jnp.sqrt(square_total / cells + epsilon) * graft
    for r in range(per_shard):
        update[r] = (scale[r : r + 1, :1] * precond[r]).astype(update.dtype)


def shards(grad_partials, owner_lists, owner_offsets, left_roots, right_roots):
    dp_count = lax.axis_size("dp")
    mp_count = lax.axis_size("mp")
    dp_index = lax.axis_index("dp")
    partial_blocks = grad_partials[0]
    per_shard = partial_blocks.shape[0]
    width = partial_blocks.shape[2]
    rows = width // dp_count
    area = width * width
    cells = owner_lists.shape[0] * area
    piece = jax.ShapeDtypeStruct((rows, width), jnp.bfloat16)
    lanes = 128

    params = pltpu.CompilerParams(vmem_limit_bytes=16 * 2**20)

    def over(rows_out, axis):
        return lax.all_to_all(rows_out, axis, split_axis=0, concat_axis=0, tiled=True)

    right_slots = over(right_roots[0, 0].reshape(dp_count, rows, width), "dp")
    total = core_sum(partial_blocks, dp_index)
    right_slots, total = lax.optimization_barrier((right_slots, total))
    plan, outgoing = pl.pallas_call(
        functools.partial(right_kernel, mp_count, per_shard),
        out_shape=[
            jax.ShapeDtypeStruct((mp_count + per_shard,), jnp.int32),
            jax.ShapeDtypeStruct((mp_count, rows, width), jnp.bfloat16),
        ],
        in_specs=[SMEM, SMEM, VMEM],
        out_specs=[SMEM, VMEM],
        compiler_params=params,
    )(owner_lists, owner_offsets, right_slots)
    right_arrived = over(outgoing, "mp")
    given = pl.pallas_call(
        functools.partial(split_kernel, dp_count),
        out_shape=[piece] * (dp_count - 1),
        in_specs=[VMEM],
        out_specs=[VMEM] * (dp_count - 1),
        compiler_params=params,
    )(left_roots)
    taken = [swap(given[d - 1], "dp", d) for d in range(1, dp_count)]
    total = chip_sum(total, dp_count)
    total_f = total.astype(jnp.float32)
    half_sq = jnp.broadcast_to(
        (jnp.sum(total_f * total_f, axis=(1, 2)) * (2 / dp_count)).reshape(per_shard, 1),
        (per_shard, lanes),
    )
    left_outgoing = pl.pallas_call(
        functools.partial(left_kernel, mp_count, dp_count),
        out_shape=jax.ShapeDtypeStruct((mp_count, rows * width // lanes + 16, lanes), jnp.bfloat16),
        in_specs=[SMEM, VMEM, VMEM] + [VMEM] * (dp_count - 1),
        out_specs=VMEM,
        scratch_shapes=[pltpu.VMEM((dp_count, rows, width), jnp.bfloat16)],
        compiler_params=params,
    )(plan, left_roots, half_sq, *taken)
    left_arrived = over(left_outgoing, "mp")
    right_rows = pl.pallas_call(
        functools.partial(pick_kernel, mp_count, per_shard),
        out_shape=jax.ShapeDtypeStruct((per_shard, rows, width), jnp.bfloat16),
        in_specs=[SMEM, VMEM],
        out_specs=VMEM,
        compiler_params=params,
    )(plan, right_arrived)
    right = gather_rows(right_rows, dp_count, dp_index)

    grad = both_halves(total, dp_index)
    right_prod = jnp.einsum(
        "bij,bjk->bik", grad, right, preferred_element_type=jnp.float32
    ).astype(jnp.bfloat16)
    precond, stats = pl.pallas_call(
        functools.partial(precond_kernel, mp_count, per_shard),
        out_shape=[
            jax.ShapeDtypeStruct((per_shard, rows, width), jnp.float32),
            jax.ShapeDtypeStruct((pl.cdiv(2 * per_shard + 1, 8) * 8, lanes), jnp.float32),
        ],
        in_specs=[SMEM, VMEM, VMEM, VMEM],
        out_specs=[VMEM, VMEM],
        scratch_shapes=[pltpu.VMEM((rows, width), jnp.bfloat16)],
        compiler_params=params,
    )(plan, right_prod, half_sq, left_arrived)
    parts = [stats] + [swap(stats, "dp", d) for d in range(1, dp_count)]
    return pl.pallas_call(
        functools.partial(finish_kernel, area, cells),
        out_shape=jax.ShapeDtypeStruct((per_shard, rows, width), jnp.bfloat16),
        in_specs=[VMEM] * (1 + dp_count),
        out_specs=VMEM,
        compiler_params=params,
    )(precond, *parts)


def solution(mesh):
    return jax.shard_map(
        shards,
        mesh=mesh,
        in_specs=(
            P("dp", "mp", None, None),
            P(),
            P(),
            P("mp", "dp", None, None),
            P("mp", "dp", None, None),
        ),
        out_specs=P("mp", "dp", None),
        check_vma=False,
    )
```

time: 215 us -> 85.5 us (0.40)
  waiting for transfers between devices: 119 us -> 55.8 us
  blocking collectives: 40.5 us -> 0 us
  between operations: 17.5 us -> 0.12 us
  local copies, waits for them, and re-layouts: 11.5 us -> 1.32 us
  starting transfers between devices: 12 us -> 19.6 us
  other arithmetic: 8 us -> 1.61 us
  Pallas kernels: 0 us -> 6.15 us
  matrix products: 5.83 us -> 0.71 us
    all_gather x1 -> x0, waiting for transfers between devices: 47.1 us -> none  [shards(): lax.all_gather(summed, 'mp', axis=0, tiled=True)]
    psum x1 -> x0, blocking collectives: 40.5 us -> none  [shards(): square_total = lax.psum(jnp.sum(slab_f * slab_f), ('dp', 'mp'))]
    unnamed x3 -> x0, waiting for transfers between devices: 37.7 us -> none
    ppermute x0 -> x11, waiting for transfers between devices: none -> 26.2 us  [swap(): return lax.ppermute(value, axis, [(i, i ^ distance) for i in range(count)])]
    unnamed x16 -> x8, local copies, waits for them, and re-layouts: 6.31 us -> 0.02 us
    pallas_call x0 -> x6, Pallas kernels: none -> 6.15 us  [the longest x1 2.02 us: shards(): pl.pallas_call(functools.partial(right_kernel, mp_count, per_shard), out_...]
    ppermute x0 -> x11, starting transfers between devices: none -> 5.96 us  [swap(): return lax.ppermute(value, axis, [(i, i ^ distance) for i in range(count)])]
    dot_general x4 -> x1, matrix products: 5.83 us -> 0.71 us  [shards(): jnp.einsum('bij,bjk->bik', grad, right, preferred_element_type=jnp.float32)]
  transfers between devices with their start and end apart: 5 -> 14, of which waited for: 4 -> 9; matrix products, arithmetic and copies ran while one was open for 1% -> 3% of each run, Pallas kernels for 0% -> 3%
where the time goes in v1:
time: 85.5 us; the launch traced here: 85.2 us
  waiting for transfers between devices  55.8 us (65%)
  starting transfers between devices  19.6 us (23%)
  Pallas kernels  6.15 us (7%)
  other arithmetic  1.61 us (2%)
  local copies, waits for them, and re-layouts  1.32 us (2%)
    all_to_all x3, waiting for transfers between devices, over(): lax.all_to_all(rows_out, axis, split_axis=0, concat_axis=0, tiled=True)  29.6 us
    ppermute x11, waiting for transfers between devices, swap(): return lax.ppermute(value, axis, [(i, i ^ distance) for i in range(count)])  26.2 us
    all_to_all x3, starting transfers between devices, over(): lax.all_to_all(rows_out, axis, split_axis=0, concat_axis=0, tiled=True)  13.6 us
    ppermute x11, starting transfers between devices, swap(): return lax.ppermute(value, axis, [(i, i ^ distance) for i in range(count)])  5.96 us
    pallas_call x1, Pallas kernels, shards(): pl.pallas_call(functools.partial(right_kernel, mp_count, per_shard), out_...  2.02 us
    pallas_call x1, Pallas kernels, shards(): pl.pallas_call(functools.partial(left_kernel, mp_count, dp_count), out_sh...  1.8 us
  transfers between devices with their start and end apart: 14, of which 9 were waited for; matrix products, arithmetic and copies ran while one was open for 3% of the time, Pallas kernels for 3%

profile of v1, /device:TPU:0, one launch (start us, length us, event | category | flops | bytes accessed | tf_op | source)
XLA Modules:
  0.0 85.2 jit_solution(7926833111724410367)
XLA Ops:
  0.0 1.2 %dynamic-slice_bitcast_fusion = bf16[2,256,512]{2,1,0:T(8,128)(2,1)S(1)} fusion(bf16[1,2,512,512]{3,2,1,0:T(8,128)(2,1)} %param.5, s32[]{:T(128)S(6)} %select_n.64), kind=kLoop, calls=%fused_computation.12 | loop fusion | bytes 1048580 | tf_op jit(solution)/shard_map/dynamic_slice | solution.py:30
  1.2 0.5 collective-permute-start
  1.7 4.0 %all-to-all-start = ((bf16[4,128,512]{2,1,0:T(8,128)(2,1)}), bf16[4,128,512]{2,1,0:T(8,128)(2,1)S(1)}, u32[]{:S(2)}, u32[]{:S(2)}) async-start(bf16[4,128,512]{2,1,0:T(8,128)(2,1)} %bitcast.27), calls=%async_computation | async-start | bytes 1048576 | tf_op jit(solution)/shard_map/all_to_all | solution.py:177
  5.7 0.0 collective-permute-done
  5.7 0.0 copy-done.3
  5.7 0.1 fusion.3
  5.9 9.1 %all-to-all-done.slots = bf16[4,128,512]{2,1,0:T(8,128)(2,1)S(1)} async-done(((bf16[4,128,512]{2,1,0:T(8,128)(2,1)}), bf16[4,128,512]{2,1,0:T(8,128)(2,1)S(1)}, u32[]{:S(2)}, u32[]{:S(2)}) %all-to-all-start) | async-done | bytes 524320 | tf_op jit(solution)/shard_map/all_to_all | solution.py:177
  15.0 0.0 copy-done.1
  15.0 0.0 copy-done.2
  15.0 2.0 %shard_map.55 = (s32[10]{0:T(128)S(1)}, bf16[8,128,512]{2,1,0:T(8,128)(2,1)}) custom-call(s32[16]{0:T(128)S(1)} %copy-done.1, s32[9]{0:T(128)S(1)} %copy-done.2, bf16[4,128,512]{2,1,0:T(8,128)(2,1)S(1)} %all-to-all-done.slots), custom_call_target="tpu_custom_call" | custom-call | tf_op jit(solution)/shard_map/pallas_call | solution.py:182
  17.0 0.0 copy-start
  17.0 6.0 %all-to-all-start.1 = ((bf16[8,128,512]{2,1,0:T(8,128)(2,1)}), bf16[8,128,512]{2,1,0:T(8,128)(2,1)S(1)}, u32[]{:S(2)}, u32[]{:S(2)}) async-start(bf16[8,128,512]{2,1,0:T(8,128)(2,1)} %get-tuple-element.17), calls=%async_computation.1 | async-start | bytes 2097152 | tf_op jit(solution)/shard_map/all_to_all | solution.py:177
  23.0 0.5 collective-permute-start.1
  23.5 0.0 copy-done
  23.5 0.1 collective-permute-start.5
  23.6 1.6 %collective-permute-start.6 = (bf16[128,512]{1,0:T(8,128)(2,1)S(1)}, bf16[128,512]{1,0:T(8,128)(2,1)S(1)}, u32[]{:S(2)}, u32[]{:S(2)}) collective-permute-start(bf16[128,512]{1,0:T(8,128)(2,1)S(1)} %get-tuple-element.19), channel_id=1, source_target_pairs={{0,16},{8,24},{16,0},{24,8},{1,17},{9,25},{17,1},{25,9},{2,18},{10... | collective-permute-start | bytes 393224 | tf_op jit(solution)/shard_map/ppermute | solution.py:19
  25.2 0.2 collective-permute-start.7
  25.5 12.4 %collective-permute-done.1 = bf16[2,256,512]{2,1,0:T(8,128)(2,1)S(1)} collective-permute-done((bf16[2,256,512]{2,1,0:T(8,128)(2,1)S(1)}, bf16[2,256,512]{2,1,0:T(8,128)(2,1)S(1)}, u32[]{:S(2)}, u32[]{:S(2)}) %collective-permute-start.1) | collective-permute-done | bytes 524320 | tf_op jit(solution)/shard_map/ppermute | solution.py:19
  37.9 0.3 multiply_reduce_fusion
  38.2 0.0 collective-permute-done.5.refs_0_
  38.2 2.2 %collective-permute-done.6.refs_1_ = bf16[128,512]{1,0:T(8,128)(2,1)S(1)} collective-permute-done((bf16[128,512]{1,0:T(8,128)(2,1)S(1)}, bf16[128,512]{1,0:T(8,128)(2,1)S(1)}, u32[]{:S(2)}, u32[]{:S(2)}) %collective-permute-start.6) | collective-permute-done | bytes 131104 | tf_op jit(solution)/shard_map/ppermute | solution.py:19
  40.4 0.0 collective-permute-done.7.refs_2_
  40.4 0.1 broadcast_in_dim.9.half_sq
  40.5 1.8 %shard_map.58 = bf16[8,528,128]{2,1,0:T(8,128)(2,1)} custom-call(s32[10]{0:T(128)S(1)} %get-tuple-element.15.plan, bf16[1,1,512,512]{3,2,1,0:T(8,128)(2,1)S(1)} %copy-done, f32[2,128]{1,0:T(2,128)S(1)} %broadcast_in_dim.9.half_sq, bf16[128,512]{1,0:T(8,128)(2,1)S(1)} %collective-permute-done.5.refs_0_, bf16[128,512]{1,0:T(8,128)(2,1)S(1)} %collective-permute-done.6.refs_1_, ...), custom_call_target="tpu_custom_call" | custom-call | tf_op jit(solution)/shard_map/pallas_call | solution.py:207
  42.3 6.4 %all-to-all-done.1.arrived = bf16[8,128,512]{2,1,0:T(8,128)(2,1)S(1)} async-done(((bf16[8,128,512]{2,1,0:T(8,128)(2,1)}), bf16[8,128,512]{2,1,0:T(8,128)(2,1)S(1)}, u32[]{:S(2)}, u32[]{:S(2)}) %all-to-all-start.1) | async-done | bytes 1048608 | tf_op jit(solution)/shard_map/all_to_all | solution.py:177
  48.7 3.6 %all-to-all-start.2 = ((bf16[8,528,128]{2,1,0:T(8,128)(2,1)}), bf16[8,528,128]{2,1,0:T(8,128)(2,1)S(1)}, u32[]{:S(2)}, u32[]{:S(2)}) async-start(bf16[8,528,128]{2,1,0:T(8,128)(2,1)} %shard_map.58), calls=%async_computation.2 | async-start | bytes 2162688 | tf_op jit(solution)/shard_map/all_to_all | solution.py:177
  52.3 0.6 shard_map.56
  52.8 0.9 %collective-permute-start.3 = (bf16[2,1,128,512]{3,2,0,1:T(8,128)(2,1)S(1)}, bf16[2,1,128,512]{3,2,0,1:T(8,128)(2,1)S(1)}, u32[]{:S(2)}, u32[]{:S(2)}) collective-permute-start(bf16[2,1,128,512]{3,2,0,1:T(8,128)(2,1)S(1)} %bitcast.25), channel_id=1, source_target_pairs={{0,16},{8,24},{16,0},{24,8},{1,17},{9,25},{17,1},{25,9},{2,18},{10... | collective-permute-start | bytes 786440 | tf_op jit(solution)/shard_map/ppermute | solution.py:19
  53.7 0.0 collective-permute-start.2
  53.7 7.1 %collective-permute-done.3 = bf16[2,1,128,512]{3,2,0,1:T(8,128)(2,1)S(1)} collective-permute-done((bf16[2,1,128,512]{3,2,0,1:T(8,128)(2,1)S(1)}, bf16[2,1,128,512]{3,2,0,1:T(8,128)(2,1)S(1)}, u32[]{:S(2)}, u32[]{:S(2)}) %collective-permute-start.3) | collective-permute-done | bytes 262176 | tf_op jit(solution)/shard_map/ppermute | solution.py:19
  60.8 0.8 maximum_bitcast_fusion
  61.7 0.0 collective-permute-start.4
  61.7 0.0 collective-permute-done.2
  61.7 0.1 broadcast_select_fusion.1
  61.7 2.0 %collective-permute-done.4 = bf16[2,2,128,512]{3,2,0,1:T(8,128)(2,1)S(1)} collective-permute-done((bf16[2,2,128,512]{3,2,0,1:T(8,128)(2,1)}, bf16[2,2,128,512]{3,2,0,1:T(8,128)(2,1)S(1)}, u32[]{:S(2)}, u32[]{:S(2)}) %collective-permute-start.4) | collective-permute-done | bytes 524320 | tf_op jit(solution)/shard_map/ppermute | solution.py:19
  63.8 0.1 select_bitcast_fusion.1
  63.9 0.1 pad_maximum_fusion
  64.0 0.1 copy.6
  64.0 0.7 convolution_convert_fusion.right_prod
  64.8 14.1 %all-to-all-done.2.arrived = bf16[8,528,128]{2,1,0:T(8,128)(2,1)S(1)} async-done(((bf16[8,528,128]{2,1,0:T(8,128)(2,1)}), bf16[8,528,128]{2,1,0:T(8,128)(2,1)S(1)}, u32[]{:S(2)}, u32[]{:S(2)}) %all-to-all-start.2) | async-done | bytes 1081376 | tf_op jit(solution)/shard_map/all_to_all | solution.py:177
  78.8 0.9 %shard_map.59 = (f32[2,128,512]{2,1,0:T(8,128)S(1)}, f32[8,128]{1,0:T(8,128)S(1)}) custom-call(s32[10]{0:T(128)S(1)} %get-tuple-element.15.plan, bf16[2,512,512]{2,1,0:T(8,128)(2,1)S(1)} %convolution_convert_fusion.right_prod, f32[2,128]{1,0:T(2,128)S(1)} %broadcast_in_dim.9.half_sq, bf16[8,528,128]{2,1,0:T(8,128)(2,1)S(1)} %all-to-all-done.2.arrived), custom_call_target="tpu_custom_call" | custom-call | tf_op jit(solution)/shard_map/pallas_call | solution.py:229
  79.8 0.1 collective-permute-start.10
  79.9 1.0 %collective-permute-start.8 = (f32[8,128]{1,0:T(8,128)S(1)}, f32[8,128]{1,0:T(8,128)S(1)}, u32[]{:S(2)}, u32[]{:S(2)}) collective-permute-start(f32[8,128]{1,0:T(8,128)S(1)} %get-tuple-element.22.refs_0_), channel_id=1, source_target_pairs={{0,8},{8,0},{16,24},{24,16},{1,9},{9,1},{17,25},{25,17},{2,10},{10... | collective-permute-start | bytes 12296 | tf_op jit(solution)/shard_map/ppermute | solution.py:19
  80.8 1.2 %collective-permute-start.9 = (f32[8,128]{1,0:T(8,128)S(1)}, f32[8,128]{1,0:T(8,128)S(1)}, u32[]{:S(2)}, u32[]{:S(2)}) collective-permute-start(f32[8,128]{1,0:T(8,128)S(1)} %get-tuple-element.22.refs_0_), channel_id=1, source_target_pairs={{0,16},{8,24},{16,0},{24,8},{1,17},{9,25},{17,1},{25,9},{2,18},{10... | collective-permute-start | bytes 12296 | tf_op jit(solution)/shard_map/ppermute | solution.py:19
  82.0 0.9 %collective-permute-done.10.refs_3_ = f32[8,128]{1,0:T(8,128)S(1)} collective-permute-done((f32[8,128]{1,0:T(8,128)S(1)}, f32[8,128]{1,0:T(8,128)S(1)}, u32[]{:S(2)}, u32[]{:S(2)}) %collective-permute-start.10) | collective-permute-done | bytes 4128 | tf_op jit(solution)/shard_map/ppermute | solution.py:19
  82.9 0.0 collective-permute-done.8.refs_1_
  82.9 1.5 %collective-permute-done.9.refs_2_ = f32[8,128]{1,0:T(8,128)S(1)} collective-permute-done((f32[8,128]{1,0:T(8,128)S(1)}, f32[8,128]{1,0:T(8,128)S(1)}, u32[]{:S(2)}, u32[]{:S(2)}) %collective-permute-start.9) | collective-permute-done | bytes 4128 | tf_op jit(solution)/shard_map/ppermute | solution.py:19
  84.4 0.8 shard_map.60
  (6 shorter events, 0.1 us)
Async XLA Ops:
  0.0 5.7 %copy-start.3 = (bf16[1,2,512,512]{3,2,1,0:T(8,128)(2,1)S(1)}, bf16[1,2,512,512]{3,2,1,0:T(8,128)(2,1)}, u32[]{:S(2)}) copy-start(bf16[1,2,512,512]{3,2,1,0:T(8,128)(2,1)} %param.5) | copy-start | bytes 3145732
  1.2 4.6 %collective-permute-start = (bf16[2,256,512]{2,1,0:T(8,128)(2,1)S(1)}, bf16[2,256,512]{2,1,0:T(8,128)(2,1)S(1)}, u32[]{:S(2)}, u32[]{:S(2)}) collective-permute-start(bf16[2,256,512]{2,1,0:T(8,128)(2,1)S(1)} %dynamic-slice_bitcast_fusion), channel_id=1, source_target_pairs={{0,8},{8,0},{16,24},{24,16},{1,9},{9,1},{17,25},{25,17},{2,10},{10... | collective-permute-start | bytes 1572872 | tf_op jit(solution)/shard_map/ppermute | solution.py:19
  1.7 13.3 %copy-start.1 = (s32[16]{0:T(128)S(1)}, s32[16]{0:T(128)}, u32[]{:S(2)}) copy-start(s32[16]{0:T(128)} %lists.1) | copy-start | bytes 196
  1.7 13.3 %copy-start.2 = (s32[9]{0:T(128)S(1)}, s32[9]{0:T(128)}, u32[]{:S(2)}) copy-start(s32[9]{0:T(128)} %offsets.1) | copy-start | bytes 112
  1.7 13.3 %all-to-all-start = ((bf16[4,128,512]{2,1,0:T(8,128)(2,1)}), bf16[4,128,512]{2,1,0:T(8,128)(2,1)S(1)}, u32[]{:S(2)}, u32[]{:S(2)}) async-start(bf16[4,128,512]{2,1,0:T(8,128)(2,1)} %bitcast.27), calls=%async_computation | async-start | bytes 1048576 | tf_op jit(solution)/shard_map/all_to_all | solution.py:177
  17.0 6.5 %copy-start = (bf16[1,1,512,512]{3,2,1,0:T(8,128)(2,1)S(1)}, bf16[1,1,512,512]{3,2,1,0:T(8,128)(2,1)}, u32[]{:S(2)}) copy-start(bf16[1,1,512,512]{3,2,1,0:T(8,128)(2,1)} %factor.3) | copy-start | bytes 1572868
  17.0 31.7 %all-to-all-start.1 = ((bf16[8,128,512]{2,1,0:T(8,128)(2,1)}), bf16[8,128,512]{2,1,0:T(8,128)(2,1)S(1)}, u32[]{:S(2)}, u32[]{:S(2)}) async-start(bf16[8,128,512]{2,1,0:T(8,128)(2,1)} %get-tuple-element.17), calls=%async_computation.1 | async-start | bytes 2097152 | tf_op jit(solution)/shard_map/all_to_all | solution.py:177
  23.0 14.9 %collective-permute-start.1 = (bf16[2,256,512]{2,1,0:T(8,128)(2,1)S(1)}, bf16[2,256,512]{2,1,0:T(8,128)(2,1)S(1)}, u32[]{:S(2)}, u32[]{:S(2)}) collective-permute-start(bf16[2,256,512]{2,1,0:T(8,128)(2,1)S(1)} %fusion.3), channel_id=1, source_target_pairs={{0,16},{8,24},{16,0},{24,8},{1,17},{9,25},{17,1},{25,9},{2,18},{10... | collective-permute-start | bytes 1572872 | tf_op jit(solution)/shard_map/ppermute | solution.py:19
  23.5 14.7 %collective-permute-start.5 = (bf16[128,512]{1,0:T(8,128)(2,1)S(1)}, bf16[128,512]{1,0:T(8,128)(2,1)S(1)}, u32[]{:S(2)}, u32[]{:S(2)}) collective-permute-start(bf16[128,512]{1,0:T(8,128)(2,1)S(1)} %get-tuple-element.18), channel_id=1, source_target_pairs={{0,8},{8,0},{16,24},{24,16},{1,9},{9,1},{17,25},{25,17},{2,10},{10... | collective-permute-start | bytes 393224 | tf_op jit(solution)/shard_map/ppermute | solution.py:19
  23.6 16.8 %collective-permute-start.6 = (bf16[128,512]{1,0:T(8,128)(2,1)S(1)}, bf16[128,512]{1,0:T(8,128)(2,1)S(1)}, u32[]{:S(2)}, u32[]{:S(2)}) collective-permute-start(bf16[128,512]{1,0:T(8,128)(2,1)S(1)} %get-tuple-element.19), channel_id=1, source_target_pairs={{0,16},{8,24},{16,0},{24,8},{1,17},{9,25},{17,1},{25,9},{2,18},{10... | collective-permute-start | bytes 393224 | tf_op jit(solution)/shard_map/ppermute | solution.py:19
  25.2 15.2 %collective-permute-start.7 = (bf16[128,512]{1,0:T(8,128)(2,1)S(1)}, bf16[128,512]{1,0:T(8,128)(2,1)S(1)}, u32[]{:S(2)}, u32[]{:S(2)}) collective-permute-start(bf16[128,512]{1,0:T(8,128)(2,1)S(1)} %get-tuple-element.20), channel_id=1, source_target_pairs={{0,24},{8,16},{16,8},{24,0},{1,25},{9,17},{17,9},{25,1},{2,26},{10... | collective-permute-start | bytes 393224 | tf_op jit(solution)/shard_map/ppermute | solution.py:19
  48.7 30.1 %all-to-all-start.2 = ((bf16[8,528,128]{2,1,0:T(8,128)(2,1)}), bf16[8,528,128]{2,1,0:T(8,128)(2,1)S(1)}, u32[]{:S(2)}, u32[]{:S(2)}) async-start(bf16[8,528,128]{2,1,0:T(8,128)(2,1)} %shard_map.58), calls=%async_computation.2 | async-start | bytes 2162688 | tf_op jit(solution)/shard_map/all_to_all | solution.py:177
  52.8 7.9 %collective-permute-start.3 = (bf16[2,1,128,512]{3,2,0,1:T(8,128)(2,1)S(1)}, bf16[2,1,128,512]{3,2,0,1:T(8,128)(2,1)S(1)}, u32[]{:S(2)}, u32[]{:S(2)}) collective-permute-start(bf16[2,1,128,512]{3,2,0,1:T(8,128)(2,1)S(1)} %bitcast.25), channel_id=1, source_target_pairs={{0,16},{8,24},{16,0},{24,8},{1,17},{9,25},{17,1},{25,9},{2,18},{10... | collective-permute-start | bytes 786440 | tf_op jit(solution)/shard_map/ppermute | solution.py:19
  53.7 8.0 %collective-permute-start.2 = (bf16[2,256,512]{2,1,0:T(8,128)(2,1)S(1)}, bf16[2,256,512]{2,1,0:T(8,128)(2,1)S(1)}, u32[]{:S(2)}, u32[]{:S(2)}) collective-permute-start(bf16[2,256,512]{2,1,0:T(8,128)(2,1)S(1)} %get-tuple-element.24), channel_id=1, source_target_pairs={{0,8},{8,0},{16,24},{24,16},{1,9},{9,1},{17,25},{25,17},{2,10},{10... | collective-permute-start | bytes 1572872 | tf_op jit(solution)/shard_map/ppermute | solution.py:19
  61.7 2.1 %collective-permute-start.4 = (bf16[2,2,128,512]{3,2,0,1:T(8,128)(2,1)}, bf16[2,2,128,512]{3,2,0,1:T(8,128)(2,1)S(1)}, u32[]{:S(2)}, u32[]{:S(2)}) collective-permute-start(bf16[2,2,128,512]{3,2,0,1:T(8,128)(2,1)} %maximum_bitcast_fusion), channel_id=1, source_target_pairs={{0,8},{8,0},{16,24},{24,16},{1,9},{9,1},{17,25},{25,17},{2,10},{10... | collective-permute-start | bytes 1572872 | tf_op jit(solution)/shard_map/ppermute | solution.py:19
  79.8 3.1 %collective-permute-start.10 = (f32[8,128]{1,0:T(8,128)S(1)}, f32[8,128]{1,0:T(8,128)S(1)}, u32[]{:S(2)}, u32[]{:S(2)}) collective-permute-start(f32[8,128]{1,0:T(8,128)S(1)} %get-tuple-element.22.refs_0_), channel_id=1, source_target_pairs={{0,24},{8,16},{16,8},{24,0},{1,25},{9,17},{17,9},{25,1},{2,26},{10... | collective-permute-start | bytes 12296 | tf_op jit(solution)/shard_map/ppermute | solution.py:19
  79.9 3.0 %collective-permute-start.8 = (f32[8,128]{1,0:T(8,128)S(1)}, f32[8,128]{1,0:T(8,128)S(1)}, u32[]{:S(2)}, u32[]{:S(2)}) collective-permute-start(f32[8,128]{1,0:T(8,128)S(1)} %get-tuple-element.22.refs_0_), channel_id=1, source_target_pairs={{0,8},{8,0},{16,24},{24,16},{1,9},{9,1},{17,25},{25,17},{2,10},{10... | collective-permute-start | bytes 12296 | tf_op jit(solution)/shard_map/ppermute | solution.py:19
  80.8 3.6 %collective-permute-start.9 = (f32[8,128]{1,0:T(8,128)S(1)}, f32[8,128]{1,0:T(8,128)S(1)}, u32[]{:S(2)}, u32[]{:S(2)}) collective-permute-start(f32[8,128]{1,0:T(8,128)S(1)} %get-tuple-element.22.refs_0_), channel_id=1, source_target_pairs={{0,16},{8,24},{16,0},{24,8},{1,17},{9,25},{17,1},{25,9},{2,18},{10... | collective-permute-start | bytes 12296 | tf_op jit(solution)/shard_map/ppermute | solution.py:19

commit v2 on v1

--- a/solution.py
+++ b/solution.py
@@ -12,6 +12,7 @@
 
 SMEM = pl.BlockSpec(memory_space=pltpu.SMEM)
 VMEM = pl.BlockSpec(memory_space=pltpu.VMEM)
+ANY = pl.BlockSpec(memory_space=pl.ANY)
 
 
 def swap(value, axis, distance):
@@ -62,7 +63,7 @@
     return parts.reshape(per_shard, -1, width)
 
 
-def plan_routes(mp_count, per_shard, lists, offsets, plan):
+def plan_kernel(mp_count, per_shard, lists, offsets, plan):
     column = lax.axis_index("mp")
     start = offsets[column]
     for j in range(mp_count):
@@ -88,10 +89,10 @@
     lax.fori_loop(0, lists.shape[0], owner, 0)
 
 
-def right_kernel(mp_count, per_shard, lists, offsets, slots, plan, out):
-    plan_routes(mp_count, per_shard, lists, offsets, plan)
-    for j in range(mp_count):
-        out[j] = slots[plan[j]]
+def right_kernel(mp_count, plan, slots, *outs):
+    column = lax.axis_index("mp")
+    for d in range(mp_count):
+        outs[d][...] = slots[plan[column ^ d]]
 
 
 def split_kernel(dp_count, factor, *outs):
@@ -123,9 +124,16 @@
         out[j, out.shape[1] - 16 :, :] = parts
 
 
-def pick_kernel(mp_count, per_shard, plan, arrived, out):
+def pick_kernel(mp_count, per_shard, plan, *refs):
+    arrived, out = refs[:mp_count], refs[-1]
+    shard = lax.axis_index("mp")
     for r in range(per_shard):
-        out[r] = arrived[plan[mp_count + r]]
+        source = plan[mp_count + r] ^ shard
+        for d in range(mp_count):
+
+            @pl.when(source == d)
+            def _(d=d, r=r):
+                out[r] = arrived[d][...]
 
 
 def precond_kernel(mp_count, per_shard, plan, right_prod, half_sq, arrived, precond, stats, left):
@@ -173,23 +181,28 @@
 
     params = pltpu.CompilerParams(vmem_limit_bytes=16 * 2**20)
 
-    def over(rows_out, axis):
-        return lax.all_to_all(rows_out, axis, split_axis=0, concat_axis=0, tiled=True)
-
-    right_slots = over(right_roots[0, 0].reshape(dp_count, rows, width), "dp")
+    def over_dp(factor):
+        return lax.all_to_all(
+            factor[0, 0].reshape(dp_count, rows, width), "dp", split_axis=0, concat_axis=0, tiled=True
+        )
+
+    plan = pl.pallas_call(
+        functools.partial(plan_kernel, mp_count, per_shard),
+        out_shape=jax.ShapeDtypeStruct((mp_count + per_shard,), jnp.int32),
+        in_specs=[SMEM, SMEM],
+        out_specs=SMEM,
+        compiler_params=params,
+    )(owner_lists, owner_offsets)
+    right_slots = over_dp(right_roots)
     total = core_sum(partial_blocks, dp_index)
-    right_slots, total = lax.optimization_barrier((right_slots, total))
-    plan, outgoing = pl.pallas_call(
-        functools.partial(right_kernel, mp_count, per_shard),
-        out_shape=[
-            jax.ShapeDtypeStruct((mp_count + per_shard,), jnp.int32),
-            jax.ShapeDtypeStruct((mp_count, rows, width), jnp.bfloat16),
-        ],
-        in_specs=[SMEM, SMEM, VMEM],
-        out_specs=[SMEM, VMEM],
-        compiler_params=params,
-    )(owner_lists, owner_offsets, right_slots)
-    right_arrived = over(outgoing, "mp")
+    right_slots, total, left_roots = lax.optimization_barrier((right_slots, total, left_roots))
+    outgoing = pl.pallas_call(
+        functools.partial(right_kernel, mp_count),
+        out_shape=[piece] * mp_count,
+        in_specs=[SMEM, VMEM],
+        out_specs=[VMEM] * mp_count,
+        compiler_params=params,
+    )(plan, right_slots)
     given = pl.pallas_call(
         functools.partial(split_kernel, dp_count),
         out_shape=[piece] * (dp_count - 1),
@@ -198,6 +211,7 @@
         compiler_params=params,
     )(left_roots)
     taken = [swap(given[d - 1], "dp", d) for d in range(1, dp_count)]
+    right_arrived = [outgoing[0]] + [swap(outgoing[d], "mp", d) for d in range(1, mp_count)]
     total = chip_sum(total, dp_count)
     total_f = total.astype(jnp.float32)
     half_sq = jnp.broadcast_to(
@@ -212,14 +226,14 @@
         scratch_shapes=[pltpu.VMEM((dp_count, rows, width), jnp.bfloat16)],
         compiler_params=params,
     )(plan, left_roots, half_sq, *taken)
-    left_arrived = over(left_outgoing, "mp")
+    left_arrived = lax.all_to_all(left_outgoing, "mp", split_axis=0, concat_axis=0, tiled=True)
     right_rows = pl.pallas_call(
         functools.partial(pick_kernel, mp_count, per_shard),
         out_shape=jax.ShapeDtypeStruct((per_shard, rows, width), jnp.bfloat16),
-        in_specs=[SMEM, VMEM],
+        in_specs=[SMEM] + [VMEM] * mp_count + [ANY],
         out_specs=VMEM,
         compiler_params=params,
-    )(plan, right_arrived)
+    )(plan, *right_arrived, left_outgoing)
     right = gather_rows(right_rows, dp_count, dp_index)
 
     grad = both_halves(total, dp_index)

time: 85.5 us -> 87.2 us (1.020)
  starting transfers between devices: 19.6 us -> 30.7 us
  waiting for transfers between devices: 55.8 us -> 46 us
    ppermute x11 -> x18, starting transfers between devices: 5.96 us -> 21.4 us  [swap(): return lax.ppermute(value, axis, [(i, i ^ distance) for i in range(count)])]
    all_to_all x3 -> x2, waiting for transfers between devices: 29.6 us -> 22.9 us  [the longest x1 13.8 us: shards(): lax.all_to_all(left_outgoing, 'mp', split_axis=0, concat_axis=0, tiled=True)]
    all_to_all x3 -> x2, starting transfers between devices: 13.6 us -> 9.31 us  [the longest x1 5.28 us: shards(): lax.all_to_all(left_outgoing, 'mp', split_axis=0, concat_axis=0, tiled=True)]
    ppermute x11 -> x18, waiting for transfers between devices: 26.2 us -> 23.1 us  [swap(): return lax.ppermute(value, axis, [(i, i ^ distance) for i in range(count)])]
    pallas_call x1 -> x2, Pallas kernels: 2.02 us -> 2.21 us  [the longest x1 1.6 us: shards(): pl.pallas_call(functools.partial(plan_kernel, mp_count, per_shard), out_s...]
  transfers between devices with their start and end apart: 14 -> 20, of which waited for: 9 -> 9; matrix products, arithmetic and copies ran while one was open for 3% -> 3% of each run, Pallas kernels for 3% -> 5%
where the time goes in v2:
time: 87.2 us; the launch traced here: 86.9 us
  waiting for transfers between devices  46 us (53%)
  starting transfers between devices  30.7 us (35%)
  Pallas kernels  6.41 us (7%)
  other arithmetic  1.67 us (2%)
  local copies, waits for them, and re-layouts  1.32 us (2%)
    ppermute x18, waiting for transfers between devices, swap(): return lax.ppermute(value, axis, [(i, i ^ distance) for i in range(count)])  23.1 us
    ppermute x18, starting transfers between devices, swap(): return lax.ppermute(value, axis, [(i, i ^ distance) for i in range(count)])  21.4 us
    all_to_all x1, waiting for transfers between devices, shards(): lax.all_to_all(left_outgoing, 'mp', split_axis=0, concat_axis=0, tiled=True)  13.8 us
    all_to_all x1, waiting for transfers between devices, over_dp(): lax.all_to_all(factor[0, 0].reshape(dp_count, rows, width), 'dp', split_a...  9.09 us
    all_to_all x1, starting transfers between devices, shards(): lax.all_to_all(left_outgoing, 'mp', split_axis=0, concat_axis=0, tiled=True)  5.28 us
    all_to_all x1, starting transfers between devices, over_dp(): lax.all_to_all(factor[0, 0].reshape(dp_count, rows, width), 'dp', split_a...  4.03 us
    pallas_call x1, Pallas kernels, shards(): pl.pallas_call(functools.partial(left_kernel, mp_count, dp_count), out_sh...  1.76 us
  transfers between devices with their start and end apart: 20, of which 9 were waited for; matrix products, arithmetic and copies ran while one was open for 3% of the time, Pallas kernels for 5%

profile of v2, /device:TPU:0, one launch (start us, length us, event | category | flops | bytes accessed | tf_op | source)
XLA Modules:
  0.0 86.9 jit_solution(3951898731302271375)
XLA Ops:
  0.0 1.2 %dynamic-slice_bitcast_fusion = bf16[2,256,512]{2,1,0:T(8,128)(2,1)S(1)} fusion(bf16[1,2,512,512]{3,2,1,0:T(8,128)(2,1)} %param.5, s32[]{:T(128)S(6)} %select_n.65), kind=kLoop, calls=%fused_computation.12 | loop fusion | bytes 1048580 | tf_op jit(solution)/shard_map/dynamic_slice | solution.py:31
  1.2 0.5 collective-permute-start
  1.7 4.0 %all-to-all-start = ((bf16[4,128,512]{2,1,0:T(8,128)(2,1)}), bf16[4,128,512]{2,1,0:T(8,128)(2,1)S(1)}, u32[]{:S(2)}, u32[]{:S(2)}) async-start(bf16[4,128,512]{2,1,0:T(8,128)(2,1)} %bitcast.27), calls=%async_computation | async-start | bytes 1048576 | tf_op jit(solution)/shard_map/all_to_all | solution.py:185
  5.7 0.0 collective-permute-done
  5.7 0.1 fusion.3
  5.9 9.1 %all-to-all-done.slots = bf16[4,128,512]{2,1,0:T(8,128)(2,1)S(1)} async-done(((bf16[4,128,512]{2,1,0:T(8,128)(2,1)}), bf16[4,128,512]{2,1,0:T(8,128)(2,1)S(1)}, u32[]{:S(2)}, u32[]{:S(2)}) %all-to-all-start) | async-done | bytes 524320 | tf_op jit(solution)/shard_map/all_to_all | solution.py:185
  15.0 0.0 collective-permute-start.1
  15.0 1.6 %shard_map.55.plan = s32[10]{0:T(128)S(1)} custom-call(s32[16]{0:T(128)S(1)} %copy-done.1, s32[9]{0:T(128)S(1)} %copy-done.2), custom_call_target="tpu_custom_call" | custom-call | tf_op jit(solution)/shard_map/pallas_call | solution.py:189
  16.6 0.1 collective-permute-start.10
  16.7 2.1 %collective-permute-start.11 = (bf16[128,512]{1,0:T(8,128)(2,1)S(1)}, bf16[128,512]{1,0:T(8,128)(2,1)S(1)}, u32[]{:S(2)}, u32[]{:S(2)}) collective-permute-start(bf16[128,512]{1,0:T(8,128)(2,1)S(1)} %get-tuple-element.33), channel_id=1, source_target_pairs={{0,16},{8,24},{16,0},{24,8},{1,17},{9,25},{17,1},{25,9},{2,18},{10... | collective-permute-start | bytes 393224 | tf_op jit(solution)/shard_map/ppermute | solution.py:20
  18.8 0.1 collective-permute-start.12
  18.9 0.6 shard_map.56
  19.5 1.8 %collective-permute-start.3 = (bf16[128,512]{1,0:T(8,128)(2,1)S(1)}, bf16[128,512]{1,0:T(8,128)(2,1)S(1)}, u32[]{:S(2)}, u32[]{:S(2)}) collective-permute-start(bf16[128,512]{1,0:T(8,128)(2,1)S(1)} %get-tuple-element.24), channel_id=1, source_target_pairs={{0,1},{1,0},{2,3},{3,2},{4,5},{5,4},{6,7},{7,6},{8,9},{9,8},{10,11... | collective-permute-start | bytes 393224 | tf_op jit(solution)/shard_map/ppermute | solution.py:20
  21.3 8.5 %collective-permute-done.1 = bf16[2,256,512]{2,1,0:T(8,128)(2,1)S(1)} collective-permute-done((bf16[2,256,512]{2,1,0:T(8,128)(2,1)S(1)}, bf16[2,256,512]{2,1,0:T(8,128)(2,1)S(1)}, u32[]{:S(2)}, u32[]{:S(2)}) %collective-permute-start.1) | collective-permute-done | bytes 524320 | tf_op jit(solution)/shard_map/ppermute | solution.py:20
  29.8 1.8 %collective-permute-start.4 = (bf16[128,512]{1,0:T(8,128)(2,1)S(1)}, bf16[128,512]{1,0:T(8,128)(2,1)S(1)}, u32[]{:S(2)}, u32[]{:S(2)}) collective-permute-start(bf16[128,512]{1,0:T(8,128)(2,1)S(1)} %get-tuple-element.25), channel_id=1, source_target_pairs={{0,2},{1,3},{2,0},{3,1},{4,6},{5,7},{6,4},{7,5},{8,10},{9,11},{10,... | collective-permute-start | bytes 393224 | tf_op jit(solution)/shard_map/ppermute | solution.py:20
  31.6 0.3 multiply_reduce_fusion
  31.9 1.4 %collective-permute-start.5 = (bf16[128,512]{1,0:T(8,128)(2,1)S(1)}, bf16[128,512]{1,0:T(8,128)(2,1)S(1)}, u32[]{:S(2)}, u32[]{:S(2)}) collective-permute-start(bf16[128,512]{1,0:T(8,128)(2,1)S(1)} %get-tuple-element.26), channel_id=1, source_target_pairs={{0,3},{1,2},{2,1},{3,0},{4,7},{5,6},{6,5},{7,4},{8,11},{9,10},{10,... | collective-permute-start | bytes 393224 | tf_op jit(solution)/shard_map/ppermute | solution.py:20
  33.3 0.0 collective-permute-done.11.refs_1_
  33.3 2.6 %collective-permute-start.6 = (bf16[128,512]{1,0:T(8,128)(2,1)S(1)}, bf16[128,512]{1,0:T(8,128)(2,1)S(1)}, u32[]{:S(2)}, u32[]{:S(2)}) collective-permute-start(bf16[128,512]{1,0:T(8,128)(2,1)S(1)} %get-tuple-element.27), channel_id=1, source_target_pairs={{0,4},{1,5},{2,6},{3,7},{4,0},{5,1},{6,2},{7,3},{8,12},{9,13},{10,... | collective-permute-start | bytes 393224 | tf_op jit(solution)/shard_map/ppermute | solution.py:20
  35.9 0.0 collective-permute-done.12.refs_2_
  35.9 0.7 collective-permute-start.7
  36.7 3.6 %collective-permute-start.8 = (bf16[128,512]{1,0:T(8,128)(2,1)S(1)}, bf16[128,512]{1,0:T(8,128)(2,1)S(1)}, u32[]{:S(2)}, u32[]{:S(2)}) collective-permute-start(bf16[128,512]{1,0:T(8,128)(2,1)S(1)} %get-tuple-element.29), channel_id=1, source_target_pairs={{0,6},{1,7},{2,4},{3,5},{4,2},{5,3},{6,0},{7,1},{8,14},{9,15},{10,... | collective-permute-start | bytes 393224 | tf_op jit(solution)/shard_map/ppermute | solution.py:20
  40.3 0.0 collective-permute-done.4.refs_2_
  40.3 0.7 collective-permute-start.9
  41.0 0.1 broadcast_in_dim.8.half_sq
  41.1 1.8 %shard_map.58.refs_8_ = bf16[8,528,128]{2,1,0:T(8,128)(2,1)} custom-call(s32[10]{0:T(128)S(1)} %shard_map.55.plan, bf16[1,1,512,512]{3,2,1,0:T(8,128)(2,1)S(1)} %copy-done, f32[2,128]{1,0:T(2,128)S(1)} %broadcast_in_dim.8.half_sq, bf16[128,512]{1,0:T(8,128)(2,1)S(1)} %collective-permute-done.10.refs_0_, ...), custom_call_target="tpu_custom_call" | custom-call | tf_op jit(solution)/shard_map/pallas_call | solution.py:221
  42.8 5.3 %all-to-all-start.1 = ((bf16[8,528,128]{2,1,0:T(8,128)(2,1)}), bf16[8,528,128]{2,1,0:T(8,128)(2,1)S(1)}, u32[]{:S(2)}, u32[]{:S(2)}) async-start(bf16[8,528,128]{2,1,0:T(8,128)(2,1)} %shard_map.58.refs_8_), calls=%async_computation.1 | async-start | bytes 2162688 | tf_op jit(solution)/shard_map/all_to_all | solution.py:229
  48.1 2.7 %collective-permute-done.6.refs_4_ = bf16[128,512]{1,0:T(8,128)(2,1)S(1)} collective-permute-done((bf16[128,512]{1,0:T(8,128)(2,1)S(1)}, bf16[128,512]{1,0:T(8,128)(2,1)S(1)}, u32[]{:S(2)}, u32[]{:S(2)}) %collective-permute-start.6) | collective-permute-done | bytes 131104 | tf_op jit(solution)/shard_map/ppermute | solution.py:20
  50.9 3.8 %collective-permute-done.7.refs_5_ = bf16[128,512]{1,0:T(8,128)(2,1)S(1)} collective-permute-done((bf16[128,512]{1,0:T(8,128)(2,1)S(1)}, bf16[128,512]{1,0:T(8,128)(2,1)S(1)}, u32[]{:S(2)}, u32[]{:S(2)}) %collective-permute-start.7) | collective-permute-done | bytes 131104 | tf_op jit(solution)/shard_map/ppermute | solution.py:20
  54.6 0.0 collective-permute-done.9.refs_7_
  54.6 0.6 shard_map.59
  55.3 4.0 %collective-permute-start.13 = (bf16[2,1,128,512]{3,2,0,1:T(8,128)(2,1)S(1)}, bf16[2,1,128,512]{3,2,0,1:T(8,128)(2,1)S(1)}, u32[]{:S(2)}, u32[]{:S(2)}) collective-permute-start(bf16[2,1,128,512]{3,2,0,1:T(8,128)(2,1)S(1)} %bitcast.25), channel_id=1, source_target_pairs={{0,16},{8,24},{16,0},{24,8},{1,17},{9,25},{17,1},{25,9},{2,18},{10... | collective-permute-start | bytes 786440 | tf_op jit(solution)/shard_map/ppermute | solution.py:20
  59.3 4.3 %collective-permute-done.13 = bf16[2,1,128,512]{3,2,0,1:T(8,128)(2,1)S(1)} collective-permute-done((bf16[2,1,128,512]{3,2,0,1:T(8,128)(2,1)S(1)}, bf16[2,1,128,512]{3,2,0,1:T(8,128)(2,1)S(1)}, u32[]{:S(2)}, u32[]{:S(2)}) %collective-permute-start.13) | collective-permute-done | bytes 262176 | tf_op jit(solution)/shard_map/ppermute | solution.py:20
  63.7 0.9 maximum_bitcast_fusion
  64.5 0.1 broadcast_select_fusion.1
  64.7 2.0 %collective-permute-done.14 = bf16[2,2,128,512]{3,2,0,1:T(8,128)(2,1)S(1)} collective-permute-done((bf16[2,2,128,512]{3,2,0,1:T(8,128)(2,1)}, bf16[2,2,128,512]{3,2,0,1:T(8,128)(2,1)S(1)}, u32[]{:S(2)}, u32[]{:S(2)}) %collective-permute-start.14) | collective-permute-done | bytes 524320 | tf_op jit(solution)/shard_map/ppermute | solution.py:20
  66.7 0.1 select_bitcast_fusion.1
  66.7 0.1 pad_maximum_fusion
  66.8 0.1 copy.6
  66.9 0.7 convolution_convert_fusion.right_prod
  67.6 13.8 %all-to-all-done.1.arrived = bf16[8,528,128]{2,1,0:T(8,128)(2,1)S(1)} async-done(((bf16[8,528,128]{2,1,0:T(8,128)(2,1)}), bf16[8,528,128]{2,1,0:T(8,128)(2,1)S(1)}, u32[]{:S(2)}, u32[]{:S(2)}) %all-to-all-start.1) | async-done | bytes 1081376 | tf_op jit(solution)/shard_map/all_to_all | solution.py:229
  81.4 1.0 %shard_map.60 = (f32[2,128,512]{2,1,0:T(8,128)S(1)}, f32[8,128]{1,0:T(8,128)S(1)}) custom-call(s32[10]{0:T(128)S(1)} %shard_map.55.plan, bf16[2,512,512]{2,1,0:T(8,128)(2,1)S(1)} %convolution_convert_fusion.right_prod, f32[2,128]{1,0:T(2,128)S(1)} %broadcast_in_dim.8.half_sq, bf16[8,528,128]{2,1,0:T(8,128)(2,1)S(1)} %all-to-all-done.1.arrived), custom_call_target="tpu_custom_call" | custom-call | tf_op jit(solution)/shard_map/pallas_call | solution.py:243
  82.4 0.1 collective-permute-start.17
  82.5 1.0 %collective-permute-start.16 = (f32[8,128]{1,0:T(8,128)S(1)}, f32[8,128]{1,0:T(8,128)S(1)}, u32[]{:S(2)}, u32[]{:S(2)}) collective-permute-start(f32[8,128]{1,0:T(8,128)S(1)} %get-tuple-element.36.refs_0_), channel_id=1, source_target_pairs={{0,16},{8,24},{16,0},{24,8},{1,17},{9,25},{17,1},{25,9},{2,18},{10... | collective-permute-start | bytes 12296 | tf_op jit(solution)/shard_map/ppermute | solution.py:20
  83.5 0.8 collective-permute-start.15
  84.3 1.2 %collective-permute-done.17.refs_3_ = f32[8,128]{1,0:T(8,128)S(1)} collective-permute-done((f32[8,128]{1,0:T(8,128)S(1)}, f32[8,128]{1,0:T(8,128)S(1)}, u32[]{:S(2)}, u32[]{:S(2)}) %collective-permute-start.17) | collective-permute-done | bytes 4128 | tf_op jit(solution)/shard_map/ppermute | solution.py:20
  85.5 0.7 collective-permute-done.16.refs_2_
  86.1 0.8 shard_map.61
  (19 shorter events, 0.1 us)
Async XLA Ops:
  0.0 5.7 %copy-start.3 = (bf16[1,2,512,512]{3,2,1,0:T(8,128)(2,1)S(1)}, bf16[1,2,512,512]{3,2,1,0:T(8,128)(2,1)}, u32[]{:S(2)}) copy-start(bf16[1,2,512,512]{3,2,1,0:T(8,128)(2,1)} %param.5) | copy-start | bytes 3145732
  1.2 4.6 %collective-permute-start = (bf16[2,256,512]{2,1,0:T(8,128)(2,1)S(1)}, bf16[2,256,512]{2,1,0:T(8,128)(2,1)S(1)}, u32[]{:S(2)}, u32[]{:S(2)}) collective-permute-start(bf16[2,256,512]{2,1,0:T(8,128)(2,1)S(1)} %dynamic-slice_bitcast_fusion), channel_id=1, source_target_pairs={{0,8},{8,0},{16,24},{24,16},{1,9},{9,1},{17,25},{25,17},{2,10},{10... | collective-permute-start | bytes 1572872 | tf_op jit(solution)/shard_map/ppermute | solution.py:20
  1.7 13.3 %copy-start.1 = (s32[16]{0:T(128)S(1)}, s32[16]{0:T(128)}, u32[]{:S(2)}) copy-start(s32[16]{0:T(128)} %lists.1) | copy-start | bytes 196
  1.7 13.3 %copy-start.2 = (s32[9]{0:T(128)S(1)}, s32[9]{0:T(128)}, u32[]{:S(2)}) copy-start(s32[9]{0:T(128)} %offsets.1) | copy-start | bytes 112
  1.7 14.9 %copy-start = (bf16[1,1,512,512]{3,2,1,0:T(8,128)(2,1)S(1)}, bf16[1,1,512,512]{3,2,1,0:T(8,128)(2,1)}, u32[]{:S(2)}) copy-start(bf16[1,1,512,512]{3,2,1,0:T(8,128)(2,1)} %factor.1) | copy-start | bytes 1572868
  1.7 13.3 %all-to-all-start = ((bf16[4,128,512]{2,1,0:T(8,128)(2,1)}), bf16[4,128,512]{2,1,0:T(8,128)(2,1)S(1)}, u32[]{:S(2)}, u32[]{:S(2)}) async-start(bf16[4,128,512]{2,1,0:T(8,128)(2,1)} %bitcast.27), calls=%async_computation | async-start | bytes 1048576 | tf_op jit(solution)/shard_map/all_to_all | solution.py:185
  15.0 14.8 %collective-permute-start.1 = (bf16[2,256,512]{2,1,0:T(8,128)(2,1)S(1)}, bf16[2,256,512]{2,1,0:T(8,128)(2,1)S(1)}, u32[]{:S(2)}, u32[]{:S(2)}) collective-permute-start(bf16[2,256,512]{2,1,0:T(8,128)(2,1)S(1)} %fusion.3), channel_id=1, source_target_pairs={{0,16},{8,24},{16,0},{24,8},{1,17},{9,25},{17,1},{25,9},{2,18},{10... | collective-permute-start | bytes 1572872 | tf_op jit(solution)/shard_map/ppermute | solution.py:20
  16.6 15.3 %collective-permute-start.10 = (bf16[128,512]{1,0:T(8,128)(2,1)S(1)}, bf16[128,512]{1,0:T(8,128)(2,1)S(1)}, u32[]{:S(2)}, u32[]{:S(2)}) collective-permute-start(bf16[128,512]{1,0:T(8,128)(2,1)S(1)} %get-tuple-element.32), channel_id=1, source_target_pairs={{0,8},{8,0},{16,24},{24,16},{1,9},{9,1},{17,25},{25,17},{2,10},{10... | collective-permute-start | bytes 393224 | tf_op jit(solution)/shard_map/ppermute | solution.py:20
  16.7 16.6 %collective-permute-start.11 = (bf16[128,512]{1,0:T(8,128)(2,1)S(1)}, bf16[128,512]{1,0:T(8,128)(2,1)S(1)}, u32[]{:S(2)}, u32[]{:S(2)}) collective-permute-start(bf16[128,512]{1,0:T(8,128)(2,1)S(1)} %get-tuple-element.33), channel_id=1, source_target_pairs={{0,16},{8,24},{16,0},{24,8},{1,17},{9,25},{17,1},{25,9},{2,18},{10... | collective-permute-start | bytes 393224 | tf_op jit(solution)/shard_map/ppermute | solution.py:20
  18.8 17.1 %collective-permute-start.12 = (bf16[128,512]{1,0:T(8,128)(2,1)S(1)}, bf16[128,512]{1,0:T(8,128)(2,1)S(1)}, u32[]{:S(2)}, u32[]{:S(2)}) collective-permute-start(bf16[128,512]{1,0:T(8,128)(2,1)S(1)} %get-tuple-element.34), channel_id=1, source_target_pairs={{0,24},{8,16},{16,8},{24,0},{1,25},{9,17},{17,9},{25,1},{2,26},{10... | collective-permute-start | bytes 393224 | tf_op jit(solution)/shard_map/ppermute | solution.py:20
  19.5 17.2 %collective-permute-start.3 = (bf16[128,512]{1,0:T(8,128)(2,1)S(1)}, bf16[128,512]{1,0:T(8,128)(2,1)S(1)}, u32[]{:S(2)}, u32[]{:S(2)}) collective-permute-start(bf16[128,512]{1,0:T(8,128)(2,1)S(1)} %get-tuple-element.24), channel_id=1, source_target_pairs={{0,1},{1,0},{2,3},{3,2},{4,5},{5,4},{6,7},{7,6},{8,9},{9,8},{10,11... | collective-permute-start | bytes 393224 | tf_op jit(solution)/shard_map/ppermute | solution.py:20
  29.8 10.5 %collective-permute-start.4 = (bf16[128,512]{1,0:T(8,128)(2,1)S(1)}, bf16[128,512]{1,0:T(8,128)(2,1)S(1)}, u32[]{:S(2)}, u32[]{:S(2)}) collective-permute-start(bf16[128,512]{1,0:T(8,128)(2,1)S(1)} %get-tuple-element.25), channel_id=1, source_target_pairs={{0,2},{1,3},{2,0},{3,1},{4,6},{5,7},{6,4},{7,5},{8,10},{9,11},{10,... | collective-permute-start | bytes 393224 | tf_op jit(solution)/shard_map/ppermute | solution.py:20
  31.9 16.2 %collective-permute-start.5 = (bf16[128,512]{1,0:T(8,128)(2,1)S(1)}, bf16[128,512]{1,0:T(8,128)(2,1)S(1)}, u32[]{:S(2)}, u32[]{:S(2)}) collective-permute-start(bf16[128,512]{1,0:T(8,128)(2,1)S(1)} %get-tuple-element.26), channel_id=1, source_target_pairs={{0,3},{1,2},{2,1},{3,0},{4,7},{5,6},{6,5},{7,4},{8,11},{9,10},{10,... | collective-permute-start | bytes 393224 | tf_op jit(solution)/shard_map/ppermute | solution.py:20
  33.3 17.5 %collective-permute-start.6 = (bf16[128,512]{1,0:T(8,128)(2,1)S(1)}, bf16[128,512]{1,0:T(8,128)(2,1)S(1)}, u32[]{:S(2)}, u32[]{:S(2)}) collective-permute-start(bf16[128,512]{1,0:T(8,128)(2,1)S(1)} %get-tuple-element.27), channel_id=1, source_target_pairs={{0,4},{1,5},{2,6},{3,7},{4,0},{5,1},{6,2},{7,3},{8,12},{9,13},{10,... | collective-permute-start | bytes 393224 | tf_op jit(solution)/shard_map/ppermute | solution.py:20
  35.9 18.7 %collective-permute-start.7 = (bf16[128,512]{1,0:T(8,128)(2,1)S(1)}, bf16[128,512]{1,0:T(8,128)(2,1)S(1)}, u32[]{:S(2)}, u32[]{:S(2)}) collective-permute-start(bf16[128,512]{1,0:T(8,128)(2,1)S(1)} %get-tuple-element.28), channel_id=1, source_target_pairs={{0,5},{1,4},{2,7},{3,6},{4,1},{5,0},{6,3},{7,2},{8,13},{9,12},{10,... | collective-permute-start | bytes 393224 | tf_op jit(solution)/shard_map/ppermute | solution.py:20
  36.7 17.9 %collective-permute-start.8 = (bf16[128,512]{1,0:T(8,128)(2,1)S(1)}, bf16[128,512]{1,0:T(8,128)(2,1)S(1)}, u32[]{:S(2)}, u32[]{:S(2)}) collective-permute-start(bf16[128,512]{1,0:T(8,128)(2,1)S(1)} %get-tuple-element.29), channel_id=1, source_target_pairs={{0,6},{1,7},{2,4},{3,5},{4,2},{5,3},{6,0},{7,1},{8,14},{9,15},{10,... | collective-permute-start | bytes 393224 | tf_op jit(solution)/shard_map/ppermute | solution.py:20
  40.3 14.3 %collective-permute-start.9 = (bf16[128,512]{1,0:T(8,128)(2,1)S(1)}, bf16[128,512]{1,0:T(8,128)(2,1)S(1)}, u32[]{:S(2)}, u32[]{:S(2)}) collective-permute-start(bf16[128,512]{1,0:T(8,128)(2,1)S(1)} %get-tuple-element.30), channel_id=1, source_target_pairs={{0,7},{1,6},{2,5},{3,4},{4,3},{5,2},{6,1},{7,0},{8,15},{9,14},{10,... | collective-permute-start | bytes 393224 | tf_op jit(solution)/shard_map/ppermute | solution.py:20
  42.8 38.6 %all-to-all-start.1 = ((bf16[8,528,128]{2,1,0:T(8,128)(2,1)}), bf16[8,528,128]{2,1,0:T(8,128)(2,1)S(1)}, u32[]{:S(2)}, u32[]{:S(2)}) async-start(bf16[8,528,128]{2,1,0:T(8,128)(2,1)} %shard_map.58.refs_8_), calls=%async_computation.1 | async-start | bytes 2162688 | tf_op jit(solution)/shard_map/all_to_all | solution.py:229
  55.3 8.4 %collective-permute-start.13 = (bf16[2,1,128,512]{3,2,0,1:T(8,128)(2,1)S(1)}, bf16[2,1,128,512]{3,2,0,1:T(8,128)(2,1)S(1)}, u32[]{:S(2)}, u32[]{:S(2)}) collective-permute-start(bf16[2,1,128,512]{3,2,0,1:T(8,128)(2,1)S(1)} %bitcast.25), channel_id=1, source_target_pairs={{0,16},{8,24},{16,0},{24,8},{1,17},{9,25},{17,1},{25,9},{2,18},{10... | collective-permute-start | bytes 786440 | tf_op jit(solution)/shard_map/ppermute | solution.py:20
  59.3 5.3 %collective-permute-start.2 = (bf16[2,256,512]{2,1,0:T(8,128)(2,1)S(1)}, bf16[2,256,512]{2,1,0:T(8,128)(2,1)S(1)}, u32[]{:S(2)}, u32[]{:S(2)}) collective-permute-start(bf16[2,256,512]{2,1,0:T(8,128)(2,1)S(1)} %get-tuple-element.38), channel_id=1, source_target_pairs={{0,8},{8,0},{16,24},{24,16},{1,9},{9,1},{17,25},{25,17},{2,10},{10... | collective-permute-start | bytes 1572872 | tf_op jit(solution)/shard_map/ppermute | solution.py:20
  64.5 2.1 %collective-permute-start.14 = (bf16[2,2,128,512]{3,2,0,1:T(8,128)(2,1)}, bf16[2,2,128,512]{3,2,0,1:T(8,128)(2,1)S(1)}, u32[]{:S(2)}, u32[]{:S(2)}) collective-permute-start(bf16[2,2,128,512]{3,2,0,1:T(8,128)(2,1)} %maximum_bitcast_fusion), channel_id=1, source_target_pairs={{0,8},{8,0},{16,24},{24,16},{1,9},{9,1},{17,25},{25,17},{2,10},{10... | collective-permute-start | bytes 1572872 | tf_op jit(solution)/shard_map/ppermute | solution.py:20
  82.4 3.1 %collective-permute-start.17 = (f32[8,128]{1,0:T(8,128)S(1)}, f32[8,128]{1,0:T(8,128)S(1)}, u32[]{:S(2)}, u32[]{:S(2)}) collective-permute-start(f32[8,128]{1,0:T(8,128)S(1)} %get-tuple-element.36.refs_0_), channel_id=1, source_target_pairs={{0,24},{8,16},{16,8},{24,0},{1,25},{9,17},{17,9},{25,1},{2,26},{10... | collective-permute-start | bytes 12296 | tf_op jit(solution)/shard_map/ppermute | solution.py:20
  82.5 3.7 %collective-permute-start.16 = (f32[8,128]{1,0:T(8,128)S(1)}, f32[8,128]{1,0:T(8,128)S(1)}, u32[]{:S(2)}, u32[]{:S(2)}) collective-permute-start(f32[8,128]{1,0:T(8,128)S(1)} %get-tuple-element.36.refs_0_), channel_id=1, source_target_pairs={{0,16},{8,24},{16,0},{24,8},{1,17},{9,25},{17,1},{25,9},{2,18},{10... | collective-permute-start | bytes 12296 | tf_op jit(solution)/shard_map/ppermute | solution.py:20
  83.5 2.6 %collective-permute-start.15 = (f32[8,128]{1,0:T(8,128)S(1)}, f32[8,128]{1,0:T(8,128)S(1)}, u32[]{:S(2)}, u32[]{:S(2)}) collective-permute-start(f32[8,128]{1,0:T(8,128)S(1)} %get-tuple-element.36.refs_0_), channel_id=1, source_target_pairs={{0,8},{8,0},{16,24},{24,16},{1,9},{9,1},{17,25},{25,17},{2,10},{10... | collective-permute-start | bytes 12296 | tf_op jit(solution)/shard_map/ppermute | solution.py:20

commit v3 on v2

--- a/solution.py
+++ b/solution.py
@@ -95,21 +95,9 @@
         outs[d][...] = slots[plan[column ^ d]]
 
 
-def split_kernel(dp_count, factor, *outs):
-    rows = outs[0].shape[0]
-    me = lax.axis_index("dp")
-    for d in range(1, dp_count):
-        outs[d - 1][...] = factor[0, 0, pl.ds(pl.multiple_of((me ^ d) * rows, rows), rows), :]
-
-
-def left_kernel(mp_count, dp_count, plan, factor, half_sq, *refs):
-    pieces, out, slots = refs[: dp_count - 1], refs[dp_count - 1], refs[dp_count]
-    rows, width = slots.shape[1:]
+def left_kernel(mp_count, plan, slots, half_sq, out):
+    rows = slots.shape[1]
     lanes = out.shape[2]
-    me = lax.axis_index("dp")
-    slots[me] = factor[0, 0, pl.ds(pl.multiple_of(me * rows, rows), rows), :]
-    for d in range(1, dp_count):
-        slots[me ^ d] = pieces[d - 1][...]
     total = jnp.sum(half_sq[...], axis=0, keepdims=True)
     first = total.astype(jnp.bfloat16).astype(jnp.float32)
     second = (total - first).astype(jnp.bfloat16).astype(jnp.float32)
@@ -119,7 +107,7 @@
     parts = parts.astype(jnp.bfloat16)
     for j in range(mp_count):
         slot = plan[j]
-        for c in range(width // lanes):
+        for c in range(slots.shape[2] // lanes):
             out[j, c * rows : (c + 1) * rows, :] = slots[slot, :, c * lanes : (c + 1) * lanes]
         out[j, out.shape[1] - 16 :, :] = parts
 
@@ -195,7 +183,7 @@
     )(owner_lists, owner_offsets)
     right_slots = over_dp(right_roots)
     total = core_sum(partial_blocks, dp_index)
-    right_slots, total, left_roots = lax.optimization_barrier((right_slots, total, left_roots))
+    right_slots, total, plan = lax.optimization_barrier((right_slots, total, plan))
     outgoing = pl.pallas_call(
         functools.partial(right_kernel, mp_count),
         out_shape=[piece] * mp_count,
@@ -203,14 +191,7 @@
         out_specs=[VMEM] * mp_count,
         compiler_params=params,
     )(plan, right_slots)
-    given = pl.pallas_call(
-        functools.partial(split_kernel, dp_count),
-        out_shape=[piece] * (dp_count - 1),
-        in_specs=[VMEM],
-        out_specs=[VMEM] * (dp_count - 1),
-        compiler_params=params,
-    )(left_roots)
-    taken = [swap(given[d - 1], "dp", d) for d in range(1, dp_count)]
+    left_slots = over_dp(left_roots)
     right_arrived = [outgoing[0]] + [swap(outgoing[d], "mp", d) for d in range(1, mp_count)]
     total = chip_sum(total, dp_count)
     total_f = total.astype(jnp.float32)
@@ -219,13 +200,12 @@
         (per_shard, lanes),
     )
     left_outgoing = pl.pallas_call(
-        functools.partial(left_kernel, mp_count, dp_count),
+        functools.partial(left_kernel, mp_count),
         out_shape=jax.ShapeDtypeStruct((mp_count, rows * width // lanes + 16, lanes), jnp.bfloat16),
-        in_specs=[SMEM, VMEM, VMEM] + [VMEM] * (dp_count - 1),
+        in_specs=[SMEM, VMEM, VMEM],
         out_specs=VMEM,
-        scratch_shapes=[pltpu.VMEM((dp_count, rows, width), jnp.bfloat16)],
-        compiler_params=params,
-    )(plan, left_roots, half_sq, *taken)
+        compiler_params=params,
+    )(plan, left_slots, half_sq)
     left_arrived = lax.all_to_all(left_outgoing, "mp", split_axis=0, concat_axis=0, tiled=True)
     right_rows = pl.pallas_call(
         functools.partial(pick_kernel, mp_count, per_shard),

time: 87.2 us -> 80.4 us (0.922)
  waiting for transfers between devices: 46 us -> 38.7 us
  starting transfers between devices: 30.7 us -> 29.3 us
  other arithmetic: 1.67 us -> 2.8 us
    ppermute x18 -> x15, waiting for transfers between devices: 23.1 us -> 15.3 us  [swap(): return lax.ppermute(value, axis, [(i, i ^ distance) for i in range(count)])]
    all_to_all x1 -> x2, starting transfers between devices: 4.03 us -> 7.37 us  [over_dp(): lax.all_to_all(factor[0, 0].reshape(dp_count, rows, width), 'dp', split_a...]
    ppermute x18 -> x15, starting transfers between devices: 21.4 us -> 18.4 us  [swap(): return lax.ppermute(value, axis, [(i, i ^ distance) for i in range(count)])]
    all_to_all x1, waiting for transfers between devices: 13.8 us -> 16 us  [shards(): lax.all_to_all(left_outgoing, 'mp', split_axis=0, concat_axis=0, tiled=True)]
    all_to_all x1, starting transfers between devices: 5.28 us -> 3.56 us  [shards(): lax.all_to_all(left_outgoing, 'mp', split_axis=0, concat_axis=0, tiled=True)]
    all_to_all x1 -> x2, waiting for transfers between devices: 9.09 us -> 7.47 us  [over_dp(): lax.all_to_all(factor[0, 0].reshape(dp_count, rows, width), 'dp', split_a...]
    reduce_sum x1, other arithmetic: 0.33 us -> 1.5 us  [shards(): jnp.sum(total_f * total_f, axis=(1, 2)) * (2 / dp_count)]
    pallas_call x2 -> x1, Pallas kernels: 1.8 us -> 1.72 us  [shards(): pl.pallas_call(functools.partial(left_kernel, mp_count), out_shape=jax.Sh...]
  transfers between devices with their start and end apart: 20 -> 18, of which waited for: 9 -> 8; matrix products, arithmetic and copies ran while one was open for 3% -> 5% of each run, Pallas kernels for 5% -> 6%
where the time goes in v3:
time: 80.4 us; the launch traced here: 80.1 us
  waiting for transfers between devices  38.7 us (48%)
  starting transfers between devices  29.3 us (36%)
  Pallas kernels  6.31 us (8%)
  other arithmetic  2.8 us (3%)
  local copies, waits for them, and re-layouts  2.12 us (3%)
    ppermute x15, starting transfers between devices, swap(): return lax.ppermute(value, axis, [(i, i ^ distance) for i in range(count)])  18.4 us
    all_to_all x1, waiting for transfers between devices, shards(): lax.all_to_all(left_outgoing, 'mp', split_axis=0, concat_axis=0, tiled=True)  16 us
    ppermute x15, waiting for transfers between devices, swap(): return lax.ppermute(value, axis, [(i, i ^ distance) for i in range(count)])  15.3 us
    all_to_all x2, waiting for transfers between devices, over_dp(): lax.all_to_all(factor[0, 0].reshape(dp_count, rows, width), 'dp', split_a...  7.47 us
    all_to_all x2, starting transfers between devices, over_dp(): lax.all_to_all(factor[0, 0].reshape(dp_count, rows, width), 'dp', split_a...  7.37 us
    all_to_all x1, starting transfers between devices, shards(): lax.all_to_all(left_outgoing, 'mp', split_axis=0, concat_axis=0, tiled=True)  3.56 us
    pallas_call x1, Pallas kernels, shards(): pl.pallas_call(functools.partial(left_kernel, mp_count), out_shape=jax.Sh...  1.72 us
  transfers between devices with their start and end apart: 18, of which 8 were waited for; matrix products, arithmetic and copies ran while one was open for 5% of the time, Pallas kernels for 6%

profile of v3, /device:TPU:0, one launch (start us, length us, event | category | flops | bytes accessed | tf_op | source)
XLA Modules:
  0.0 80.1 jit_solution(6273536073939524078)
XLA Ops:
  0.0 1.2 %dynamic-slice_bitcast_fusion = bf16[2,256,512]{2,1,0:T(8,128)(2,1)S(1)} fusion(bf16[1,2,512,512]{3,2,1,0:T(8,128)(2,1)} %param.5, s32[]{:T(128)S(6)} %select_n.64), kind=kLoop, calls=%fused_computation.12 | loop fusion | bytes 1048580 | tf_op jit(solution)/shard_map/dynamic_slice | solution.py:31
  1.2 0.5 collective-permute-start
  1.7 3.9 %all-to-all-start = ((bf16[4,128,512]{2,1,0:T(8,128)(2,1)}), bf16[4,128,512]{2,1,0:T(8,128)(2,1)S(1)}, u32[]{:S(2)}, u32[]{:S(2)}) async-start(bf16[4,128,512]{2,1,0:T(8,128)(2,1)} %bitcast.28), calls=%async_computation | async-start | bytes 1048576 | tf_op jit(solution)/shard_map/all_to_all | solution.py:173
  5.6 1.6 %shard_map.55.plan = s32[10]{0:T(128)S(1)} custom-call(s32[16]{0:T(128)S(1)} %copy-done, s32[9]{0:T(128)S(1)} %copy-done.1), custom_call_target="tpu_custom_call" | custom-call | tf_op jit(solution)/shard_map/pallas_call | solution.py:177
  7.2 0.0 collective-permute-done
  7.2 0.1 fusion.3
  7.4 7.5 %all-to-all-done.slots = bf16[4,128,512]{2,1,0:T(8,128)(2,1)S(1)} async-done(((bf16[4,128,512]{2,1,0:T(8,128)(2,1)}), bf16[4,128,512]{2,1,0:T(8,128)(2,1)S(1)}, u32[]{:S(2)}, u32[]{:S(2)}) %all-to-all-start) | async-done | bytes 524320 | tf_op jit(solution)/shard_map/all_to_all | solution.py:173
  14.9 3.5 %all-to-all-start.1 = ((bf16[4,128,512]{2,1,0:T(8,128)(2,1)}), bf16[4,128,512]{2,1,0:T(8,128)(2,1)S(1)}, u32[]{:S(2)}, u32[]{:S(2)}) async-start(bf16[4,128,512]{2,1,0:T(8,128)(2,1)} %bitcast.3), calls=%async_computation.1 | async-start | bytes 1048576 | tf_op jit(solution)/shard_map/all_to_all | solution.py:173
  18.3 0.6 shard_map.56
  19.0 2.1 %collective-permute-start.3 = (bf16[128,512]{1,0:T(8,128)(2,1)S(1)}, bf16[128,512]{1,0:T(8,128)(2,1)S(1)}, u32[]{:S(2)}, u32[]{:S(2)}) collective-permute-start(bf16[128,512]{1,0:T(8,128)(2,1)S(1)} %get-tuple-element.22), channel_id=1, source_target_pairs={{0,1},{1,0},{2,3},{3,2},{4,5},{5,4},{6,7},{7,6},{8,9},{9,8},{10,11... | collective-permute-start | bytes 393224 | tf_op jit(solution)/shard_map/ppermute | solution.py:20
  21.1 1.6 %collective-permute-start.4 = (bf16[128,512]{1,0:T(8,128)(2,1)S(1)}, bf16[128,512]{1,0:T(8,128)(2,1)S(1)}, u32[]{:S(2)}, u32[]{:S(2)}) collective-permute-start(bf16[128,512]{1,0:T(8,128)(2,1)S(1)} %get-tuple-element.23), channel_id=1, source_target_pairs={{0,2},{1,3},{2,0},{3,1},{4,6},{5,7},{6,4},{7,5},{8,10},{9,11},{10,... | collective-permute-start | bytes 393224 | tf_op jit(solution)/shard_map/ppermute | solution.py:20
  22.6 3.0 %collective-permute-start.6 = (bf16[128,512]{1,0:T(8,128)(2,1)S(1)}, bf16[128,512]{1,0:T(8,128)(2,1)S(1)}, u32[]{:S(2)}, u32[]{:S(2)}) collective-permute-start(bf16[128,512]{1,0:T(8,128)(2,1)S(1)} %get-tuple-element.25), channel_id=1, source_target_pairs={{0,4},{1,5},{2,6},{3,7},{4,0},{5,1},{6,2},{7,3},{8,12},{9,13},{10,... | collective-permute-start | bytes 393224 | tf_op jit(solution)/shard_map/ppermute | solution.py:20
  25.6 4.0 %collective-permute-done.1 = bf16[2,256,512]{2,1,0:T(8,128)(2,1)S(1)} collective-permute-done((bf16[2,256,512]{2,1,0:T(8,128)(2,1)S(1)}, bf16[2,256,512]{2,1,0:T(8,128)(2,1)S(1)}, u32[]{:S(2)}, u32[]{:S(2)}) %collective-permute-start.1) | collective-permute-done | bytes 524320 | tf_op jit(solution)/shard_map/ppermute | solution.py:20
  29.7 0.8 %copy-done.4 = bf16[2,256,512]{2,1,0:T(8,128)(2,1)} copy-done((bf16[2,256,512]{2,1,0:T(8,128)(2,1)}, bf16[2,256,512]{2,1,0:T(8,128)(2,1)S(1)}, u32[]{:S(2)}) %copy-start.4) | copy-done | bytes 524312
  30.5 3.7 %collective-permute-start.7 = (bf16[128,512]{1,0:T(8,128)(2,1)S(1)}, bf16[128,512]{1,0:T(8,128)(2,1)S(1)}, u32[]{:S(2)}, u32[]{:S(2)}) collective-permute-start(bf16[128,512]{1,0:T(8,128)(2,1)S(1)} %get-tuple-element.26), channel_id=1, source_target_pairs={{0,5},{1,4},{2,7},{3,6},{4,1},{5,0},{6,3},{7,2},{8,13},{9,12},{10,... | collective-permute-start | bytes 393224 | tf_op jit(solution)/shard_map/ppermute | solution.py:20
  34.2 1.5 %multiply_reduce_fusion = (f32[2]{0:T(128)S(1)}, bf16[2,256,512]{2,1,0:T(8,128)(2,1)S(1)}) fusion(bf16[2,256,512]{2,1,0:T(8,128)(2,1)} %copy-done.4, bf16[2,256,512]{2,1,0:T(8,128)(2,1)} %copy-done.2), kind=kLoop, calls=%fused_computation.7 | loop fusion | flops 1835006 | bytes 1572872 | tf_op jit(solution)/shard_map/reduce_sum | solution.py:199
  35.7 0.0 collective-permute-done.3.refs_1_
  35.7 1.4 %collective-permute-start.8 = (bf16[128,512]{1,0:T(8,128)(2,1)S(1)}, bf16[128,512]{1,0:T(8,128)(2,1)S(1)}, u32[]{:S(2)}, u32[]{:S(2)}) collective-permute-start(bf16[128,512]{1,0:T(8,128)(2,1)S(1)} %get-tuple-element.27), channel_id=1, source_target_pairs={{0,6},{1,7},{2,4},{3,5},{4,2},{5,3},{6,0},{7,1},{8,14},{9,15},{10,... | collective-permute-start | bytes 393224 | tf_op jit(solution)/shard_map/ppermute | solution.py:20
  37.1 0.0 collective-permute-done.4.refs_2_
  37.1 2.4 %collective-permute-start.9 = (bf16[128,512]{1,0:T(8,128)(2,1)S(1)}, bf16[128,512]{1,0:T(8,128)(2,1)S(1)}, u32[]{:S(2)}, u32[]{:S(2)}) collective-permute-start(bf16[128,512]{1,0:T(8,128)(2,1)S(1)} %get-tuple-element.28), channel_id=1, source_target_pairs={{0,7},{1,6},{2,5},{3,4},{4,3},{5,2},{6,1},{7,0},{8,15},{9,14},{10,... | collective-permute-start | bytes 393224 | tf_op jit(solution)/shard_map/ppermute | solution.py:20
  39.5 0.0 all-to-all-done.1.slots
  39.5 0.1 broadcast_in_dim.8.half_sq
  39.6 1.7 %shard_map.57.refs_8_ = bf16[8,528,128]{2,1,0:T(8,128)(2,1)} custom-call(s32[10]{0:T(128)S(1)} %shard_map.55.plan, bf16[4,128,512]{2,1,0:T(8,128)(2,1)S(1)} %all-to-all-done.1.slots, f32[2,128]{1,0:T(2,128)S(1)} %broadcast_in_dim.8.half_sq), custom_call_target="tpu_custom_call" | custom-call | tf_op jit(solution)/shard_map/pallas_call | solution.py:202
  41.3 3.6 %all-to-all-start.2 = ((bf16[8,528,128]{2,1,0:T(8,128)(2,1)}), bf16[8,528,128]{2,1,0:T(8,128)(2,1)S(1)}, u32[]{:S(2)}, u32[]{:S(2)}) async-start(bf16[8,528,128]{2,1,0:T(8,128)(2,1)} %shard_map.57.refs_8_), calls=%async_computation.2 | async-start | bytes 2162688 | tf_op jit(solution)/shard_map/all_to_all | solution.py:209
  44.9 0.0 collective-permute-done.6.refs_4_
  44.9 0.7 collective-permute-done.7.refs_5_
  45.7 0.0 collective-permute-done.8.refs_6_
  45.7 0.0 collective-permute-done.9.refs_7_
  45.7 0.6 shard_map.58
  46.3 1.7 %collective-permute-start.10 = (bf16[2,1,128,512]{3,2,0,1:T(8,128)(2,1)S(1)}, bf16[2,1,128,512]{3,2,0,1:T(8,128)(2,1)S(1)}, u32[]{:S(2)}, u32[]{:S(2)}) collective-permute-start(bf16[2,1,128,512]{3,2,0,1:T(8,128)(2,1)S(1)} %bitcast.26), channel_id=1, source_target_pairs={{0,16},{8,24},{16,0},{24,8},{1,17},{9,25},{17,1},{25,9},{2,18},{10... | collective-permute-start | bytes 786440 | tf_op jit(solution)/shard_map/ppermute | solution.py:20
  48.0 0.0 collective-permute-start.2
  48.0 6.3 %collective-permute-done.10 = bf16[2,1,128,512]{3,2,0,1:T(8,128)(2,1)S(1)} collective-permute-done((bf16[2,1,128,512]{3,2,0,1:T(8,128)(2,1)S(1)}, bf16[2,1,128,512]{3,2,0,1:T(8,128)(2,1)S(1)}, u32[]{:S(2)}, u32[]{:S(2)}) %collective-permute-start.10) | collective-permute-done | bytes 262176 | tf_op jit(solution)/shard_map/ppermute | solution.py:20
  54.4 0.9 %maximum_bitcast_fusion = bf16[2,2,128,512]{3,2,0,1:T(8,128)(2,1)} fusion(bf16[2,1,1,128,512]{4,3,0,2,1:T(8,128)(2,1)S(1)} %get-tuple-element.38, bf16[2,1,1,128,512]{4,3,0,2,1:T(8,128)(2,1)S(1)} %get-tuple-element.37), kind=kLoop, calls=%fused_computation.9 | loop fusion | flops 262144 | bytes 1048576 | tf_op jit(solution)/shard_map/reshape | solution.py:61
  55.3 0.0 collective-permute-done.2
  55.3 0.1 broadcast_select_fusion.1
  55.3 2.0 %collective-permute-done.11 = bf16[2,2,128,512]{3,2,0,1:T(8,128)(2,1)S(1)} collective-permute-done((bf16[2,2,128,512]{3,2,0,1:T(8,128)(2,1)}, bf16[2,2,128,512]{3,2,0,1:T(8,128)(2,1)S(1)}, u32[]{:S(2)}, u32[]{:S(2)}) %collective-permute-start.11) | collective-permute-done | bytes 524320 | tf_op jit(solution)/shard_map/ppermute | solution.py:20
  57.4 0.1 select_bitcast_fusion.1
  57.5 0.1 pad_maximum_fusion
  57.6 0.1 copy.6
  57.6 0.7 convolution_convert_fusion.right_prod
  58.4 16.0 %all-to-all-done.2.arrived = bf16[8,528,128]{2,1,0:T(8,128)(2,1)S(1)} async-done(((bf16[8,528,128]{2,1,0:T(8,128)(2,1)}), bf16[8,528,128]{2,1,0:T(8,128)(2,1)S(1)}, u32[]{:S(2)}, u32[]{:S(2)}) %all-to-all-start.2) | async-done | bytes 1081376 | tf_op jit(solution)/shard_map/all_to_all | solution.py:209
  74.3 0.9 %shard_map.59 = (f32[2,128,512]{2,1,0:T(8,128)S(1)}, f32[8,128]{1,0:T(8,128)S(1)}) custom-call(s32[10]{0:T(128)S(1)} %shard_map.55.plan, bf16[2,512,512]{2,1,0:T(8,128)(2,1)S(1)} %convolution_convert_fusion.right_prod, f32[2,128]{1,0:T(2,128)S(1)} %broadcast_in_dim.8.half_sq, bf16[8,528,128]{2,1,0:T(8,128)(2,1)S(1)} %all-to-all-done.2.arrived), custom_call_target="tpu_custom_call" | custom-call | tf_op jit(solution)/shard_map/pallas_call | solution.py:223
  75.3 0.4 collective-permute-start.14
  75.7 1.0 %collective-permute-start.13 = (f32[8,128]{1,0:T(8,128)S(1)}, f32[8,128]{1,0:T(8,128)S(1)}, u32[]{:S(2)}, u32[]{:S(2)}) collective-permute-start(f32[8,128]{1,0:T(8,128)S(1)} %get-tuple-element.30.refs_0_), channel_id=1, source_target_pairs={{0,16},{8,24},{16,0},{24,8},{1,17},{9,25},{17,1},{25,9},{2,18},{10... | collective-permute-start | bytes 12296 | tf_op jit(solution)/shard_map/ppermute | solution.py:20
  76.6 0.5 collective-permute-start.12
  77.2 1.2 %collective-permute-done.14.refs_3_ = f32[8,128]{1,0:T(8,128)S(1)} collective-permute-done((f32[8,128]{1,0:T(8,128)S(1)}, f32[8,128]{1,0:T(8,128)S(1)}, u32[]{:S(2)}, u32[]{:S(2)}) %collective-permute-start.14) | collective-permute-done | bytes 4128 | tf_op jit(solution)/shard_map/ppermute | solution.py:20
  78.4 1.0 %collective-permute-done.13.refs_2_ = f32[8,128]{1,0:T(8,128)S(1)} collective-permute-done((f32[8,128]{1,0:T(8,128)S(1)}, f32[8,128]{1,0:T(8,128)S(1)}, u32[]{:S(2)}, u32[]{:S(2)}) %collective-permute-start.13) | collective-permute-done | bytes 4128 | tf_op jit(solution)/shard_map/ppermute | solution.py:20
  79.3 0.8 shard_map.60
  (16 shorter events, 0.1 us)
Async XLA Ops:
  0.0 7.2 %copy-start.3 = (bf16[1,2,512,512]{3,2,1,0:T(8,128)(2,1)S(1)}, bf16[1,2,512,512]{3,2,1,0:T(8,128)(2,1)}, u32[]{:S(2)}) copy-start(bf16[1,2,512,512]{3,2,1,0:T(8,128)(2,1)} %param.5) | copy-start | bytes 3145732
  0.0 5.6 %copy-start.1 = (s32[9]{0:T(128)S(1)}, s32[9]{0:T(128)}, u32[]{:S(2)}) copy-start(s32[9]{0:T(128)} %offsets.1) | copy-start | bytes 112
  0.0 5.6 %copy-start = (s32[16]{0:T(128)S(1)}, s32[16]{0:T(128)}, u32[]{:S(2)}) copy-start(s32[16]{0:T(128)} %lists.1) | copy-start | bytes 196
  1.2 6.0 %collective-permute-start = (bf16[2,256,512]{2,1,0:T(8,128)(2,1)S(1)}, bf16[2,256,512]{2,1,0:T(8,128)(2,1)S(1)}, u32[]{:S(2)}, u32[]{:S(2)}) collective-permute-start(bf16[2,256,512]{2,1,0:T(8,128)(2,1)S(1)} %dynamic-slice_bitcast_fusion), channel_id=1, source_target_pairs={{0,8},{8,0},{16,24},{24,16},{1,9},{9,1},{17,25},{25,17},{2,10},{10... | collective-permute-start | bytes 1572872 | tf_op jit(solution)/shard_map/ppermute | solution.py:20
  1.7 13.1 %all-to-all-start = ((bf16[4,128,512]{2,1,0:T(8,128)(2,1)}), bf16[4,128,512]{2,1,0:T(8,128)(2,1)S(1)}, u32[]{:S(2)}, u32[]{:S(2)}) async-start(bf16[4,128,512]{2,1,0:T(8,128)(2,1)} %bitcast.28), calls=%async_computation | async-start | bytes 1048576 | tf_op jit(solution)/shard_map/all_to_all | solution.py:173
  7.4 22.3 %copy-start.2 = (bf16[2,256,512]{2,1,0:T(8,128)(2,1)}, bf16[2,256,512]{2,1,0:T(8,128)(2,1)S(1)}, u32[]{:S(2)}) copy-start(bf16[2,256,512]{2,1,0:T(8,128)(2,1)S(1)} %fusion.3) | copy-start | bytes 1572868
  14.9 14.8 %collective-permute-start.1 = (bf16[2,256,512]{2,1,0:T(8,128)(2,1)S(1)}, bf16[2,256,512]{2,1,0:T(8,128)(2,1)S(1)}, u32[]{:S(2)}, u32[]{:S(2)}) collective-permute-start(bf16[2,256,512]{2,1,0:T(8,128)(2,1)S(1)} %fusion.3), channel_id=1, source_target_pairs={{0,16},{8,24},{16,0},{24,8},{1,17},{9,25},{17,1},{25,9},{2,18},{10... | collective-permute-start | bytes 1572872 | tf_op jit(solution)/shard_map/ppermute | solution.py:20
  14.9 24.7 %all-to-all-start.1 = ((bf16[4,128,512]{2,1,0:T(8,128)(2,1)}), bf16[4,128,512]{2,1,0:T(8,128)(2,1)S(1)}, u32[]{:S(2)}, u32[]{:S(2)}) async-start(bf16[4,128,512]{2,1,0:T(8,128)(2,1)} %bitcast.3), calls=%async_computation.1 | async-start | bytes 1048576 | tf_op jit(solution)/shard_map/all_to_all | solution.py:173
  19.0 16.7 %collective-permute-start.3 = (bf16[128,512]{1,0:T(8,128)(2,1)S(1)}, bf16[128,512]{1,0:T(8,128)(2,1)S(1)}, u32[]{:S(2)}, u32[]{:S(2)}) collective-permute-start(bf16[128,512]{1,0:T(8,128)(2,1)S(1)} %get-tuple-element.22), channel_id=1, source_target_pairs={{0,1},{1,0},{2,3},{3,2},{4,5},{5,4},{6,7},{7,6},{8,9},{9,8},{10,11... | collective-permute-start | bytes 393224 | tf_op jit(solution)/shard_map/ppermute | solution.py:20
  21.1 16.0 %collective-permute-start.4 = (bf16[128,512]{1,0:T(8,128)(2,1)S(1)}, bf16[128,512]{1,0:T(8,128)(2,1)S(1)}, u32[]{:S(2)}, u32[]{:S(2)}) collective-permute-start(bf16[128,512]{1,0:T(8,128)(2,1)S(1)} %get-tuple-element.23), channel_id=1, source_target_pairs={{0,2},{1,3},{2,0},{3,1},{4,6},{5,7},{6,4},{7,5},{8,10},{9,11},{10,... | collective-permute-start | bytes 393224 | tf_op jit(solution)/shard_map/ppermute | solution.py:20
  22.6 22.3 %collective-permute-start.5 = (bf16[128,512]{1,0:T(8,128)(2,1)S(1)}, bf16[128,512]{1,0:T(8,128)(2,1)S(1)}, u32[]{:S(2)}, u32[]{:S(2)}) collective-permute-start(bf16[128,512]{1,0:T(8,128)(2,1)S(1)} %get-tuple-element.24), channel_id=1, source_target_pairs={{0,3},{1,2},{2,1},{3,0},{4,7},{5,6},{6,5},{7,4},{8,11},{9,10},{10,... | collective-permute-start | bytes 393224 | tf_op jit(solution)/shard_map/ppermute | solution.py:20
  22.6 22.3 %collective-permute-start.6 = (bf16[128,512]{1,0:T(8,128)(2,1)S(1)}, bf16[128,512]{1,0:T(8,128)(2,1)S(1)}, u32[]{:S(2)}, u32[]{:S(2)}) collective-permute-start(bf16[128,512]{1,0:T(8,128)(2,1)S(1)} %get-tuple-element.25), channel_id=1, source_target_pairs={{0,4},{1,5},{2,6},{3,7},{4,0},{5,1},{6,2},{7,3},{8,12},{9,13},{10,... | collective-permute-start | bytes 393224 | tf_op jit(solution)/shard_map/ppermute | solution.py:20
  29.7 0.8 %copy-start.4 = (bf16[2,256,512]{2,1,0:T(8,128)(2,1)}, bf16[2,256,512]{2,1,0:T(8,128)(2,1)S(1)}, u32[]{:S(2)}) copy-start(bf16[2,256,512]{2,1,0:T(8,128)(2,1)S(1)} %collective-permute-done.1) | copy-start | bytes 1572868
  30.5 15.2 %collective-permute-start.7 = (bf16[128,512]{1,0:T(8,128)(2,1)S(1)}, bf16[128,512]{1,0:T(8,128)(2,1)S(1)}, u32[]{:S(2)}, u32[]{:S(2)}) collective-permute-start(bf16[128,512]{1,0:T(8,128)(2,1)S(1)} %get-tuple-element.26), channel_id=1, source_target_pairs={{0,5},{1,4},{2,7},{3,6},{4,1},{5,0},{6,3},{7,2},{8,13},{9,12},{10,... | collective-permute-start | bytes 393224 | tf_op jit(solution)/shard_map/ppermute | solution.py:20
  35.7 10.0 %collective-permute-start.8 = (bf16[128,512]{1,0:T(8,128)(2,1)S(1)}, bf16[128,512]{1,0:T(8,128)(2,1)S(1)}, u32[]{:S(2)}, u32[]{:S(2)}) collective-permute-start(bf16[128,512]{1,0:T(8,128)(2,1)S(1)} %get-tuple-element.27), channel_id=1, source_target_pairs={{0,6},{1,7},{2,4},{3,5},{4,2},{5,3},{6,0},{7,1},{8,14},{9,15},{10,... | collective-permute-start | bytes 393224 | tf_op jit(solution)/shard_map/ppermute | solution.py:20
  37.1 8.6 %collective-permute-start.9 = (bf16[128,512]{1,0:T(8,128)(2,1)S(1)}, bf16[128,512]{1,0:T(8,128)(2,1)S(1)}, u32[]{:S(2)}, u32[]{:S(2)}) collective-permute-start(bf16[128,512]{1,0:T(8,128)(2,1)S(1)} %get-tuple-element.28), channel_id=1, source_target_pairs={{0,7},{1,6},{2,5},{3,4},{4,3},{5,2},{6,1},{7,0},{8,15},{9,14},{10,... | collective-permute-start | bytes 393224 | tf_op jit(solution)/shard_map/ppermute | solution.py:20
  41.3 33.0 %all-to-all-start.2 = ((bf16[8,528,128]{2,1,0:T(8,128)(2,1)}), bf16[8,528,128]{2,1,0:T(8,128)(2,1)S(1)}, u32[]{:S(2)}, u32[]{:S(2)}) async-start(bf16[8,528,128]{2,1,0:T(8,128)(2,1)} %shard_map.57.refs_8_), calls=%async_computation.2 | async-start | bytes 2162688 | tf_op jit(solution)/shard_map/all_to_all | solution.py:209
  46.3 8.0 %collective-permute-start.10 = (bf16[2,1,128,512]{3,2,0,1:T(8,128)(2,1)S(1)}, bf16[2,1,128,512]{3,2,0,1:T(8,128)(2,1)S(1)}, u32[]{:S(2)}, u32[]{:S(2)}) collective-permute-start(bf16[2,1,128,512]{3,2,0,1:T(8,128)(2,1)S(1)} %bitcast.26), channel_id=1, source_target_pairs={{0,16},{8,24},{16,0},{24,8},{1,17},{9,25},{17,1},{25,9},{2,18},{10... | collective-permute-start | bytes 786440 | tf_op jit(solution)/shard_map/ppermute | solution.py:20
  48.0 7.2 %collective-permute-start.2 = (bf16[2,256,512]{2,1,0:T(8,128)(2,1)S(1)}, bf16[2,256,512]{2,1,0:T(8,128)(2,1)S(1)}, u32[]{:S(2)}, u32[]{:S(2)}) collective-permute-start(bf16[2,256,512]{2,1,0:T(8,128)(2,1)S(1)} %get-tuple-element.32), channel_id=1, source_target_pairs={{0,8},{8,0},{16,24},{24,16},{1,9},{9,1},{17,25},{25,17},{2,10},{10... | collective-permute-start | bytes 1572872 | tf_op jit(solution)/shard_map/ppermute | solution.py:20
  55.3 2.1 %collective-permute-start.11 = (bf16[2,2,128,512]{3,2,0,1:T(8,128)(2,1)}, bf16[2,2,128,512]{3,2,0,1:T(8,128)(2,1)S(1)}, u32[]{:S(2)}, u32[]{:S(2)}) collective-permute-start(bf16[2,2,128,512]{3,2,0,1:T(8,128)(2,1)} %maximum_bitcast_fusion), channel_id=1, source_target_pairs={{0,8},{8,0},{16,24},{24,16},{1,9},{9,1},{17,25},{25,17},{2,10},{10... | collective-permute-start | bytes 1572872 | tf_op jit(solution)/shard_map/ppermute | solution.py:20
  75.3 3.1 %collective-permute-start.14 = (f32[8,128]{1,0:T(8,128)S(1)}, f32[8,128]{1,0:T(8,128)S(1)}, u32[]{:S(2)}, u32[]{:S(2)}) collective-permute-start(f32[8,128]{1,0:T(8,128)S(1)} %get-tuple-element.30.refs_0_), channel_id=1, source_target_pairs={{0,24},{8,16},{16,8},{24,0},{1,25},{9,17},{17,9},{25,1},{2,26},{10... | collective-permute-start | bytes 12296 | tf_op jit(solution)/shard_map/ppermute | solution.py:20
  75.7 3.6 %collective-permute-start.13 = (f32[8,128]{1,0:T(8,128)S(1)}, f32[8,128]{1,0:T(8,128)S(1)}, u32[]{:S(2)}, u32[]{:S(2)}) collective-permute-start(f32[8,128]{1,0:T(8,128)S(1)} %get-tuple-element.30.refs_0_), channel_id=1, source_target_pairs={{0,16},{8,24},{16,0},{24,8},{1,17},{9,25},{17,1},{25,9},{2,18},{10... | collective-permute-start | bytes 12296 | tf_op jit(solution)/shard_map/ppermute | solution.py:20
  76.6 2.7 %collective-permute-start.12 = (f32[8,128]{1,0:T(8,128)S(1)}, f32[8,128]{1,0:T(8,128)S(1)}, u32[]{:S(2)}, u32[]{:S(2)}) collective-permute-start(f32[8,128]{1,0:T(8,128)S(1)} %get-tuple-element.30.refs_0_), channel_id=1, source_target_pairs={{0,8},{8,0},{16,24},{24,16},{1,9},{9,1},{17,25},{25,17},{2,10},{10... | collective-permute-start | bytes 12296 | tf_op jit(solution)/shard_map/ppermute | solution.py:20

commit v4 on v3

--- a/solution.py
+++ b/solution.py
@@ -112,8 +112,8 @@
         out[j, out.shape[1] - 16 :, :] = parts
 
 
-def pick_kernel(mp_count, per_shard, plan, *refs):
-    arrived, out = refs[:mp_count], refs[-1]
+def pick_kernel(mp_count, per_shard, order, plan, *refs):
+    arrived, out = dict(zip(order, refs)), refs[-1]
     shard = lax.axis_index("mp")
     for r in range(per_shard):
         source = plan[mp_count + r] ^ shard
@@ -192,7 +192,9 @@
         compiler_params=params,
     )(plan, right_slots)
     left_slots = over_dp(left_roots)
-    right_arrived = [outgoing[0]] + [swap(outgoing[d], "mp", d) for d in range(1, mp_count)]
+    far = mp_count // 2
+    order = [1, far, *range(2, far), *range(far + 1, mp_count)]
+    right_arrived = [outgoing[0]] + [swap(outgoing[d], "mp", d) for d in order]
     total = chip_sum(total, dp_count)
     total_f = total.astype(jnp.float32)
     half_sq = jnp.broadcast_to(
@@ -208,7 +210,7 @@
     )(plan, left_slots, half_sq)
     left_arrived = lax.all_to_all(left_outgoing, "mp", split_axis=0, concat_axis=0, tiled=True)
     right_rows = pl.pallas_call(
-        functools.partial(pick_kernel, mp_count, per_shard),
+        functools.partial(pick_kernel, mp_count, per_shard, [0] + order),
         out_shape=jax.ShapeDtypeStruct((per_shard, rows, width), jnp.bfloat16),
         in_specs=[SMEM] + [VMEM] * mp_count + [ANY],
         out_specs=VMEM,

time: 80.4 us -> 79.1 us (0.984)
    ppermute x15, waiting for transfers between devices: 15.3 us -> 13.6 us  [swap(): return lax.ppermute(value, axis, [(i, i ^ distance) for i in range(count)])]
    all_to_all x1, waiting for transfers between devices: 16 us -> 17 us  [shards(): lax.all_to_all(left_outgoing, 'mp', split_axis=0, concat_axis=0, tiled=True)]
where the time goes in v4:
time: 79.1 us; the launch traced here: 78.8 us
  waiting for transfers between devices  38.1 us (48%)
  starting transfers between devices  28.6 us (36%)
  Pallas kernels  6.32 us (8%)
  other arithmetic  2.8 us (4%)
  local copies, waits for them, and re-layouts  2.12 us (3%)
    ppermute x15, starting transfers between devices, swap(): return lax.ppermute(value, axis, [(i, i ^ distance) for i in range(count)])  17.7 us
    all_to_all x1, waiting for transfers between devices, shards(): lax.all_to_all(left_outgoing, 'mp', split_axis=0, concat_axis=0, tiled=True)  17 us
    ppermute x15, waiting for transfers between devices, swap(): return lax.ppermute(value, axis, [(i, i ^ distance) for i in range(count)])  13.6 us
    all_to_all x2, waiting for transfers between devices, over_dp(): lax.all_to_all(factor[0, 0].reshape(dp_count, rows, width), 'dp', split_a...  7.46 us
    all_to_all x2, starting transfers between devices, over_dp(): lax.all_to_all(factor[0, 0].reshape(dp_count, rows, width), 'dp', split_a...  7.37 us
    all_to_all x1, starting transfers between devices, shards(): lax.all_to_all(left_outgoing, 'mp', split_axis=0, concat_axis=0, tiled=True)  3.56 us
    pallas_call x1, Pallas kernels, shards(): pl.pallas_call(functools.partial(left_kernel, mp_count), out_shape=jax.Sh...  1.72 us
    pallas_call x1, Pallas kernels, shards(): pl.pallas_call(functools.partial(plan_kernel, mp_count, per_shard), out_s...  1.6 us
  transfers between devices with their start and end apart: 18, of which 8 were waited for; matrix products, arithmetic and copies ran while one was open for 5% of the time, Pallas kernels for 6%

profile of v4, /device:TPU:0, one launch (start us, length us, event | category | flops | bytes accessed | tf_op | source)
XLA Modules:
  0.0 78.8 jit_solution(11720834755571945738)
XLA Ops:
  0.0 1.2 %dynamic-slice_bitcast_fusion = bf16[2,256,512]{2,1,0:T(8,128)(2,1)S(1)} fusion(bf16[1,2,512,512]{3,2,1,0:T(8,128)(2,1)} %param.5, s32[]{:T(128)S(6)} %select_n.64), kind=kLoop, calls=%fused_computation.12 | loop fusion | bytes 1048580 | tf_op jit(solution)/shard_map/dynamic_slice | solution.py:31
  1.2 0.5 collective-permute-start
  1.7 3.9 %all-to-all-start = ((bf16[4,128,512]{2,1,0:T(8,128)(2,1)}), bf16[4,128,512]{2,1,0:T(8,128)(2,1)S(1)}, u32[]{:S(2)}, u32[]{:S(2)}) async-start(bf16[4,128,512]{2,1,0:T(8,128)(2,1)} %bitcast.28), calls=%async_computation | async-start | bytes 1048576 | tf_op jit(solution)/shard_map/all_to_all | solution.py:173
  5.6 1.6 %shard_map.55.plan = s32[10]{0:T(128)S(1)} custom-call(s32[16]{0:T(128)S(1)} %copy-done, s32[9]{0:T(128)S(1)} %copy-done.1), custom_call_target="tpu_custom_call" | custom-call | tf_op jit(solution)/shard_map/pallas_call | solution.py:177
  7.2 0.0 collective-permute-done
  7.2 0.1 fusion.3
  7.4 7.5 %all-to-all-done.slots = bf16[4,128,512]{2,1,0:T(8,128)(2,1)S(1)} async-done(((bf16[4,128,512]{2,1,0:T(8,128)(2,1)}), bf16[4,128,512]{2,1,0:T(8,128)(2,1)S(1)}, u32[]{:S(2)}, u32[]{:S(2)}) %all-to-all-start) | async-done | bytes 524320 | tf_op jit(solution)/shard_map/all_to_all | solution.py:173
  14.9 0.0 collective-permute-start.1
  14.9 3.5 %all-to-all-start.1 = ((bf16[4,128,512]{2,1,0:T(8,128)(2,1)}), bf16[4,128,512]{2,1,0:T(8,128)(2,1)S(1)}, u32[]{:S(2)}, u32[]{:S(2)}) async-start(bf16[4,128,512]{2,1,0:T(8,128)(2,1)} %bitcast.3), calls=%async_computation.1 | async-start | bytes 1048576 | tf_op jit(solution)/shard_map/all_to_all | solution.py:173
  18.3 0.6 shard_map.56
  19.0 2.1 %collective-permute-start.3 = (bf16[128,512]{1,0:T(8,128)(2,1)S(1)}, bf16[128,512]{1,0:T(8,128)(2,1)S(1)}, u32[]{:S(2)}, u32[]{:S(2)}) collective-permute-start(bf16[128,512]{1,0:T(8,128)(2,1)S(1)} %get-tuple-element.22), channel_id=1, source_target_pairs={{0,1},{1,0},{2,3},{3,2},{4,5},{5,4},{6,7},{7,6},{8,9},{9,8},{10,11... | collective-permute-start | bytes 393224 | tf_op jit(solution)/shard_map/ppermute | solution.py:20
  21.1 2.6 %collective-permute-start.4 = (bf16[128,512]{1,0:T(8,128)(2,1)S(1)}, bf16[128,512]{1,0:T(8,128)(2,1)S(1)}, u32[]{:S(2)}, u32[]{:S(2)}) collective-permute-start(bf16[128,512]{1,0:T(8,128)(2,1)S(1)} %get-tuple-element.23), channel_id=1, source_target_pairs={{0,4},{1,5},{2,6},{3,7},{4,0},{5,1},{6,2},{7,3},{8,12},{9,13},{10,... | collective-permute-start | bytes 393224 | tf_op jit(solution)/shard_map/ppermute | solution.py:20
  23.6 1.6 %collective-permute-start.5 = (bf16[128,512]{1,0:T(8,128)(2,1)S(1)}, bf16[128,512]{1,0:T(8,128)(2,1)S(1)}, u32[]{:S(2)}, u32[]{:S(2)}) collective-permute-start(bf16[128,512]{1,0:T(8,128)(2,1)S(1)} %get-tuple-element.24), channel_id=1, source_target_pairs={{0,2},{1,3},{2,0},{3,1},{4,6},{5,7},{6,4},{7,5},{8,10},{9,11},{10,... | collective-permute-start | bytes 393224 | tf_op jit(solution)/shard_map/ppermute | solution.py:20
  25.2 0.4 collective-permute-start.6
  25.6 4.0 %collective-permute-done.1 = bf16[2,256,512]{2,1,0:T(8,128)(2,1)S(1)} collective-permute-done((bf16[2,256,512]{2,1,0:T(8,128)(2,1)S(1)}, bf16[2,256,512]{2,1,0:T(8,128)(2,1)S(1)}, u32[]{:S(2)}, u32[]{:S(2)}) %collective-permute-start.1) | collective-permute-done | bytes 524320 | tf_op jit(solution)/shard_map/ppermute | solution.py:20
  29.7 0.8 %copy-done.4 = bf16[2,256,512]{2,1,0:T(8,128)(2,1)} copy-done((bf16[2,256,512]{2,1,0:T(8,128)(2,1)}, bf16[2,256,512]{2,1,0:T(8,128)(2,1)S(1)}, u32[]{:S(2)}) %copy-start.4) | copy-done | bytes 524312
  30.5 3.7 %collective-permute-start.7 = (bf16[128,512]{1,0:T(8,128)(2,1)S(1)}, bf16[128,512]{1,0:T(8,128)(2,1)S(1)}, u32[]{:S(2)}, u32[]{:S(2)}) collective-permute-start(bf16[128,512]{1,0:T(8,128)(2,1)S(1)} %get-tuple-element.26), channel_id=1, source_target_pairs={{0,5},{1,4},{2,7},{3,6},{4,1},{5,0},{6,3},{7,2},{8,13},{9,12},{10,... | collective-permute-start | bytes 393224 | tf_op jit(solution)/shard_map/ppermute | solution.py:20
  34.2 1.5 %multiply_reduce_fusion = (f32[2]{0:T(128)S(1)}, bf16[2,256,512]{2,1,0:T(8,128)(2,1)S(1)}) fusion(bf16[2,256,512]{2,1,0:T(8,128)(2,1)} %copy-done.4, bf16[2,256,512]{2,1,0:T(8,128)(2,1)} %copy-done.2), kind=kLoop, calls=%fused_computation.7 | loop fusion | flops 1835006 | bytes 1572872 | tf_op jit(solution)/shard_map/reduce_sum | solution.py:201
  35.7 1.4 %collective-permute-start.8 = (bf16[128,512]{1,0:T(8,128)(2,1)S(1)}, bf16[128,512]{1,0:T(8,128)(2,1)S(1)}, u32[]{:S(2)}, u32[]{:S(2)}) collective-permute-start(bf16[128,512]{1,0:T(8,128)(2,1)S(1)} %get-tuple-element.27), channel_id=1, source_target_pairs={{0,6},{1,7},{2,4},{3,5},{4,2},{5,3},{6,0},{7,1},{8,14},{9,15},{10,... | collective-permute-start | bytes 393224 | tf_op jit(solution)/shard_map/ppermute | solution.py:20
  37.1 2.4 %collective-permute-start.9 = (bf16[128,512]{1,0:T(8,128)(2,1)S(1)}, bf16[128,512]{1,0:T(8,128)(2,1)S(1)}, u32[]{:S(2)}, u32[]{:S(2)}) collective-permute-start(bf16[128,512]{1,0:T(8,128)(2,1)S(1)} %get-tuple-element.28), channel_id=1, source_target_pairs={{0,7},{1,6},{2,5},{3,4},{4,3},{5,2},{6,1},{7,0},{8,15},{9,14},{10,... | collective-permute-start | bytes 393224 | tf_op jit(solution)/shard_map/ppermute | solution.py:20
  39.5 0.0 all-to-all-done.1.slots
  39.5 0.1 broadcast_in_dim.8.half_sq
  39.6 1.7 %shard_map.57.refs_8_ = bf16[8,528,128]{2,1,0:T(8,128)(2,1)} custom-call(s32[10]{0:T(128)S(1)} %shard_map.55.plan, bf16[4,128,512]{2,1,0:T(8,128)(2,1)S(1)} %all-to-all-done.1.slots, f32[2,128]{1,0:T(2,128)S(1)} %broadcast_in_dim.8.half_sq), custom_call_target="tpu_custom_call" | custom-call | tf_op jit(solution)/shard_map/pallas_call | solution.py:204
  41.3 3.6 %all-to-all-start.2 = ((bf16[8,528,128]{2,1,0:T(8,128)(2,1)}), bf16[8,528,128]{2,1,0:T(8,128)(2,1)S(1)}, u32[]{:S(2)}, u32[]{:S(2)}) async-start(bf16[8,528,128]{2,1,0:T(8,128)(2,1)} %shard_map.57.refs_8_), calls=%async_computation.2 | async-start | bytes 2162688 | tf_op jit(solution)/shard_map/all_to_all | solution.py:211
  44.9 0.0 collective-permute-done.6.refs_4_
  44.9 0.2 collective-permute-done.7.refs_5_
  45.2 0.0 collective-permute-done.8.refs_6_
  45.2 0.0 collective-permute-done.9.refs_7_
  45.2 0.6 shard_map.58
  45.8 1.0 %collective-permute-start.10 = (bf16[2,1,128,512]{3,2,0,1:T(8,128)(2,1)S(1)}, bf16[2,1,128,512]{3,2,0,1:T(8,128)(2,1)S(1)}, u32[]{:S(2)}, u32[]{:S(2)}) collective-permute-start(bf16[2,1,128,512]{3,2,0,1:T(8,128)(2,1)S(1)} %bitcast.26), channel_id=1, source_target_pairs={{0,16},{8,24},{16,0},{24,8},{1,17},{9,25},{17,1},{25,9},{2,18},{10... | collective-permute-start | bytes 786440 | tf_op jit(solution)/shard_map/ppermute | solution.py:20
  46.8 5.4 %collective-permute-done.10 = bf16[2,1,128,512]{3,2,0,1:T(8,128)(2,1)S(1)} collective-permute-done((bf16[2,1,128,512]{3,2,0,1:T(8,128)(2,1)S(1)}, bf16[2,1,128,512]{3,2,0,1:T(8,128)(2,1)S(1)}, u32[]{:S(2)}, u32[]{:S(2)}) %collective-permute-start.10) | collective-permute-done | bytes 262176 | tf_op jit(solution)/shard_map/ppermute | solution.py:20
  52.3 0.9 %maximum_bitcast_fusion = bf16[2,2,128,512]{3,2,0,1:T(8,128)(2,1)} fusion(bf16[2,1,1,128,512]{4,3,0,2,1:T(8,128)(2,1)S(1)} %get-tuple-element.38, bf16[2,1,1,128,512]{4,3,0,2,1:T(8,128)(2,1)S(1)} %get-tuple-element.37), kind=kLoop, calls=%fused_computation.9 | loop fusion | flops 262144 | bytes 1048576 | tf_op jit(solution)/shard_map/reshape | solution.py:61
  53.1 0.0 collective-permute-start.11
  53.2 0.0 collective-permute-done.2
  53.2 0.1 broadcast_select_fusion.1
  53.2 2.0 %collective-permute-done.11 = bf16[2,2,128,512]{3,2,0,1:T(8,128)(2,1)S(1)} collective-permute-done((bf16[2,2,128,512]{3,2,0,1:T(8,128)(2,1)}, bf16[2,2,128,512]{3,2,0,1:T(8,128)(2,1)S(1)}, u32[]{:S(2)}, u32[]{:S(2)}) %collective-permute-start.11) | collective-permute-done | bytes 524320 | tf_op jit(solution)/shard_map/ppermute | solution.py:20
  55.3 0.1 select_bitcast_fusion.1
  55.3 0.1 pad_maximum_fusion
  55.5 0.1 copy.6
  55.5 0.7 convolution_convert_fusion.right_prod
  56.2 17.0 %all-to-all-done.2.arrived = bf16[8,528,128]{2,1,0:T(8,128)(2,1)S(1)} async-done(((bf16[8,528,128]{2,1,0:T(8,128)(2,1)}), bf16[8,528,128]{2,1,0:T(8,128)(2,1)S(1)}, u32[]{:S(2)}, u32[]{:S(2)}) %all-to-all-start.2) | async-done | bytes 1081376 | tf_op jit(solution)/shard_map/all_to_all | solution.py:211
  73.3 0.9 %shard_map.59 = (f32[2,128,512]{2,1,0:T(8,128)S(1)}, f32[8,128]{1,0:T(8,128)S(1)}) custom-call(s32[10]{0:T(128)S(1)} %shard_map.55.plan, bf16[2,512,512]{2,1,0:T(8,128)(2,1)S(1)} %convolution_convert_fusion.right_prod, f32[2,128]{1,0:T(2,128)S(1)} %broadcast_in_dim.8.half_sq, bf16[8,528,128]{2,1,0:T(8,128)(2,1)S(1)} %all-to-all-done.2.arrived), custom_call_target="tpu_custom_call" | custom-call | tf_op jit(solution)/shard_map/pallas_call | solution.py:225
  74.2 0.1 collective-permute-start.14
  74.3 1.0 %collective-permute-start.13 = (f32[8,128]{1,0:T(8,128)S(1)}, f32[8,128]{1,0:T(8,128)S(1)}, u32[]{:S(2)}, u32[]{:S(2)}) collective-permute-start(f32[8,128]{1,0:T(8,128)S(1)} %get-tuple-element.30.refs_0_), channel_id=1, source_target_pairs={{0,16},{8,24},{16,0},{24,8},{1,17},{9,25},{17,1},{25,9},{2,18},{10... | collective-permute-start | bytes 12296 | tf_op jit(solution)/shard_map/ppermute | solution.py:20
  75.4 0.8 %collective-permute-start.12 = (f32[8,128]{1,0:T(8,128)S(1)}, f32[8,128]{1,0:T(8,128)S(1)}, u32[]{:S(2)}, u32[]{:S(2)}) collective-permute-start(f32[8,128]{1,0:T(8,128)S(1)} %get-tuple-element.30.refs_0_), channel_id=1, source_target_pairs={{0,8},{8,0},{16,24},{24,16},{1,9},{9,1},{17,25},{25,17},{2,10},{10... | collective-permute-start | bytes 12296 | tf_op jit(solution)/shard_map/ppermute | solution.py:20
  76.2 1.2 %collective-permute-done.14.refs_3_ = f32[8,128]{1,0:T(8,128)S(1)} collective-permute-done((f32[8,128]{1,0:T(8,128)S(1)}, f32[8,128]{1,0:T(8,128)S(1)}, u32[]{:S(2)}, u32[]{:S(2)}) %collective-permute-start.14) | collective-permute-done | bytes 4128 | tf_op jit(solution)/shard_map/ppermute | solution.py:20
  77.3 0.7 collective-permute-done.13.refs_2_
  78.0 0.8 %shard_map.60 = bf16[2,128,512]{2,1,0:T(8,128)(2,1)} custom-call(f32[2,128,512]{2,1,0:T(8,128)S(1)} %get-tuple-element.29.precond, f32[8,128]{1,0:T(8,128)S(1)} %get-tuple-element.30.refs_0_, f32[8,128]{1,0:T(8,128)S(1)} %collective-permute-done.12.refs_1_, f32[8,128]{1,0:T(8,128)S(1)} %collective-permute-done.13.refs_2_, ...), custom_call_target="tpu_custom_call" | custom-call | tf_op jit(solution)/shard_map/pallas_call | solution.py:237
  (16 shorter events, 0.1 us)
Async XLA Ops:
  0.0 7.2 %copy-start.3 = (bf16[1,2,512,512]{3,2,1,0:T(8,128)(2,1)S(1)}, bf16[1,2,512,512]{3,2,1,0:T(8,128)(2,1)}, u32[]{:S(2)}) copy-start(bf16[1,2,512,512]{3,2,1,0:T(8,128)(2,1)} %param.5) | copy-start | bytes 3145732
  0.0 5.6 %copy-start.1 = (s32[9]{0:T(128)S(1)}, s32[9]{0:T(128)}, u32[]{:S(2)}) copy-start(s32[9]{0:T(128)} %offsets.1) | copy-start | bytes 112
  0.0 5.6 %copy-start = (s32[16]{0:T(128)S(1)}, s32[16]{0:T(128)}, u32[]{:S(2)}) copy-start(s32[16]{0:T(128)} %lists.1) | copy-start | bytes 196
  1.2 6.1 %collective-permute-start = (bf16[2,256,512]{2,1,0:T(8,128)(2,1)S(1)}, bf16[2,256,512]{2,1,0:T(8,128)(2,1)S(1)}, u32[]{:S(2)}, u32[]{:S(2)}) collective-permute-start(bf16[2,256,512]{2,1,0:T(8,128)(2,1)S(1)} %dynamic-slice_bitcast_fusion), channel_id=1, source_target_pairs={{0,8},{8,0},{16,24},{24,16},{1,9},{9,1},{17,25},{25,17},{2,10},{10... | collective-permute-start | bytes 1572872 | tf_op jit(solution)/shard_map/ppermute | solution.py:20
  1.7 13.1 %all-to-all-start = ((bf16[4,128,512]{2,1,0:T(8,128)(2,1)}), bf16[4,128,512]{2,1,0:T(8,128)(2,1)S(1)}, u32[]{:S(2)}, u32[]{:S(2)}) async-start(bf16[4,128,512]{2,1,0:T(8,128)(2,1)} %bitcast.28), calls=%async_computation | async-start | bytes 1048576 | tf_op jit(solution)/shard_map/all_to_all | solution.py:173
  7.4 22.3 %copy-start.2 = (bf16[2,256,512]{2,1,0:T(8,128)(2,1)}, bf16[2,256,512]{2,1,0:T(8,128)(2,1)S(1)}, u32[]{:S(2)}) copy-start(bf16[2,256,512]{2,1,0:T(8,128)(2,1)S(1)} %fusion.3) | copy-start | bytes 1572868
  14.9 14.8 %collective-permute-start.1 = (bf16[2,256,512]{2,1,0:T(8,128)(2,1)S(1)}, bf16[2,256,512]{2,1,0:T(8,128)(2,1)S(1)}, u32[]{:S(2)}, u32[]{:S(2)}) collective-permute-start(bf16[2,256,512]{2,1,0:T(8,128)(2,1)S(1)} %fusion.3), channel_id=1, source_target_pairs={{0,16},{8,24},{16,0},{24,8},{1,17},{9,25},{17,1},{25,9},{2,18},{10... | collective-permute-start | bytes 1572872 | tf_op jit(solution)/shard_map/ppermute | solution.py:20
  14.9 24.7 %all-to-all-start.1 = ((bf16[4,128,512]{2,1,0:T(8,128)(2,1)}), bf16[4,128,512]{2,1,0:T(8,128)(2,1)S(1)}, u32[]{:S(2)}, u32[]{:S(2)}) async-start(bf16[4,128,512]{2,1,0:T(8,128)(2,1)} %bitcast.3), calls=%async_computation.1 | async-start | bytes 1048576 | tf_op jit(solution)/shard_map/all_to_all | solution.py:173
  19.0 16.7 %collective-permute-start.3 = (bf16[128,512]{1,0:T(8,128)(2,1)S(1)}, bf16[128,512]{1,0:T(8,128)(2,1)S(1)}, u32[]{:S(2)}, u32[]{:S(2)}) collective-permute-start(bf16[128,512]{1,0:T(8,128)(2,1)S(1)} %get-tuple-element.22), channel_id=1, source_target_pairs={{0,1},{1,0},{2,3},{3,2},{4,5},{5,4},{6,7},{7,6},{8,9},{9,8},{10,11... | collective-permute-start | bytes 393224 | tf_op jit(solution)/shard_map/ppermute | solution.py:20
  21.1 16.0 %collective-permute-start.4 = (bf16[128,512]{1,0:T(8,128)(2,1)S(1)}, bf16[128,512]{1,0:T(8,128)(2,1)S(1)}, u32[]{:S(2)}, u32[]{:S(2)}) collective-permute-start(bf16[128,512]{1,0:T(8,128)(2,1)S(1)} %get-tuple-element.23), channel_id=1, source_target_pairs={{0,4},{1,5},{2,6},{3,7},{4,0},{5,1},{6,2},{7,3},{8,12},{9,13},{10,... | collective-permute-start | bytes 393224 | tf_op jit(solution)/shard_map/ppermute | solution.py:20
  23.6 21.3 %collective-permute-start.5 = (bf16[128,512]{1,0:T(8,128)(2,1)S(1)}, bf16[128,512]{1,0:T(8,128)(2,1)S(1)}, u32[]{:S(2)}, u32[]{:S(2)}) collective-permute-start(bf16[128,512]{1,0:T(8,128)(2,1)S(1)} %get-tuple-element.24), channel_id=1, source_target_pairs={{0,2},{1,3},{2,0},{3,1},{4,6},{5,7},{6,4},{7,5},{8,10},{9,11},{10,... | collective-permute-start | bytes 393224 | tf_op jit(solution)/shard_map/ppermute | solution.py:20
  25.2 19.7 %collective-permute-start.6 = (bf16[128,512]{1,0:T(8,128)(2,1)S(1)}, bf16[128,512]{1,0:T(8,128)(2,1)S(1)}, u32[]{:S(2)}, u32[]{:S(2)}) collective-permute-start(bf16[128,512]{1,0:T(8,128)(2,1)S(1)} %get-tuple-element.25), channel_id=1, source_target_pairs={{0,3},{1,2},{2,1},{3,0},{4,7},{5,6},{6,5},{7,4},{8,11},{9,10},{10,... | collective-permute-start | bytes 393224 | tf_op jit(solution)/shard_map/ppermute | solution.py:20
  29.7 0.8 %copy-start.4 = (bf16[2,256,512]{2,1,0:T(8,128)(2,1)}, bf16[2,256,512]{2,1,0:T(8,128)(2,1)S(1)}, u32[]{:S(2)}) copy-start(bf16[2,256,512]{2,1,0:T(8,128)(2,1)S(1)} %collective-permute-done.1) | copy-start | bytes 1572868
  30.5 14.7 %collective-permute-start.7 = (bf16[128,512]{1,0:T(8,128)(2,1)S(1)}, bf16[128,512]{1,0:T(8,128)(2,1)S(1)}, u32[]{:S(2)}, u32[]{:S(2)}) collective-permute-start(bf16[128,512]{1,0:T(8,128)(2,1)S(1)} %get-tuple-element.26), channel_id=1, source_target_pairs={{0,5},{1,4},{2,7},{3,6},{4,1},{5,0},{6,3},{7,2},{8,13},{9,12},{10,... | collective-permute-start | bytes 393224 | tf_op jit(solution)/shard_map/ppermute | solution.py:20
  35.7 9.5 %collective-permute-start.8 = (bf16[128,512]{1,0:T(8,128)(2,1)S(1)}, bf16[128,512]{1,0:T(8,128)(2,1)S(1)}, u32[]{:S(2)}, u32[]{:S(2)}) collective-permute-start(bf16[128,512]{1,0:T(8,128)(2,1)S(1)} %get-tuple-element.27), channel_id=1, source_target_pairs={{0,6},{1,7},{2,4},{3,5},{4,2},{5,3},{6,0},{7,1},{8,14},{9,15},{10,... | collective-permute-start | bytes 393224 | tf_op jit(solution)/shard_map/ppermute | solution.py:20
  37.1 8.1 %collective-permute-start.9 = (bf16[128,512]{1,0:T(8,128)(2,1)S(1)}, bf16[128,512]{1,0:T(8,128)(2,1)S(1)}, u32[]{:S(2)}, u32[]{:S(2)}) collective-permute-start(bf16[128,512]{1,0:T(8,128)(2,1)S(1)} %get-tuple-element.28), channel_id=1, source_target_pairs={{0,7},{1,6},{2,5},{3,4},{4,3},{5,2},{6,1},{7,0},{8,15},{9,14},{10,... | collective-permute-start | bytes 393224 | tf_op jit(solution)/shard_map/ppermute | solution.py:20
  41.3 32.0 %all-to-all-start.2 = ((bf16[8,528,128]{2,1,0:T(8,128)(2,1)}), bf16[8,528,128]{2,1,0:T(8,128)(2,1)S(1)}, u32[]{:S(2)}, u32[]{:S(2)}) async-start(bf16[8,528,128]{2,1,0:T(8,128)(2,1)} %shard_map.57.refs_8_), calls=%async_computation.2 | async-start | bytes 2162688 | tf_op jit(solution)/shard_map/all_to_all | solution.py:211
  45.8 6.4 %collective-permute-start.10 = (bf16[2,1,128,512]{3,2,0,1:T(8,128)(2,1)S(1)}, bf16[2,1,128,512]{3,2,0,1:T(8,128)(2,1)S(1)}, u32[]{:S(2)}, u32[]{:S(2)}) collective-permute-start(bf16[2,1,128,512]{3,2,0,1:T(8,128)(2,1)S(1)} %bitcast.26), channel_id=1, source_target_pairs={{0,16},{8,24},{16,0},{24,8},{1,17},{9,25},{17,1},{25,9},{2,18},{10... | collective-permute-start | bytes 786440 | tf_op jit(solution)/shard_map/ppermute | solution.py:20
  46.8 6.4 %collective-permute-start.2 = (bf16[2,256,512]{2,1,0:T(8,128)(2,1)S(1)}, bf16[2,256,512]{2,1,0:T(8,128)(2,1)S(1)}, u32[]{:S(2)}, u32[]{:S(2)}) collective-permute-start(bf16[2,256,512]{2,1,0:T(8,128)(2,1)S(1)} %get-tuple-element.32), channel_id=1, source_target_pairs={{0,8},{8,0},{16,24},{24,16},{1,9},{9,1},{17,25},{25,17},{2,10},{10... | collective-permute-start | bytes 1572872 | tf_op jit(solution)/shard_map/ppermute | solution.py:20
  53.1 2.1 %collective-permute-start.11 = (bf16[2,2,128,512]{3,2,0,1:T(8,128)(2,1)}, bf16[2,2,128,512]{3,2,0,1:T(8,128)(2,1)S(1)}, u32[]{:S(2)}, u32[]{:S(2)}) collective-permute-start(bf16[2,2,128,512]{3,2,0,1:T(8,128)(2,1)} %maximum_bitcast_fusion), channel_id=1, source_target_pairs={{0,8},{8,0},{16,24},{24,16},{1,9},{9,1},{17,25},{25,17},{2,10},{10... | collective-permute-start | bytes 1572872 | tf_op jit(solution)/shard_map/ppermute | solution.py:20
  74.2 3.1 %collective-permute-start.14 = (f32[8,128]{1,0:T(8,128)S(1)}, f32[8,128]{1,0:T(8,128)S(1)}, u32[]{:S(2)}, u32[]{:S(2)}) collective-permute-start(f32[8,128]{1,0:T(8,128)S(1)} %get-tuple-element.30.refs_0_), channel_id=1, source_target_pairs={{0,24},{8,16},{16,8},{24,0},{1,25},{9,17},{17,9},{25,1},{2,26},{10... | collective-permute-start | bytes 12296 | tf_op jit(solution)/shard_map/ppermute | solution.py:20
  74.3 3.7 %collective-permute-start.13 = (f32[8,128]{1,0:T(8,128)S(1)}, f32[8,128]{1,0:T(8,128)S(1)}, u32[]{:S(2)}, u32[]{:S(2)}) collective-permute-start(f32[8,128]{1,0:T(8,128)S(1)} %get-tuple-element.30.refs_0_), channel_id=1, source_target_pairs={{0,16},{8,24},{16,0},{24,8},{1,17},{9,25},{17,1},{25,9},{2,18},{10... | collective-permute-start | bytes 12296 | tf_op jit(solution)/shard_map/ppermute | solution.py:20
  75.4 2.6 %collective-permute-start.12 = (f32[8,128]{1,0:T(8,128)S(1)}, f32[8,128]{1,0:T(8,128)S(1)}, u32[]{:S(2)}, u32[]{:S(2)}) collective-permute-start(f32[8,128]{1,0:T(8,128)S(1)} %get-tuple-element.30.refs_0_), channel_id=1, source_target_pairs={{0,8},{8,0},{16,24},{24,16},{1,9},{9,1},{17,25},{25,17},{2,10},{10... | collective-permute-start | bytes 12296 | tf_op jit(solution)/shard_map/ppermute | solution.py:20

commit v5 on v4

--- a/solution.py
+++ b/solution.py
@@ -32,20 +32,29 @@
     return add_rounded(kept, swap(given, "dp", 1))
 
 
-def chip_sum(total, dp_count):
+def chip_sum(total, dp_count, dp_index):
     distance = 2
     while distance < dp_count:
-        total = add_rounded(total, swap(total, "dp", distance))
+        part = total.shape[1] // 2
+        bit = (dp_index // distance) % 2
+        kept = lax.dynamic_slice_in_dim(total, bit * part, part, axis=1)
+        given = lax.dynamic_slice_in_dim(total, (1 - bit) * part, part, axis=1)
+        total = add_rounded(kept, swap(given, "dp", distance))
         distance *= 2
     return total
 
 
-def both_halves(total, dp_index):
-    core = dp_index % 2
-    other = swap(total, "dp", 1)
-    low = jnp.where(core == 0, total, other)
-    high = jnp.where(core == 0, other, total)
-    return jnp.concatenate([low, high], axis=1)
+def whole_rows(total, dp_count, dp_index):
+    part = total.shape[1]
+    whole = jnp.zeros((total.shape[0], part * dp_count, total.shape[2]), total.dtype)
+    for d in range(dp_count):
+        piece = swap(total, "dp", d) if d else total
+        holder, place, distance = dp_index ^ d, 0, 1
+        while distance < dp_count:
+            place = 2 * place + (holder // distance) % 2
+            distance *= 2
+        whole = lax.dynamic_update_slice_in_dim(whole, piece, place * part, axis=1)
+    return whole
 
 
 def gather_rows(rows, dp_count, dp_index):
@@ -195,10 +204,10 @@
     far = mp_count // 2
     order = [1, far, *range(2, far), *range(far + 1, mp_count)]
     right_arrived = [outgoing[0]] + [swap(outgoing[d], "mp", d) for d in order]
-    total = chip_sum(total, dp_count)
+    total = chip_sum(total, dp_count, dp_index)
     total_f = total.astype(jnp.float32)
     half_sq = jnp.broadcast_to(
-        (jnp.sum(total_f * total_f, axis=(1, 2)) * (2 / dp_count)).reshape(per_shard, 1),
+        jnp.sum(total_f * total_f, axis=(1, 2)).reshape(per_shard, 1),
         (per_shard, lanes),
     )
     left_outgoing = pl.pallas_call(
@@ -218,7 +227,7 @@
     )(plan, *right_arrived, left_outgoing)
     right = gather_rows(right_rows, dp_count, dp_index)
 
-    grad = both_halves(total, dp_index)
+    grad = whole_rows(total, dp_count, dp_index)
     right_prod = jnp.einsum(
         "bij,bjk->bik", grad, right, preferred_element_type=jnp.float32
     ).astype(jnp.bfloat16)

time: 79.1 us -> 82.9 us (1.048)
  the two profiles are of different devices: /device:TPU:0 before, /device:TPU:17 now
where the time goes in v5:
time: 82.9 us; the launch traced here: 82.6 us
  starting transfers between devices  39.1 us (47%)
  waiting for transfers between devices  31.8 us (38%)
  Pallas kernels  6.32 us (8%)
  local copies, waits for them, and re-layouts  2.21 us (3%)
  other arithmetic  2.19 us (3%)
    ppermute x17, waiting for transfers between devices, swap(): return lax.ppermute(value, axis, [(i, i ^ distance) for i in range(count)])  25.7 us
    ppermute x17, starting transfers between devices, swap(): return lax.ppermute(value, axis, [(i, i ^ distance) for i in range(count)])  21.8 us
    all_to_all x1, starting transfers between devices, shards(): lax.all_to_all(left_outgoing, 'mp', split_axis=0, concat_axis=0, tiled=True)  9.43 us
    all_to_all x2, starting transfers between devices, over_dp(): lax.all_to_all(factor[0, 0].reshape(dp_count, rows, width), 'dp', split_a...  7.79 us
    all_to_all x2, waiting for transfers between devices, over_dp(): lax.all_to_all(factor[0, 0].reshape(dp_count, rows, width), 'dp', split_a...  6.15 us
    reduce_sum x1, other arithmetic, shards(): jnp.sum(total_f * total_f, axis=(1, 2)).reshape(per_shard, 1)  1.78 us
    pallas_call x1, Pallas kernels, shards(): pl.pallas_call(functools.partial(left_kernel, mp_count), out_shape=jax.Sh...  1.71 us
  transfers between devices with their start and end apart: 20, of which 9 were waited for; matrix products, arithmetic and copies ran while one was open for 4% of the time, Pallas kernels for 6%

profile of v5, /device:TPU:17, one launch (start us, length us, event | category | flops | bytes accessed | tf_op | source)
XLA Modules:
  0.0 82.6 jit_solution(1277343266343037959)
XLA Ops:
  0.0 1.2 %dynamic-slice_bitcast_fusion = bf16[2,256,512]{2,1,0:T(8,128)(2,1)S(1)} fusion(bf16[1,2,512,512]{3,2,1,0:T(8,128)(2,1)} %param.5, s32[]{:T(128)S(6)} %select_n.113), kind=kLoop, calls=%fused_computation.9 | loop fusion | bytes 1048580 | tf_op jit(solution)/shard_map/dynamic_slice | solution.py:31
  1.2 0.7 collective-permute-start
  1.9 3.5 %all-to-all-start = ((bf16[4,128,512]{2,1,0:T(8,128)(2,1)}), bf16[4,128,512]{2,1,0:T(8,128)(2,1)S(1)}, u32[]{:S(2)}, u32[]{:S(2)}) async-start(bf16[4,128,512]{2,1,0:T(8,128)(2,1)} %bitcast), calls=%async_computation | async-start | bytes 1048576 | tf_op jit(solution)/shard_map/all_to_all | solution.py:182
  5.5 1.6 %shard_map.55.plan = s32[10]{0:T(128)S(1)} custom-call(s32[16]{0:T(128)S(1)} %copy-done, s32[9]{0:T(128)S(1)} %copy-done.1), custom_call_target="tpu_custom_call" | custom-call | tf_op jit(solution)/shard_map/pallas_call | solution.py:186
  7.1 0.0 collective-permute-done
  7.1 0.1 fusion
  7.2 6.1 %all-to-all-done.slots = bf16[4,128,512]{2,1,0:T(8,128)(2,1)S(1)} async-done(((bf16[4,128,512]{2,1,0:T(8,128)(2,1)}), bf16[4,128,512]{2,1,0:T(8,128)(2,1)S(1)}, u32[]{:S(2)}, u32[]{:S(2)}) %all-to-all-start) | async-done | bytes 524320 | tf_op jit(solution)/shard_map/all_to_all | solution.py:182
  13.4 0.4 collective-permute-start.1
  13.8 4.3 %all-to-all-start.1 = ((bf16[4,128,512]{2,1,0:T(8,128)(2,1)}), bf16[4,128,512]{2,1,0:T(8,128)(2,1)S(1)}, u32[]{:S(2)}, u32[]{:S(2)}) async-start(bf16[4,128,512]{2,1,0:T(8,128)(2,1)} %bitcast.3), calls=%async_computation.1 | async-start | bytes 1048576 | tf_op jit(solution)/shard_map/all_to_all | solution.py:182
  18.1 0.6 shard_map.56
  18.8 1.3 %collective-permute-start.5 = (bf16[128,512]{1,0:T(8,128)(2,1)S(1)}, bf16[128,512]{1,0:T(8,128)(2,1)S(1)}, u32[]{:S(2)}, u32[]{:S(2)}) collective-permute-start(bf16[128,512]{1,0:T(8,128)(2,1)S(1)} %get-tuple-element.22), channel_id=1, source_target_pairs={{0,1},{1,0},{2,3},{3,2},{4,5},{5,4},{6,7},{7,6},{8,9},{9,8},{10,11... | collective-permute-start | bytes 393224 | tf_op jit(solution)/shard_map/ppermute | solution.py:20
  20.0 0.1 collective-permute-start.6
  20.1 1.3 %collective-permute-start.7 = (bf16[128,512]{1,0:T(8,128)(2,1)S(1)}, bf16[128,512]{1,0:T(8,128)(2,1)S(1)}, u32[]{:S(2)}, u32[]{:S(2)}) collective-permute-start(bf16[128,512]{1,0:T(8,128)(2,1)S(1)} %get-tuple-element.24), channel_id=1, source_target_pairs={{0,2},{1,3},{2,0},{3,1},{4,6},{5,7},{6,4},{7,5},{8,10},{9,11},{10,... | collective-permute-start | bytes 393224 | tf_op jit(solution)/shard_map/ppermute | solution.py:20
  21.4 0.1 collective-permute-start.8
  21.5 2.4 %collective-permute-done.5.refs_1_ = bf16[128,512]{1,0:T(8,128)(2,1)S(1)} collective-permute-done((bf16[128,512]{1,0:T(8,128)(2,1)S(1)}, bf16[128,512]{1,0:T(8,128)(2,1)S(1)}, u32[]{:S(2)}, u32[]{:S(2)}) %collective-permute-start.5) | collective-permute-done | bytes 131104 | tf_op jit(solution)/shard_map/ppermute | solution.py:20
  23.9 1.0 %collective-permute-start.9 = (bf16[128,512]{1,0:T(8,128)(2,1)S(1)}, bf16[128,512]{1,0:T(8,128)(2,1)S(1)}, u32[]{:S(2)}, u32[]{:S(2)}) collective-permute-start(bf16[128,512]{1,0:T(8,128)(2,1)S(1)} %get-tuple-element.26), channel_id=1, source_target_pairs={{0,5},{1,4},{2,7},{3,6},{4,1},{5,0},{6,3},{7,2},{8,13},{9,12},{10,... | collective-permute-start | bytes 393224 | tf_op jit(solution)/shard_map/ppermute | solution.py:20
  24.9 0.9 %collective-permute-done.6.refs_2_ = bf16[128,512]{1,0:T(8,128)(2,1)S(1)} collective-permute-done((bf16[128,512]{1,0:T(8,128)(2,1)S(1)}, bf16[128,512]{1,0:T(8,128)(2,1)S(1)}, u32[]{:S(2)}, u32[]{:S(2)}) %collective-permute-start.6) | collective-permute-done | bytes 131104 | tf_op jit(solution)/shard_map/ppermute | solution.py:20
  25.7 2.8 %collective-permute-start.10 = (bf16[128,512]{1,0:T(8,128)(2,1)S(1)}, bf16[128,512]{1,0:T(8,128)(2,1)S(1)}, u32[]{:S(2)}, u32[]{:S(2)}) collective-permute-start(bf16[128,512]{1,0:T(8,128)(2,1)S(1)} %get-tuple-element.27), channel_id=1, source_target_pairs={{0,6},{1,7},{2,4},{3,5},{4,2},{5,3},{6,0},{7,1},{8,14},{9,15},{10,... | collective-permute-start | bytes 393224 | tf_op jit(solution)/shard_map/ppermute | solution.py:20
  28.5 0.7 copy-done.4
  29.2 0.0 collective-permute-start.11
  29.2 1.8 %multiply_reduce_fusion = (f32[2]{0:T(128)S(1)}, bf16[2,128,512]{2,1,0:T(8,128)(2,1)}) fusion(bf16[2,128,512]{2,1,0:T(8,128)(2,1)} %copy-done.4, bf16[2,256,512]{2,1,0:T(8,128)(2,1)S(1)} %fusion, s32[]{:T(128)S(6)} %select_n.116), kind=kLoop, calls=%fused_computation.7 | loop fusion | flops 917502 | bytes 786444 | tf_op jit(solution)/shard_map/reduce_sum | solution.py:210
  31.0 0.0 all-to-all-done.1.slots
  31.0 0.1 broadcast_in_dim.12.half_sq
  31.1 1.7 %shard_map.57.refs_8_ = bf16[8,528,128]{2,1,0:T(8,128)(2,1)} custom-call(s32[10]{0:T(128)S(1)} %shard_map.55.plan, bf16[4,128,512]{2,1,0:T(8,128)(2,1)S(1)} %all-to-all-done.1.slots, f32[2,128]{1,0:T(2,128)S(1)} %broadcast_in_dim.12.half_sq), custom_call_target="tpu_custom_call" | custom-call | tf_op jit(solution)/shard_map/pallas_call | solution.py:213
  32.8 9.4 %all-to-all-start.2 = ((bf16[8,528,128]{2,1,0:T(8,128)(2,1)}), bf16[8,528,128]{2,1,0:T(8,128)(2,1)S(1)}, u32[]{:S(2)}, u32[]{:S(2)}) async-start(bf16[8,528,128]{2,1,0:T(8,128)(2,1)} %shard_map.57.refs_8_), calls=%async_computation.2 | async-start | bytes 2162688 | tf_op jit(solution)/shard_map/all_to_all | solution.py:220
  42.2 0.5 collective-permute-done.10.refs_6_
  42.7 7.3 %collective-permute-done.11.refs_7_ = bf16[128,512]{1,0:T(8,128)(2,1)S(1)} collective-permute-done((bf16[128,512]{1,0:T(8,128)(2,1)S(1)}, bf16[128,512]{1,0:T(8,128)(2,1)S(1)}, u32[]{:S(2)}, u32[]{:S(2)}) %collective-permute-start.11) | collective-permute-done | bytes 131104 | tf_op jit(solution)/shard_map/ppermute | solution.py:20
  50.0 0.6 shard_map.58
  50.7 1.3 %collective-permute-start.12 = (bf16[2,1,128,512]{3,2,0,1:T(8,128)(2,1)S(1)}, bf16[2,1,128,512]{3,2,0,1:T(8,128)(2,1)S(1)}, u32[]{:S(2)}, u32[]{:S(2)}) collective-permute-start(bf16[2,1,128,512]{3,2,0,1:T(8,128)(2,1)S(1)} %bitcast.27), channel_id=1, source_target_pairs={{0,16},{8,24},{16,0},{24,8},{1,17},{9,25},{17,1},{25,9},{2,18},{10... | collective-permute-start | bytes 786440 | tf_op jit(solution)/shard_map/ppermute | solution.py:20
  52.0 4.4 %collective-permute-start.2 = (bf16[2,128,512]{2,1,0:T(8,128)(2,1)S(1)}, bf16[2,128,512]{2,1,0:T(8,128)(2,1)S(1)}, u32[]{:S(2)}, u32[]{:S(2)}) collective-permute-start(bf16[2,128,512]{2,1,0:T(8,128)(2,1)S(1)} %copy-done.2), channel_id=1, source_target_pairs={{0,8},{8,0},{16,24},{24,16},{1,9},{9,1},{17,25},{25,17},{2,10},{10... | collective-permute-start | bytes 786440 | tf_op jit(solution)/shard_map/ppermute | solution.py:20
  56.4 0.1 maximum_bitcast_fusion
  56.5 4.6 %collective-permute-start.13 = (bf16[2,2,128,512]{3,2,0,1:T(8,128)(2,1)S(1)}, bf16[2,2,128,512]{3,2,0,1:T(8,128)(2,1)S(1)}, u32[]{:S(2)}, u32[]{:S(2)}) collective-permute-start(bf16[2,2,128,512]{3,2,0,1:T(8,128)(2,1)S(1)} %maximum_bitcast_fusion), channel_id=1, source_target_pairs={{0,8},{8,0},{16,24},{24,16},{1,9},{9,1},{17,25},{25,17},{2,10},{10... | collective-permute-start | bytes 1572872 | tf_op jit(solution)/shard_map/ppermute | solution.py:20
  61.1 1.6 %collective-permute-start.3 = (bf16[2,128,512]{2,1,0:T(8,128)(2,1)S(1)}, bf16[2,128,512]{2,1,0:T(8,128)(2,1)S(1)}, u32[]{:S(2)}, u32[]{:S(2)}) collective-permute-start(bf16[2,128,512]{2,1,0:T(8,128)(2,1)S(1)} %copy-done.2), channel_id=1, source_target_pairs={{0,16},{8,24},{16,0},{24,8},{1,17},{9,25},{17,1},{25,9},{2,18},{10... | collective-permute-start | bytes 786440 | tf_op jit(solution)/shard_map/ppermute | solution.py:20
  62.6 0.2 collective-permute-start.4
  62.8 0.1 broadcast_in_dim.11
  63.0 6.2 %collective-permute-done.3 = bf16[2,128,512]{2,1,0:T(8,128)(2,1)S(1)} collective-permute-done((bf16[2,128,512]{2,1,0:T(8,128)(2,1)S(1)}, bf16[2,128,512]{2,1,0:T(8,128)(2,1)S(1)}, u32[]{:S(2)}, u32[]{:S(2)}) %collective-permute-start.3) | collective-permute-done | bytes 262176 | tf_op jit(solution)/shard_map/ppermute | solution.py:20
  69.2 5.6 %collective-permute-done.4 = bf16[2,128,512]{2,1,0:T(8,128)(2,1)S(1)} collective-permute-done((bf16[2,128,512]{2,1,0:T(8,128)(2,1)S(1)}, bf16[2,128,512]{2,1,0:T(8,128)(2,1)S(1)}, u32[]{:S(2)}, u32[]{:S(2)}) %collective-permute-start.4) | collective-permute-done | bytes 262176 | tf_op jit(solution)/shard_map/ppermute | solution.py:20
  74.8 0.1 select_bitcast_fusion.1
  74.9 0.1 pad_maximum_fusion
  75.0 0.1 copy.6
  75.1 0.7 convolution_convert_fusion.right_prod
  75.8 1.0 %shard_map.59 = (f32[2,128,512]{2,1,0:T(8,128)S(1)}, f32[8,128]{1,0:T(8,128)S(1)}) custom-call(s32[10]{0:T(128)S(1)} %shard_map.55.plan, bf16[2,512,512]{2,1,0:T(8,128)(2,1)S(1)} %convolution_convert_fusion.right_prod, f32[2,128]{1,0:T(2,128)S(1)} %broadcast_in_dim.12.half_sq, bf16[8,528,128]{2,1,0:T(8,128)(2,1)S(1)} %all-to-all-done.2.arrived), custom_call_target="tpu_custom_call" | custom-call | tf_op jit(solution)/shard_map/pallas_call | solution.py:234
  76.8 0.4 collective-permute-start.14
  77.2 1.4 %collective-permute-start.15 = (f32[8,128]{1,0:T(8,128)S(1)}, f32[8,128]{1,0:T(8,128)S(1)}, u32[]{:S(2)}, u32[]{:S(2)}) collective-permute-start(f32[8,128]{1,0:T(8,128)S(1)} %get-tuple-element.30.refs_0_), channel_id=1, source_target_pairs={{0,16},{8,24},{16,0},{24,8},{1,17},{9,25},{17,1},{25,9},{2,18},{10... | collective-permute-start | bytes 12296 | tf_op jit(solution)/shard_map/ppermute | solution.py:20
  78.6 0.4 collective-permute-start.16
  79.0 0.7 collective-permute-done.15.refs_2_
  79.7 2.1 %collective-permute-done.16.refs_3_ = f32[8,128]{1,0:T(8,128)S(1)} collective-permute-done((f32[8,128]{1,0:T(8,128)S(1)}, f32[8,128]{1,0:T(8,128)S(1)}, u32[]{:S(2)}, u32[]{:S(2)}) %collective-permute-start.16) | collective-permute-done | bytes 4128 | tf_op jit(solution)/shard_map/ppermute | solution.py:20
  81.8 0.8 shard_map.60
  (24 shorter events, 0.2 us)
Async XLA Ops:
  0.0 5.4 %copy-start = (s32[16]{0:T(128)S(1)}, s32[16]{0:T(128)}, u32[]{:S(2)}) copy-start(s32[16]{0:T(128)} %lists.1) | copy-start | bytes 196
  0.0 5.5 %copy-start.1 = (s32[9]{0:T(128)S(1)}, s32[9]{0:T(128)}, u32[]{:S(2)}) copy-start(s32[9]{0:T(128)} %offsets.1) | copy-start | bytes 112
  0.0 7.1 %copy-start.3 = (bf16[1,2,512,512]{3,2,1,0:T(8,128)(2,1)S(1)}, bf16[1,2,512,512]{3,2,1,0:T(8,128)(2,1)}, u32[]{:S(2)}) copy-start(bf16[1,2,512,512]{3,2,1,0:T(8,128)(2,1)} %param.5) | copy-start | bytes 3145732
  1.2 5.9 %collective-permute-start = (bf16[2,256,512]{2,1,0:T(8,128)(2,1)S(1)}, bf16[2,256,512]{2,1,0:T(8,128)(2,1)S(1)}, u32[]{:S(2)}, u32[]{:S(2)}) collective-permute-start(bf16[2,256,512]{2,1,0:T(8,128)(2,1)S(1)} %dynamic-slice_bitcast_fusion), channel_id=1, source_target_pairs={{0,8},{8,0},{16,24},{24,16},{1,9},{9,1},{17,25},{25,17},{2,10},{10... | collective-permute-start | bytes 1572872 | tf_op jit(solution)/shard_map/ppermute | solution.py:20
  1.9 11.4 %all-to-all-start = ((bf16[4,128,512]{2,1,0:T(8,128)(2,1)}), bf16[4,128,512]{2,1,0:T(8,128)(2,1)S(1)}, u32[]{:S(2)}, u32[]{:S(2)}) async-start(bf16[4,128,512]{2,1,0:T(8,128)(2,1)} %bitcast), calls=%async_computation | async-start | bytes 1048576 | tf_op jit(solution)/shard_map/all_to_all | solution.py:182
  13.4 15.1 %collective-permute-start.1 = (bf16[2,128,512]{2,1,0:T(8,128)(2,1)S(1)}, bf16[2,128,512]{2,1,0:T(8,128)(2,1)S(1)}, u32[]{:S(2)}, u32[]{:S(2)}) collective-permute-start(bf16[2,128,512]{2,1,0:T(8,128)(2,1)S(1)} %constant_dynamic-slice_fusion), channel_id=1, source_target_pairs={{0,16},{8,24},{16,0},{24,8},{1,17},{9,25},{17,1},{25,9},{2,18},{10... | collective-permute-start | bytes 786440 | tf_op jit(solution)/shard_map/ppermute | solution.py:20
  13.8 17.2 %all-to-all-start.1 = ((bf16[4,128,512]{2,1,0:T(8,128)(2,1)}), bf16[4,128,512]{2,1,0:T(8,128)(2,1)S(1)}, u32[]{:S(2)}, u32[]{:S(2)}) async-start(bf16[4,128,512]{2,1,0:T(8,128)(2,1)} %bitcast.3), calls=%async_computation.1 | async-start | bytes 1048576 | tf_op jit(solution)/shard_map/all_to_all | solution.py:182
  18.8 5.1 %collective-permute-start.5 = (bf16[128,512]{1,0:T(8,128)(2,1)S(1)}, bf16[128,512]{1,0:T(8,128)(2,1)S(1)}, u32[]{:S(2)}, u32[]{:S(2)}) collective-permute-start(bf16[128,512]{1,0:T(8,128)(2,1)S(1)} %get-tuple-element.22), channel_id=1, source_target_pairs={{0,1},{1,0},{2,3},{3,2},{4,5},{5,4},{6,7},{7,6},{8,9},{9,8},{10,11... | collective-permute-start | bytes 393224 | tf_op jit(solution)/shard_map/ppermute | solution.py:20
  20.0 5.7 %collective-permute-start.6 = (bf16[128,512]{1,0:T(8,128)(2,1)S(1)}, bf16[128,512]{1,0:T(8,128)(2,1)S(1)}, u32[]{:S(2)}, u32[]{:S(2)}) collective-permute-start(bf16[128,512]{1,0:T(8,128)(2,1)S(1)} %get-tuple-element.23), channel_id=1, source_target_pairs={{0,4},{1,5},{2,6},{3,7},{4,0},{5,1},{6,2},{7,3},{8,12},{9,13},{10,... | collective-permute-start | bytes 393224 | tf_op jit(solution)/shard_map/ppermute | solution.py:20
  20.1 22.1 %collective-permute-start.7 = (bf16[128,512]{1,0:T(8,128)(2,1)S(1)}, bf16[128,512]{1,0:T(8,128)(2,1)S(1)}, u32[]{:S(2)}, u32[]{:S(2)}) collective-permute-start(bf16[128,512]{1,0:T(8,128)(2,1)S(1)} %get-tuple-element.24), channel_id=1, source_target_pairs={{0,2},{1,3},{2,0},{3,1},{4,6},{5,7},{6,4},{7,5},{8,10},{9,11},{10,... | collective-permute-start | bytes 393224 | tf_op jit(solution)/shard_map/ppermute | solution.py:20
  21.4 20.8 %collective-permute-start.8 = (bf16[128,512]{1,0:T(8,128)(2,1)S(1)}, bf16[128,512]{1,0:T(8,128)(2,1)S(1)}, u32[]{:S(2)}, u32[]{:S(2)}) collective-permute-start(bf16[128,512]{1,0:T(8,128)(2,1)S(1)} %get-tuple-element.25), channel_id=1, source_target_pairs={{0,3},{1,2},{2,1},{3,0},{4,7},{5,6},{6,5},{7,4},{8,11},{9,10},{10,... | collective-permute-start | bytes 393224 | tf_op jit(solution)/shard_map/ppermute | solution.py:20
  23.9 18.3 %collective-permute-start.9 = (bf16[128,512]{1,0:T(8,128)(2,1)S(1)}, bf16[128,512]{1,0:T(8,128)(2,1)S(1)}, u32[]{:S(2)}, u32[]{:S(2)}) collective-permute-start(bf16[128,512]{1,0:T(8,128)(2,1)S(1)} %get-tuple-element.26), channel_id=1, source_target_pairs={{0,5},{1,4},{2,7},{3,6},{4,1},{5,0},{6,3},{7,2},{8,13},{9,12},{10,... | collective-permute-start | bytes 393224 | tf_op jit(solution)/shard_map/ppermute | solution.py:20
  25.7 17.0 %collective-permute-start.10 = (bf16[128,512]{1,0:T(8,128)(2,1)S(1)}, bf16[128,512]{1,0:T(8,128)(2,1)S(1)}, u32[]{:S(2)}, u32[]{:S(2)}) collective-permute-start(bf16[128,512]{1,0:T(8,128)(2,1)S(1)} %get-tuple-element.27), channel_id=1, source_target_pairs={{0,6},{1,7},{2,4},{3,5},{4,2},{5,3},{6,0},{7,1},{8,14},{9,15},{10,... | collective-permute-start | bytes 393224 | tf_op jit(solution)/shard_map/ppermute | solution.py:20
  28.5 0.7 copy-start.4
  29.2 20.8 %collective-permute-start.11 = (bf16[128,512]{1,0:T(8,128)(2,1)S(1)}, bf16[128,512]{1,0:T(8,128)(2,1)S(1)}, u32[]{:S(2)}, u32[]{:S(2)}) collective-permute-start(bf16[128,512]{1,0:T(8,128)(2,1)S(1)} %get-tuple-element.28), channel_id=1, source_target_pairs={{0,7},{1,6},{2,5},{3,4},{4,3},{5,2},{6,1},{7,0},{8,15},{9,14},{10,... | collective-permute-start | bytes 393224 | tf_op jit(solution)/shard_map/ppermute | solution.py:20
  32.8 43.1 %all-to-all-start.2 = ((bf16[8,528,128]{2,1,0:T(8,128)(2,1)}), bf16[8,528,128]{2,1,0:T(8,128)(2,1)S(1)}, u32[]{:S(2)}, u32[]{:S(2)}) async-start(bf16[8,528,128]{2,1,0:T(8,128)(2,1)} %shard_map.57.refs_8_), calls=%async_computation.2 | async-start | bytes 2162688 | tf_op jit(solution)/shard_map/all_to_all | solution.py:220
  50.0 2.0 %copy-start.2 = (bf16[2,128,512]{2,1,0:T(8,128)(2,1)S(1)}, bf16[2,128,512]{2,1,0:T(8,128)(2,1)}, u32[]{:S(2)}) copy-start(bf16[2,128,512]{2,1,0:T(8,128)(2,1)} %get-tuple-element.32) | copy-start | bytes 786436
  50.7 5.7 %collective-permute-start.12 = (bf16[2,1,128,512]{3,2,0,1:T(8,128)(2,1)S(1)}, bf16[2,1,128,512]{3,2,0,1:T(8,128)(2,1)S(1)}, u32[]{:S(2)}, u32[]{:S(2)}) collective-permute-start(bf16[2,1,128,512]{3,2,0,1:T(8,128)(2,1)S(1)} %bitcast.27), channel_id=1, source_target_pairs={{0,16},{8,24},{16,0},{24,8},{1,17},{9,25},{17,1},{25,9},{2,18},{10... | collective-permute-start | bytes 786440 | tf_op jit(solution)/shard_map/ppermute | solution.py:20
  52.0 10.9 %collective-permute-start.2 = (bf16[2,128,512]{2,1,0:T(8,128)(2,1)S(1)}, bf16[2,128,512]{2,1,0:T(8,128)(2,1)S(1)}, u32[]{:S(2)}, u32[]{:S(2)}) collective-permute-start(bf16[2,128,512]{2,1,0:T(8,128)(2,1)S(1)} %copy-done.2), channel_id=1, source_target_pairs={{0,8},{8,0},{16,24},{24,16},{1,9},{9,1},{17,25},{25,17},{2,10},{10... | collective-permute-start | bytes 786440 | tf_op jit(solution)/shard_map/ppermute | solution.py:20
  56.5 18.4 %collective-permute-start.13 = (bf16[2,2,128,512]{3,2,0,1:T(8,128)(2,1)S(1)}, bf16[2,2,128,512]{3,2,0,1:T(8,128)(2,1)S(1)}, u32[]{:S(2)}, u32[]{:S(2)}) collective-permute-start(bf16[2,2,128,512]{3,2,0,1:T(8,128)(2,1)S(1)} %maximum_bitcast_fusion), channel_id=1, source_target_pairs={{0,8},{8,0},{16,24},{24,16},{1,9},{9,1},{17,25},{25,17},{2,10},{10... | collective-permute-start | bytes 1572872 | tf_op jit(solution)/shard_map/ppermute | solution.py:20
  61.1 8.1 %collective-permute-start.3 = (bf16[2,128,512]{2,1,0:T(8,128)(2,1)S(1)}, bf16[2,128,512]{2,1,0:T(8,128)(2,1)S(1)}, u32[]{:S(2)}, u32[]{:S(2)}) collective-permute-start(bf16[2,128,512]{2,1,0:T(8,128)(2,1)S(1)} %copy-done.2), channel_id=1, source_target_pairs={{0,16},{8,24},{16,0},{24,8},{1,17},{9,25},{17,1},{25,9},{2,18},{10... | collective-permute-start | bytes 786440 | tf_op jit(solution)/shard_map/ppermute | solution.py:20
  62.6 12.2 %collective-permute-start.4 = (bf16[2,128,512]{2,1,0:T(8,128)(2,1)S(1)}, bf16[2,128,512]{2,1,0:T(8,128)(2,1)S(1)}, u32[]{:S(2)}, u32[]{:S(2)}) collective-permute-start(bf16[2,128,512]{2,1,0:T(8,128)(2,1)S(1)} %copy-done.2), channel_id=1, source_target_pairs={{0,24},{8,16},{16,8},{24,0},{1,25},{9,17},{17,9},{25,1},{2,26},{10... | collective-permute-start | bytes 786440 | tf_op jit(solution)/shard_map/ppermute | solution.py:20
  76.8 2.2 %collective-permute-start.14 = (f32[8,128]{1,0:T(8,128)S(1)}, f32[8,128]{1,0:T(8,128)S(1)}, u32[]{:S(2)}, u32[]{:S(2)}) collective-permute-start(f32[8,128]{1,0:T(8,128)S(1)} %get-tuple-element.30.refs_0_), channel_id=1, source_target_pairs={{0,8},{8,0},{16,24},{24,16},{1,9},{9,1},{17,25},{25,17},{2,10},{10... | collective-permute-start | bytes 12296 | tf_op jit(solution)/shard_map/ppermute | solution.py:20
  77.2 2.5 %collective-permute-start.15 = (f32[8,128]{1,0:T(8,128)S(1)}, f32[8,128]{1,0:T(8,128)S(1)}, u32[]{:S(2)}, u32[]{:S(2)}) collective-permute-start(f32[8,128]{1,0:T(8,128)S(1)} %get-tuple-element.30.refs_0_), channel_id=1, source_target_pairs={{0,16},{8,24},{16,0},{24,8},{1,17},{9,25},{17,1},{25,9},{2,18},{10... | collective-permute-start | bytes 12296 | tf_op jit(solution)/shard_map/ppermute | solution.py:20
  78.6 3.2 %collective-permute-start.16 = (f32[8,128]{1,0:T(8,128)S(1)}, f32[8,128]{1,0:T(8,128)S(1)}, u32[]{:S(2)}, u32[]{:S(2)}) collective-permute-start(f32[8,128]{1,0:T(8,128)S(1)} %get-tuple-element.30.refs_0_), channel_id=1, source_target_pairs={{0,24},{8,16},{16,8},{24,0},{1,25},{9,17},{17,9},{25,1},{2,26},{10... | collective-permute-start | bytes 12296 | tf_op jit(solution)/shard_map/ppermute | solution.py:20

commit v6 on v5

--- a/solution.py
+++ b/solution.py
@@ -46,9 +46,12 @@
 
 def whole_rows(total, dp_count, dp_index):
     part = total.shape[1]
+    pieces, distance = {0: total}, dp_count // 2
+    while distance >= 1:
+        pieces |= {d ^ distance: swap(piece, "dp", distance) for d, piece in pieces.items()}
+        distance //= 2
     whole = jnp.zeros((total.shape[0], part * dp_count, total.shape[2]), total.dtype)
-    for d in range(dp_count):
-        piece = swap(total, "dp", d) if d else total
+    for d, piece in pieces.items():
         holder, place, distance = dp_index ^ d, 0, 1
         while distance < dp_count:
             place = 2 * place + (holder // distance) % 2

time: 82.9 us -> 78.6 us (0.948)
  the two profiles are of different devices: /device:TPU:17 before, /device:TPU:0 now
where the time goes in v6:
time: 78.6 us; the launch traced here: 78.2 us
  waiting for transfers between devices  34.3 us (44%)
  starting transfers between devices  31.3 us (40%)
  Pallas kernels  6.32 us (8%)
  other arithmetic  3.22 us (4%)
  local copies, waits for them, and re-layouts  2.21 us (3%)
    ppermute x17, starting transfers between devices, swap(): return lax.ppermute(value, axis, [(i, i ^ distance) for i in range(count)])  18.5 us
    ppermute x17, waiting for transfers between devices, swap(): return lax.ppermute(value, axis, [(i, i ^ distance) for i in range(count)])  16.7 us
    all_to_all x1, waiting for transfers between devices, shards(): lax.all_to_all(left_outgoing, 'mp', split_axis=0, concat_axis=0, tiled=True)  11.1 us
    all_to_all x2, starting transfers between devices, over_dp(): lax.all_to_all(factor[0, 0].reshape(dp_count, rows, width), 'dp', split_a...  7.37 us
    all_to_all x2, waiting for transfers between devices, over_dp(): lax.all_to_all(factor[0, 0].reshape(dp_count, rows, width), 'dp', split_a...  6.43 us
    all_to_all x1, starting transfers between devices, shards(): lax.all_to_all(left_outgoing, 'mp', split_axis=0, concat_axis=0, tiled=True)  5.39 us
    reduce_sum x1, other arithmetic, shards(): jnp.sum(total_f * total_f, axis=(1, 2)).reshape(per_shard, 1)  1.78 us
    pallas_call x1, Pallas kernels, shards(): pl.pallas_call(functools.partial(left_kernel, mp_count), out_shape=jax.Sh...  1.72 us
  transfers between devices with their start and end apart: 20, of which 8 were waited for; matrix products, arithmetic and copies ran while one was open for 5% of the time, Pallas kernels for 6%

profile of v6, /device:TPU:0, one launch (start us, length us, event | category | flops | bytes accessed | tf_op | source)
XLA Modules:
  0.0 78.2 jit_solution(2287490618569742803)
XLA Ops:
  0.0 1.2 %dynamic-slice_bitcast_fusion = bf16[2,256,512]{2,1,0:T(8,128)(2,1)S(1)} fusion(bf16[1,2,512,512]{3,2,1,0:T(8,128)(2,1)} %param.5, s32[]{:T(128)S(6)} %select_n.113), kind=kLoop, calls=%fused_computation.9 | loop fusion | bytes 1048580 | tf_op jit(solution)/shard_map/dynamic_slice | solution.py:31
  1.2 0.5 collective-permute-start
  1.7 3.9 %all-to-all-start = ((bf16[4,128,512]{2,1,0:T(8,128)(2,1)}), bf16[4,128,512]{2,1,0:T(8,128)(2,1)S(1)}, u32[]{:S(2)}, u32[]{:S(2)}) async-start(bf16[4,128,512]{2,1,0:T(8,128)(2,1)} %bitcast), calls=%async_computation | async-start | bytes 1048576 | tf_op jit(solution)/shard_map/all_to_all | solution.py:185
  5.6 1.6 %shard_map.55.plan = s32[10]{0:T(128)S(1)} custom-call(s32[16]{0:T(128)S(1)} %copy-done, s32[9]{0:T(128)S(1)} %copy-done.1), custom_call_target="tpu_custom_call" | custom-call | tf_op jit(solution)/shard_map/pallas_call | solution.py:189
  7.2 0.0 collective-permute-done
  7.2 1.2 %fusion = bf16[2,256,512]{2,1,0:T(8,128)(2,1)S(1)} fusion(bf16[2,256,512]{2,1,0:T(8,128)(2,1)} %collective-permute-done, bf16[1,2,512,512]{3,2,1,0:T(8,128)(2,1)S(1)} %copy-done.3, s32[]{:T(128)S(6)} %select_n.112), kind=kLoop, calls=%fused_computation.3 | loop fusion | flops 1048576 | bytes 1572868 | tf_op jit(solution)/shard_map/convert_element_type | solution.py:24
  8.4 6.4 %all-to-all-done.slots = bf16[4,128,512]{2,1,0:T(8,128)(2,1)S(1)} async-done(((bf16[4,128,512]{2,1,0:T(8,128)(2,1)}), bf16[4,128,512]{2,1,0:T(8,128)(2,1)S(1)}, u32[]{:S(2)}, u32[]{:S(2)}) %all-to-all-start) | async-done | bytes 524320 | tf_op jit(solution)/shard_map/all_to_all | solution.py:185
  14.9 0.7 constant_dynamic-slice_fusion
  15.6 3.5 %all-to-all-start.1 = ((bf16[4,128,512]{2,1,0:T(8,128)(2,1)}), bf16[4,128,512]{2,1,0:T(8,128)(2,1)S(1)}, u32[]{:S(2)}, u32[]{:S(2)}) async-start(bf16[4,128,512]{2,1,0:T(8,128)(2,1)} %bitcast.29), calls=%async_computation.1 | async-start | bytes 1048576 | tf_op jit(solution)/shard_map/all_to_all | solution.py:185
  19.1 0.6 shard_map.56
  19.7 2.1 %collective-permute-start.5 = (bf16[128,512]{1,0:T(8,128)(2,1)S(1)}, bf16[128,512]{1,0:T(8,128)(2,1)S(1)}, u32[]{:S(2)}, u32[]{:S(2)}) collective-permute-start(bf16[128,512]{1,0:T(8,128)(2,1)S(1)} %get-tuple-element.22), channel_id=1, source_target_pairs={{0,1},{1,0},{2,3},{3,2},{4,5},{5,4},{6,7},{7,6},{8,9},{9,8},{10,11... | collective-permute-start | bytes 393224 | tf_op jit(solution)/shard_map/ppermute | solution.py:20
  21.8 2.6 %collective-permute-start.6 = (bf16[128,512]{1,0:T(8,128)(2,1)S(1)}, bf16[128,512]{1,0:T(8,128)(2,1)S(1)}, u32[]{:S(2)}, u32[]{:S(2)}) collective-permute-start(bf16[128,512]{1,0:T(8,128)(2,1)S(1)} %get-tuple-element.23), channel_id=1, source_target_pairs={{0,4},{1,5},{2,6},{3,7},{4,0},{5,1},{6,2},{7,3},{8,12},{9,13},{10,... | collective-permute-start | bytes 393224 | tf_op jit(solution)/shard_map/ppermute | solution.py:20
  24.4 1.6 %collective-permute-start.7 = (bf16[128,512]{1,0:T(8,128)(2,1)S(1)}, bf16[128,512]{1,0:T(8,128)(2,1)S(1)}, u32[]{:S(2)}, u32[]{:S(2)}) collective-permute-start(bf16[128,512]{1,0:T(8,128)(2,1)S(1)} %get-tuple-element.24), channel_id=1, source_target_pairs={{0,2},{1,3},{2,0},{3,1},{4,6},{5,7},{6,4},{7,5},{8,10},{9,11},{10,... | collective-permute-start | bytes 393224 | tf_op jit(solution)/shard_map/ppermute | solution.py:20
  25.9 0.4 collective-permute-start.8
  26.4 0.0 collective-permute-done.5.refs_1_
  26.4 3.3 %collective-permute-start.9 = (bf16[128,512]{1,0:T(8,128)(2,1)S(1)}, bf16[128,512]{1,0:T(8,128)(2,1)S(1)}, u32[]{:S(2)}, u32[]{:S(2)}) collective-permute-start(bf16[128,512]{1,0:T(8,128)(2,1)S(1)} %get-tuple-element.26), channel_id=1, source_target_pairs={{0,5},{1,4},{2,7},{3,6},{4,1},{5,0},{6,3},{7,2},{8,13},{9,12},{10,... | collective-permute-start | bytes 393224 | tf_op jit(solution)/shard_map/ppermute | solution.py:20
  29.7 2.2 %collective-permute-done.6.refs_2_ = bf16[128,512]{1,0:T(8,128)(2,1)S(1)} collective-permute-done((bf16[128,512]{1,0:T(8,128)(2,1)S(1)}, bf16[128,512]{1,0:T(8,128)(2,1)S(1)}, u32[]{:S(2)}, u32[]{:S(2)}) %collective-permute-start.6) | collective-permute-done | bytes 131104 | tf_op jit(solution)/shard_map/ppermute | solution.py:20
  31.9 2.8 %collective-permute-start.10 = (bf16[128,512]{1,0:T(8,128)(2,1)S(1)}, bf16[128,512]{1,0:T(8,128)(2,1)S(1)}, u32[]{:S(2)}, u32[]{:S(2)}) collective-permute-start(bf16[128,512]{1,0:T(8,128)(2,1)S(1)} %get-tuple-element.27), channel_id=1, source_target_pairs={{0,6},{1,7},{2,4},{3,5},{4,2},{5,3},{6,0},{7,1},{8,14},{9,15},{10,... | collective-permute-start | bytes 393224 | tf_op jit(solution)/shard_map/ppermute | solution.py:20
  34.7 0.0 collective-permute-done.1
  34.7 0.6 collective-permute-start.11
  35.3 1.8 %multiply_reduce_fusion = (f32[2]{0:T(128)S(1)}, bf16[2,128,512]{2,1,0:T(8,128)(2,1)}) fusion(bf16[2,128,512]{2,1,0:T(8,128)(2,1)} %collective-permute-done.1, bf16[2,256,512]{2,1,0:T(8,128)(2,1)S(1)} %fusion, s32[]{:T(128)S(6)} %select_n.116), kind=kLoop, calls=%fused_computation.7 | loop fusion | flops 917502 | bytes 786444 | tf_op jit(solution)/shard_map/reduce_sum | solution.py:213
  37.1 0.0 all-to-all-done.1.slots
  37.1 0.1 broadcast_in_dim.12.half_sq
  37.2 1.7 %shard_map.57.refs_8_ = bf16[8,528,128]{2,1,0:T(8,128)(2,1)} custom-call(s32[10]{0:T(128)S(1)} %shard_map.55.plan, bf16[4,128,512]{2,1,0:T(8,128)(2,1)S(1)} %all-to-all-done.1.slots, f32[2,128]{1,0:T(2,128)S(1)} %broadcast_in_dim.12.half_sq), custom_call_target="tpu_custom_call" | custom-call | tf_op jit(solution)/shard_map/pallas_call | solution.py:216
  38.9 5.4 %all-to-all-start.2 = ((bf16[8,528,128]{2,1,0:T(8,128)(2,1)}), bf16[8,528,128]{2,1,0:T(8,128)(2,1)S(1)}, u32[]{:S(2)}, u32[]{:S(2)}) async-start(bf16[8,528,128]{2,1,0:T(8,128)(2,1)} %shard_map.57.refs_8_), calls=%async_computation.2 | async-start | bytes 2162688 | tf_op jit(solution)/shard_map/all_to_all | solution.py:223
  44.3 0.0 copy-start.2
  44.4 0.6 shard_map.58
  45.0 1.8 %collective-permute-start.12 = (bf16[2,1,128,512]{3,2,0,1:T(8,128)(2,1)S(1)}, bf16[2,1,128,512]{3,2,0,1:T(8,128)(2,1)S(1)}, u32[]{:S(2)}, u32[]{:S(2)}) collective-permute-start(bf16[2,1,128,512]{3,2,0,1:T(8,128)(2,1)S(1)} %bitcast.27), channel_id=1, source_target_pairs={{0,16},{8,24},{16,0},{24,8},{1,17},{9,25},{17,1},{25,9},{2,18},{10... | collective-permute-start | bytes 786440 | tf_op jit(solution)/shard_map/ppermute | solution.py:20
  46.8 0.3 collective-permute-start.2
  47.1 7.2 %collective-permute-done.12 = bf16[2,1,128,512]{3,2,0,1:T(8,128)(2,1)S(1)} collective-permute-done((bf16[2,1,128,512]{3,2,0,1:T(8,128)(2,1)S(1)}, bf16[2,1,128,512]{3,2,0,1:T(8,128)(2,1)S(1)}, u32[]{:S(2)}, u32[]{:S(2)}) %collective-permute-start.12) | collective-permute-done | bytes 262176 | tf_op jit(solution)/shard_map/ppermute | solution.py:20
  54.4 0.1 maximum_bitcast_fusion
  54.4 0.1 collective-permute-start.13
  54.5 0.5 collective-permute-start.3
  55.0 3.0 %collective-permute-done.2 = bf16[2,128,512]{2,1,0:T(8,128)(2,1)S(1)} collective-permute-done((bf16[2,128,512]{2,1,0:T(8,128)(2,1)S(1)}, bf16[2,128,512]{2,1,0:T(8,128)(2,1)S(1)}, u32[]{:S(2)}, u32[]{:S(2)}) %collective-permute-start.2) | collective-permute-done | bytes 262176 | tf_op jit(solution)/shard_map/ppermute | solution.py:20
  58.0 0.1 broadcast_in_dim.11
  58.2 1.3 %collective-permute-done.4 = bf16[2,128,512]{2,1,0:T(8,128)(2,1)S(1)} collective-permute-done((bf16[2,128,512]{2,1,0:T(8,128)(2,1)S(1)}, bf16[2,128,512]{2,1,0:T(8,128)(2,1)S(1)}, u32[]{:S(2)}, u32[]{:S(2)}) %collective-permute-start.4) | collective-permute-done | bytes 262176 | tf_op jit(solution)/shard_map/ppermute | solution.py:20
  59.5 0.1 select_bitcast_fusion.1
  59.6 0.1 pad_maximum_fusion
  59.7 0.1 copy.6
  59.8 0.7 convolution_convert_fusion.right_prod
  60.5 11.1 %all-to-all-done.2.arrived = bf16[8,528,128]{2,1,0:T(8,128)(2,1)S(1)} async-done(((bf16[8,528,128]{2,1,0:T(8,128)(2,1)}), bf16[8,528,128]{2,1,0:T(8,128)(2,1)S(1)}, u32[]{:S(2)}, u32[]{:S(2)}) %all-to-all-start.2) | async-done | bytes 1081376 | tf_op jit(solution)/shard_map/all_to_all | solution.py:223
  71.6 0.9 %shard_map.59 = (f32[2,128,512]{2,1,0:T(8,128)S(1)}, f32[8,128]{1,0:T(8,128)S(1)}) custom-call(s32[10]{0:T(128)S(1)} %shard_map.55.plan, bf16[2,512,512]{2,1,0:T(8,128)(2,1)S(1)} %convolution_convert_fusion.right_prod, f32[2,128]{1,0:T(2,128)S(1)} %broadcast_in_dim.12.half_sq, bf16[8,528,128]{2,1,0:T(8,128)(2,1)S(1)} %all-to-all-done.2.arrived), custom_call_target="tpu_custom_call" | custom-call | tf_op jit(solution)/shard_map/pallas_call | solution.py:237
  72.6 0.1 collective-permute-start.14
  72.7 1.7 %collective-permute-start.15 = (f32[8,128]{1,0:T(8,128)S(1)}, f32[8,128]{1,0:T(8,128)S(1)}, u32[]{:S(2)}, u32[]{:S(2)}) collective-permute-start(f32[8,128]{1,0:T(8,128)S(1)} %get-tuple-element.30.refs_0_), channel_id=1, source_target_pairs={{0,16},{8,24},{16,0},{24,8},{1,17},{9,25},{17,1},{25,9},{2,18},{10... | collective-permute-start | bytes 12296 | tf_op jit(solution)/shard_map/ppermute | solution.py:20
  74.4 0.1 collective-permute-start.16
  74.5 1.8 %collective-permute-done.15.refs_2_ = f32[8,128]{1,0:T(8,128)S(1)} collective-permute-done((f32[8,128]{1,0:T(8,128)S(1)}, f32[8,128]{1,0:T(8,128)S(1)}, u32[]{:S(2)}, u32[]{:S(2)}) %collective-permute-start.15) | collective-permute-done | bytes 4128 | tf_op jit(solution)/shard_map/ppermute | solution.py:20
  76.3 1.1 %collective-permute-done.16.refs_3_ = f32[8,128]{1,0:T(8,128)S(1)} collective-permute-done((f32[8,128]{1,0:T(8,128)S(1)}, f32[8,128]{1,0:T(8,128)S(1)}, u32[]{:S(2)}, u32[]{:S(2)}) %collective-permute-start.16) | collective-permute-done | bytes 4128 | tf_op jit(solution)/shard_map/ppermute | solution.py:20
  77.4 0.8 %shard_map.60 = bf16[2,128,512]{2,1,0:T(8,128)(2,1)} custom-call(f32[2,128,512]{2,1,0:T(8,128)S(1)} %get-tuple-element.29.precond, f32[8,128]{1,0:T(8,128)S(1)} %get-tuple-element.30.refs_0_, f32[8,128]{1,0:T(8,128)S(1)} %collective-permute-done.14.refs_1_, f32[8,128]{1,0:T(8,128)S(1)} %collective-permute-done.15.refs_2_, ...), custom_call_target="tpu_custom_call" | custom-call | tf_op jit(solution)/shard_map/pallas_call | solution.py:249
  (22 shorter events, 0.2 us)
Async XLA Ops:
  0.0 5.6 %copy-start = (s32[16]{0:T(128)S(1)}, s32[16]{0:T(128)}, u32[]{:S(2)}) copy-start(s32[16]{0:T(128)} %lists.1) | copy-start | bytes 196
  0.0 5.6 %copy-start.1 = (s32[9]{0:T(128)S(1)}, s32[9]{0:T(128)}, u32[]{:S(2)}) copy-start(s32[9]{0:T(128)} %offsets.1) | copy-start | bytes 112
  0.0 7.2 %copy-start.3 = (bf16[1,2,512,512]{3,2,1,0:T(8,128)(2,1)S(1)}, bf16[1,2,512,512]{3,2,1,0:T(8,128)(2,1)}, u32[]{:S(2)}) copy-start(bf16[1,2,512,512]{3,2,1,0:T(8,128)(2,1)} %param.5) | copy-start | bytes 3145732
  1.2 6.0 %collective-permute-start = (bf16[2,256,512]{2,1,0:T(8,128)(2,1)S(1)}, bf16[2,256,512]{2,1,0:T(8,128)(2,1)}, u32[]{:S(2)}, u32[]{:S(2)}) collective-permute-start(bf16[2,256,512]{2,1,0:T(8,128)(2,1)S(1)} %dynamic-slice_bitcast_fusion), channel_id=1, source_target_pairs={{0,8},{8,0},{16,24},{24,16},{1,9},{9,1},{17,25},{25,17},{2,10},{10... | collective-permute-start | bytes 1572872 | tf_op jit(solution)/shard_map/ppermute | solution.py:20
  1.7 13.1 %all-to-all-start = ((bf16[4,128,512]{2,1,0:T(8,128)(2,1)}), bf16[4,128,512]{2,1,0:T(8,128)(2,1)S(1)}, u32[]{:S(2)}, u32[]{:S(2)}) async-start(bf16[4,128,512]{2,1,0:T(8,128)(2,1)} %bitcast), calls=%async_computation | async-start | bytes 1048576 | tf_op jit(solution)/shard_map/all_to_all | solution.py:185
  15.6 19.2 %collective-permute-start.1 = (bf16[2,128,512]{2,1,0:T(8,128)(2,1)}, bf16[2,128,512]{2,1,0:T(8,128)(2,1)}, u32[]{:S(2)}, u32[]{:S(2)}) collective-permute-start(bf16[2,128,512]{2,1,0:T(8,128)(2,1)} %constant_dynamic-slice_fusion), channel_id=1, source_target_pairs={{0,16},{8,24},{16,0},{24,8},{1,17},{9,25},{17,1},{25,9},{2,18},{10... | collective-permute-start | bytes 786440 | tf_op jit(solution)/shard_map/ppermute | solution.py:20
  15.6 21.5 %all-to-all-start.1 = ((bf16[4,128,512]{2,1,0:T(8,128)(2,1)}), bf16[4,128,512]{2,1,0:T(8,128)(2,1)S(1)}, u32[]{:S(2)}, u32[]{:S(2)}) async-start(bf16[4,128,512]{2,1,0:T(8,128)(2,1)} %bitcast.29), calls=%async_computation.1 | async-start | bytes 1048576 | tf_op jit(solution)/shard_map/all_to_all | solution.py:185
  19.7 6.7 %collective-permute-start.5 = (bf16[128,512]{1,0:T(8,128)(2,1)S(1)}, bf16[128,512]{1,0:T(8,128)(2,1)S(1)}, u32[]{:S(2)}, u32[]{:S(2)}) collective-permute-start(bf16[128,512]{1,0:T(8,128)(2,1)S(1)} %get-tuple-element.22), channel_id=1, source_target_pairs={{0,1},{1,0},{2,3},{3,2},{4,5},{5,4},{6,7},{7,6},{8,9},{9,8},{10,11... | collective-permute-start | bytes 393224 | tf_op jit(solution)/shard_map/ppermute | solution.py:20
  21.8 10.1 %collective-permute-start.6 = (bf16[128,512]{1,0:T(8,128)(2,1)S(1)}, bf16[128,512]{1,0:T(8,128)(2,1)S(1)}, u32[]{:S(2)}, u32[]{:S(2)}) collective-permute-start(bf16[128,512]{1,0:T(8,128)(2,1)S(1)} %get-tuple-element.23), channel_id=1, source_target_pairs={{0,4},{1,5},{2,6},{3,7},{4,0},{5,1},{6,2},{7,3},{8,12},{9,13},{10,... | collective-permute-start | bytes 393224 | tf_op jit(solution)/shard_map/ppermute | solution.py:20
  24.4 19.9 %collective-permute-start.7 = (bf16[128,512]{1,0:T(8,128)(2,1)S(1)}, bf16[128,512]{1,0:T(8,128)(2,1)S(1)}, u32[]{:S(2)}, u32[]{:S(2)}) collective-permute-start(bf16[128,512]{1,0:T(8,128)(2,1)S(1)} %get-tuple-element.24), channel_id=1, source_target_pairs={{0,2},{1,3},{2,0},{3,1},{4,6},{5,7},{6,4},{7,5},{8,10},{9,11},{10,... | collective-permute-start | bytes 393224 | tf_op jit(solution)/shard_map/ppermute | solution.py:20
  25.9 18.4 %collective-permute-start.8 = (bf16[128,512]{1,0:T(8,128)(2,1)S(1)}, bf16[128,512]{1,0:T(8,128)(2,1)S(1)}, u32[]{:S(2)}, u32[]{:S(2)}) collective-permute-start(bf16[128,512]{1,0:T(8,128)(2,1)S(1)} %get-tuple-element.25), channel_id=1, source_target_pairs={{0,3},{1,2},{2,1},{3,0},{4,7},{5,6},{6,5},{7,4},{8,11},{9,10},{10,... | collective-permute-start | bytes 393224 | tf_op jit(solution)/shard_map/ppermute | solution.py:20
  26.4 18.0 %collective-permute-start.9 = (bf16[128,512]{1,0:T(8,128)(2,1)S(1)}, bf16[128,512]{1,0:T(8,128)(2,1)S(1)}, u32[]{:S(2)}, u32[]{:S(2)}) collective-permute-start(bf16[128,512]{1,0:T(8,128)(2,1)S(1)} %get-tuple-element.26), channel_id=1, source_target_pairs={{0,5},{1,4},{2,7},{3,6},{4,1},{5,0},{6,3},{7,2},{8,13},{9,12},{10,... | collective-permute-start | bytes 393224 | tf_op jit(solution)/shard_map/ppermute | solution.py:20
  31.9 12.4 %collective-permute-start.10 = (bf16[128,512]{1,0:T(8,128)(2,1)S(1)}, bf16[128,512]{1,0:T(8,128)(2,1)S(1)}, u32[]{:S(2)}, u32[]{:S(2)}) collective-permute-start(bf16[128,512]{1,0:T(8,128)(2,1)S(1)} %get-tuple-element.27), channel_id=1, source_target_pairs={{0,6},{1,7},{2,4},{3,5},{4,2},{5,3},{6,0},{7,1},{8,14},{9,15},{10,... | collective-permute-start | bytes 393224 | tf_op jit(solution)/shard_map/ppermute | solution.py:20
  34.7 9.6 %collective-permute-start.11 = (bf16[128,512]{1,0:T(8,128)(2,1)S(1)}, bf16[128,512]{1,0:T(8,128)(2,1)S(1)}, u32[]{:S(2)}, u32[]{:S(2)}) collective-permute-start(bf16[128,512]{1,0:T(8,128)(2,1)S(1)} %get-tuple-element.28), channel_id=1, source_target_pairs={{0,7},{1,6},{2,5},{3,4},{4,3},{5,2},{6,1},{7,0},{8,15},{9,14},{10,... | collective-permute-start | bytes 393224 | tf_op jit(solution)/shard_map/ppermute | solution.py:20
  38.9 32.7 %all-to-all-start.2 = ((bf16[8,528,128]{2,1,0:T(8,128)(2,1)}), bf16[8,528,128]{2,1,0:T(8,128)(2,1)S(1)}, u32[]{:S(2)}, u32[]{:S(2)}) async-start(bf16[8,528,128]{2,1,0:T(8,128)(2,1)} %shard_map.57.refs_8_), calls=%async_computation.2 | async-start | bytes 2162688 | tf_op jit(solution)/shard_map/all_to_all | solution.py:223
  44.3 2.4 %copy-start.2 = (bf16[2,128,512]{2,1,0:T(8,128)(2,1)S(1)}, bf16[2,128,512]{2,1,0:T(8,128)(2,1)}, u32[]{:S(2)}) copy-start(bf16[2,128,512]{2,1,0:T(8,128)(2,1)} %get-tuple-element.32) | copy-start | bytes 786436
  45.0 9.3 %collective-permute-start.12 = (bf16[2,1,128,512]{3,2,0,1:T(8,128)(2,1)S(1)}, bf16[2,1,128,512]{3,2,0,1:T(8,128)(2,1)S(1)}, u32[]{:S(2)}, u32[]{:S(2)}) collective-permute-start(bf16[2,1,128,512]{3,2,0,1:T(8,128)(2,1)S(1)} %bitcast.27), channel_id=1, source_target_pairs={{0,16},{8,24},{16,0},{24,8},{1,17},{9,25},{17,1},{25,9},{2,18},{10... | collective-permute-start | bytes 786440 | tf_op jit(solution)/shard_map/ppermute | solution.py:20
  46.8 11.2 %collective-permute-start.2 = (bf16[2,128,512]{2,1,0:T(8,128)(2,1)S(1)}, bf16[2,128,512]{2,1,0:T(8,128)(2,1)S(1)}, u32[]{:S(2)}, u32[]{:S(2)}) collective-permute-start(bf16[2,128,512]{2,1,0:T(8,128)(2,1)S(1)} %copy-done.2), channel_id=1, source_target_pairs={{0,16},{8,24},{16,0},{24,8},{1,17},{9,25},{17,1},{25,9},{2,18},{10... | collective-permute-start | bytes 786440 | tf_op jit(solution)/shard_map/ppermute | solution.py:20
  54.4 5.1 %collective-permute-start.13 = (bf16[2,2,128,512]{3,2,0,1:T(8,128)(2,1)S(1)}, bf16[2,2,128,512]{3,2,0,1:T(8,128)(2,1)S(1)}, u32[]{:S(2)}, u32[]{:S(2)}) collective-permute-start(bf16[2,2,128,512]{3,2,0,1:T(8,128)(2,1)S(1)} %maximum_bitcast_fusion), channel_id=1, source_target_pairs={{0,8},{8,0},{16,24},{24,16},{1,9},{9,1},{17,25},{25,17},{2,10},{10... | collective-permute-start | bytes 1572872 | tf_op jit(solution)/shard_map/ppermute | solution.py:20
  54.5 3.6 %collective-permute-start.3 = (bf16[2,128,512]{2,1,0:T(8,128)(2,1)S(1)}, bf16[2,128,512]{2,1,0:T(8,128)(2,1)S(1)}, u32[]{:S(2)}, u32[]{:S(2)}) collective-permute-start(bf16[2,128,512]{2,1,0:T(8,128)(2,1)S(1)} %copy-done.2), channel_id=1, source_target_pairs={{0,8},{8,0},{16,24},{24,16},{1,9},{9,1},{17,25},{25,17},{2,10},{10... | collective-permute-start | bytes 786440 | tf_op jit(solution)/shard_map/ppermute | solution.py:20
  58.0 1.5 %collective-permute-start.4 = (bf16[2,128,512]{2,1,0:T(8,128)(2,1)S(1)}, bf16[2,128,512]{2,1,0:T(8,128)(2,1)S(1)}, u32[]{:S(2)}, u32[]{:S(2)}) collective-permute-start(bf16[2,128,512]{2,1,0:T(8,128)(2,1)S(1)} %collective-permute-done.2), channel_id=1, source_target_pairs={{0,8},{8,0},{16,24},{24,16},{1,9},{9,1},{17,25},{25,17},{2,10},{10... | collective-permute-start | bytes 786440 | tf_op jit(solution)/shard_map/ppermute | solution.py:20
  72.6 1.9 %collective-permute-start.14 = (f32[8,128]{1,0:T(8,128)S(1)}, f32[8,128]{1,0:T(8,128)S(1)}, u32[]{:S(2)}, u32[]{:S(2)}) collective-permute-start(f32[8,128]{1,0:T(8,128)S(1)} %get-tuple-element.30.refs_0_), channel_id=1, source_target_pairs={{0,8},{8,0},{16,24},{24,16},{1,9},{9,1},{17,25},{25,17},{2,10},{10... | collective-permute-start | bytes 12296 | tf_op jit(solution)/shard_map/ppermute | solution.py:20
  72.7 3.7 %collective-permute-start.15 = (f32[8,128]{1,0:T(8,128)S(1)}, f32[8,128]{1,0:T(8,128)S(1)}, u32[]{:S(2)}, u32[]{:S(2)}) collective-permute-start(f32[8,128]{1,0:T(8,128)S(1)} %get-tuple-element.30.refs_0_), channel_id=1, source_target_pairs={{0,16},{8,24},{16,0},{24,8},{1,17},{9,25},{17,1},{25,9},{2,18},{10... | collective-permute-start | bytes 12296 | tf_op jit(solution)/shard_map/ppermute | solution.py:20
  74.4 3.0 %collective-permute-start.16 = (f32[8,128]{1,0:T(8,128)S(1)}, f32[8,128]{1,0:T(8,128)S(1)}, u32[]{:S(2)}, u32[]{:S(2)}) collective-permute-start(f32[8,128]{1,0:T(8,128)S(1)} %get-tuple-element.30.refs_0_), channel_id=1, source_target_pairs={{0,24},{8,16},{16,8},{24,0},{1,25},{9,17},{17,9},{25,1},{2,26},{10... | collective-permute-start | bytes 12296 | tf_op jit(solution)/shard_map/ppermute | solution.py:20

commit v7 on v6

--- a/solution.py
+++ b/solution.py
@@ -194,8 +194,8 @@
         compiler_params=params,
     )(owner_lists, owner_offsets)
     right_slots = over_dp(right_roots)
+    right_slots, plan, partial_blocks = lax.optimization_barrier((right_slots, plan, partial_blocks))
     total = core_sum(partial_blocks, dp_index)
-    right_slots, total, plan = lax.optimization_barrier((right_slots, total, plan))
     outgoing = pl.pallas_call(
         functools.partial(right_kernel, mp_count),
         out_shape=[piece] * mp_count,

time: 78.6 us -> 79 us (level)
  waiting for transfers between devices: 34.3 us -> 36.9 us
  local copies, waits for them, and re-layouts: 2.21 us -> 0.38 us
  other arithmetic: 3.22 us -> 2.19 us
    ppermute x17, waiting for transfers between devices: 16.7 us -> 18.6 us  [swap(): return lax.ppermute(value, axis, [(i, i ^ distance) for i in range(count)])]
    dynamic_slice x1, local copies, waits for them, and re-layouts: 1.17 us -> 0.03 us  [core_sum(): lax.dynamic_slice_in_dim(partial_blocks, (1 - core) * half, half, axis=1)]
    convert_element_type x1, other arithmetic: 1.18 us -> 0.14 us  [add_rounded(): return (a.astype(jnp.float32) + b.astype(jnp.float32)).astype(jnp.bfloat16)]
    all_to_all x2, waiting for transfers between devices: 6.43 us -> 7.24 us  [over_dp(): lax.all_to_all(factor[0, 0].reshape(dp_count, rows, width), 'dp', split_a...]
  transfers between devices with their start and end apart: 20 -> 20, of which waited for: 8 -> 9; matrix products, arithmetic and copies ran while one was open for 5% -> 4% of each run, Pallas kernels for 6% -> 6%
where the time goes in v7:
time: 79 us; the launch traced here: 78.6 us
  waiting for transfers between devices  36.9 us (47%)
  starting transfers between devices  31.9 us (40%)
  Pallas kernels  6.31 us (8%)
  other arithmetic  2.19 us (3%)
    ppermute x17, starting transfers between devices, swap(): return lax.ppermute(value, axis, [(i, i ^ distance) for i in range(count)])  18.6 us
    ppermute x17, waiting for transfers between devices, swap(): return lax.ppermute(value, axis, [(i, i ^ distance) for i in range(count)])  18.6 us
    all_to_all x1, waiting for transfers between devices, shards(): lax.all_to_all(left_outgoing, 'mp', split_axis=0, concat_axis=0, tiled=True)  11.1 us
    all_to_all x2, starting transfers between devices, over_dp(): lax.all_to_all(factor[0, 0].reshape(dp_count, rows, width), 'dp', split_a...  7.85 us
    all_to_all x2, waiting for transfers between devices, over_dp(): lax.all_to_all(factor[0, 0].reshape(dp_count, rows, width), 'dp', split_a...  7.24 us
    all_to_all x1, starting transfers between devices, shards(): lax.all_to_all(left_outgoing, 'mp', split_axis=0, concat_axis=0, tiled=True)  5.39 us
    reduce_sum x1, other arithmetic, shards(): jnp.sum(total_f * total_f, axis=(1, 2)).reshape(per_shard, 1)  1.78 us
    pallas_call x1, Pallas kernels, shards(): pl.pallas_call(functools.partial(left_kernel, mp_count), out_shape=jax.Sh...  1.72 us
  transfers between devices with their start and end apart: 20, of which 9 were waited for; matrix products, arithmetic and copies ran while one was open for 4% of the time, Pallas kernels for 6%

profile of v7, /device:TPU:0, one launch (start us, length us, event | category | flops | bytes accessed | tf_op | source)
XLA Modules:
  0.0 78.6 jit_solution(14235923335616849313)
XLA Ops:
  0.0 4.4 %all-to-all-start = ((bf16[4,128,512]{2,1,0:T(8,128)(2,1)}), bf16[4,128,512]{2,1,0:T(8,128)(2,1)S(1)}, u32[]{:S(2)}, u32[]{:S(2)}) async-start(bf16[4,128,512]{2,1,0:T(8,128)(2,1)} %bitcast.27), calls=%async_computation | async-start | bytes 1048576 | tf_op jit(solution)/shard_map/all_to_all | solution.py:185
  4.4 1.6 %shard_map.55.plan = s32[10]{0:T(128)S(1)} custom-call(s32[16]{0:T(128)S(1)} %copy-done, s32[9]{0:T(128)S(1)} %copy-done.1), custom_call_target="tpu_custom_call" | custom-call | tf_op jit(solution)/shard_map/pallas_call | solution.py:189
  6.0 7.2 %all-to-all-done.slots = bf16[4,128,512]{2,1,0:T(8,128)(2,1)S(1)} async-done(((bf16[4,128,512]{2,1,0:T(8,128)(2,1)}), bf16[4,128,512]{2,1,0:T(8,128)(2,1)S(1)}, u32[]{:S(2)}, u32[]{:S(2)}) %all-to-all-start) | async-done | bytes 524320 | tf_op jit(solution)/shard_map/all_to_all | solution.py:185
  13.3 0.1 collective-permute-start
  13.4 1.9 %collective-permute-done = bf16[2,256,512]{2,1,0:T(8,128)(2,1)S(1)} collective-permute-done((bf16[2,256,512]{2,1,0:T(8,128)(2,1)S(1)}, bf16[2,256,512]{2,1,0:T(8,128)(2,1)S(1)}, u32[]{:S(2)}, u32[]{:S(2)}) %collective-permute-start) | collective-permute-done | bytes 524320 | tf_op jit(solution)/shard_map/ppermute | solution.py:20
  15.3 0.1 add_convert_fusion
  15.4 0.4 collective-permute-start.1
  15.9 3.5 %all-to-all-start.1 = ((bf16[4,128,512]{2,1,0:T(8,128)(2,1)}), bf16[4,128,512]{2,1,0:T(8,128)(2,1)S(1)}, u32[]{:S(2)}, u32[]{:S(2)}) async-start(bf16[4,128,512]{2,1,0:T(8,128)(2,1)} %bitcast.2), calls=%async_computation.1 | async-start | bytes 1048576 | tf_op jit(solution)/shard_map/all_to_all | solution.py:185
  19.3 0.6 shard_map.56
  20.0 2.2 %collective-permute-start.5 = (bf16[128,512]{1,0:T(8,128)(2,1)S(1)}, bf16[128,512]{1,0:T(8,128)(2,1)S(1)}, u32[]{:S(2)}, u32[]{:S(2)}) collective-permute-start(bf16[128,512]{1,0:T(8,128)(2,1)S(1)} %get-tuple-element.22), channel_id=1, source_target_pairs={{0,1},{1,0},{2,3},{3,2},{4,5},{5,4},{6,7},{7,6},{8,9},{9,8},{10,11... | collective-permute-start | bytes 393224 | tf_op jit(solution)/shard_map/ppermute | solution.py:20
  22.2 2.6 %collective-permute-start.6 = (bf16[128,512]{1,0:T(8,128)(2,1)S(1)}, bf16[128,512]{1,0:T(8,128)(2,1)S(1)}, u32[]{:S(2)}, u32[]{:S(2)}) collective-permute-start(bf16[128,512]{1,0:T(8,128)(2,1)S(1)} %get-tuple-element.23), channel_id=1, source_target_pairs={{0,4},{1,5},{2,6},{3,7},{4,0},{5,1},{6,2},{7,3},{8,12},{9,13},{10,... | collective-permute-start | bytes 393224 | tf_op jit(solution)/shard_map/ppermute | solution.py:20
  24.8 1.6 %collective-permute-start.7 = (bf16[128,512]{1,0:T(8,128)(2,1)S(1)}, bf16[128,512]{1,0:T(8,128)(2,1)S(1)}, u32[]{:S(2)}, u32[]{:S(2)}) collective-permute-start(bf16[128,512]{1,0:T(8,128)(2,1)S(1)} %get-tuple-element.24), channel_id=1, source_target_pairs={{0,2},{1,3},{2,0},{3,1},{4,6},{5,7},{6,4},{7,5},{8,10},{9,11},{10,... | collective-permute-start | bytes 393224 | tf_op jit(solution)/shard_map/ppermute | solution.py:20
  26.3 0.4 collective-permute-start.8
  26.8 3.3 %collective-permute-start.9 = (bf16[128,512]{1,0:T(8,128)(2,1)S(1)}, bf16[128,512]{1,0:T(8,128)(2,1)S(1)}, u32[]{:S(2)}, u32[]{:S(2)}) collective-permute-start(bf16[128,512]{1,0:T(8,128)(2,1)S(1)} %get-tuple-element.26), channel_id=1, source_target_pairs={{0,5},{1,4},{2,7},{3,6},{4,1},{5,0},{6,3},{7,2},{8,13},{9,12},{10,... | collective-permute-start | bytes 393224 | tf_op jit(solution)/shard_map/ppermute | solution.py:20
  30.1 2.2 %collective-permute-done.6.refs_2_ = bf16[128,512]{1,0:T(8,128)(2,1)S(1)} collective-permute-done((bf16[128,512]{1,0:T(8,128)(2,1)S(1)}, bf16[128,512]{1,0:T(8,128)(2,1)S(1)}, u32[]{:S(2)}, u32[]{:S(2)}) %collective-permute-start.6) | collective-permute-done | bytes 131104 | tf_op jit(solution)/shard_map/ppermute | solution.py:20
  32.3 2.8 %collective-permute-start.10 = (bf16[128,512]{1,0:T(8,128)(2,1)S(1)}, bf16[128,512]{1,0:T(8,128)(2,1)S(1)}, u32[]{:S(2)}, u32[]{:S(2)}) collective-permute-start(bf16[128,512]{1,0:T(8,128)(2,1)S(1)} %get-tuple-element.27), channel_id=1, source_target_pairs={{0,6},{1,7},{2,4},{3,5},{4,2},{5,3},{6,0},{7,1},{8,14},{9,15},{10,... | collective-permute-start | bytes 393224 | tf_op jit(solution)/shard_map/ppermute | solution.py:20
  35.1 0.6 collective-permute-start.11
  35.7 1.8 %multiply_reduce_fusion = (f32[2]{0:T(128)S(1)}, bf16[2,128,512]{2,1,0:T(8,128)(2,1)}) fusion(bf16[2,128,512]{2,1,0:T(8,128)(2,1)} %collective-permute-done.1, bf16[2,256,512]{2,1,0:T(8,128)(2,1)S(1)} %add_convert_fusion, s32[]{:T(128)S(6)} %select_n.116), kind=kLoop, calls=%fused_computation.6 | loop fusion | flops 917502 | bytes 786444 | tf_op jit(solution)/shard_map/reduce_sum | solution.py:213
  37.5 0.1 broadcast_in_dim.12.half_sq
  37.6 1.7 %shard_map.57.refs_8_ = bf16[8,528,128]{2,1,0:T(8,128)(2,1)} custom-call(s32[10]{0:T(128)S(1)} %shard_map.55.plan, bf16[4,128,512]{2,1,0:T(8,128)(2,1)S(1)} %all-to-all-done.1.slots, f32[2,128]{1,0:T(2,128)S(1)} %broadcast_in_dim.12.half_sq), custom_call_target="tpu_custom_call" | custom-call | tf_op jit(solution)/shard_map/pallas_call | solution.py:216
  39.3 5.4 %all-to-all-start.2 = ((bf16[8,528,128]{2,1,0:T(8,128)(2,1)}), bf16[8,528,128]{2,1,0:T(8,128)(2,1)S(1)}, u32[]{:S(2)}, u32[]{:S(2)}) async-start(bf16[8,528,128]{2,1,0:T(8,128)(2,1)} %shard_map.57.refs_8_), calls=%async_computation.2 | async-start | bytes 2162688 | tf_op jit(solution)/shard_map/all_to_all | solution.py:223
  44.7 0.0 collective-permute-done.8.refs_4_
  44.7 0.0 collective-permute-done.11.refs_7_
  44.8 0.0 copy-start.2
  44.8 0.6 shard_map.58
  45.4 1.8 %collective-permute-start.12 = (bf16[2,1,128,512]{3,2,0,1:T(8,128)(2,1)S(1)}, bf16[2,1,128,512]{3,2,0,1:T(8,128)(2,1)S(1)}, u32[]{:S(2)}, u32[]{:S(2)}) collective-permute-start(bf16[2,1,128,512]{3,2,0,1:T(8,128)(2,1)S(1)} %bitcast.23), channel_id=1, source_target_pairs={{0,16},{8,24},{16,0},{24,8},{1,17},{9,25},{17,1},{25,9},{2,18},{10... | collective-permute-start | bytes 786440 | tf_op jit(solution)/shard_map/ppermute | solution.py:20
  47.2 0.3 collective-permute-start.2
  47.5 7.2 %collective-permute-done.12 = bf16[2,1,128,512]{3,2,0,1:T(8,128)(2,1)S(1)} collective-permute-done((bf16[2,1,128,512]{3,2,0,1:T(8,128)(2,1)S(1)}, bf16[2,1,128,512]{3,2,0,1:T(8,128)(2,1)S(1)}, u32[]{:S(2)}, u32[]{:S(2)}) %collective-permute-start.12) | collective-permute-done | bytes 262176 | tf_op jit(solution)/shard_map/ppermute | solution.py:20
  54.8 0.1 maximum_bitcast_fusion
  54.8 0.1 collective-permute-start.13
  54.9 0.5 collective-permute-start.3
  55.4 3.0 %collective-permute-done.2 = bf16[2,128,512]{2,1,0:T(8,128)(2,1)S(1)} collective-permute-done((bf16[2,128,512]{2,1,0:T(8,128)(2,1)S(1)}, bf16[2,128,512]{2,1,0:T(8,128)(2,1)S(1)}, u32[]{:S(2)}, u32[]{:S(2)}) %collective-permute-start.2) | collective-permute-done | bytes 262176 | tf_op jit(solution)/shard_map/ppermute | solution.py:20
  58.4 0.0 collective-permute-start.4
  58.4 0.1 broadcast_in_dim.11
  58.6 1.3 %collective-permute-done.4 = bf16[2,128,512]{2,1,0:T(8,128)(2,1)S(1)} collective-permute-done((bf16[2,128,512]{2,1,0:T(8,128)(2,1)S(1)}, bf16[2,128,512]{2,1,0:T(8,128)(2,1)S(1)}, u32[]{:S(2)}, u32[]{:S(2)}) %collective-permute-start.4) | collective-permute-done | bytes 262176 | tf_op jit(solution)/shard_map/ppermute | solution.py:20
  60.0 0.1 select_bitcast_fusion.1
  60.0 0.1 pad_maximum_fusion
  60.1 0.1 copy.6
  60.2 0.7 convolution_convert_fusion.right_prod
  60.9 11.1 %all-to-all-done.2.arrived = bf16[8,528,128]{2,1,0:T(8,128)(2,1)S(1)} async-done(((bf16[8,528,128]{2,1,0:T(8,128)(2,1)}), bf16[8,528,128]{2,1,0:T(8,128)(2,1)S(1)}, u32[]{:S(2)}, u32[]{:S(2)}) %all-to-all-start.2) | async-done | bytes 1081376 | tf_op jit(solution)/shard_map/all_to_all | solution.py:223
  72.0 0.9 %shard_map.59 = (f32[2,128,512]{2,1,0:T(8,128)S(1)}, f32[8,128]{1,0:T(8,128)S(1)}) custom-call(s32[10]{0:T(128)S(1)} %shard_map.55.plan, bf16[2,512,512]{2,1,0:T(8,128)(2,1)S(1)} %convolution_convert_fusion.right_prod, f32[2,128]{1,0:T(2,128)S(1)} %broadcast_in_dim.12.half_sq, bf16[8,528,128]{2,1,0:T(8,128)(2,1)S(1)} %all-to-all-done.2.arrived), custom_call_target="tpu_custom_call" | custom-call | tf_op jit(solution)/shard_map/pallas_call | solution.py:237
  73.0 0.1 collective-permute-start.14
  73.1 1.7 %collective-permute-start.15 = (f32[8,128]{1,0:T(8,128)S(1)}, f32[8,128]{1,0:T(8,128)S(1)}, u32[]{:S(2)}, u32[]{:S(2)}) collective-permute-start(f32[8,128]{1,0:T(8,128)S(1)} %get-tuple-element.30.refs_0_), channel_id=1, source_target_pairs={{0,16},{8,24},{16,0},{24,8},{1,17},{9,25},{17,1},{25,9},{2,18},{10... | collective-permute-start | bytes 12296 | tf_op jit(solution)/shard_map/ppermute | solution.py:20
  74.8 0.1 collective-permute-start.16
  74.9 0.0 collective-permute-done.14.refs_1_
  74.9 1.8 %collective-permute-done.15.refs_2_ = f32[8,128]{1,0:T(8,128)S(1)} collective-permute-done((f32[8,128]{1,0:T(8,128)S(1)}, f32[8,128]{1,0:T(8,128)S(1)}, u32[]{:S(2)}, u32[]{:S(2)}) %collective-permute-start.15) | collective-permute-done | bytes 4128 | tf_op jit(solution)/shard_map/ppermute | solution.py:20
  76.7 1.1 %collective-permute-done.16.refs_3_ = f32[8,128]{1,0:T(8,128)S(1)} collective-permute-done((f32[8,128]{1,0:T(8,128)S(1)}, f32[8,128]{1,0:T(8,128)S(1)}, u32[]{:S(2)}, u32[]{:S(2)}) %collective-permute-start.16) | collective-permute-done | bytes 4128 | tf_op jit(solution)/shard_map/ppermute | solution.py:20
  77.8 0.8 %shard_map.60 = bf16[2,128,512]{2,1,0:T(8,128)(2,1)} custom-call(f32[2,128,512]{2,1,0:T(8,128)S(1)} %get-tuple-element.29.precond, f32[8,128]{1,0:T(8,128)S(1)} %get-tuple-element.30.refs_0_, f32[8,128]{1,0:T(8,128)S(1)} %collective-permute-done.14.refs_1_, f32[8,128]{1,0:T(8,128)S(1)} %collective-permute-done.15.refs_2_, ...), custom_call_target="tpu_custom_call" | custom-call | tf_op jit(solution)/shard_map/pallas_call | solution.py:249
  (22 shorter events, 0.2 us)
Async XLA Ops:
  0.0 4.4 %copy-start = (s32[16]{0:T(128)S(1)}, s32[16]{0:T(128)}, u32[]{:S(2)}) copy-start(s32[16]{0:T(128)} %lists.1) | copy-start | bytes 196
  0.0 4.4 %copy-start.1 = (s32[9]{0:T(128)S(1)}, s32[9]{0:T(128)}, u32[]{:S(2)}) copy-start(s32[9]{0:T(128)} %offsets.1) | copy-start | bytes 112
  0.0 13.2 %copy-start.3 = (bf16[1,2,512,512]{3,2,1,0:T(8,128)(2,1)S(1)}, bf16[1,2,512,512]{3,2,1,0:T(8,128)(2,1)}, u32[]{:S(2)}) copy-start(bf16[1,2,512,512]{3,2,1,0:T(8,128)(2,1)} %param.5) | copy-start | bytes 3145732
  0.0 13.2 %all-to-all-start = ((bf16[4,128,512]{2,1,0:T(8,128)(2,1)}), bf16[4,128,512]{2,1,0:T(8,128)(2,1)S(1)}, u32[]{:S(2)}, u32[]{:S(2)}) async-start(bf16[4,128,512]{2,1,0:T(8,128)(2,1)} %bitcast.27), calls=%async_computation | async-start | bytes 1048576 | tf_op jit(solution)/shard_map/all_to_all | solution.py:185
  13.3 2.0 %collective-permute-start = (bf16[2,256,512]{2,1,0:T(8,128)(2,1)S(1)}, bf16[2,256,512]{2,1,0:T(8,128)(2,1)S(1)}, u32[]{:S(2)}, u32[]{:S(2)}) collective-permute-start(bf16[2,256,512]{2,1,0:T(8,128)(2,1)S(1)} %constant_dynamic-slice_fusion.1), channel_id=1, source_target_pairs={{0,8},{8,0},{16,24},{24,16},{1,9},{9,1},{17,25},{25,17},{2,10},{10... | collective-permute-start | bytes 1572872 | tf_op jit(solution)/shard_map/ppermute | solution.py:20
  15.4 19.7 %collective-permute-start.1 = (bf16[2,128,512]{2,1,0:T(8,128)(2,1)S(1)}, bf16[2,128,512]{2,1,0:T(8,128)(2,1)}, u32[]{:S(2)}, u32[]{:S(2)}) collective-permute-start(bf16[2,128,512]{2,1,0:T(8,128)(2,1)S(1)} %constant_dynamic-slice_fusion), channel_id=1, source_target_pairs={{0,16},{8,24},{16,0},{24,8},{1,17},{9,25},{17,1},{25,9},{2,18},{10... | collective-permute-start | bytes 786440 | tf_op jit(solution)/shard_map/ppermute | solution.py:20
  15.9 21.7 %all-to-all-start.1 = ((bf16[4,128,512]{2,1,0:T(8,128)(2,1)}), bf16[4,128,512]{2,1,0:T(8,128)(2,1)S(1)}, u32[]{:S(2)}, u32[]{:S(2)}) async-start(bf16[4,128,512]{2,1,0:T(8,128)(2,1)} %bitcast.2), calls=%async_computation.1 | async-start | bytes 1048576 | tf_op jit(solution)/shard_map/all_to_all | solution.py:185
  20.0 6.8 %collective-permute-start.5 = (bf16[128,512]{1,0:T(8,128)(2,1)S(1)}, bf16[128,512]{1,0:T(8,128)(2,1)S(1)}, u32[]{:S(2)}, u32[]{:S(2)}) collective-permute-start(bf16[128,512]{1,0:T(8,128)(2,1)S(1)} %get-tuple-element.22), channel_id=1, source_target_pairs={{0,1},{1,0},{2,3},{3,2},{4,5},{5,4},{6,7},{7,6},{8,9},{9,8},{10,11... | collective-permute-start | bytes 393224 | tf_op jit(solution)/shard_map/ppermute | solution.py:20
  22.2 10.1 %collective-permute-start.6 = (bf16[128,512]{1,0:T(8,128)(2,1)S(1)}, bf16[128,512]{1,0:T(8,128)(2,1)S(1)}, u32[]{:S(2)}, u32[]{:S(2)}) collective-permute-start(bf16[128,512]{1,0:T(8,128)(2,1)S(1)} %get-tuple-element.23), channel_id=1, source_target_pairs={{0,4},{1,5},{2,6},{3,7},{4,0},{5,1},{6,2},{7,3},{8,12},{9,13},{10,... | collective-permute-start | bytes 393224 | tf_op jit(solution)/shard_map/ppermute | solution.py:20
  24.8 19.9 %collective-permute-start.7 = (bf16[128,512]{1,0:T(8,128)(2,1)S(1)}, bf16[128,512]{1,0:T(8,128)(2,1)S(1)}, u32[]{:S(2)}, u32[]{:S(2)}) collective-permute-start(bf16[128,512]{1,0:T(8,128)(2,1)S(1)} %get-tuple-element.24), channel_id=1, source_target_pairs={{0,2},{1,3},{2,0},{3,1},{4,6},{5,7},{6,4},{7,5},{8,10},{9,11},{10,... | collective-permute-start | bytes 393224 | tf_op jit(solution)/shard_map/ppermute | solution.py:20
  26.3 18.4 %collective-permute-start.8 = (bf16[128,512]{1,0:T(8,128)(2,1)S(1)}, bf16[128,512]{1,0:T(8,128)(2,1)S(1)}, u32[]{:S(2)}, u32[]{:S(2)}) collective-permute-start(bf16[128,512]{1,0:T(8,128)(2,1)S(1)} %get-tuple-element.25), channel_id=1, source_target_pairs={{0,3},{1,2},{2,1},{3,0},{4,7},{5,6},{6,5},{7,4},{8,11},{9,10},{10,... | collective-permute-start | bytes 393224 | tf_op jit(solution)/shard_map/ppermute | solution.py:20
  26.8 18.0 %collective-permute-start.9 = (bf16[128,512]{1,0:T(8,128)(2,1)S(1)}, bf16[128,512]{1,0:T(8,128)(2,1)S(1)}, u32[]{:S(2)}, u32[]{:S(2)}) collective-permute-start(bf16[128,512]{1,0:T(8,128)(2,1)S(1)} %get-tuple-element.26), channel_id=1, source_target_pairs={{0,5},{1,4},{2,7},{3,6},{4,1},{5,0},{6,3},{7,2},{8,13},{9,12},{10,... | collective-permute-start | bytes 393224 | tf_op jit(solution)/shard_map/ppermute | solution.py:20
  32.3 12.4 %collective-permute-start.10 = (bf16[128,512]{1,0:T(8,128)(2,1)S(1)}, bf16[128,512]{1,0:T(8,128)(2,1)S(1)}, u32[]{:S(2)}, u32[]{:S(2)}) collective-permute-start(bf16[128,512]{1,0:T(8,128)(2,1)S(1)} %get-tuple-element.27), channel_id=1, source_target_pairs={{0,6},{1,7},{2,4},{3,5},{4,2},{5,3},{6,0},{7,1},{8,14},{9,15},{10,... | collective-permute-start | bytes 393224 | tf_op jit(solution)/shard_map/ppermute | solution.py:20
  35.1 9.6 %collective-permute-start.11 = (bf16[128,512]{1,0:T(8,128)(2,1)S(1)}, bf16[128,512]{1,0:T(8,128)(2,1)S(1)}, u32[]{:S(2)}, u32[]{:S(2)}) collective-permute-start(bf16[128,512]{1,0:T(8,128)(2,1)S(1)} %get-tuple-element.28), channel_id=1, source_target_pairs={{0,7},{1,6},{2,5},{3,4},{4,3},{5,2},{6,1},{7,0},{8,15},{9,14},{10,... | collective-permute-start | bytes 393224 | tf_op jit(solution)/shard_map/ppermute | solution.py:20
  39.3 32.7 %all-to-all-start.2 = ((bf16[8,528,128]{2,1,0:T(8,128)(2,1)}), bf16[8,528,128]{2,1,0:T(8,128)(2,1)S(1)}, u32[]{:S(2)}, u32[]{:S(2)}) async-start(bf16[8,528,128]{2,1,0:T(8,128)(2,1)} %shard_map.57.refs_8_), calls=%async_computation.2 | async-start | bytes 2162688 | tf_op jit(solution)/shard_map/all_to_all | solution.py:223
  44.8 2.4 %copy-start.2 = (bf16[2,128,512]{2,1,0:T(8,128)(2,1)S(1)}, bf16[2,128,512]{2,1,0:T(8,128)(2,1)}, u32[]{:S(2)}) copy-start(bf16[2,128,512]{2,1,0:T(8,128)(2,1)} %get-tuple-element.32) | copy-start | bytes 786436
  45.4 9.3 %collective-permute-start.12 = (bf16[2,1,128,512]{3,2,0,1:T(8,128)(2,1)S(1)}, bf16[2,1,128,512]{3,2,0,1:T(8,128)(2,1)S(1)}, u32[]{:S(2)}, u32[]{:S(2)}) collective-permute-start(bf16[2,1,128,512]{3,2,0,1:T(8,128)(2,1)S(1)} %bitcast.23), channel_id=1, source_target_pairs={{0,16},{8,24},{16,0},{24,8},{1,17},{9,25},{17,1},{25,9},{2,18},{10... | collective-permute-start | bytes 786440 | tf_op jit(solution)/shard_map/ppermute | solution.py:20
  47.2 11.2 %collective-permute-start.2 = (bf16[2,128,512]{2,1,0:T(8,128)(2,1)S(1)}, bf16[2,128,512]{2,1,0:T(8,128)(2,1)S(1)}, u32[]{:S(2)}, u32[]{:S(2)}) collective-permute-start(bf16[2,128,512]{2,1,0:T(8,128)(2,1)S(1)} %copy-done.2), channel_id=1, source_target_pairs={{0,16},{8,24},{16,0},{24,8},{1,17},{9,25},{17,1},{25,9},{2,18},{10... | collective-permute-start | bytes 786440 | tf_op jit(solution)/shard_map/ppermute | solution.py:20
  54.8 5.1 %collective-permute-start.13 = (bf16[2,2,128,512]{3,2,0,1:T(8,128)(2,1)S(1)}, bf16[2,2,128,512]{3,2,0,1:T(8,128)(2,1)S(1)}, u32[]{:S(2)}, u32[]{:S(2)}) collective-permute-start(bf16[2,2,128,512]{3,2,0,1:T(8,128)(2,1)S(1)} %maximum_bitcast_fusion), channel_id=1, source_target_pairs={{0,8},{8,0},{16,24},{24,16},{1,9},{9,1},{17,25},{25,17},{2,10},{10... | collective-permute-start | bytes 1572872 | tf_op jit(solution)/shard_map/ppermute | solution.py:20
  54.9 3.6 %collective-permute-start.3 = (bf16[2,128,512]{2,1,0:T(8,128)(2,1)S(1)}, bf16[2,128,512]{2,1,0:T(8,128)(2,1)S(1)}, u32[]{:S(2)}, u32[]{:S(2)}) collective-permute-start(bf16[2,128,512]{2,1,0:T(8,128)(2,1)S(1)} %copy-done.2), channel_id=1, source_target_pairs={{0,8},{8,0},{16,24},{24,16},{1,9},{9,1},{17,25},{25,17},{2,10},{10... | collective-permute-start | bytes 786440 | tf_op jit(solution)/shard_map/ppermute | solution.py:20
  58.4 1.5 %collective-permute-start.4 = (bf16[2,128,512]{2,1,0:T(8,128)(2,1)S(1)}, bf16[2,128,512]{2,1,0:T(8,128)(2,1)S(1)}, u32[]{:S(2)}, u32[]{:S(2)}) collective-permute-start(bf16[2,128,512]{2,1,0:T(8,128)(2,1)S(1)} %collective-permute-done.2), channel_id=1, source_target_pairs={{0,8},{8,0},{16,24},{24,16},{1,9},{9,1},{17,25},{25,17},{2,10},{10... | collective-permute-start | bytes 786440 | tf_op jit(solution)/shard_map/ppermute | solution.py:20
  73.0 1.9 %collective-permute-start.14 = (f32[8,128]{1,0:T(8,128)S(1)}, f32[8,128]{1,0:T(8,128)S(1)}, u32[]{:S(2)}, u32[]{:S(2)}) collective-permute-start(f32[8,128]{1,0:T(8,128)S(1)} %get-tuple-element.30.refs_0_), channel_id=1, source_target_pairs={{0,8},{8,0},{16,24},{24,16},{1,9},{9,1},{17,25},{25,17},{2,10},{10... | collective-permute-start | bytes 12296 | tf_op jit(solution)/shard_map/ppermute | solution.py:20
  73.1 3.7 %collective-permute-start.15 = (f32[8,128]{1,0:T(8,128)S(1)}, f32[8,128]{1,0:T(8,128)S(1)}, u32[]{:S(2)}, u32[]{:S(2)}) collective-permute-start(f32[8,128]{1,0:T(8,128)S(1)} %get-tuple-element.30.refs_0_), channel_id=1, source_target_pairs={{0,16},{8,24},{16,0},{24,8},{1,17},{9,25},{17,1},{25,9},{2,18},{10... | collective-permute-start | bytes 12296 | tf_op jit(solution)/shard_map/ppermute | solution.py:20
  74.8 3.0 %collective-permute-start.16 = (f32[8,128]{1,0:T(8,128)S(1)}, f32[8,128]{1,0:T(8,128)S(1)}, u32[]{:S(2)}, u32[]{:S(2)}) collective-permute-start(f32[8,128]{1,0:T(8,128)S(1)} %get-tuple-element.30.refs_0_), channel_id=1, source_target_pairs={{0,24},{8,16},{16,8},{24,0},{1,25},{9,17},{17,9},{25,1},{2,26},{10... | collective-permute-start | bytes 12296 | tf_op jit(solution)/shard_map/ppermute | solution.py:20

commit v8 on v6

--- a/solution.py
+++ b/solution.py
@@ -27,9 +27,10 @@
 def core_sum(partial_blocks, dp_index):
     half = partial_blocks.shape[1] // 2
     core = dp_index % 2
+    other = swap(partial_blocks, "dp", 1)
     kept = lax.dynamic_slice_in_dim(partial_blocks, core * half, half, axis=1)
-    given = lax.dynamic_slice_in_dim(partial_blocks, (1 - core) * half, half, axis=1)
-    return add_rounded(kept, swap(given, "dp", 1))
+    taken = lax.dynamic_slice_in_dim(other, core * half, half, axis=1)
+    return add_rounded(kept, taken)
 
 
 def chip_sum(total, dp_count, dp_index):

time: 78.6 us -> 76.3 us (0.971)
  local copies, waits for them, and re-layouts: 2.21 us -> 0.34 us
  other arithmetic: 3.22 us -> 2.19 us
    dynamic_slice x1 -> x0, local copies, waits for them, and re-layouts: 1.17 us -> none  [core_sum(): lax.dynamic_slice_in_dim(partial_blocks, (1 - core) * half, half, axis=1)]
    convert_element_type x1, other arithmetic: 1.18 us -> 0.14 us  [add_rounded(): return (a.astype(jnp.float32) + b.astype(jnp.float32)).astype(jnp.bfloat16)]
    all_to_all x2, waiting for transfers between devices: 6.43 us -> 7.43 us  [over_dp(): lax.all_to_all(factor[0, 0].reshape(dp_count, rows, width), 'dp', split_a...]
  transfers between devices with their start and end apart: 20 -> 20, of which waited for: 8 -> 8; matrix products, arithmetic and copies ran while one was open for 5% -> 4% of each run, Pallas kernels for 6% -> 6%
where the time goes in v8:
time: 76.3 us; the launch traced here: 76 us
  waiting for transfers between devices  34.7 us (45%)
  starting transfers between devices  31.5 us (41%)
  Pallas kernels  6.33 us (8%)
  other arithmetic  2.19 us (3%)
    ppermute x17, starting transfers between devices, swap(): return lax.ppermute(value, axis, [(i, i ^ distance) for i in range(count)])  18.7 us
    ppermute x17, waiting for transfers between devices, swap(): return lax.ppermute(value, axis, [(i, i ^ distance) for i in range(count)])  16.2 us
    all_to_all x1, waiting for transfers between devices, shards(): lax.all_to_all(left_outgoing, 'mp', split_axis=0, concat_axis=0, tiled=True)  11.1 us
    all_to_all x2, waiting for transfers between devices, over_dp(): lax.all_to_all(factor[0, 0].reshape(dp_count, rows, width), 'dp', split_a...  7.43 us
    all_to_all x2, starting transfers between devices, over_dp(): lax.all_to_all(factor[0, 0].reshape(dp_count, rows, width), 'dp', split_a...  7.42 us
    all_to_all x1, starting transfers between devices, shards(): lax.all_to_all(left_outgoing, 'mp', split_axis=0, concat_axis=0, tiled=True)  5.39 us
    reduce_sum x1, other arithmetic, shards(): jnp.sum(total_f * total_f, axis=(1, 2)).reshape(per_shard, 1)  1.78 us
    pallas_call x1, Pallas kernels, shards(): pl.pallas_call(functools.partial(left_kernel, mp_count), out_shape=jax.Sh...  1.72 us
  transfers between devices with their start and end apart: 20, of which 8 were waited for; matrix products, arithmetic and copies ran while one was open for 4% of the time, Pallas kernels for 6%

profile of v8, /device:TPU:0, one launch (start us, length us, event | category | flops | bytes accessed | tf_op | source)
XLA Modules:
  0.0 76.0 jit_solution(13844771373966188111)
XLA Ops:
  0.0 0.5 collective-permute-start
  0.5 3.9 %all-to-all-start = ((bf16[4,128,512]{2,1,0:T(8,128)(2,1)}), bf16[4,128,512]{2,1,0:T(8,128)(2,1)S(1)}, u32[]{:S(2)}, u32[]{:S(2)}) async-start(bf16[4,128,512]{2,1,0:T(8,128)(2,1)} %bitcast.28), calls=%async_computation | async-start | bytes 1048576 | tf_op jit(solution)/shard_map/all_to_all | solution.py:186
  4.5 1.6 %shard_map.55.plan = s32[10]{0:T(128)S(1)} custom-call(s32[16]{0:T(128)S(1)} %copy-done, s32[9]{0:T(128)S(1)} %copy-done.1), custom_call_target="tpu_custom_call" | custom-call | tf_op jit(solution)/shard_map/pallas_call | solution.py:190
  6.1 0.1 fusion
  6.2 7.4 %all-to-all-done.slots = bf16[4,128,512]{2,1,0:T(8,128)(2,1)S(1)} async-done(((bf16[4,128,512]{2,1,0:T(8,128)(2,1)}), bf16[4,128,512]{2,1,0:T(8,128)(2,1)S(1)}, u32[]{:S(2)}, u32[]{:S(2)}) %all-to-all-start) | async-done | bytes 524320 | tf_op jit(solution)/shard_map/all_to_all | solution.py:186
  13.7 0.1 collective-permute-start.1
  13.8 3.5 %all-to-all-start.1 = ((bf16[4,128,512]{2,1,0:T(8,128)(2,1)}), bf16[4,128,512]{2,1,0:T(8,128)(2,1)S(1)}, u32[]{:S(2)}, u32[]{:S(2)}) async-start(bf16[4,128,512]{2,1,0:T(8,128)(2,1)} %bitcast.3), calls=%async_computation.1 | async-start | bytes 1048576 | tf_op jit(solution)/shard_map/all_to_all | solution.py:186
  17.3 0.6 shard_map.56
  17.9 2.2 %collective-permute-start.5 = (bf16[128,512]{1,0:T(8,128)(2,1)S(1)}, bf16[128,512]{1,0:T(8,128)(2,1)S(1)}, u32[]{:S(2)}, u32[]{:S(2)}) collective-permute-start(bf16[128,512]{1,0:T(8,128)(2,1)S(1)} %get-tuple-element.22), channel_id=1, source_target_pairs={{0,1},{1,0},{2,3},{3,2},{4,5},{5,4},{6,7},{7,6},{8,9},{9,8},{10,11... | collective-permute-start | bytes 393224 | tf_op jit(solution)/shard_map/ppermute | solution.py:20
  20.1 2.6 %collective-permute-start.6 = (bf16[128,512]{1,0:T(8,128)(2,1)S(1)}, bf16[128,512]{1,0:T(8,128)(2,1)S(1)}, u32[]{:S(2)}, u32[]{:S(2)}) collective-permute-start(bf16[128,512]{1,0:T(8,128)(2,1)S(1)} %get-tuple-element.23), channel_id=1, source_target_pairs={{0,4},{1,5},{2,6},{3,7},{4,0},{5,1},{6,2},{7,3},{8,12},{9,13},{10,... | collective-permute-start | bytes 393224 | tf_op jit(solution)/shard_map/ppermute | solution.py:20
  22.7 1.6 %collective-permute-start.7 = (bf16[128,512]{1,0:T(8,128)(2,1)S(1)}, bf16[128,512]{1,0:T(8,128)(2,1)S(1)}, u32[]{:S(2)}, u32[]{:S(2)}) collective-permute-start(bf16[128,512]{1,0:T(8,128)(2,1)S(1)} %get-tuple-element.24), channel_id=1, source_target_pairs={{0,2},{1,3},{2,0},{3,1},{4,6},{5,7},{6,4},{7,5},{8,10},{9,11},{10,... | collective-permute-start | bytes 393224 | tf_op jit(solution)/shard_map/ppermute | solution.py:20
  24.2 0.4 collective-permute-start.8
  24.7 3.3 %collective-permute-start.9 = (bf16[128,512]{1,0:T(8,128)(2,1)S(1)}, bf16[128,512]{1,0:T(8,128)(2,1)S(1)}, u32[]{:S(2)}, u32[]{:S(2)}) collective-permute-start(bf16[128,512]{1,0:T(8,128)(2,1)S(1)} %get-tuple-element.26), channel_id=1, source_target_pairs={{0,5},{1,4},{2,7},{3,6},{4,1},{5,0},{6,3},{7,2},{8,13},{9,12},{10,... | collective-permute-start | bytes 393224 | tf_op jit(solution)/shard_map/ppermute | solution.py:20
  28.0 2.2 %collective-permute-done.6.refs_2_ = bf16[128,512]{1,0:T(8,128)(2,1)S(1)} collective-permute-done((bf16[128,512]{1,0:T(8,128)(2,1)S(1)}, bf16[128,512]{1,0:T(8,128)(2,1)S(1)}, u32[]{:S(2)}, u32[]{:S(2)}) %collective-permute-start.6) | collective-permute-done | bytes 131104 | tf_op jit(solution)/shard_map/ppermute | solution.py:20
  30.2 2.8 %collective-permute-start.10 = (bf16[128,512]{1,0:T(8,128)(2,1)S(1)}, bf16[128,512]{1,0:T(8,128)(2,1)S(1)}, u32[]{:S(2)}, u32[]{:S(2)}) collective-permute-start(bf16[128,512]{1,0:T(8,128)(2,1)S(1)} %get-tuple-element.27), channel_id=1, source_target_pairs={{0,6},{1,7},{2,4},{3,5},{4,2},{5,3},{6,0},{7,1},{8,14},{9,15},{10,... | collective-permute-start | bytes 393224 | tf_op jit(solution)/shard_map/ppermute | solution.py:20
  33.0 0.6 collective-permute-start.11
  33.7 1.8 %multiply_reduce_fusion = (f32[2]{0:T(128)S(1)}, bf16[2,128,512]{2,1,0:T(8,128)(2,1)}) fusion(bf16[2,128,512]{2,1,0:T(8,128)(2,1)} %collective-permute-done.1, bf16[2,256,512]{2,1,0:T(8,128)(2,1)S(1)} %fusion, s32[]{:T(128)S(6)} %select_n.113), kind=kLoop, calls=%fused_computation.7 | loop fusion | flops 917502 | bytes 786444 | tf_op jit(solution)/shard_map/reduce_sum | solution.py:214
  35.4 0.1 broadcast_in_dim.12.half_sq
  35.5 1.7 %shard_map.57.refs_8_ = bf16[8,528,128]{2,1,0:T(8,128)(2,1)} custom-call(s32[10]{0:T(128)S(1)} %shard_map.55.plan, bf16[4,128,512]{2,1,0:T(8,128)(2,1)S(1)} %all-to-all-done.1.slots, f32[2,128]{1,0:T(2,128)S(1)} %broadcast_in_dim.12.half_sq), custom_call_target="tpu_custom_call" | custom-call | tf_op jit(solution)/shard_map/pallas_call | solution.py:217
  37.2 5.4 %all-to-all-start.2 = ((bf16[8,528,128]{2,1,0:T(8,128)(2,1)}), bf16[8,528,128]{2,1,0:T(8,128)(2,1)S(1)}, u32[]{:S(2)}, u32[]{:S(2)}) async-start(bf16[8,528,128]{2,1,0:T(8,128)(2,1)} %shard_map.57.refs_8_), calls=%async_computation.2 | async-start | bytes 2162688 | tf_op jit(solution)/shard_map/all_to_all | solution.py:224
  42.6 0.0 collective-permute-done.8.refs_4_
  42.6 0.0 collective-permute-done.9.refs_5_
  42.7 0.0 collective-permute-done.11.refs_7_
  42.7 0.0 copy-start.2
  42.7 0.6 shard_map.58
  43.3 1.8 %collective-permute-start.12 = (bf16[2,1,128,512]{3,2,0,1:T(8,128)(2,1)S(1)}, bf16[2,1,128,512]{3,2,0,1:T(8,128)(2,1)S(1)}, u32[]{:S(2)}, u32[]{:S(2)}) collective-permute-start(bf16[2,1,128,512]{3,2,0,1:T(8,128)(2,1)S(1)} %bitcast.26), channel_id=1, source_target_pairs={{0,16},{8,24},{16,0},{24,8},{1,17},{9,25},{17,1},{25,9},{2,18},{10... | collective-permute-start | bytes 786440 | tf_op jit(solution)/shard_map/ppermute | solution.py:20
  45.1 0.3 collective-permute-start.2
  45.4 7.2 %collective-permute-done.12 = bf16[2,1,128,512]{3,2,0,1:T(8,128)(2,1)S(1)} collective-permute-done((bf16[2,1,128,512]{3,2,0,1:T(8,128)(2,1)S(1)}, bf16[2,1,128,512]{3,2,0,1:T(8,128)(2,1)S(1)}, u32[]{:S(2)}, u32[]{:S(2)}) %collective-permute-start.12) | collective-permute-done | bytes 262176 | tf_op jit(solution)/shard_map/ppermute | solution.py:20
  52.7 0.1 maximum_bitcast_fusion
  52.7 0.1 collective-permute-start.13
  52.8 0.5 collective-permute-start.3
  53.3 3.0 %collective-permute-done.2 = bf16[2,128,512]{2,1,0:T(8,128)(2,1)S(1)} collective-permute-done((bf16[2,128,512]{2,1,0:T(8,128)(2,1)S(1)}, bf16[2,128,512]{2,1,0:T(8,128)(2,1)S(1)}, u32[]{:S(2)}, u32[]{:S(2)}) %collective-permute-start.2) | collective-permute-done | bytes 262176 | tf_op jit(solution)/shard_map/ppermute | solution.py:20
  56.3 0.1 broadcast_in_dim.11
  56.5 1.3 %collective-permute-done.4 = bf16[2,128,512]{2,1,0:T(8,128)(2,1)S(1)} collective-permute-done((bf16[2,128,512]{2,1,0:T(8,128)(2,1)S(1)}, bf16[2,128,512]{2,1,0:T(8,128)(2,1)S(1)}, u32[]{:S(2)}, u32[]{:S(2)}) %collective-permute-start.4) | collective-permute-done | bytes 262176 | tf_op jit(solution)/shard_map/ppermute | solution.py:20
  57.9 0.0 collective-permute-done.13
  57.9 0.1 select_bitcast_fusion.1
  57.9 0.1 pad_maximum_fusion
  58.1 0.1 copy.6
  58.1 0.7 convolution_convert_fusion.right_prod
  58.8 11.1 %all-to-all-done.2.arrived = bf16[8,528,128]{2,1,0:T(8,128)(2,1)S(1)} async-done(((bf16[8,528,128]{2,1,0:T(8,128)(2,1)}), bf16[8,528,128]{2,1,0:T(8,128)(2,1)S(1)}, u32[]{:S(2)}, u32[]{:S(2)}) %all-to-all-start.2) | async-done | bytes 1081376 | tf_op jit(solution)/shard_map/all_to_all | solution.py:224
  69.9 1.0 %shard_map.59 = (f32[2,128,512]{2,1,0:T(8,128)S(1)}, f32[8,128]{1,0:T(8,128)S(1)}) custom-call(s32[10]{0:T(128)S(1)} %shard_map.55.plan, bf16[2,512,512]{2,1,0:T(8,128)(2,1)S(1)} %convolution_convert_fusion.right_prod, f32[2,128]{1,0:T(2,128)S(1)} %broadcast_in_dim.12.half_sq, bf16[8,528,128]{2,1,0:T(8,128)(2,1)S(1)} %all-to-all-done.2.arrived), custom_call_target="tpu_custom_call" | custom-call | tf_op jit(solution)/shard_map/pallas_call | solution.py:238
  70.9 0.7 collective-permute-start.16
  71.6 1.2 %collective-permute-start.15 = (f32[8,128]{1,0:T(8,128)S(1)}, f32[8,128]{1,0:T(8,128)S(1)}, u32[]{:S(2)}, u32[]{:S(2)}) collective-permute-start(f32[8,128]{1,0:T(8,128)S(1)} %get-tuple-element.30.refs_0_), channel_id=1, source_target_pairs={{0,16},{8,24},{16,0},{24,8},{1,17},{9,25},{17,1},{25,9},{2,18},{10... | collective-permute-start | bytes 12296 | tf_op jit(solution)/shard_map/ppermute | solution.py:20
  72.7 0.1 collective-permute-start.14
  72.8 1.2 %collective-permute-done.16.refs_3_ = f32[8,128]{1,0:T(8,128)S(1)} collective-permute-done((f32[8,128]{1,0:T(8,128)S(1)}, f32[8,128]{1,0:T(8,128)S(1)}, u32[]{:S(2)}, u32[]{:S(2)}) %collective-permute-start.16) | collective-permute-done | bytes 4128 | tf_op jit(solution)/shard_map/ppermute | solution.py:20
  74.0 1.2 %collective-permute-done.15.refs_2_ = f32[8,128]{1,0:T(8,128)S(1)} collective-permute-done((f32[8,128]{1,0:T(8,128)S(1)}, f32[8,128]{1,0:T(8,128)S(1)}, u32[]{:S(2)}, u32[]{:S(2)}) %collective-permute-start.15) | collective-permute-done | bytes 4128 | tf_op jit(solution)/shard_map/ppermute | solution.py:20
  75.2 0.0 collective-permute-done.14.refs_1_
  75.2 0.8 %shard_map.60 = bf16[2,128,512]{2,1,0:T(8,128)(2,1)} custom-call(f32[2,128,512]{2,1,0:T(8,128)S(1)} %get-tuple-element.29.precond, f32[8,128]{1,0:T(8,128)S(1)} %get-tuple-element.30.refs_0_, f32[8,128]{1,0:T(8,128)S(1)} %collective-permute-done.14.refs_1_, f32[8,128]{1,0:T(8,128)S(1)} %collective-permute-done.15.refs_2_, ...), custom_call_target="tpu_custom_call" | custom-call | tf_op jit(solution)/shard_map/pallas_call | solution.py:250
  (21 shorter events, 0.2 us)
Async XLA Ops:
  0.0 6.1 %copy-start.3 = (bf16[1,2,512,512]{3,2,1,0:T(8,128)(2,1)S(1)}, bf16[1,2,512,512]{3,2,1,0:T(8,128)(2,1)}, u32[]{:S(2)}) copy-start(bf16[1,2,512,512]{3,2,1,0:T(8,128)(2,1)} %param.5) | copy-start | bytes 3145732
  0.0 4.5 %copy-start.1 = (s32[9]{0:T(128)S(1)}, s32[9]{0:T(128)}, u32[]{:S(2)}) copy-start(s32[9]{0:T(128)} %offsets.1) | copy-start | bytes 112
  0.0 4.5 %copy-start = (s32[16]{0:T(128)S(1)}, s32[16]{0:T(128)}, u32[]{:S(2)}) copy-start(s32[16]{0:T(128)} %lists.1) | copy-start | bytes 196
  0.0 6.1 %collective-permute-start = (bf16[2,512,512]{2,1,0:T(8,128)(2,1)}, bf16[2,512,512]{2,1,0:T(8,128)(2,1)S(1)}, u32[]{:S(2)}, u32[]{:S(2)}) collective-permute-start(bf16[2,512,512]{2,1,0:T(8,128)(2,1)} %bitcast.29), channel_id=1, source_target_pairs={{0,8},{8,0},{16,24},{24,16},{1,9},{9,1},{17,25},{25,17},{2,10},{10... | collective-permute-start | bytes 3145736 | tf_op jit(solution)/shard_map/ppermute | solution.py:20
  0.5 13.1 %all-to-all-start = ((bf16[4,128,512]{2,1,0:T(8,128)(2,1)}), bf16[4,128,512]{2,1,0:T(8,128)(2,1)S(1)}, u32[]{:S(2)}, u32[]{:S(2)}) async-start(bf16[4,128,512]{2,1,0:T(8,128)(2,1)} %bitcast.28), calls=%async_computation | async-start | bytes 1048576 | tf_op jit(solution)/shard_map/all_to_all | solution.py:186
  13.7 19.3 %collective-permute-start.1 = (bf16[2,128,512]{2,1,0:T(8,128)(2,1)S(1)}, bf16[2,128,512]{2,1,0:T(8,128)(2,1)}, u32[]{:S(2)}, u32[]{:S(2)}) collective-permute-start(bf16[2,128,512]{2,1,0:T(8,128)(2,1)S(1)} %constant_dynamic-slice_fusion), channel_id=1, source_target_pairs={{0,16},{8,24},{16,0},{24,8},{1,17},{9,25},{17,1},{25,9},{2,18},{10... | collective-permute-start | bytes 786440 | tf_op jit(solution)/shard_map/ppermute | solution.py:20
  13.8 21.7 %all-to-all-start.1 = ((bf16[4,128,512]{2,1,0:T(8,128)(2,1)}), bf16[4,128,512]{2,1,0:T(8,128)(2,1)S(1)}, u32[]{:S(2)}, u32[]{:S(2)}) async-start(bf16[4,128,512]{2,1,0:T(8,128)(2,1)} %bitcast.3), calls=%async_computation.1 | async-start | bytes 1048576 | tf_op jit(solution)/shard_map/all_to_all | solution.py:186
  17.9 6.8 %collective-permute-start.5 = (bf16[128,512]{1,0:T(8,128)(2,1)S(1)}, bf16[128,512]{1,0:T(8,128)(2,1)S(1)}, u32[]{:S(2)}, u32[]{:S(2)}) collective-permute-start(bf16[128,512]{1,0:T(8,128)(2,1)S(1)} %get-tuple-element.22), channel_id=1, source_target_pairs={{0,1},{1,0},{2,3},{3,2},{4,5},{5,4},{6,7},{7,6},{8,9},{9,8},{10,11... | collective-permute-start | bytes 393224 | tf_op jit(solution)/shard_map/ppermute | solution.py:20
  20.1 10.1 %collective-permute-start.6 = (bf16[128,512]{1,0:T(8,128)(2,1)S(1)}, bf16[128,512]{1,0:T(8,128)(2,1)S(1)}, u32[]{:S(2)}, u32[]{:S(2)}) collective-permute-start(bf16[128,512]{1,0:T(8,128)(2,1)S(1)} %get-tuple-element.23), channel_id=1, source_target_pairs={{0,4},{1,5},{2,6},{3,7},{4,0},{5,1},{6,2},{7,3},{8,12},{9,13},{10,... | collective-permute-start | bytes 393224 | tf_op jit(solution)/shard_map/ppermute | solution.py:20
  22.7 19.9 %collective-permute-start.7 = (bf16[128,512]{1,0:T(8,128)(2,1)S(1)}, bf16[128,512]{1,0:T(8,128)(2,1)S(1)}, u32[]{:S(2)}, u32[]{:S(2)}) collective-permute-start(bf16[128,512]{1,0:T(8,128)(2,1)S(1)} %get-tuple-element.24), channel_id=1, source_target_pairs={{0,2},{1,3},{2,0},{3,1},{4,6},{5,7},{6,4},{7,5},{8,10},{9,11},{10,... | collective-permute-start | bytes 393224 | tf_op jit(solution)/shard_map/ppermute | solution.py:20
  24.2 18.4 %collective-permute-start.8 = (bf16[128,512]{1,0:T(8,128)(2,1)S(1)}, bf16[128,512]{1,0:T(8,128)(2,1)S(1)}, u32[]{:S(2)}, u32[]{:S(2)}) collective-permute-start(bf16[128,512]{1,0:T(8,128)(2,1)S(1)} %get-tuple-element.25), channel_id=1, source_target_pairs={{0,3},{1,2},{2,1},{3,0},{4,7},{5,6},{6,5},{7,4},{8,11},{9,10},{10,... | collective-permute-start | bytes 393224 | tf_op jit(solution)/shard_map/ppermute | solution.py:20
  24.7 18.0 %collective-permute-start.9 = (bf16[128,512]{1,0:T(8,128)(2,1)S(1)}, bf16[128,512]{1,0:T(8,128)(2,1)S(1)}, u32[]{:S(2)}, u32[]{:S(2)}) collective-permute-start(bf16[128,512]{1,0:T(8,128)(2,1)S(1)} %get-tuple-element.26), channel_id=1, source_target_pairs={{0,5},{1,4},{2,7},{3,6},{4,1},{5,0},{6,3},{7,2},{8,13},{9,12},{10,... | collective-permute-start | bytes 393224 | tf_op jit(solution)/shard_map/ppermute | solution.py:20
  30.2 12.4 %collective-permute-start.10 = (bf16[128,512]{1,0:T(8,128)(2,1)S(1)}, bf16[128,512]{1,0:T(8,128)(2,1)S(1)}, u32[]{:S(2)}, u32[]{:S(2)}) collective-permute-start(bf16[128,512]{1,0:T(8,128)(2,1)S(1)} %get-tuple-element.27), channel_id=1, source_target_pairs={{0,6},{1,7},{2,4},{3,5},{4,2},{5,3},{6,0},{7,1},{8,14},{9,15},{10,... | collective-permute-start | bytes 393224 | tf_op jit(solution)/shard_map/ppermute | solution.py:20
  33.0 9.6 %collective-permute-start.11 = (bf16[128,512]{1,0:T(8,128)(2,1)S(1)}, bf16[128,512]{1,0:T(8,128)(2,1)S(1)}, u32[]{:S(2)}, u32[]{:S(2)}) collective-permute-start(bf16[128,512]{1,0:T(8,128)(2,1)S(1)} %get-tuple-element.28), channel_id=1, source_target_pairs={{0,7},{1,6},{2,5},{3,4},{4,3},{5,2},{6,1},{7,0},{8,15},{9,14},{10,... | collective-permute-start | bytes 393224 | tf_op jit(solution)/shard_map/ppermute | solution.py:20
  37.2 32.7 %all-to-all-start.2 = ((bf16[8,528,128]{2,1,0:T(8,128)(2,1)}), bf16[8,528,128]{2,1,0:T(8,128)(2,1)S(1)}, u32[]{:S(2)}, u32[]{:S(2)}) async-start(bf16[8,528,128]{2,1,0:T(8,128)(2,1)} %shard_map.57.refs_8_), calls=%async_computation.2 | async-start | bytes 2162688 | tf_op jit(solution)/shard_map/all_to_all | solution.py:224
  42.7 2.4 %copy-start.2 = (bf16[2,128,512]{2,1,0:T(8,128)(2,1)S(1)}, bf16[2,128,512]{2,1,0:T(8,128)(2,1)}, u32[]{:S(2)}) copy-start(bf16[2,128,512]{2,1,0:T(8,128)(2,1)} %get-tuple-element.32) | copy-start | bytes 786436
  43.3 9.3 %collective-permute-start.12 = (bf16[2,1,128,512]{3,2,0,1:T(8,128)(2,1)S(1)}, bf16[2,1,128,512]{3,2,0,1:T(8,128)(2,1)S(1)}, u32[]{:S(2)}, u32[]{:S(2)}) collective-permute-start(bf16[2,1,128,512]{3,2,0,1:T(8,128)(2,1)S(1)} %bitcast.26), channel_id=1, source_target_pairs={{0,16},{8,24},{16,0},{24,8},{1,17},{9,25},{17,1},{25,9},{2,18},{10... | collective-permute-start | bytes 786440 | tf_op jit(solution)/shard_map/ppermute | solution.py:20
  45.1 11.2 %collective-permute-start.2 = (bf16[2,128,512]{2,1,0:T(8,128)(2,1)S(1)}, bf16[2,128,512]{2,1,0:T(8,128)(2,1)S(1)}, u32[]{:S(2)}, u32[]{:S(2)}) collective-permute-start(bf16[2,128,512]{2,1,0:T(8,128)(2,1)S(1)} %copy-done.2), channel_id=1, source_target_pairs={{0,16},{8,24},{16,0},{24,8},{1,17},{9,25},{17,1},{25,9},{2,18},{10... | collective-permute-start | bytes 786440 | tf_op jit(solution)/shard_map/ppermute | solution.py:20
  52.7 5.1 %collective-permute-start.13 = (bf16[2,2,128,512]{3,2,0,1:T(8,128)(2,1)S(1)}, bf16[2,2,128,512]{3,2,0,1:T(8,128)(2,1)S(1)}, u32[]{:S(2)}, u32[]{:S(2)}) collective-permute-start(bf16[2,2,128,512]{3,2,0,1:T(8,128)(2,1)S(1)} %maximum_bitcast_fusion), channel_id=1, source_target_pairs={{0,8},{8,0},{16,24},{24,16},{1,9},{9,1},{17,25},{25,17},{2,10},{10... | collective-permute-start | bytes 1572872 | tf_op jit(solution)/shard_map/ppermute | solution.py:20
  52.8 3.6 %collective-permute-start.3 = (bf16[2,128,512]{2,1,0:T(8,128)(2,1)S(1)}, bf16[2,128,512]{2,1,0:T(8,128)(2,1)S(1)}, u32[]{:S(2)}, u32[]{:S(2)}) collective-permute-start(bf16[2,128,512]{2,1,0:T(8,128)(2,1)S(1)} %copy-done.2), channel_id=1, source_target_pairs={{0,8},{8,0},{16,24},{24,16},{1,9},{9,1},{17,25},{25,17},{2,10},{10... | collective-permute-start | bytes 786440 | tf_op jit(solution)/shard_map/ppermute | solution.py:20
  56.3 1.5 %collective-permute-start.4 = (bf16[2,128,512]{2,1,0:T(8,128)(2,1)S(1)}, bf16[2,128,512]{2,1,0:T(8,128)(2,1)S(1)}, u32[]{:S(2)}, u32[]{:S(2)}) collective-permute-start(bf16[2,128,512]{2,1,0:T(8,128)(2,1)S(1)} %collective-permute-done.2), channel_id=1, source_target_pairs={{0,8},{8,0},{16,24},{24,16},{1,9},{9,1},{17,25},{25,17},{2,10},{10... | collective-permute-start | bytes 786440 | tf_op jit(solution)/shard_map/ppermute | solution.py:20
  70.9 3.1 %collective-permute-start.16 = (f32[8,128]{1,0:T(8,128)S(1)}, f32[8,128]{1,0:T(8,128)S(1)}, u32[]{:S(2)}, u32[]{:S(2)}) collective-permute-start(f32[8,128]{1,0:T(8,128)S(1)} %get-tuple-element.30.refs_0_), channel_id=1, source_target_pairs={{0,24},{8,16},{16,8},{24,0},{1,25},{9,17},{17,9},{25,1},{2,26},{10... | collective-permute-start | bytes 12296 | tf_op jit(solution)/shard_map/ppermute | solution.py:20
  71.6 3.6 %collective-permute-start.15 = (f32[8,128]{1,0:T(8,128)S(1)}, f32[8,128]{1,0:T(8,128)S(1)}, u32[]{:S(2)}, u32[]{:S(2)}) collective-permute-start(f32[8,128]{1,0:T(8,128)S(1)} %get-tuple-element.30.refs_0_), channel_id=1, source_target_pairs={{0,16},{8,24},{16,0},{24,8},{1,17},{9,25},{17,1},{25,9},{2,18},{10... | collective-permute-start | bytes 12296 | tf_op jit(solution)/shard_map/ppermute | solution.py:20
  72.7 2.5 %collective-permute-start.14 = (f32[8,128]{1,0:T(8,128)S(1)}, f32[8,128]{1,0:T(8,128)S(1)}, u32[]{:S(2)}, u32[]{:S(2)}) collective-permute-start(f32[8,128]{1,0:T(8,128)S(1)} %get-tuple-element.30.refs_0_), channel_id=1, source_target_pairs={{0,8},{8,0},{16,24},{24,16},{1,9},{9,1},{17,25},{25,17},{2,10},{10... | collective-permute-start | bytes 12296 | tf_op jit(solution)/shard_map/ppermute | solution.py:20

commit v9 on v8

--- a/solution.py
+++ b/solution.py
@@ -206,7 +206,9 @@
     )(plan, right_slots)
     left_slots = over_dp(left_roots)
     far = mp_count // 2
-    order = [1, far, *range(2, far), *range(far + 1, mp_count)]
+    middle = far + far // 2
+    distant = [*range(middle, mp_count), *range(far, middle)]
+    order = [1, distant[0], *range(2, far), *distant[1:]]
     right_arrived = [outgoing[0]] + [swap(outgoing[d], "mp", d) for d in order]
     total = chip_sum(total, dp_count, dp_index)
     total_f = total.astype(jnp.float32)

time: 76.3 us -> 76 us (level)
    all_to_all x1, waiting for transfers between devices: 11.1 us -> 3.01 us  [shards(): lax.all_to_all(left_outgoing, 'mp', split_axis=0, concat_axis=0, tiled=True)]
    ppermute x17, waiting for transfers between devices: 16.2 us -> 23.8 us  [swap(): return lax.ppermute(value, axis, [(i, i ^ distance) for i in range(count)])]
  transfers between devices with their start and end apart: 20 -> 20, of which waited for: 8 -> 9; matrix products, arithmetic and copies ran while one was open for 4% -> 4% of each run, Pallas kernels for 6% -> 6%
where the time goes in v9:
time: 76 us; the launch traced here: 75.7 us
  waiting for transfers between devices  34.3 us (45%)
  starting transfers between devices  31.7 us (42%)
  Pallas kernels  6.34 us (8%)
  other arithmetic  2.19 us (3%)
    ppermute x17, waiting for transfers between devices, swap(): return lax.ppermute(value, axis, [(i, i ^ distance) for i in range(count)])  23.8 us
    ppermute x17, starting transfers between devices, swap(): return lax.ppermute(value, axis, [(i, i ^ distance) for i in range(count)])  19.2 us
    all_to_all x2, starting transfers between devices, over_dp(): lax.all_to_all(factor[0, 0].reshape(dp_count, rows, width), 'dp', split_a...  7.42 us
    all_to_all x2, waiting for transfers between devices, over_dp(): lax.all_to_all(factor[0, 0].reshape(dp_count, rows, width), 'dp', split_a...  7.4 us
    all_to_all x1, starting transfers between devices, shards(): lax.all_to_all(left_outgoing, 'mp', split_axis=0, concat_axis=0, tiled=True)  5.08 us
    all_to_all x1, waiting for transfers between devices, shards(): lax.all_to_all(left_outgoing, 'mp', split_axis=0, concat_axis=0, tiled=True)  3.01 us
    reduce_sum x1, other arithmetic, shards(): jnp.sum(total_f * total_f, axis=(1, 2)).reshape(per_shard, 1)  1.78 us
    pallas_call x1, Pallas kernels, shards(): pl.pallas_call(functools.partial(left_kernel, mp_count), out_shape=jax.Sh...  1.72 us
  transfers between devices with their start and end apart: 20, of which 9 were waited for; matrix products, arithmetic and copies ran while one was open for 4% of the time, Pallas kernels for 6%

profile of v9, /device:TPU:0, one launch (start us, length us, event | category | flops | bytes accessed | tf_op | source)
XLA Modules:
  0.0 75.7 jit_solution(3508898171935255077)
XLA Ops:
  0.0 0.5 collective-permute-start
  0.5 3.9 %all-to-all-start = ((bf16[4,128,512]{2,1,0:T(8,128)(2,1)}), bf16[4,128,512]{2,1,0:T(8,128)(2,1)S(1)}, u32[]{:S(2)}, u32[]{:S(2)}) async-start(bf16[4,128,512]{2,1,0:T(8,128)(2,1)} %bitcast.28), calls=%async_computation | async-start | bytes 1048576 | tf_op jit(solution)/shard_map/all_to_all | solution.py:186
  4.5 1.6 %shard_map.55.plan = s32[10]{0:T(128)S(1)} custom-call(s32[16]{0:T(128)S(1)} %copy-done, s32[9]{0:T(128)S(1)} %copy-done.1), custom_call_target="tpu_custom_call" | custom-call | tf_op jit(solution)/shard_map/pallas_call | solution.py:190
  6.1 0.0 collective-permute-done
  6.1 0.1 fusion
  6.3 7.4 %all-to-all-done.slots = bf16[4,128,512]{2,1,0:T(8,128)(2,1)S(1)} async-done(((bf16[4,128,512]{2,1,0:T(8,128)(2,1)}), bf16[4,128,512]{2,1,0:T(8,128)(2,1)S(1)}, u32[]{:S(2)}, u32[]{:S(2)}) %all-to-all-start) | async-done | bytes 524320 | tf_op jit(solution)/shard_map/all_to_all | solution.py:186
  13.7 0.1 collective-permute-start.1
  13.8 3.5 %all-to-all-start.1 = ((bf16[4,128,512]{2,1,0:T(8,128)(2,1)}), bf16[4,128,512]{2,1,0:T(8,128)(2,1)S(1)}, u32[]{:S(2)}, u32[]{:S(2)}) async-start(bf16[4,128,512]{2,1,0:T(8,128)(2,1)} %bitcast.3), calls=%async_computation.1 | async-start | bytes 1048576 | tf_op jit(solution)/shard_map/all_to_all | solution.py:186
  17.3 0.6 shard_map.56
  17.9 2.2 %collective-permute-start.5 = (bf16[128,512]{1,0:T(8,128)(2,1)S(1)}, bf16[128,512]{1,0:T(8,128)(2,1)S(1)}, u32[]{:S(2)}, u32[]{:S(2)}) collective-permute-start(bf16[128,512]{1,0:T(8,128)(2,1)S(1)} %get-tuple-element.22), channel_id=1, source_target_pairs={{0,1},{1,0},{2,3},{3,2},{4,5},{5,4},{6,7},{7,6},{8,9},{9,8},{10,11... | collective-permute-start | bytes 393224 | tf_op jit(solution)/shard_map/ppermute | solution.py:20
  20.1 3.6 %collective-permute-start.6 = (bf16[128,512]{1,0:T(8,128)(2,1)S(1)}, bf16[128,512]{1,0:T(8,128)(2,1)S(1)}, u32[]{:S(2)}, u32[]{:S(2)}) collective-permute-start(bf16[128,512]{1,0:T(8,128)(2,1)S(1)} %get-tuple-element.23), channel_id=1, source_target_pairs={{0,6},{1,7},{2,4},{3,5},{4,2},{5,3},{6,0},{7,1},{8,14},{9,15},{10,... | collective-permute-start | bytes 393224 | tf_op jit(solution)/shard_map/ppermute | solution.py:20
  23.7 2.0 %collective-permute-start.8 = (bf16[128,512]{1,0:T(8,128)(2,1)S(1)}, bf16[128,512]{1,0:T(8,128)(2,1)S(1)}, u32[]{:S(2)}, u32[]{:S(2)}) collective-permute-start(bf16[128,512]{1,0:T(8,128)(2,1)S(1)} %get-tuple-element.25), channel_id=1, source_target_pairs={{0,3},{1,2},{2,1},{3,0},{4,7},{5,6},{6,5},{7,4},{8,11},{9,10},{10,... | collective-permute-start | bytes 393224 | tf_op jit(solution)/shard_map/ppermute | solution.py:20
  25.7 3.3 %collective-permute-start.9 = (bf16[128,512]{1,0:T(8,128)(2,1)S(1)}, bf16[128,512]{1,0:T(8,128)(2,1)S(1)}, u32[]{:S(2)}, u32[]{:S(2)}) collective-permute-start(bf16[128,512]{1,0:T(8,128)(2,1)S(1)} %get-tuple-element.26), channel_id=1, source_target_pairs={{0,7},{1,6},{2,5},{3,4},{4,3},{5,2},{6,1},{7,0},{8,15},{9,14},{10,... | collective-permute-start | bytes 393224 | tf_op jit(solution)/shard_map/ppermute | solution.py:20
  29.0 0.0 collective-permute-done.6.refs_2_
  29.0 2.5 %collective-permute-start.10 = (bf16[128,512]{1,0:T(8,128)(2,1)S(1)}, bf16[128,512]{1,0:T(8,128)(2,1)S(1)}, u32[]{:S(2)}, u32[]{:S(2)}) collective-permute-start(bf16[128,512]{1,0:T(8,128)(2,1)S(1)} %get-tuple-element.27), channel_id=1, source_target_pairs={{0,4},{1,5},{2,6},{3,7},{4,0},{5,1},{6,2},{7,3},{8,12},{9,13},{10,... | collective-permute-start | bytes 393224 | tf_op jit(solution)/shard_map/ppermute | solution.py:20
  31.5 0.0 collective-permute-done.1
  31.5 0.4 collective-permute-start.11
  31.9 1.8 %multiply_reduce_fusion = (f32[2]{0:T(128)S(1)}, bf16[2,128,512]{2,1,0:T(8,128)(2,1)}) fusion(bf16[2,128,512]{2,1,0:T(8,128)(2,1)} %collective-permute-done.1, bf16[2,256,512]{2,1,0:T(8,128)(2,1)S(1)} %fusion, s32[]{:T(128)S(6)} %select_n.113), kind=kLoop, calls=%fused_computation.7 | loop fusion | flops 917502 | bytes 786444 | tf_op jit(solution)/shard_map/reduce_sum | solution.py:216
  33.7 0.0 all-to-all-done.1.slots
  33.7 0.1 broadcast_in_dim.12.half_sq
  33.7 1.7 %shard_map.57.refs_8_ = bf16[8,528,128]{2,1,0:T(8,128)(2,1)} custom-call(s32[10]{0:T(128)S(1)} %shard_map.55.plan, bf16[4,128,512]{2,1,0:T(8,128)(2,1)S(1)} %all-to-all-done.1.slots, f32[2,128]{1,0:T(2,128)S(1)} %broadcast_in_dim.12.half_sq), custom_call_target="tpu_custom_call" | custom-call | tf_op jit(solution)/shard_map/pallas_call | solution.py:219
  35.5 5.1 %all-to-all-start.2 = ((bf16[8,528,128]{2,1,0:T(8,128)(2,1)}), bf16[8,528,128]{2,1,0:T(8,128)(2,1)S(1)}, u32[]{:S(2)}, u32[]{:S(2)}) async-start(bf16[8,528,128]{2,1,0:T(8,128)(2,1)} %shard_map.57.refs_8_), calls=%async_computation.2 | async-start | bytes 2162688 | tf_op jit(solution)/shard_map/all_to_all | solution.py:226
  40.5 0.0 collective-permute-done.7.refs_3_
  40.6 4.1 %collective-permute-done.10.refs_6_ = bf16[128,512]{1,0:T(8,128)(2,1)S(1)} collective-permute-done((bf16[128,512]{1,0:T(8,128)(2,1)S(1)}, bf16[128,512]{1,0:T(8,128)(2,1)S(1)}, u32[]{:S(2)}, u32[]{:S(2)}) %collective-permute-start.10) | collective-permute-done | bytes 131104 | tf_op jit(solution)/shard_map/ppermute | solution.py:20
  44.7 7.3 %collective-permute-done.11.refs_7_ = bf16[128,512]{1,0:T(8,128)(2,1)S(1)} collective-permute-done((bf16[128,512]{1,0:T(8,128)(2,1)S(1)}, bf16[128,512]{1,0:T(8,128)(2,1)S(1)}, u32[]{:S(2)}, u32[]{:S(2)}) %collective-permute-start.11) | collective-permute-done | bytes 131104 | tf_op jit(solution)/shard_map/ppermute | solution.py:20
  52.0 0.6 shard_map.58
  52.7 1.6 %collective-permute-start.12 = (bf16[2,1,128,512]{3,2,0,1:T(8,128)(2,1)S(1)}, bf16[2,1,128,512]{3,2,0,1:T(8,128)(2,1)S(1)}, u32[]{:S(2)}, u32[]{:S(2)}) collective-permute-start(bf16[2,1,128,512]{3,2,0,1:T(8,128)(2,1)S(1)} %bitcast.26), channel_id=1, source_target_pairs={{0,16},{8,24},{16,0},{24,8},{1,17},{9,25},{17,1},{25,9},{2,18},{10... | collective-permute-start | bytes 786440 | tf_op jit(solution)/shard_map/ppermute | solution.py:20
  54.3 0.5 collective-permute-start.2
  54.8 6.5 %collective-permute-done.12 = bf16[2,1,128,512]{3,2,0,1:T(8,128)(2,1)S(1)} collective-permute-done((bf16[2,1,128,512]{3,2,0,1:T(8,128)(2,1)S(1)}, bf16[2,1,128,512]{3,2,0,1:T(8,128)(2,1)S(1)}, u32[]{:S(2)}, u32[]{:S(2)}) %collective-permute-start.12) | collective-permute-done | bytes 262176 | tf_op jit(solution)/shard_map/ppermute | solution.py:20
  61.3 0.1 maximum_bitcast_fusion
  61.4 0.1 collective-permute-start.13
  61.4 0.5 collective-permute-start.3
  61.9 2.1 %collective-permute-done.2 = bf16[2,128,512]{2,1,0:T(8,128)(2,1)S(1)} collective-permute-done((bf16[2,128,512]{2,1,0:T(8,128)(2,1)S(1)}, bf16[2,128,512]{2,1,0:T(8,128)(2,1)S(1)}, u32[]{:S(2)}, u32[]{:S(2)}) %collective-permute-start.2) | collective-permute-done | bytes 262176 | tf_op jit(solution)/shard_map/ppermute | solution.py:20
  64.1 0.1 broadcast_in_dim.11
  64.3 1.3 %collective-permute-done.4 = bf16[2,128,512]{2,1,0:T(8,128)(2,1)S(1)} collective-permute-done((bf16[2,128,512]{2,1,0:T(8,128)(2,1)S(1)}, bf16[2,128,512]{2,1,0:T(8,128)(2,1)S(1)}, u32[]{:S(2)}, u32[]{:S(2)}) %collective-permute-start.4) | collective-permute-done | bytes 262176 | tf_op jit(solution)/shard_map/ppermute | solution.py:20
  65.6 0.0 collective-permute-done.13
  65.7 0.1 select_bitcast_fusion.1
  65.7 0.1 pad_maximum_fusion
  65.8 0.1 copy.6
  65.9 0.7 convolution_convert_fusion.right_prod
  66.6 3.0 %all-to-all-done.2.arrived = bf16[8,528,128]{2,1,0:T(8,128)(2,1)S(1)} async-done(((bf16[8,528,128]{2,1,0:T(8,128)(2,1)}), bf16[8,528,128]{2,1,0:T(8,128)(2,1)S(1)}, u32[]{:S(2)}, u32[]{:S(2)}) %all-to-all-start.2) | async-done | bytes 1081376 | tf_op jit(solution)/shard_map/all_to_all | solution.py:226
  69.6 0.9 %shard_map.59 = (f32[2,128,512]{2,1,0:T(8,128)S(1)}, f32[8,128]{1,0:T(8,128)S(1)}) custom-call(s32[10]{0:T(128)S(1)} %shard_map.55.plan, bf16[2,512,512]{2,1,0:T(8,128)(2,1)S(1)} %convolution_convert_fusion.right_prod, f32[2,128]{1,0:T(2,128)S(1)} %broadcast_in_dim.12.half_sq, bf16[8,528,128]{2,1,0:T(8,128)(2,1)S(1)} %all-to-all-done.2.arrived), custom_call_target="tpu_custom_call" | custom-call | tf_op jit(solution)/shard_map/pallas_call | solution.py:240
  70.6 0.7 collective-permute-start.16
  71.3 1.1 %collective-permute-start.15 = (f32[8,128]{1,0:T(8,128)S(1)}, f32[8,128]{1,0:T(8,128)S(1)}, u32[]{:S(2)}, u32[]{:S(2)}) collective-permute-start(f32[8,128]{1,0:T(8,128)S(1)} %get-tuple-element.30.refs_0_), channel_id=1, source_target_pairs={{0,16},{8,24},{16,0},{24,8},{1,17},{9,25},{17,1},{25,9},{2,18},{10... | collective-permute-start | bytes 12296 | tf_op jit(solution)/shard_map/ppermute | solution.py:20
  72.4 0.2 collective-permute-start.14
  72.5 1.2 %collective-permute-done.16.refs_3_ = f32[8,128]{1,0:T(8,128)S(1)} collective-permute-done((f32[8,128]{1,0:T(8,128)S(1)}, f32[8,128]{1,0:T(8,128)S(1)}, u32[]{:S(2)}, u32[]{:S(2)}) %collective-permute-start.16) | collective-permute-done | bytes 4128 | tf_op jit(solution)/shard_map/ppermute | solution.py:20
  73.7 1.2 %collective-permute-done.15.refs_2_ = f32[8,128]{1,0:T(8,128)S(1)} collective-permute-done((f32[8,128]{1,0:T(8,128)S(1)}, f32[8,128]{1,0:T(8,128)S(1)}, u32[]{:S(2)}, u32[]{:S(2)}) %collective-permute-start.15) | collective-permute-done | bytes 4128 | tf_op jit(solution)/shard_map/ppermute | solution.py:20
  74.9 0.8 %shard_map.60 = bf16[2,128,512]{2,1,0:T(8,128)(2,1)} custom-call(f32[2,128,512]{2,1,0:T(8,128)S(1)} %get-tuple-element.29.precond, f32[8,128]{1,0:T(8,128)S(1)} %get-tuple-element.30.refs_0_, f32[8,128]{1,0:T(8,128)S(1)} %collective-permute-done.14.refs_1_, f32[8,128]{1,0:T(8,128)S(1)} %collective-permute-done.15.refs_2_, ...), custom_call_target="tpu_custom_call" | custom-call | tf_op jit(solution)/shard_map/pallas_call | solution.py:252
  (21 shorter events, 0.2 us)
Async XLA Ops:
  0.0 6.1 %copy-start.3 = (bf16[1,2,512,512]{3,2,1,0:T(8,128)(2,1)S(1)}, bf16[1,2,512,512]{3,2,1,0:T(8,128)(2,1)}, u32[]{:S(2)}) copy-start(bf16[1,2,512,512]{3,2,1,0:T(8,128)(2,1)} %param.5) | copy-start | bytes 3145732
  0.0 4.5 %copy-start.1 = (s32[9]{0:T(128)S(1)}, s32[9]{0:T(128)}, u32[]{:S(2)}) copy-start(s32[9]{0:T(128)} %offsets.1) | copy-start | bytes 112
  0.0 4.5 %copy-start = (s32[16]{0:T(128)S(1)}, s32[16]{0:T(128)}, u32[]{:S(2)}) copy-start(s32[16]{0:T(128)} %lists.1) | copy-start | bytes 196
  0.0 6.1 %collective-permute-start = (bf16[2,512,512]{2,1,0:T(8,128)(2,1)}, bf16[2,512,512]{2,1,0:T(8,128)(2,1)S(1)}, u32[]{:S(2)}, u32[]{:S(2)}) collective-permute-start(bf16[2,512,512]{2,1,0:T(8,128)(2,1)} %bitcast.29), channel_id=1, source_target_pairs={{0,8},{8,0},{16,24},{24,16},{1,9},{9,1},{17,25},{25,17},{2,10},{10... | collective-permute-start | bytes 3145736 | tf_op jit(solution)/shard_map/ppermute | solution.py:20
  0.5 13.1 %all-to-all-start = ((bf16[4,128,512]{2,1,0:T(8,128)(2,1)}), bf16[4,128,512]{2,1,0:T(8,128)(2,1)S(1)}, u32[]{:S(2)}, u32[]{:S(2)}) async-start(bf16[4,128,512]{2,1,0:T(8,128)(2,1)} %bitcast.28), calls=%async_computation | async-start | bytes 1048576 | tf_op jit(solution)/shard_map/all_to_all | solution.py:186
  13.7 17.8 %collective-permute-start.1 = (bf16[2,128,512]{2,1,0:T(8,128)(2,1)S(1)}, bf16[2,128,512]{2,1,0:T(8,128)(2,1)}, u32[]{:S(2)}, u32[]{:S(2)}) collective-permute-start(bf16[2,128,512]{2,1,0:T(8,128)(2,1)S(1)} %constant_dynamic-slice_fusion), channel_id=1, source_target_pairs={{0,16},{8,24},{16,0},{24,8},{1,17},{9,25},{17,1},{25,9},{2,18},{10... | collective-permute-start | bytes 786440 | tf_op jit(solution)/shard_map/ppermute | solution.py:20
  13.8 19.9 %all-to-all-start.1 = ((bf16[4,128,512]{2,1,0:T(8,128)(2,1)}), bf16[4,128,512]{2,1,0:T(8,128)(2,1)S(1)}, u32[]{:S(2)}, u32[]{:S(2)}) async-start(bf16[4,128,512]{2,1,0:T(8,128)(2,1)} %bitcast.3), calls=%async_computation.1 | async-start | bytes 1048576 | tf_op jit(solution)/shard_map/all_to_all | solution.py:186
  17.9 7.8 %collective-permute-start.5 = (bf16[128,512]{1,0:T(8,128)(2,1)S(1)}, bf16[128,512]{1,0:T(8,128)(2,1)S(1)}, u32[]{:S(2)}, u32[]{:S(2)}) collective-permute-start(bf16[128,512]{1,0:T(8,128)(2,1)S(1)} %get-tuple-element.22), channel_id=1, source_target_pairs={{0,1},{1,0},{2,3},{3,2},{4,5},{5,4},{6,7},{7,6},{8,9},{9,8},{10,11... | collective-permute-start | bytes 393224 | tf_op jit(solution)/shard_map/ppermute | solution.py:20
  20.1 8.9 %collective-permute-start.6 = (bf16[128,512]{1,0:T(8,128)(2,1)S(1)}, bf16[128,512]{1,0:T(8,128)(2,1)S(1)}, u32[]{:S(2)}, u32[]{:S(2)}) collective-permute-start(bf16[128,512]{1,0:T(8,128)(2,1)S(1)} %get-tuple-element.23), channel_id=1, source_target_pairs={{0,6},{1,7},{2,4},{3,5},{4,2},{5,3},{6,0},{7,1},{8,14},{9,15},{10,... | collective-permute-start | bytes 393224 | tf_op jit(solution)/shard_map/ppermute | solution.py:20
  23.7 16.9 %collective-permute-start.7 = (bf16[128,512]{1,0:T(8,128)(2,1)S(1)}, bf16[128,512]{1,0:T(8,128)(2,1)S(1)}, u32[]{:S(2)}, u32[]{:S(2)}) collective-permute-start(bf16[128,512]{1,0:T(8,128)(2,1)S(1)} %get-tuple-element.24), channel_id=1, source_target_pairs={{0,2},{1,3},{2,0},{3,1},{4,6},{5,7},{6,4},{7,5},{8,10},{9,11},{10,... | collective-permute-start | bytes 393224 | tf_op jit(solution)/shard_map/ppermute | solution.py:20
  23.7 16.9 %collective-permute-start.8 = (bf16[128,512]{1,0:T(8,128)(2,1)S(1)}, bf16[128,512]{1,0:T(8,128)(2,1)S(1)}, u32[]{:S(2)}, u32[]{:S(2)}) collective-permute-start(bf16[128,512]{1,0:T(8,128)(2,1)S(1)} %get-tuple-element.25), channel_id=1, source_target_pairs={{0,3},{1,2},{2,1},{3,0},{4,7},{5,6},{6,5},{7,4},{8,11},{9,10},{10,... | collective-permute-start | bytes 393224 | tf_op jit(solution)/shard_map/ppermute | solution.py:20
  25.7 14.9 %collective-permute-start.9 = (bf16[128,512]{1,0:T(8,128)(2,1)S(1)}, bf16[128,512]{1,0:T(8,128)(2,1)S(1)}, u32[]{:S(2)}, u32[]{:S(2)}) collective-permute-start(bf16[128,512]{1,0:T(8,128)(2,1)S(1)} %get-tuple-element.26), channel_id=1, source_target_pairs={{0,7},{1,6},{2,5},{3,4},{4,3},{5,2},{6,1},{7,0},{8,15},{9,14},{10,... | collective-permute-start | bytes 393224 | tf_op jit(solution)/shard_map/ppermute | solution.py:20
  29.0 15.7 %collective-permute-start.10 = (bf16[128,512]{1,0:T(8,128)(2,1)S(1)}, bf16[128,512]{1,0:T(8,128)(2,1)S(1)}, u32[]{:S(2)}, u32[]{:S(2)}) collective-permute-start(bf16[128,512]{1,0:T(8,128)(2,1)S(1)} %get-tuple-element.27), channel_id=1, source_target_pairs={{0,4},{1,5},{2,6},{3,7},{4,0},{5,1},{6,2},{7,3},{8,12},{9,13},{10,... | collective-permute-start | bytes 393224 | tf_op jit(solution)/shard_map/ppermute | solution.py:20
  31.5 20.6 %collective-permute-start.11 = (bf16[128,512]{1,0:T(8,128)(2,1)S(1)}, bf16[128,512]{1,0:T(8,128)(2,1)S(1)}, u32[]{:S(2)}, u32[]{:S(2)}) collective-permute-start(bf16[128,512]{1,0:T(8,128)(2,1)S(1)} %get-tuple-element.28), channel_id=1, source_target_pairs={{0,5},{1,4},{2,7},{3,6},{4,1},{5,0},{6,3},{7,2},{8,13},{9,12},{10,... | collective-permute-start | bytes 393224 | tf_op jit(solution)/shard_map/ppermute | solution.py:20
  35.5 34.2 %all-to-all-start.2 = ((bf16[8,528,128]{2,1,0:T(8,128)(2,1)}), bf16[8,528,128]{2,1,0:T(8,128)(2,1)S(1)}, u32[]{:S(2)}, u32[]{:S(2)}) async-start(bf16[8,528,128]{2,1,0:T(8,128)(2,1)} %shard_map.57.refs_8_), calls=%async_computation.2 | async-start | bytes 2162688 | tf_op jit(solution)/shard_map/all_to_all | solution.py:226
  52.0 2.3 %copy-start.2 = (bf16[2,128,512]{2,1,0:T(8,128)(2,1)S(1)}, bf16[2,128,512]{2,1,0:T(8,128)(2,1)}, u32[]{:S(2)}) copy-start(bf16[2,128,512]{2,1,0:T(8,128)(2,1)} %get-tuple-element.32) | copy-start | bytes 786436
  52.7 8.6 %collective-permute-start.12 = (bf16[2,1,128,512]{3,2,0,1:T(8,128)(2,1)S(1)}, bf16[2,1,128,512]{3,2,0,1:T(8,128)(2,1)S(1)}, u32[]{:S(2)}, u32[]{:S(2)}) collective-permute-start(bf16[2,1,128,512]{3,2,0,1:T(8,128)(2,1)S(1)} %bitcast.26), channel_id=1, source_target_pairs={{0,16},{8,24},{16,0},{24,8},{1,17},{9,25},{17,1},{25,9},{2,18},{10... | collective-permute-start | bytes 786440 | tf_op jit(solution)/shard_map/ppermute | solution.py:20
  54.3 9.8 %collective-permute-start.2 = (bf16[2,128,512]{2,1,0:T(8,128)(2,1)S(1)}, bf16[2,128,512]{2,1,0:T(8,128)(2,1)S(1)}, u32[]{:S(2)}, u32[]{:S(2)}) collective-permute-start(bf16[2,128,512]{2,1,0:T(8,128)(2,1)S(1)} %copy-done.2), channel_id=1, source_target_pairs={{0,16},{8,24},{16,0},{24,8},{1,17},{9,25},{17,1},{25,9},{2,18},{10... | collective-permute-start | bytes 786440 | tf_op jit(solution)/shard_map/ppermute | solution.py:20
  61.4 4.3 %collective-permute-start.13 = (bf16[2,2,128,512]{3,2,0,1:T(8,128)(2,1)S(1)}, bf16[2,2,128,512]{3,2,0,1:T(8,128)(2,1)S(1)}, u32[]{:S(2)}, u32[]{:S(2)}) collective-permute-start(bf16[2,2,128,512]{3,2,0,1:T(8,128)(2,1)S(1)} %maximum_bitcast_fusion), channel_id=1, source_target_pairs={{0,8},{8,0},{16,24},{24,16},{1,9},{9,1},{17,25},{25,17},{2,10},{10... | collective-permute-start | bytes 1572872 | tf_op jit(solution)/shard_map/ppermute | solution.py:20
  61.4 2.8 %collective-permute-start.3 = (bf16[2,128,512]{2,1,0:T(8,128)(2,1)S(1)}, bf16[2,128,512]{2,1,0:T(8,128)(2,1)S(1)}, u32[]{:S(2)}, u32[]{:S(2)}) collective-permute-start(bf16[2,128,512]{2,1,0:T(8,128)(2,1)S(1)} %copy-done.2), channel_id=1, source_target_pairs={{0,8},{8,0},{16,24},{24,16},{1,9},{9,1},{17,25},{25,17},{2,10},{10... | collective-permute-start | bytes 786440 | tf_op jit(solution)/shard_map/ppermute | solution.py:20
  64.1 1.5 %collective-permute-start.4 = (bf16[2,128,512]{2,1,0:T(8,128)(2,1)S(1)}, bf16[2,128,512]{2,1,0:T(8,128)(2,1)S(1)}, u32[]{:S(2)}, u32[]{:S(2)}) collective-permute-start(bf16[2,128,512]{2,1,0:T(8,128)(2,1)S(1)} %collective-permute-done.2), channel_id=1, source_target_pairs={{0,8},{8,0},{16,24},{24,16},{1,9},{9,1},{17,25},{25,17},{2,10},{10... | collective-permute-start | bytes 786440 | tf_op jit(solution)/shard_map/ppermute | solution.py:20
  70.6 3.1 %collective-permute-start.16 = (f32[8,128]{1,0:T(8,128)S(1)}, f32[8,128]{1,0:T(8,128)S(1)}, u32[]{:S(2)}, u32[]{:S(2)}) collective-permute-start(f32[8,128]{1,0:T(8,128)S(1)} %get-tuple-element.30.refs_0_), channel_id=1, source_target_pairs={{0,24},{8,16},{16,8},{24,0},{1,25},{9,17},{17,9},{25,1},{2,26},{10... | collective-permute-start | bytes 12296 | tf_op jit(solution)/shard_map/ppermute | solution.py:20
  71.3 3.6 %collective-permute-start.15 = (f32[8,128]{1,0:T(8,128)S(1)}, f32[8,128]{1,0:T(8,128)S(1)}, u32[]{:S(2)}, u32[]{:S(2)}) collective-permute-start(f32[8,128]{1,0:T(8,128)S(1)} %get-tuple-element.30.refs_0_), channel_id=1, source_target_pairs={{0,16},{8,24},{16,0},{24,8},{1,17},{9,25},{17,1},{25,9},{2,18},{10... | collective-permute-start | bytes 12296 | tf_op jit(solution)/shard_map/ppermute | solution.py:20
  72.4 2.5 %collective-permute-start.14 = (f32[8,128]{1,0:T(8,128)S(1)}, f32[8,128]{1,0:T(8,128)S(1)}, u32[]{:S(2)}, u32[]{:S(2)}) collective-permute-start(f32[8,128]{1,0:T(8,128)S(1)} %get-tuple-element.30.refs_0_), channel_id=1, source_target_pairs={{0,8},{8,0},{16,24},{24,16},{1,9},{9,1},{17,25},{25,17},{2,10},{10... | collective-permute-start | bytes 12296 | tf_op jit(solution)/shard_map/ppermute | solution.py:20

commit v10 on v9

--- a/solution.py
+++ b/solution.py
@@ -207,7 +207,7 @@
     left_slots = over_dp(left_roots)
     far = mp_count // 2
     middle = far + far // 2
-    distant = [*range(middle, mp_count), *range(far, middle)]
+    distant = [d for pair in zip(range(middle, mp_count), range(far, middle)) for d in pair]
     order = [1, distant[0], *range(2, far), *distant[1:]]
     right_arrived = [outgoing[0]] + [swap(outgoing[d], "mp", d) for d in order]
     total = chip_sum(total, dp_count, dp_index)

time: 76 us -> 75.6 us (level)
    all_to_all x1, starting transfers between devices: 5.08 us -> 3.8 us  [shards(): lax.all_to_all(left_outgoing, 'mp', split_axis=0, concat_axis=0, tiled=True)]
    ppermute x17, waiting for transfers between devices: 23.8 us -> 25 us  [swap(): return lax.ppermute(value, axis, [(i, i ^ distance) for i in range(count)])]
    all_to_all x1, waiting for transfers between devices: 3.01 us -> 1.97 us  [shards(): lax.all_to_all(left_outgoing, 'mp', split_axis=0, concat_axis=0, tiled=True)]
where the time goes in v10:
time: 75.6 us; the launch traced here: 75.3 us
  waiting for transfers between devices  34.4 us (46%)
  starting transfers between devices  31.1 us (41%)
  Pallas kernels  6.33 us (8%)
  other arithmetic  2.19 us (3%)
    ppermute x17, waiting for transfers between devices, swap(): return lax.ppermute(value, axis, [(i, i ^ distance) for i in range(count)])  25 us
    ppermute x17, starting transfers between devices, swap(): return lax.ppermute(value, axis, [(i, i ^ distance) for i in range(count)])  19.9 us
    all_to_all x2, waiting for transfers between devices, over_dp(): lax.all_to_all(factor[0, 0].reshape(dp_count, rows, width), 'dp', split_a...  7.43 us
    all_to_all x2, starting transfers between devices, over_dp(): lax.all_to_all(factor[0, 0].reshape(dp_count, rows, width), 'dp', split_a...  7.42 us
    all_to_all x1, starting transfers between devices, shards(): lax.all_to_all(left_outgoing, 'mp', split_axis=0, concat_axis=0, tiled=True)  3.8 us
    all_to_all x1, waiting for transfers between devices, shards(): lax.all_to_all(left_outgoing, 'mp', split_axis=0, concat_axis=0, tiled=True)  1.97 us
    reduce_sum x1, other arithmetic, shards(): jnp.sum(total_f * total_f, axis=(1, 2)).reshape(per_shard, 1)  1.78 us
    pallas_call x1, Pallas kernels, shards(): pl.pallas_call(functools.partial(left_kernel, mp_count), out_shape=jax.Sh...  1.72 us
  transfers between devices with their start and end apart: 20, of which 9 were waited for; matrix products, arithmetic and copies ran while one was open for 4% of the time, Pallas kernels for 6%

profile of v10, /device:TPU:0, one launch (start us, length us, event | category | flops | bytes accessed | tf_op | source)
XLA Modules:
  0.0 75.3 jit_solution(13575663279179200127)
XLA Ops:
  0.0 0.5 collective-permute-start
  0.5 3.9 %all-to-all-start = ((bf16[4,128,512]{2,1,0:T(8,128)(2,1)}), bf16[4,128,512]{2,1,0:T(8,128)(2,1)S(1)}, u32[]{:S(2)}, u32[]{:S(2)}) async-start(bf16[4,128,512]{2,1,0:T(8,128)(2,1)} %bitcast.28), calls=%async_computation | async-start | bytes 1048576 | tf_op jit(solution)/shard_map/all_to_all | solution.py:186
  4.5 1.6 %shard_map.55.plan = s32[10]{0:T(128)S(1)} custom-call(s32[16]{0:T(128)S(1)} %copy-done, s32[9]{0:T(128)S(1)} %copy-done.1), custom_call_target="tpu_custom_call" | custom-call | tf_op jit(solution)/shard_map/pallas_call | solution.py:190
  6.1 0.0 collective-permute-done
  6.1 0.1 fusion
  6.2 7.4 %all-to-all-done.slots = bf16[4,128,512]{2,1,0:T(8,128)(2,1)S(1)} async-done(((bf16[4,128,512]{2,1,0:T(8,128)(2,1)}), bf16[4,128,512]{2,1,0:T(8,128)(2,1)S(1)}, u32[]{:S(2)}, u32[]{:S(2)}) %all-to-all-start) | async-done | bytes 524320 | tf_op jit(solution)/shard_map/all_to_all | solution.py:186
  13.7 0.1 collective-permute-start.1
  13.8 3.5 %all-to-all-start.1 = ((bf16[4,128,512]{2,1,0:T(8,128)(2,1)}), bf16[4,128,512]{2,1,0:T(8,128)(2,1)S(1)}, u32[]{:S(2)}, u32[]{:S(2)}) async-start(bf16[4,128,512]{2,1,0:T(8,128)(2,1)} %bitcast.3), calls=%async_computation.1 | async-start | bytes 1048576 | tf_op jit(solution)/shard_map/all_to_all | solution.py:186
  17.3 0.6 shard_map.56
  17.9 2.2 %collective-permute-start.5 = (bf16[128,512]{1,0:T(8,128)(2,1)S(1)}, bf16[128,512]{1,0:T(8,128)(2,1)S(1)}, u32[]{:S(2)}, u32[]{:S(2)}) collective-permute-start(bf16[128,512]{1,0:T(8,128)(2,1)S(1)} %get-tuple-element.22), channel_id=1, source_target_pairs={{0,1},{1,0},{2,3},{3,2},{4,5},{5,4},{6,7},{7,6},{8,9},{9,8},{10,11... | collective-permute-start | bytes 393224 | tf_op jit(solution)/shard_map/ppermute | solution.py:20
  20.1 3.6 %collective-permute-start.6 = (bf16[128,512]{1,0:T(8,128)(2,1)S(1)}, bf16[128,512]{1,0:T(8,128)(2,1)S(1)}, u32[]{:S(2)}, u32[]{:S(2)}) collective-permute-start(bf16[128,512]{1,0:T(8,128)(2,1)S(1)} %get-tuple-element.23), channel_id=1, source_target_pairs={{0,6},{1,7},{2,4},{3,5},{4,2},{5,3},{6,0},{7,1},{8,14},{9,15},{10,... | collective-permute-start | bytes 393224 | tf_op jit(solution)/shard_map/ppermute | solution.py:20
  23.7 0.0 collective-permute-start.7
  23.7 2.0 %collective-permute-start.8 = (bf16[128,512]{1,0:T(8,128)(2,1)S(1)}, bf16[128,512]{1,0:T(8,128)(2,1)S(1)}, u32[]{:S(2)}, u32[]{:S(2)}) collective-permute-start(bf16[128,512]{1,0:T(8,128)(2,1)S(1)} %get-tuple-element.25), channel_id=1, source_target_pairs={{0,3},{1,2},{2,1},{3,0},{4,7},{5,6},{6,5},{7,4},{8,11},{9,10},{10,... | collective-permute-start | bytes 393224 | tf_op jit(solution)/shard_map/ppermute | solution.py:20
  25.7 0.0 collective-permute-done.5.refs_1_
  25.7 1.4 %collective-permute-start.9 = (bf16[128,512]{1,0:T(8,128)(2,1)S(1)}, bf16[128,512]{1,0:T(8,128)(2,1)S(1)}, u32[]{:S(2)}, u32[]{:S(2)}) collective-permute-start(bf16[128,512]{1,0:T(8,128)(2,1)S(1)} %get-tuple-element.26), channel_id=1, source_target_pairs={{0,4},{1,5},{2,6},{3,7},{4,0},{5,1},{6,2},{7,3},{8,12},{9,13},{10,... | collective-permute-start | bytes 393224 | tf_op jit(solution)/shard_map/ppermute | solution.py:20
  27.0 1.2 %collective-permute-done.6.refs_2_ = bf16[128,512]{1,0:T(8,128)(2,1)S(1)} collective-permute-done((bf16[128,512]{1,0:T(8,128)(2,1)S(1)}, bf16[128,512]{1,0:T(8,128)(2,1)S(1)}, u32[]{:S(2)}, u32[]{:S(2)}) %collective-permute-start.6) | collective-permute-done | bytes 131104 | tf_op jit(solution)/shard_map/ppermute | solution.py:20
  28.3 3.6 %collective-permute-start.10 = (bf16[128,512]{1,0:T(8,128)(2,1)S(1)}, bf16[128,512]{1,0:T(8,128)(2,1)S(1)}, u32[]{:S(2)}, u32[]{:S(2)}) collective-permute-start(bf16[128,512]{1,0:T(8,128)(2,1)S(1)} %get-tuple-element.27), channel_id=1, source_target_pairs={{0,7},{1,6},{2,5},{3,4},{4,3},{5,2},{6,1},{7,0},{8,15},{9,14},{10,... | collective-permute-start | bytes 393224 | tf_op jit(solution)/shard_map/ppermute | solution.py:20
  31.8 1.3 %collective-permute-start.11 = (bf16[128,512]{1,0:T(8,128)(2,1)S(1)}, bf16[128,512]{1,0:T(8,128)(2,1)S(1)}, u32[]{:S(2)}, u32[]{:S(2)}) collective-permute-start(bf16[128,512]{1,0:T(8,128)(2,1)S(1)} %get-tuple-element.28), channel_id=1, source_target_pairs={{0,5},{1,4},{2,7},{3,6},{4,1},{5,0},{6,3},{7,2},{8,13},{9,12},{10,... | collective-permute-start | bytes 393224 | tf_op jit(solution)/shard_map/ppermute | solution.py:20
  33.2 1.8 %multiply_reduce_fusion = (f32[2]{0:T(128)S(1)}, bf16[2,128,512]{2,1,0:T(8,128)(2,1)}) fusion(bf16[2,128,512]{2,1,0:T(8,128)(2,1)} %collective-permute-done.1, bf16[2,256,512]{2,1,0:T(8,128)(2,1)S(1)} %fusion, s32[]{:T(128)S(6)} %select_n.113), kind=kLoop, calls=%fused_computation.7 | loop fusion | flops 917502 | bytes 786444 | tf_op jit(solution)/shard_map/reduce_sum | solution.py:216
  35.0 0.1 broadcast_in_dim.12.half_sq
  35.0 1.7 %shard_map.57.refs_8_ = bf16[8,528,128]{2,1,0:T(8,128)(2,1)} custom-call(s32[10]{0:T(128)S(1)} %shard_map.55.plan, bf16[4,128,512]{2,1,0:T(8,128)(2,1)S(1)} %all-to-all-done.1.slots, f32[2,128]{1,0:T(2,128)S(1)} %broadcast_in_dim.12.half_sq), custom_call_target="tpu_custom_call" | custom-call | tf_op jit(solution)/shard_map/pallas_call | solution.py:219
  36.7 3.8 %all-to-all-start.2 = ((bf16[8,528,128]{2,1,0:T(8,128)(2,1)}), bf16[8,528,128]{2,1,0:T(8,128)(2,1)S(1)}, u32[]{:S(2)}, u32[]{:S(2)}) async-start(bf16[8,528,128]{2,1,0:T(8,128)(2,1)} %shard_map.57.refs_8_), calls=%async_computation.2 | async-start | bytes 2162688 | tf_op jit(solution)/shard_map/all_to_all | solution.py:226
  40.5 0.0 collective-permute-done.8.refs_4_
  40.6 11.2 %collective-permute-done.11.refs_7_ = bf16[128,512]{1,0:T(8,128)(2,1)S(1)} collective-permute-done((bf16[128,512]{1,0:T(8,128)(2,1)S(1)}, bf16[128,512]{1,0:T(8,128)(2,1)S(1)}, u32[]{:S(2)}, u32[]{:S(2)}) %collective-permute-start.11) | collective-permute-done | bytes 131104 | tf_op jit(solution)/shard_map/ppermute | solution.py:20
  51.8 0.6 shard_map.58
  52.4 2.5 %collective-permute-start.12 = (bf16[2,1,128,512]{3,2,0,1:T(8,128)(2,1)S(1)}, bf16[2,1,128,512]{3,2,0,1:T(8,128)(2,1)S(1)}, u32[]{:S(2)}, u32[]{:S(2)}) collective-permute-start(bf16[2,1,128,512]{3,2,0,1:T(8,128)(2,1)S(1)} %bitcast.26), channel_id=1, source_target_pairs={{0,16},{8,24},{16,0},{24,8},{1,17},{9,25},{17,1},{25,9},{2,18},{10... | collective-permute-start | bytes 786440 | tf_op jit(solution)/shard_map/ppermute | solution.py:20
  54.9 0.2 collective-permute-start.2
  55.2 7.0 %collective-permute-done.12 = bf16[2,1,128,512]{3,2,0,1:T(8,128)(2,1)S(1)} collective-permute-done((bf16[2,1,128,512]{3,2,0,1:T(8,128)(2,1)S(1)}, bf16[2,1,128,512]{3,2,0,1:T(8,128)(2,1)S(1)}, u32[]{:S(2)}, u32[]{:S(2)}) %collective-permute-start.12) | collective-permute-done | bytes 262176 | tf_op jit(solution)/shard_map/ppermute | solution.py:20
  62.2 0.1 maximum_bitcast_fusion
  62.3 0.1 collective-permute-start.13
  62.3 0.5 collective-permute-start.3
  62.8 2.3 %collective-permute-done.2 = bf16[2,128,512]{2,1,0:T(8,128)(2,1)S(1)} collective-permute-done((bf16[2,128,512]{2,1,0:T(8,128)(2,1)S(1)}, bf16[2,128,512]{2,1,0:T(8,128)(2,1)S(1)}, u32[]{:S(2)}, u32[]{:S(2)}) %collective-permute-start.2) | collective-permute-done | bytes 262176 | tf_op jit(solution)/shard_map/ppermute | solution.py:20
  65.1 0.1 broadcast_in_dim.11
  65.3 0.0 collective-permute-done.3
  65.3 1.3 %collective-permute-done.4 = bf16[2,128,512]{2,1,0:T(8,128)(2,1)S(1)} collective-permute-done((bf16[2,128,512]{2,1,0:T(8,128)(2,1)S(1)}, bf16[2,128,512]{2,1,0:T(8,128)(2,1)S(1)}, u32[]{:S(2)}, u32[]{:S(2)}) %collective-permute-start.4) | collective-permute-done | bytes 262176 | tf_op jit(solution)/shard_map/ppermute | solution.py:20
  66.7 0.0 collective-permute-done.13
  66.7 0.1 select_bitcast_fusion.1
  66.8 0.1 pad_maximum_fusion
  66.9 0.1 copy.6
  66.9 0.7 convolution_convert_fusion.right_prod
  67.7 2.0 %all-to-all-done.2.arrived = bf16[8,528,128]{2,1,0:T(8,128)(2,1)S(1)} async-done(((bf16[8,528,128]{2,1,0:T(8,128)(2,1)}), bf16[8,528,128]{2,1,0:T(8,128)(2,1)S(1)}, u32[]{:S(2)}, u32[]{:S(2)}) %all-to-all-start.2) | async-done | bytes 1081376 | tf_op jit(solution)/shard_map/all_to_all | solution.py:226
  69.6 1.0 %shard_map.59 = (f32[2,128,512]{2,1,0:T(8,128)S(1)}, f32[8,128]{1,0:T(8,128)S(1)}) custom-call(s32[10]{0:T(128)S(1)} %shard_map.55.plan, bf16[2,512,512]{2,1,0:T(8,128)(2,1)S(1)} %convolution_convert_fusion.right_prod, f32[2,128]{1,0:T(2,128)S(1)} %broadcast_in_dim.12.half_sq, bf16[8,528,128]{2,1,0:T(8,128)(2,1)S(1)} %all-to-all-done.2.arrived), custom_call_target="tpu_custom_call" | custom-call | tf_op jit(solution)/shard_map/pallas_call | solution.py:240
  70.6 0.3 collective-permute-start.16
  70.9 1.4 %collective-permute-start.15 = (f32[8,128]{1,0:T(8,128)S(1)}, f32[8,128]{1,0:T(8,128)S(1)}, u32[]{:S(2)}, u32[]{:S(2)}) collective-permute-start(f32[8,128]{1,0:T(8,128)S(1)} %get-tuple-element.30.refs_0_), channel_id=1, source_target_pairs={{0,16},{8,24},{16,0},{24,8},{1,17},{9,25},{17,1},{25,9},{2,18},{10... | collective-permute-start | bytes 12296 | tf_op jit(solution)/shard_map/ppermute | solution.py:20
  72.3 0.2 collective-permute-start.14
  72.5 1.2 %collective-permute-done.16.refs_3_ = f32[8,128]{1,0:T(8,128)S(1)} collective-permute-done((f32[8,128]{1,0:T(8,128)S(1)}, f32[8,128]{1,0:T(8,128)S(1)}, u32[]{:S(2)}, u32[]{:S(2)}) %collective-permute-start.16) | collective-permute-done | bytes 4128 | tf_op jit(solution)/shard_map/ppermute | solution.py:20
  73.7 0.8 %collective-permute-done.15.refs_2_ = f32[8,128]{1,0:T(8,128)S(1)} collective-permute-done((f32[8,128]{1,0:T(8,128)S(1)}, f32[8,128]{1,0:T(8,128)S(1)}, u32[]{:S(2)}, u32[]{:S(2)}) %collective-permute-start.15) | collective-permute-done | bytes 4128 | tf_op jit(solution)/shard_map/ppermute | solution.py:20
  74.5 0.8 %shard_map.60 = bf16[2,128,512]{2,1,0:T(8,128)(2,1)} custom-call(f32[2,128,512]{2,1,0:T(8,128)S(1)} %get-tuple-element.29.precond, f32[8,128]{1,0:T(8,128)S(1)} %get-tuple-element.30.refs_0_, f32[8,128]{1,0:T(8,128)S(1)} %collective-permute-done.14.refs_1_, f32[8,128]{1,0:T(8,128)S(1)} %collective-permute-done.15.refs_2_, ...), custom_call_target="tpu_custom_call" | custom-call | tf_op jit(solution)/shard_map/pallas_call | solution.py:252
  (21 shorter events, 0.2 us)
Async XLA Ops:
  0.0 6.1 %copy-start.3 = (bf16[1,2,512,512]{3,2,1,0:T(8,128)(2,1)S(1)}, bf16[1,2,512,512]{3,2,1,0:T(8,128)(2,1)}, u32[]{:S(2)}) copy-start(bf16[1,2,512,512]{3,2,1,0:T(8,128)(2,1)} %param.5) | copy-start | bytes 3145732
  0.0 4.5 %copy-start.1 = (s32[9]{0:T(128)S(1)}, s32[9]{0:T(128)}, u32[]{:S(2)}) copy-start(s32[9]{0:T(128)} %offsets.1) | copy-start | bytes 112
  0.0 4.5 %copy-start = (s32[16]{0:T(128)S(1)}, s32[16]{0:T(128)}, u32[]{:S(2)}) copy-start(s32[16]{0:T(128)} %lists.1) | copy-start | bytes 196
  0.0 6.1 %collective-permute-start = (bf16[2,512,512]{2,1,0:T(8,128)(2,1)}, bf16[2,512,512]{2,1,0:T(8,128)(2,1)S(1)}, u32[]{:S(2)}, u32[]{:S(2)}) collective-permute-start(bf16[2,512,512]{2,1,0:T(8,128)(2,1)} %bitcast.29), channel_id=1, source_target_pairs={{0,8},{8,0},{16,24},{24,16},{1,9},{9,1},{17,25},{25,17},{2,10},{10... | collective-permute-start | bytes 3145736 | tf_op jit(solution)/shard_map/ppermute | solution.py:20
  0.5 13.1 %all-to-all-start = ((bf16[4,128,512]{2,1,0:T(8,128)(2,1)}), bf16[4,128,512]{2,1,0:T(8,128)(2,1)S(1)}, u32[]{:S(2)}, u32[]{:S(2)}) async-start(bf16[4,128,512]{2,1,0:T(8,128)(2,1)} %bitcast.28), calls=%async_computation | async-start | bytes 1048576 | tf_op jit(solution)/shard_map/all_to_all | solution.py:186
  13.7 18.1 %collective-permute-start.1 = (bf16[2,128,512]{2,1,0:T(8,128)(2,1)S(1)}, bf16[2,128,512]{2,1,0:T(8,128)(2,1)}, u32[]{:S(2)}, u32[]{:S(2)}) collective-permute-start(bf16[2,128,512]{2,1,0:T(8,128)(2,1)S(1)} %constant_dynamic-slice_fusion), channel_id=1, source_target_pairs={{0,16},{8,24},{16,0},{24,8},{1,17},{9,25},{17,1},{25,9},{2,18},{10... | collective-permute-start | bytes 786440 | tf_op jit(solution)/shard_map/ppermute | solution.py:20
  13.8 21.2 %all-to-all-start.1 = ((bf16[4,128,512]{2,1,0:T(8,128)(2,1)}), bf16[4,128,512]{2,1,0:T(8,128)(2,1)S(1)}, u32[]{:S(2)}, u32[]{:S(2)}) async-start(bf16[4,128,512]{2,1,0:T(8,128)(2,1)} %bitcast.3), calls=%async_computation.1 | async-start | bytes 1048576 | tf_op jit(solution)/shard_map/all_to_all | solution.py:186
  17.9 7.8 %collective-permute-start.5 = (bf16[128,512]{1,0:T(8,128)(2,1)S(1)}, bf16[128,512]{1,0:T(8,128)(2,1)S(1)}, u32[]{:S(2)}, u32[]{:S(2)}) collective-permute-start(bf16[128,512]{1,0:T(8,128)(2,1)S(1)} %get-tuple-element.22), channel_id=1, source_target_pairs={{0,1},{1,0},{2,3},{3,2},{4,5},{5,4},{6,7},{7,6},{8,9},{9,8},{10,11... | collective-permute-start | bytes 393224 | tf_op jit(solution)/shard_map/ppermute | solution.py:20
  20.1 8.2 %collective-permute-start.6 = (bf16[128,512]{1,0:T(8,128)(2,1)S(1)}, bf16[128,512]{1,0:T(8,128)(2,1)S(1)}, u32[]{:S(2)}, u32[]{:S(2)}) collective-permute-start(bf16[128,512]{1,0:T(8,128)(2,1)S(1)} %get-tuple-element.23), channel_id=1, source_target_pairs={{0,6},{1,7},{2,4},{3,5},{4,2},{5,3},{6,0},{7,1},{8,14},{9,15},{10,... | collective-permute-start | bytes 393224 | tf_op jit(solution)/shard_map/ppermute | solution.py:20
  23.7 16.9 %collective-permute-start.7 = (bf16[128,512]{1,0:T(8,128)(2,1)S(1)}, bf16[128,512]{1,0:T(8,128)(2,1)S(1)}, u32[]{:S(2)}, u32[]{:S(2)}) collective-permute-start(bf16[128,512]{1,0:T(8,128)(2,1)S(1)} %get-tuple-element.24), channel_id=1, source_target_pairs={{0,2},{1,3},{2,0},{3,1},{4,6},{5,7},{6,4},{7,5},{8,10},{9,11},{10,... | collective-permute-start | bytes 393224 | tf_op jit(solution)/shard_map/ppermute | solution.py:20
  23.7 16.9 %collective-permute-start.8 = (bf16[128,512]{1,0:T(8,128)(2,1)S(1)}, bf16[128,512]{1,0:T(8,128)(2,1)S(1)}, u32[]{:S(2)}, u32[]{:S(2)}) collective-permute-start(bf16[128,512]{1,0:T(8,128)(2,1)S(1)} %get-tuple-element.25), channel_id=1, source_target_pairs={{0,3},{1,2},{2,1},{3,0},{4,7},{5,6},{6,5},{7,4},{8,11},{9,10},{10,... | collective-permute-start | bytes 393224 | tf_op jit(solution)/shard_map/ppermute | solution.py:20
  25.7 14.9 %collective-permute-start.9 = (bf16[128,512]{1,0:T(8,128)(2,1)S(1)}, bf16[128,512]{1,0:T(8,128)(2,1)S(1)}, u32[]{:S(2)}, u32[]{:S(2)}) collective-permute-start(bf16[128,512]{1,0:T(8,128)(2,1)S(1)} %get-tuple-element.26), channel_id=1, source_target_pairs={{0,4},{1,5},{2,6},{3,7},{4,0},{5,1},{6,2},{7,3},{8,12},{9,13},{10,... | collective-permute-start | bytes 393224 | tf_op jit(solution)/shard_map/ppermute | solution.py:20
  28.3 12.3 %collective-permute-start.10 = (bf16[128,512]{1,0:T(8,128)(2,1)S(1)}, bf16[128,512]{1,0:T(8,128)(2,1)S(1)}, u32[]{:S(2)}, u32[]{:S(2)}) collective-permute-start(bf16[128,512]{1,0:T(8,128)(2,1)S(1)} %get-tuple-element.27), channel_id=1, source_target_pairs={{0,7},{1,6},{2,5},{3,4},{4,3},{5,2},{6,1},{7,0},{8,15},{9,14},{10,... | collective-permute-start | bytes 393224 | tf_op jit(solution)/shard_map/ppermute | solution.py:20
  31.8 19.9 %collective-permute-start.11 = (bf16[128,512]{1,0:T(8,128)(2,1)S(1)}, bf16[128,512]{1,0:T(8,128)(2,1)S(1)}, u32[]{:S(2)}, u32[]{:S(2)}) collective-permute-start(bf16[128,512]{1,0:T(8,128)(2,1)S(1)} %get-tuple-element.28), channel_id=1, source_target_pairs={{0,5},{1,4},{2,7},{3,6},{4,1},{5,0},{6,3},{7,2},{8,13},{9,12},{10,... | collective-permute-start | bytes 393224 | tf_op jit(solution)/shard_map/ppermute | solution.py:20
  36.7 32.9 %all-to-all-start.2 = ((bf16[8,528,128]{2,1,0:T(8,128)(2,1)}), bf16[8,528,128]{2,1,0:T(8,128)(2,1)S(1)}, u32[]{:S(2)}, u32[]{:S(2)}) async-start(bf16[8,528,128]{2,1,0:T(8,128)(2,1)} %shard_map.57.refs_8_), calls=%async_computation.2 | async-start | bytes 2162688 | tf_op jit(solution)/shard_map/all_to_all | solution.py:226
  51.8 3.2 %copy-start.2 = (bf16[2,128,512]{2,1,0:T(8,128)(2,1)S(1)}, bf16[2,128,512]{2,1,0:T(8,128)(2,1)}, u32[]{:S(2)}) copy-start(bf16[2,128,512]{2,1,0:T(8,128)(2,1)} %get-tuple-element.32) | copy-start | bytes 786436
  52.4 9.7 %collective-permute-start.12 = (bf16[2,1,128,512]{3,2,0,1:T(8,128)(2,1)S(1)}, bf16[2,1,128,512]{3,2,0,1:T(8,128)(2,1)S(1)}, u32[]{:S(2)}, u32[]{:S(2)}) collective-permute-start(bf16[2,1,128,512]{3,2,0,1:T(8,128)(2,1)S(1)} %bitcast.26), channel_id=1, source_target_pairs={{0,16},{8,24},{16,0},{24,8},{1,17},{9,25},{17,1},{25,9},{2,18},{10... | collective-permute-start | bytes 786440 | tf_op jit(solution)/shard_map/ppermute | solution.py:20
  54.9 10.2 %collective-permute-start.2 = (bf16[2,128,512]{2,1,0:T(8,128)(2,1)S(1)}, bf16[2,128,512]{2,1,0:T(8,128)(2,1)S(1)}, u32[]{:S(2)}, u32[]{:S(2)}) collective-permute-start(bf16[2,128,512]{2,1,0:T(8,128)(2,1)S(1)} %copy-done.2), channel_id=1, source_target_pairs={{0,16},{8,24},{16,0},{24,8},{1,17},{9,25},{17,1},{25,9},{2,18},{10... | collective-permute-start | bytes 786440 | tf_op jit(solution)/shard_map/ppermute | solution.py:20
  62.3 4.4 %collective-permute-start.13 = (bf16[2,2,128,512]{3,2,0,1:T(8,128)(2,1)S(1)}, bf16[2,2,128,512]{3,2,0,1:T(8,128)(2,1)S(1)}, u32[]{:S(2)}, u32[]{:S(2)}) collective-permute-start(bf16[2,2,128,512]{3,2,0,1:T(8,128)(2,1)S(1)} %maximum_bitcast_fusion), channel_id=1, source_target_pairs={{0,8},{8,0},{16,24},{24,16},{1,9},{9,1},{17,25},{25,17},{2,10},{10... | collective-permute-start | bytes 1572872 | tf_op jit(solution)/shard_map/ppermute | solution.py:20
  62.3 2.9 %collective-permute-start.3 = (bf16[2,128,512]{2,1,0:T(8,128)(2,1)S(1)}, bf16[2,128,512]{2,1,0:T(8,128)(2,1)S(1)}, u32[]{:S(2)}, u32[]{:S(2)}) collective-permute-start(bf16[2,128,512]{2,1,0:T(8,128)(2,1)S(1)} %copy-done.2), channel_id=1, source_target_pairs={{0,8},{8,0},{16,24},{24,16},{1,9},{9,1},{17,25},{25,17},{2,10},{10... | collective-permute-start | bytes 786440 | tf_op jit(solution)/shard_map/ppermute | solution.py:20
  65.1 1.5 %collective-permute-start.4 = (bf16[2,128,512]{2,1,0:T(8,128)(2,1)S(1)}, bf16[2,128,512]{2,1,0:T(8,128)(2,1)S(1)}, u32[]{:S(2)}, u32[]{:S(2)}) collective-permute-start(bf16[2,128,512]{2,1,0:T(8,128)(2,1)S(1)} %collective-permute-done.2), channel_id=1, source_target_pairs={{0,8},{8,0},{16,24},{24,16},{1,9},{9,1},{17,25},{25,17},{2,10},{10... | collective-permute-start | bytes 786440 | tf_op jit(solution)/shard_map/ppermute | solution.py:20
  70.6 3.1 %collective-permute-start.16 = (f32[8,128]{1,0:T(8,128)S(1)}, f32[8,128]{1,0:T(8,128)S(1)}, u32[]{:S(2)}, u32[]{:S(2)}) collective-permute-start(f32[8,128]{1,0:T(8,128)S(1)} %get-tuple-element.30.refs_0_), channel_id=1, source_target_pairs={{0,24},{8,16},{16,8},{24,0},{1,25},{9,17},{17,9},{25,1},{2,26},{10... | collective-permute-start | bytes 12296 | tf_op jit(solution)/shard_map/ppermute | solution.py:20
  70.9 3.6 %collective-permute-start.15 = (f32[8,128]{1,0:T(8,128)S(1)}, f32[8,128]{1,0:T(8,128)S(1)}, u32[]{:S(2)}, u32[]{:S(2)}) collective-permute-start(f32[8,128]{1,0:T(8,128)S(1)} %get-tuple-element.30.refs_0_), channel_id=1, source_target_pairs={{0,16},{8,24},{16,0},{24,8},{1,17},{9,25},{17,1},{25,9},{2,18},{10... | collective-permute-start | bytes 12296 | tf_op jit(solution)/shard_map/ppermute | solution.py:20
  72.3 2.2 %collective-permute-start.14 = (f32[8,128]{1,0:T(8,128)S(1)}, f32[8,128]{1,0:T(8,128)S(1)}, u32[]{:S(2)}, u32[]{:S(2)}) collective-permute-start(f32[8,128]{1,0:T(8,128)S(1)} %get-tuple-element.30.refs_0_), channel_id=1, source_target_pairs={{0,8},{8,0},{16,24},{24,16},{1,9},{9,1},{17,25},{25,17},{2,10},{10... | collective-permute-start | bytes 12296 | tf_op jit(solution)/shard_map/ppermute | solution.py:20

commit v11 on v10

--- a/solution.py
+++ b/solution.py
@@ -108,10 +108,15 @@
         outs[d][...] = slots[plan[column ^ d]]
 
 
-def left_kernel(mp_count, plan, slots, half_sq, out):
+def left_kernel(mp_count, plan, slots, own_rows, out, half_sq):
     rows = slots.shape[1]
     lanes = out.shape[2]
-    total = jnp.sum(half_sq[...], axis=0, keepdims=True)
+    total = jnp.zeros((1, lanes), jnp.float32)
+    for r in range(own_rows.shape[0]):
+        block = own_rows[r].astype(jnp.float32)
+        square = jnp.sum(jnp.sum(block * block, axis=1, keepdims=True), axis=0, keepdims=True)
+        half_sq[r : r + 1, :] = jnp.broadcast_to(square, (1, lanes))
+        total += square
     first = total.astype(jnp.bfloat16).astype(jnp.float32)
     second = (total - first).astype(jnp.bfloat16).astype(jnp.float32)
     third = total - first - second
@@ -211,18 +216,16 @@
     order = [1, distant[0], *range(2, far), *distant[1:]]
     right_arrived = [outgoing[0]] + [swap(outgoing[d], "mp", d) for d in order]
     total = chip_sum(total, dp_count, dp_index)
-    total_f = total.astype(jnp.float32)
-    half_sq = jnp.broadcast_to(
-        jnp.sum(total_f * total_f, axis=(1, 2)).reshape(per_shard, 1),
-        (per_shard, lanes),
-    )
-    left_outgoing = pl.pallas_call(
+    left_outgoing, half_sq = pl.pallas_call(
         functools.partial(left_kernel, mp_count),
-        out_shape=jax.ShapeDtypeStruct((mp_count, rows * width // lanes + 16, lanes), jnp.bfloat16),
+        out_shape=[
+            jax.ShapeDtypeStruct((mp_count, rows * width // lanes + 16, lanes), jnp.bfloat16),
+            jax.ShapeDtypeStruct((per_shard, lanes), jnp.float32),
+        ],
         in_specs=[SMEM, VMEM, VMEM],
-        out_specs=VMEM,
-        compiler_params=params,
-    )(plan, left_slots, half_sq)
+        out_specs=[VMEM, VMEM],
+        compiler_params=params,
+    )(plan, left_slots, total)
     left_arrived = lax.all_to_all(left_outgoing, "mp", split_axis=0, concat_axis=0, tiled=True)
     right_rows = pl.pallas_call(
         functools.partial(pick_kernel, mp_count, per_shard, [0] + order),

time: 75.6 us -> 79.1 us (1.046)
  local copies, waits for them, and re-layouts: 0.34 us -> 4.94 us
  waiting for transfers between devices: 34.4 us -> 32.5 us
  matrix products: 0.71 us -> 1.94 us
  other arithmetic: 2.19 us -> 1.19 us
    dynamic_update_slice x4 -> x3, local copies, waits for them, and re-layouts: 0.1 us -> 3.1 us  [whole_rows(): whole = lax.dynamic_update_slice_in_dim(whole, piece, place * part, axis=1)]
    all_to_all x1, waiting for transfers between devices: 1.97 us -> 0.01 us  [shards(): lax.all_to_all(left_outgoing, 'mp', split_axis=0, concat_axis=0, tiled=True)]
    reduce_sum x1 -> x0, other arithmetic: 1.78 us -> none  [shards(): jnp.sum(total_f * total_f, axis=(1, 2)).reshape(per_shard, 1)]
    dot_general x1, matrix products: 0.71 us -> 1.94 us  [shards(): jnp.einsum('bij,bjk->bik', grad, right, preferred_element_type=jnp.float32)]
    broadcast_in_dim x1, local copies, waits for them, and re-layouts: 0.07 us -> 1.03 us  [whole_rows(): jnp.zeros((total.shape[0], part * dp_count, total.shape[2]), total.dtype)]
  transfers between devices with their start and end apart: 20 -> 20, of which waited for: 9 -> 7; matrix products, arithmetic and copies ran while one was open for 4% -> 9% of each run, Pallas kernels for 6% -> 6%
where the time goes in v11:
time: 79.1 us; the launch traced here: 78.4 us
  waiting for transfers between devices  32.5 us (41%)
  starting transfers between devices  31.2 us (39%)
  Pallas kernels  6.36 us (8%)
  local copies, waits for them, and re-layouts  4.94 us (6%)
  matrix products  1.94 us (2%)
  other arithmetic  1.19 us (2%)
    ppermute x17, waiting for transfers between devices, swap(): return lax.ppermute(value, axis, [(i, i ^ distance) for i in range(count)])  25.1 us
    ppermute x17, starting transfers between devices, swap(): return lax.ppermute(value, axis, [(i, i ^ distance) for i in range(count)])  20 us
    all_to_all x2, waiting for transfers between devices, over_dp(): lax.all_to_all(factor[0, 0].reshape(dp_count, rows, width), 'dp', split_a...  7.43 us
    all_to_all x2, starting transfers between devices, over_dp(): lax.all_to_all(factor[0, 0].reshape(dp_count, rows, width), 'dp', split_a...  7.41 us
    all_to_all x1, starting transfers between devices, shards(): lax.all_to_all(left_outgoing, 'mp', split_axis=0, concat_axis=0, tiled=True)  3.8 us
    dynamic_update_slice x3, local copies, waits for them, and re-layouts, whole_rows(): whole = lax.dynamic_update_slice_in_dim(whole, piece, place * part, axis=1)  3.1 us
    dot_general x1, matrix products, shards(): jnp.einsum('bij,bjk->bik', grad, right, preferred_element_type=jnp.float32)  1.94 us
    pallas_call x1, Pallas kernels, shards(): pl.pallas_call(functools.partial(left_kernel, mp_count), out_shape=[jax.S...  1.76 us
  transfers between devices with their start and end apart: 20, of which 7 were waited for; matrix products, arithmetic and copies ran while one was open for 9% of the time, Pallas kernels for 6%

profile of v11, /device:TPU:0, one launch (start us, length us, event | category | flops | bytes accessed | tf_op | source)
XLA Modules:
  0.0 78.4 jit_solution(3704254074328436286)
XLA Ops:
  0.0 0.5 collective-permute-start
  0.5 3.9 %all-to-all-start = ((bf16[4,128,512]{2,1,0:T(8,128)(2,1)}), bf16[4,128,512]{2,1,0:T(8,128)(2,1)S(1)}, u32[]{:S(2)}, u32[]{:S(2)}) async-start(bf16[4,128,512]{2,1,0:T(8,128)(2,1)} %bitcast.28), calls=%async_computation | async-start | bytes 1048576 | tf_op jit(solution)/shard_map/all_to_all | solution.py:191
  4.5 1.6 %shard_map.55.plan = s32[10]{0:T(128)S(1)} custom-call(s32[16]{0:T(128)S(1)} %copy-done, s32[9]{0:T(128)S(1)} %copy-done.1), custom_call_target="tpu_custom_call" | custom-call | tf_op jit(solution)/shard_map/pallas_call | solution.py:195
  6.1 0.0 collective-permute-done
  6.1 0.1 fusion
  6.2 7.4 %all-to-all-done.slots = bf16[4,128,512]{2,1,0:T(8,128)(2,1)S(1)} async-done(((bf16[4,128,512]{2,1,0:T(8,128)(2,1)}), bf16[4,128,512]{2,1,0:T(8,128)(2,1)S(1)}, u32[]{:S(2)}, u32[]{:S(2)}) %all-to-all-start) | async-done | bytes 524320 | tf_op jit(solution)/shard_map/all_to_all | solution.py:191
  13.7 0.7 constant_dynamic-slice_fusion
  14.4 0.0 collective-permute-start.1
  14.4 3.5 %all-to-all-start.1 = ((bf16[4,128,512]{2,1,0:T(8,128)(2,1)}), bf16[4,128,512]{2,1,0:T(8,128)(2,1)S(1)}, u32[]{:S(2)}, u32[]{:S(2)}) async-start(bf16[4,128,512]{2,1,0:T(8,128)(2,1)} %bitcast.3), calls=%async_computation.1 | async-start | bytes 1048576 | tf_op jit(solution)/shard_map/all_to_all | solution.py:191
  17.9 0.6 shard_map.56
  18.5 2.2 %collective-permute-start.5 = (bf16[128,512]{1,0:T(8,128)(2,1)S(1)}, bf16[128,512]{1,0:T(8,128)(2,1)S(1)}, u32[]{:S(2)}, u32[]{:S(2)}) collective-permute-start(bf16[128,512]{1,0:T(8,128)(2,1)S(1)} %get-tuple-element.24), channel_id=1, source_target_pairs={{0,1},{1,0},{2,3},{3,2},{4,5},{5,4},{6,7},{7,6},{8,9},{9,8},{10,11... | collective-permute-start | bytes 393224 | tf_op jit(solution)/shard_map/ppermute | solution.py:20
  20.7 3.6 %collective-permute-start.6 = (bf16[128,512]{1,0:T(8,128)(2,1)S(1)}, bf16[128,512]{1,0:T(8,128)(2,1)S(1)}, u32[]{:S(2)}, u32[]{:S(2)}) collective-permute-start(bf16[128,512]{1,0:T(8,128)(2,1)S(1)} %get-tuple-element.25), channel_id=1, source_target_pairs={{0,6},{1,7},{2,4},{3,5},{4,2},{5,3},{6,0},{7,1},{8,14},{9,15},{10,... | collective-permute-start | bytes 393224 | tf_op jit(solution)/shard_map/ppermute | solution.py:20
  24.3 0.0 collective-permute-start.7
  24.3 2.0 %collective-permute-start.8 = (bf16[128,512]{1,0:T(8,128)(2,1)S(1)}, bf16[128,512]{1,0:T(8,128)(2,1)S(1)}, u32[]{:S(2)}, u32[]{:S(2)}) collective-permute-start(bf16[128,512]{1,0:T(8,128)(2,1)S(1)} %get-tuple-element.27), channel_id=1, source_target_pairs={{0,3},{1,2},{2,1},{3,0},{4,7},{5,6},{6,5},{7,4},{8,11},{9,10},{10,... | collective-permute-start | bytes 393224 | tf_op jit(solution)/shard_map/ppermute | solution.py:20
  26.3 0.0 collective-permute-done.5.refs_1_
  26.3 1.4 %collective-permute-start.9 = (bf16[128,512]{1,0:T(8,128)(2,1)S(1)}, bf16[128,512]{1,0:T(8,128)(2,1)S(1)}, u32[]{:S(2)}, u32[]{:S(2)}) collective-permute-start(bf16[128,512]{1,0:T(8,128)(2,1)S(1)} %get-tuple-element.28), channel_id=1, source_target_pairs={{0,4},{1,5},{2,6},{3,7},{4,0},{5,1},{6,2},{7,3},{8,12},{9,13},{10,... | collective-permute-start | bytes 393224 | tf_op jit(solution)/shard_map/ppermute | solution.py:20
  27.7 1.2 %collective-permute-done.6.refs_2_ = bf16[128,512]{1,0:T(8,128)(2,1)S(1)} collective-permute-done((bf16[128,512]{1,0:T(8,128)(2,1)S(1)}, bf16[128,512]{1,0:T(8,128)(2,1)S(1)}, u32[]{:S(2)}, u32[]{:S(2)}) %collective-permute-start.6) | collective-permute-done | bytes 131104 | tf_op jit(solution)/shard_map/ppermute | solution.py:20
  28.9 3.6 %collective-permute-start.10 = (bf16[128,512]{1,0:T(8,128)(2,1)S(1)}, bf16[128,512]{1,0:T(8,128)(2,1)S(1)}, u32[]{:S(2)}, u32[]{:S(2)}) collective-permute-start(bf16[128,512]{1,0:T(8,128)(2,1)S(1)} %get-tuple-element.29), channel_id=1, source_target_pairs={{0,7},{1,6},{2,5},{3,4},{4,3},{5,2},{6,1},{7,0},{8,15},{9,14},{10,... | collective-permute-start | bytes 393224 | tf_op jit(solution)/shard_map/ppermute | solution.py:20
  32.5 1.3 %collective-permute-start.11 = (bf16[128,512]{1,0:T(8,128)(2,1)S(1)}, bf16[128,512]{1,0:T(8,128)(2,1)S(1)}, u32[]{:S(2)}, u32[]{:S(2)}) collective-permute-start(bf16[128,512]{1,0:T(8,128)(2,1)S(1)} %get-tuple-element.30), channel_id=1, source_target_pairs={{0,5},{1,4},{2,7},{3,6},{4,1},{5,0},{6,3},{7,2},{8,13},{9,12},{10,... | collective-permute-start | bytes 393224 | tf_op jit(solution)/shard_map/ppermute | solution.py:20
  33.8 1.0 %broadcast_in_dim.6 = bf16[2,512,512]{2,1,0:T(8,128)(2,1)} broadcast(bf16[]{:T(256)} %constant.132.clone.1), dimensions={} | broadcast | bytes 1048578 | tf_op jit(solution)/shard_map/broadcast_in_dim | solution.py:54
  34.9 0.8 constant_dynamic-update-slice_fusion.3
  35.6 0.0 all-to-all-done.1.slots
  35.6 1.8 %shard_map.57 = (bf16[8,528,128]{2,1,0:T(8,128)(2,1)}, f32[2,128]{1,0:T(2,128)S(1)}) custom-call(s32[10]{0:T(128)S(1)} %shard_map.55.plan, bf16[4,128,512]{2,1,0:T(8,128)(2,1)S(1)} %all-to-all-done.1.slots, bf16[2,128,512]{2,1,0:T(8,128)(2,1)S(1)} %get-tuple-element.36.own_rows), custom_call_target="tpu_custom_call" | custom-call | tf_op jit(solution)/shard_map/pallas_call | solution.py:219
  37.4 3.8 %all-to-all-start.2 = ((bf16[8,528,128]{2,1,0:T(8,128)(2,1)}), bf16[8,528,128]{2,1,0:T(8,128)(2,1)S(1)}, u32[]{:S(2)}, u32[]{:S(2)}) async-start(bf16[8,528,128]{2,1,0:T(8,128)(2,1)} %get-tuple-element.31.refs_8_), calls=%async_computation.2 | async-start | bytes 2162688 | tf_op jit(solution)/shard_map/all_to_all | solution.py:229
  41.2 0.0 collective-permute-done.8.refs_4_
  41.2 0.0 collective-permute-done.9.refs_5_
  41.2 11.2 %collective-permute-done.11.refs_7_ = bf16[128,512]{1,0:T(8,128)(2,1)S(1)} collective-permute-done((bf16[128,512]{1,0:T(8,128)(2,1)S(1)}, bf16[128,512]{1,0:T(8,128)(2,1)S(1)}, u32[]{:S(2)}, u32[]{:S(2)}) %collective-permute-start.11) | collective-permute-done | bytes 131104 | tf_op jit(solution)/shard_map/ppermute | solution.py:20
  52.4 0.6 shard_map.58
  53.0 2.6 %collective-permute-start.12 = (bf16[2,1,128,512]{3,2,0,1:T(8,128)(2,1)S(1)}, bf16[2,1,128,512]{3,2,0,1:T(8,128)(2,1)S(1)}, u32[]{:S(2)}, u32[]{:S(2)}) collective-permute-start(bf16[2,1,128,512]{3,2,0,1:T(8,128)(2,1)S(1)} %bitcast.26), channel_id=1, source_target_pairs={{0,16},{8,24},{16,0},{24,8},{1,17},{9,25},{17,1},{25,9},{2,18},{10... | collective-permute-start | bytes 786440 | tf_op jit(solution)/shard_map/ppermute | solution.py:20
  55.6 0.1 collective-permute-start.2
  55.7 7.1 %collective-permute-done.12 = bf16[2,1,128,512]{3,2,0,1:T(8,128)(2,1)S(1)} collective-permute-done((bf16[2,1,128,512]{3,2,0,1:T(8,128)(2,1)S(1)}, bf16[2,1,128,512]{3,2,0,1:T(8,128)(2,1)S(1)}, u32[]{:S(2)}, u32[]{:S(2)}) %collective-permute-start.12) | collective-permute-done | bytes 262176 | tf_op jit(solution)/shard_map/ppermute | solution.py:20
  62.9 0.1 maximum_bitcast_fusion
  62.9 0.1 collective-permute-start.13
  63.0 0.5 collective-permute-start.3
  63.5 2.2 %collective-permute-done.2 = bf16[2,128,512]{2,1,0:T(8,128)(2,1)S(1)} collective-permute-done((bf16[2,128,512]{2,1,0:T(8,128)(2,1)S(1)}, bf16[2,128,512]{2,1,0:T(8,128)(2,1)S(1)}, u32[]{:S(2)}, u32[]{:S(2)}) %collective-permute-start.2) | collective-permute-done | bytes 262176 | tf_op jit(solution)/shard_map/ppermute | solution.py:20
  65.8 0.7 constant_dynamic-update-slice_fusion.2
  66.5 1.7 %constant_dynamic-update-slice_fusion.1 = bf16[2,512,512]{2,1,0:T(8,128)(2,1)} fusion(bf16[2,512,512]{2,1,0:T(8,128)(2,1)} %constant_dynamic-update-slice_fusion.2, bf16[2,128,512]{2,1,0:T(8,128)(2,1)} %collective-permute-done.3, s32[]{:T(128)S(6)} %select_n.123), kind=kLoop, calls=%fused_computation.11 | loop fusion | bytes 524292 | tf_op jit(solution)/shard_map/dynamic_update_slice | solution.py:60
  68.2 0.7 constant_dynamic-update-slice_fusion
  68.9 0.1 select_bitcast_fusion.1
  68.9 0.1 pad_maximum_fusion
  69.1 0.1 copy.6
  69.1 1.9 %convolution_convert_fusion.right_prod = bf16[2,512,512]{2,1,0:T(8,128)(2,1)S(1)} fusion(bf16[2,512,512]{2,1,0:T(8,128)(2,1)} %constant_dynamic-update-slice_fusion, bf16[2,512,512]{2,1,0:T(8,128)(2,1)S(1)} %bitcast.27), kind=kOutput, calls=%fused_computation | convolution fusion | flops 537395200 | bytes 3145728 | tf_op jit(solution)/shard_map/bij,bjk->bik/dot_general | solution.py:240
  71.1 1.0 %shard_map.59 = (f32[2,128,512]{2,1,0:T(8,128)S(1)}, f32[8,128]{1,0:T(8,128)S(1)}) custom-call(s32[10]{0:T(128)S(1)} %shard_map.55.plan, bf16[2,512,512]{2,1,0:T(8,128)(2,1)S(1)} %convolution_convert_fusion.right_prod, f32[2,128]{1,0:T(2,128)S(1)} %get-tuple-element.32.half_sq, bf16[8,528,128]{2,1,0:T(8,128)(2,1)S(1)} %all-to-all-done.2.arrived), custom_call_target="tpu_custom_call" | custom-call | tf_op jit(solution)/shard_map/pallas_call | solution.py:243
  72.0 1.9 %collective-permute-start.16 = (f32[8,128]{1,0:T(8,128)S(1)}, f32[8,128]{1,0:T(8,128)S(1)}, u32[]{:S(2)}, u32[]{:S(2)}) collective-permute-start(f32[8,128]{1,0:T(8,128)S(1)} %get-tuple-element.34.refs_0_), channel_id=1, source_target_pairs={{0,24},{8,16},{16,8},{24,0},{1,25},{9,17},{17,9},{25,1},{2,26},{10... | collective-permute-start | bytes 12296 | tf_op jit(solution)/shard_map/ppermute | solution.py:20
  74.0 0.3 collective-permute-start.15
  74.3 1.0 %collective-permute-done.16.refs_3_ = f32[8,128]{1,0:T(8,128)S(1)} collective-permute-done((f32[8,128]{1,0:T(8,128)S(1)}, f32[8,128]{1,0:T(8,128)S(1)}, u32[]{:S(2)}, u32[]{:S(2)}) %collective-permute-start.16) | collective-permute-done | bytes 4128 | tf_op jit(solution)/shard_map/ppermute | solution.py:20
  75.3 2.3 %collective-permute-done.15.refs_2_ = f32[8,128]{1,0:T(8,128)S(1)} collective-permute-done((f32[8,128]{1,0:T(8,128)S(1)}, f32[8,128]{1,0:T(8,128)S(1)}, u32[]{:S(2)}, u32[]{:S(2)}) %collective-permute-start.15) | collective-permute-done | bytes 4128 | tf_op jit(solution)/shard_map/ppermute | solution.py:20
  77.6 0.8 %shard_map.60 = bf16[2,128,512]{2,1,0:T(8,128)(2,1)} custom-call(f32[2,128,512]{2,1,0:T(8,128)S(1)} %get-tuple-element.33.precond, f32[8,128]{1,0:T(8,128)S(1)} %get-tuple-element.34.refs_0_, f32[8,128]{1,0:T(8,128)S(1)} %collective-permute-done.14.refs_1_, f32[8,128]{1,0:T(8,128)S(1)} %collective-permute-done.15.refs_2_, ...), custom_call_target="tpu_custom_call" | custom-call | tf_op jit(solution)/shard_map/pallas_call | solution.py:255
  (21 shorter events, 0.1 us)
Async XLA Ops:
  0.0 6.1 %copy-start.4 = (bf16[1,2,512,512]{3,2,1,0:T(8,128)(2,1)S(1)}, bf16[1,2,512,512]{3,2,1,0:T(8,128)(2,1)}, u32[]{:S(2)}) copy-start(bf16[1,2,512,512]{3,2,1,0:T(8,128)(2,1)} %param.5) | copy-start | bytes 3145732
  0.0 4.5 %copy-start.1 = (s32[9]{0:T(128)S(1)}, s32[9]{0:T(128)}, u32[]{:S(2)}) copy-start(s32[9]{0:T(128)} %offsets.1) | copy-start | bytes 112
  0.0 4.5 %copy-start = (s32[16]{0:T(128)S(1)}, s32[16]{0:T(128)}, u32[]{:S(2)}) copy-start(s32[16]{0:T(128)} %lists.1) | copy-start | bytes 196
  0.0 6.1 %collective-permute-start = (bf16[2,512,512]{2,1,0:T(8,128)(2,1)}, bf16[2,512,512]{2,1,0:T(8,128)(2,1)S(1)}, u32[]{:S(2)}, u32[]{:S(2)}) collective-permute-start(bf16[2,512,512]{2,1,0:T(8,128)(2,1)} %bitcast.29), channel_id=1, source_target_pairs={{0,8},{8,0},{16,24},{24,16},{1,9},{9,1},{17,25},{25,17},{2,10},{10... | collective-permute-start | bytes 3145736 | tf_op jit(solution)/shard_map/ppermute | solution.py:20
  0.5 13.1 %all-to-all-start = ((bf16[4,128,512]{2,1,0:T(8,128)(2,1)}), bf16[4,128,512]{2,1,0:T(8,128)(2,1)S(1)}, u32[]{:S(2)}, u32[]{:S(2)}) async-start(bf16[4,128,512]{2,1,0:T(8,128)(2,1)} %bitcast.28), calls=%async_computation | async-start | bytes 1048576 | tf_op jit(solution)/shard_map/all_to_all | solution.py:191
  6.2 8.2 %copy-start.2 = (bf16[2,256,512]{2,1,0:T(8,128)(2,1)}, bf16[2,256,512]{2,1,0:T(8,128)(2,1)S(1)}, u32[]{:S(2)}) copy-start(bf16[2,256,512]{2,1,0:T(8,128)(2,1)S(1)} %fusion) | copy-start | bytes 1572868
  14.4 18.1 %collective-permute-start.1 = (bf16[2,128,512]{2,1,0:T(8,128)(2,1)}, bf16[2,128,512]{2,1,0:T(8,128)(2,1)S(1)}, u32[]{:S(2)}, u32[]{:S(2)}) collective-permute-start(bf16[2,128,512]{2,1,0:T(8,128)(2,1)} %constant_dynamic-slice_fusion), channel_id=1, source_target_pairs={{0,16},{8,24},{16,0},{24,8},{1,17},{9,25},{17,1},{25,9},{2,18},{10... | collective-permute-start | bytes 786440 | tf_op jit(solution)/shard_map/ppermute | solution.py:20
  14.4 21.2 %all-to-all-start.1 = ((bf16[4,128,512]{2,1,0:T(8,128)(2,1)}), bf16[4,128,512]{2,1,0:T(8,128)(2,1)S(1)}, u32[]{:S(2)}, u32[]{:S(2)}) async-start(bf16[4,128,512]{2,1,0:T(8,128)(2,1)} %bitcast.3), calls=%async_computation.1 | async-start | bytes 1048576 | tf_op jit(solution)/shard_map/all_to_all | solution.py:191
  18.5 16.3 %copy-start.3 = (bf16[2,256,512]{2,1,0:T(8,128)(2,1)S(1)}, bf16[2,256,512]{2,1,0:T(8,128)(2,1)}, u32[]{:S(2)}) copy-start(bf16[2,256,512]{2,1,0:T(8,128)(2,1)} %copy-done.2) | copy-start | bytes 1572868
  18.5 7.8 %collective-permute-start.5 = (bf16[128,512]{1,0:T(8,128)(2,1)S(1)}, bf16[128,512]{1,0:T(8,128)(2,1)S(1)}, u32[]{:S(2)}, u32[]{:S(2)}) collective-permute-start(bf16[128,512]{1,0:T(8,128)(2,1)S(1)} %get-tuple-element.24), channel_id=1, source_target_pairs={{0,1},{1,0},{2,3},{3,2},{4,5},{5,4},{6,7},{7,6},{8,9},{9,8},{10,11... | collective-permute-start | bytes 393224 | tf_op jit(solution)/shard_map/ppermute | solution.py:20
  20.7 8.2 %collective-permute-start.6 = (bf16[128,512]{1,0:T(8,128)(2,1)S(1)}, bf16[128,512]{1,0:T(8,128)(2,1)S(1)}, u32[]{:S(2)}, u32[]{:S(2)}) collective-permute-start(bf16[128,512]{1,0:T(8,128)(2,1)S(1)} %get-tuple-element.25), channel_id=1, source_target_pairs={{0,6},{1,7},{2,4},{3,5},{4,2},{5,3},{6,0},{7,1},{8,14},{9,15},{10,... | collective-permute-start | bytes 393224 | tf_op jit(solution)/shard_map/ppermute | solution.py:20
  24.3 16.9 %collective-permute-start.7 = (bf16[128,512]{1,0:T(8,128)(2,1)S(1)}, bf16[128,512]{1,0:T(8,128)(2,1)S(1)}, u32[]{:S(2)}, u32[]{:S(2)}) collective-permute-start(bf16[128,512]{1,0:T(8,128)(2,1)S(1)} %get-tuple-element.26), channel_id=1, source_target_pairs={{0,2},{1,3},{2,0},{3,1},{4,6},{5,7},{6,4},{7,5},{8,10},{9,11},{10,... | collective-permute-start | bytes 393224 | tf_op jit(solution)/shard_map/ppermute | solution.py:20
  24.3 16.9 %collective-permute-start.8 = (bf16[128,512]{1,0:T(8,128)(2,1)S(1)}, bf16[128,512]{1,0:T(8,128)(2,1)S(1)}, u32[]{:S(2)}, u32[]{:S(2)}) collective-permute-start(bf16[128,512]{1,0:T(8,128)(2,1)S(1)} %get-tuple-element.27), channel_id=1, source_target_pairs={{0,3},{1,2},{2,1},{3,0},{4,7},{5,6},{6,5},{7,4},{8,11},{9,10},{10,... | collective-permute-start | bytes 393224 | tf_op jit(solution)/shard_map/ppermute | solution.py:20
  26.3 14.9 %collective-permute-start.9 = (bf16[128,512]{1,0:T(8,128)(2,1)S(1)}, bf16[128,512]{1,0:T(8,128)(2,1)S(1)}, u32[]{:S(2)}, u32[]{:S(2)}) collective-permute-start(bf16[128,512]{1,0:T(8,128)(2,1)S(1)} %get-tuple-element.28), channel_id=1, source_target_pairs={{0,4},{1,5},{2,6},{3,7},{4,0},{5,1},{6,2},{7,3},{8,12},{9,13},{10,... | collective-permute-start | bytes 393224 | tf_op jit(solution)/shard_map/ppermute | solution.py:20
  28.9 12.3 %collective-permute-start.10 = (bf16[128,512]{1,0:T(8,128)(2,1)S(1)}, bf16[128,512]{1,0:T(8,128)(2,1)S(1)}, u32[]{:S(2)}, u32[]{:S(2)}) collective-permute-start(bf16[128,512]{1,0:T(8,128)(2,1)S(1)} %get-tuple-element.29), channel_id=1, source_target_pairs={{0,7},{1,6},{2,5},{3,4},{4,3},{5,2},{6,1},{7,0},{8,15},{9,14},{10,... | collective-permute-start | bytes 393224 | tf_op jit(solution)/shard_map/ppermute | solution.py:20
  32.5 19.9 %collective-permute-start.11 = (bf16[128,512]{1,0:T(8,128)(2,1)S(1)}, bf16[128,512]{1,0:T(8,128)(2,1)S(1)}, u32[]{:S(2)}, u32[]{:S(2)}) collective-permute-start(bf16[128,512]{1,0:T(8,128)(2,1)S(1)} %get-tuple-element.30), channel_id=1, source_target_pairs={{0,5},{1,4},{2,7},{3,6},{4,1},{5,0},{6,3},{7,2},{8,13},{9,12},{10,... | collective-permute-start | bytes 393224 | tf_op jit(solution)/shard_map/ppermute | solution.py:20
  37.4 33.7 %all-to-all-start.2 = ((bf16[8,528,128]{2,1,0:T(8,128)(2,1)}), bf16[8,528,128]{2,1,0:T(8,128)(2,1)S(1)}, u32[]{:S(2)}, u32[]{:S(2)}) async-start(bf16[8,528,128]{2,1,0:T(8,128)(2,1)} %get-tuple-element.31.refs_8_), calls=%async_computation.2 | async-start | bytes 2162688 | tf_op jit(solution)/shard_map/all_to_all | solution.py:229
  53.0 9.8 %collective-permute-start.12 = (bf16[2,1,128,512]{3,2,0,1:T(8,128)(2,1)S(1)}, bf16[2,1,128,512]{3,2,0,1:T(8,128)(2,1)S(1)}, u32[]{:S(2)}, u32[]{:S(2)}) collective-permute-start(bf16[2,1,128,512]{3,2,0,1:T(8,128)(2,1)S(1)} %bitcast.26), channel_id=1, source_target_pairs={{0,16},{8,24},{16,0},{24,8},{1,17},{9,25},{17,1},{25,9},{2,18},{10... | collective-permute-start | bytes 786440 | tf_op jit(solution)/shard_map/ppermute | solution.py:20
  55.6 10.1 %collective-permute-start.2 = (bf16[2,128,512]{2,1,0:T(8,128)(2,1)S(1)}, bf16[2,128,512]{2,1,0:T(8,128)(2,1)S(1)}, u32[]{:S(2)}, u32[]{:S(2)}) collective-permute-start(bf16[2,128,512]{2,1,0:T(8,128)(2,1)S(1)} %get-tuple-element.36.own_rows), channel_id=1, source_target_pairs={{0,16},{8,24},{16,0},{24,8},{1,17},{9,25},{17,1},{25,9},{2,18},{10... | collective-permute-start | bytes 786440 | tf_op jit(solution)/shard_map/ppermute | solution.py:20
  62.9 5.9 %collective-permute-start.13 = (bf16[2,2,128,512]{3,2,0,1:T(8,128)(2,1)S(1)}, bf16[2,2,128,512]{3,2,0,1:T(8,128)(2,1)S(1)}, u32[]{:S(2)}, u32[]{:S(2)}) collective-permute-start(bf16[2,2,128,512]{3,2,0,1:T(8,128)(2,1)S(1)} %maximum_bitcast_fusion), channel_id=1, source_target_pairs={{0,8},{8,0},{16,24},{24,16},{1,9},{9,1},{17,25},{25,17},{2,10},{10... | collective-permute-start | bytes 1572872 | tf_op jit(solution)/shard_map/ppermute | solution.py:20
  63.0 3.5 %collective-permute-start.3 = (bf16[2,128,512]{2,1,0:T(8,128)(2,1)S(1)}, bf16[2,128,512]{2,1,0:T(8,128)(2,1)}, u32[]{:S(2)}, u32[]{:S(2)}) collective-permute-start(bf16[2,128,512]{2,1,0:T(8,128)(2,1)S(1)} %get-tuple-element.36.own_rows), channel_id=1, source_target_pairs={{0,8},{8,0},{16,24},{24,16},{1,9},{9,1},{17,25},{25,17},{2,10},{10... | collective-permute-start | bytes 786440 | tf_op jit(solution)/shard_map/ppermute | solution.py:20
  65.8 2.4 %collective-permute-start.4 = (bf16[2,128,512]{2,1,0:T(8,128)(2,1)S(1)}, bf16[2,128,512]{2,1,0:T(8,128)(2,1)S(1)}, u32[]{:S(2)}, u32[]{:S(2)}) collective-permute-start(bf16[2,128,512]{2,1,0:T(8,128)(2,1)S(1)} %collective-permute-done.2), channel_id=1, source_target_pairs={{0,8},{8,0},{16,24},{24,16},{1,9},{9,1},{17,25},{25,17},{2,10},{10... | collective-permute-start | bytes 786440 | tf_op jit(solution)/shard_map/ppermute | solution.py:20
  72.0 3.2 %collective-permute-start.16 = (f32[8,128]{1,0:T(8,128)S(1)}, f32[8,128]{1,0:T(8,128)S(1)}, u32[]{:S(2)}, u32[]{:S(2)}) collective-permute-start(f32[8,128]{1,0:T(8,128)S(1)} %get-tuple-element.34.refs_0_), channel_id=1, source_target_pairs={{0,24},{8,16},{16,8},{24,0},{1,25},{9,17},{17,9},{25,1},{2,26},{10... | collective-permute-start | bytes 12296 | tf_op jit(solution)/shard_map/ppermute | solution.py:20
  74.0 3.6 %collective-permute-start.15 = (f32[8,128]{1,0:T(8,128)S(1)}, f32[8,128]{1,0:T(8,128)S(1)}, u32[]{:S(2)}, u32[]{:S(2)}) collective-permute-start(f32[8,128]{1,0:T(8,128)S(1)} %get-tuple-element.34.refs_0_), channel_id=1, source_target_pairs={{0,16},{8,24},{16,0},{24,8},{1,17},{9,25},{17,1},{25,9},{2,18},{10... | collective-permute-start | bytes 12296 | tf_op jit(solution)/shard_map/ppermute | solution.py:20
  74.2 3.3 %collective-permute-start.14 = (f32[8,128]{1,0:T(8,128)S(1)}, f32[8,128]{1,0:T(8,128)S(1)}, u32[]{:S(2)}, u32[]{:S(2)}) collective-permute-start(f32[8,128]{1,0:T(8,128)S(1)} %get-tuple-element.34.refs_0_), channel_id=1, source_target_pairs={{0,8},{8,0},{16,24},{24,16},{1,9},{9,1},{17,25},{25,17},{2,10},{10... | collective-permute-start | bytes 12296 | tf_op jit(solution)/shard_map/ppermute | solution.py:20

commit v12 on v10

--- a/solution.py
+++ b/solution.py
@@ -207,7 +207,7 @@
     left_slots = over_dp(left_roots)
     far = mp_count // 2
     middle = far + far // 2
-    distant = [d for pair in zip(range(middle, mp_count), range(far, middle)) for d in pair]
+    distant = [d for pair in zip(range(far, middle), range(middle, mp_count)) for d in pair]
     order = [1, distant[0], *range(2, far), *distant[1:]]
     right_arrived = [outgoing[0]] + [swap(outgoing[d], "mp", d) for d in order]
     total = chip_sum(total, dp_count, dp_index)

time: 75.6 us -> 76.6 us (1.013); the launches traced: 75.3 us -> 75.4 us
  waiting for transfers between devices: 34.4 us -> 35.8 us
  starting transfers between devices: 31.1 us -> 29.8 us
    all_to_all x1, waiting for transfers between devices: 1.97 us -> 9.27 us  [shards(): lax.all_to_all(left_outgoing, 'mp', split_axis=0, concat_axis=0, tiled=True)]
    ppermute x17, waiting for transfers between devices: 25 us -> 19.2 us  [swap(): return lax.ppermute(value, axis, [(i, i ^ distance) for i in range(count)])]
    ppermute x17, starting transfers between devices: 19.9 us -> 18.6 us  [swap(): return lax.ppermute(value, axis, [(i, i ^ distance) for i in range(count)])]
where the time goes in v12:
time: 76.6 us; the launch traced here: 75.4 us
  waiting for transfers between devices  35.8 us (47%)
  starting transfers between devices  29.8 us (39%)
  Pallas kernels  6.34 us (8%)
  other arithmetic  2.19 us (3%)
    ppermute x17, waiting for transfers between devices, swap(): return lax.ppermute(value, axis, [(i, i ^ distance) for i in range(count)])  19.2 us
    ppermute x17, starting transfers between devices, swap(): return lax.ppermute(value, axis, [(i, i ^ distance) for i in range(count)])  18.6 us
    all_to_all x1, waiting for transfers between devices, shards(): lax.all_to_all(left_outgoing, 'mp', split_axis=0, concat_axis=0, tiled=True)  9.27 us
    all_to_all x2, starting transfers between devices, over_dp(): lax.all_to_all(factor[0, 0].reshape(dp_count, rows, width), 'dp', split_a...  7.42 us
    all_to_all x2, waiting for transfers between devices, over_dp(): lax.all_to_all(factor[0, 0].reshape(dp_count, rows, width), 'dp', split_a...  7.4 us
    all_to_all x1, starting transfers between devices, shards(): lax.all_to_all(left_outgoing, 'mp', split_axis=0, concat_axis=0, tiled=True)  3.76 us
    reduce_sum x1, other arithmetic, shards(): jnp.sum(total_f * total_f, axis=(1, 2)).reshape(per_shard, 1)  1.78 us
    pallas_call x1, Pallas kernels, shards(): pl.pallas_call(functools.partial(left_kernel, mp_count), out_shape=jax.Sh...  1.72 us
  transfers between devices with their start and end apart: 20, of which 9 were waited for; matrix products, arithmetic and copies ran while one was open for 4% of the time, Pallas kernels for 6%

profile of v12, /device:TPU:0, one launch (start us, length us, event | category | flops | bytes accessed | tf_op | source)
XLA Modules:
  0.0 75.4 jit_solution(8099551915494161761)
XLA Ops:
  0.0 0.5 collective-permute-start
  0.5 3.9 %all-to-all-start = ((bf16[4,128,512]{2,1,0:T(8,128)(2,1)}), bf16[4,128,512]{2,1,0:T(8,128)(2,1)S(1)}, u32[]{:S(2)}, u32[]{:S(2)}) async-start(bf16[4,128,512]{2,1,0:T(8,128)(2,1)} %bitcast.28), calls=%async_computation | async-start | bytes 1048576 | tf_op jit(solution)/shard_map/all_to_all | solution.py:186
  4.5 1.6 %shard_map.55.plan = s32[10]{0:T(128)S(1)} custom-call(s32[16]{0:T(128)S(1)} %copy-done, s32[9]{0:T(128)S(1)} %copy-done.1), custom_call_target="tpu_custom_call" | custom-call | tf_op jit(solution)/shard_map/pallas_call | solution.py:190
  6.1 0.1 fusion
  6.3 7.4 %all-to-all-done.slots = bf16[4,128,512]{2,1,0:T(8,128)(2,1)S(1)} async-done(((bf16[4,128,512]{2,1,0:T(8,128)(2,1)}), bf16[4,128,512]{2,1,0:T(8,128)(2,1)S(1)}, u32[]{:S(2)}, u32[]{:S(2)}) %all-to-all-start) | async-done | bytes 524320 | tf_op jit(solution)/shard_map/all_to_all | solution.py:186
  13.7 0.1 collective-permute-start.1
  13.8 3.5 %all-to-all-start.1 = ((bf16[4,128,512]{2,1,0:T(8,128)(2,1)}), bf16[4,128,512]{2,1,0:T(8,128)(2,1)S(1)}, u32[]{:S(2)}, u32[]{:S(2)}) async-start(bf16[4,128,512]{2,1,0:T(8,128)(2,1)} %bitcast.3), calls=%async_computation.1 | async-start | bytes 1048576 | tf_op jit(solution)/shard_map/all_to_all | solution.py:186
  17.3 0.6 shard_map.56
  17.9 2.2 %collective-permute-start.5 = (bf16[128,512]{1,0:T(8,128)(2,1)S(1)}, bf16[128,512]{1,0:T(8,128)(2,1)S(1)}, u32[]{:S(2)}, u32[]{:S(2)}) collective-permute-start(bf16[128,512]{1,0:T(8,128)(2,1)S(1)} %get-tuple-element.22), channel_id=1, source_target_pairs={{0,1},{1,0},{2,3},{3,2},{4,5},{5,4},{6,7},{7,6},{8,9},{9,8},{10,11... | collective-permute-start | bytes 393224 | tf_op jit(solution)/shard_map/ppermute | solution.py:20
  20.1 2.6 %collective-permute-start.6 = (bf16[128,512]{1,0:T(8,128)(2,1)S(1)}, bf16[128,512]{1,0:T(8,128)(2,1)S(1)}, u32[]{:S(2)}, u32[]{:S(2)}) collective-permute-start(bf16[128,512]{1,0:T(8,128)(2,1)S(1)} %get-tuple-element.23), channel_id=1, source_target_pairs={{0,4},{1,5},{2,6},{3,7},{4,0},{5,1},{6,2},{7,3},{8,12},{9,13},{10,... | collective-permute-start | bytes 393224 | tf_op jit(solution)/shard_map/ppermute | solution.py:20
  22.7 1.6 %collective-permute-start.7 = (bf16[128,512]{1,0:T(8,128)(2,1)S(1)}, bf16[128,512]{1,0:T(8,128)(2,1)S(1)}, u32[]{:S(2)}, u32[]{:S(2)}) collective-permute-start(bf16[128,512]{1,0:T(8,128)(2,1)S(1)} %get-tuple-element.24), channel_id=1, source_target_pairs={{0,2},{1,3},{2,0},{3,1},{4,6},{5,7},{6,4},{7,5},{8,10},{9,11},{10,... | collective-permute-start | bytes 393224 | tf_op jit(solution)/shard_map/ppermute | solution.py:20
  24.2 0.4 collective-permute-start.8
  24.7 3.4 %collective-permute-start.9 = (bf16[128,512]{1,0:T(8,128)(2,1)S(1)}, bf16[128,512]{1,0:T(8,128)(2,1)S(1)}, u32[]{:S(2)}, u32[]{:S(2)}) collective-permute-start(bf16[128,512]{1,0:T(8,128)(2,1)S(1)} %get-tuple-element.26), channel_id=1, source_target_pairs={{0,6},{1,7},{2,4},{3,5},{4,2},{5,3},{6,0},{7,1},{8,14},{9,15},{10,... | collective-permute-start | bytes 393224 | tf_op jit(solution)/shard_map/ppermute | solution.py:20
  28.1 2.1 %collective-permute-done.6.refs_2_ = bf16[128,512]{1,0:T(8,128)(2,1)S(1)} collective-permute-done((bf16[128,512]{1,0:T(8,128)(2,1)S(1)}, bf16[128,512]{1,0:T(8,128)(2,1)S(1)}, u32[]{:S(2)}, u32[]{:S(2)}) %collective-permute-start.6) | collective-permute-done | bytes 131104 | tf_op jit(solution)/shard_map/ppermute | solution.py:20
  30.1 0.0 collective-permute-start.10
  30.1 0.0 collective-permute-done.1
  30.1 3.3 %collective-permute-start.11 = (bf16[128,512]{1,0:T(8,128)(2,1)S(1)}, bf16[128,512]{1,0:T(8,128)(2,1)S(1)}, u32[]{:S(2)}, u32[]{:S(2)}) collective-permute-start(bf16[128,512]{1,0:T(8,128)(2,1)S(1)} %get-tuple-element.28), channel_id=1, source_target_pairs={{0,7},{1,6},{2,5},{3,4},{4,3},{5,2},{6,1},{7,0},{8,15},{9,14},{10,... | collective-permute-start | bytes 393224 | tf_op jit(solution)/shard_map/ppermute | solution.py:20
  33.4 1.8 %multiply_reduce_fusion = (f32[2]{0:T(128)S(1)}, bf16[2,128,512]{2,1,0:T(8,128)(2,1)}) fusion(bf16[2,128,512]{2,1,0:T(8,128)(2,1)} %collective-permute-done.1, bf16[2,256,512]{2,1,0:T(8,128)(2,1)S(1)} %fusion, s32[]{:T(128)S(6)} %select_n.113), kind=kLoop, calls=%fused_computation.7 | loop fusion | flops 917502 | bytes 786444 | tf_op jit(solution)/shard_map/reduce_sum | solution.py:216
  35.2 0.0 all-to-all-done.1.slots
  35.2 0.1 broadcast_in_dim.12.half_sq
  35.3 1.7 %shard_map.57.refs_8_ = bf16[8,528,128]{2,1,0:T(8,128)(2,1)} custom-call(s32[10]{0:T(128)S(1)} %shard_map.55.plan, bf16[4,128,512]{2,1,0:T(8,128)(2,1)S(1)} %all-to-all-done.1.slots, f32[2,128]{1,0:T(2,128)S(1)} %broadcast_in_dim.12.half_sq), custom_call_target="tpu_custom_call" | custom-call | tf_op jit(solution)/shard_map/pallas_call | solution.py:219
  37.0 3.8 %all-to-all-start.2 = ((bf16[8,528,128]{2,1,0:T(8,128)(2,1)}), bf16[8,528,128]{2,1,0:T(8,128)(2,1)S(1)}, u32[]{:S(2)}, u32[]{:S(2)}) async-start(bf16[8,528,128]{2,1,0:T(8,128)(2,1)} %shard_map.57.refs_8_), calls=%async_computation.2 | async-start | bytes 2162688 | tf_op jit(solution)/shard_map/all_to_all | solution.py:226
  40.8 0.0 collective-permute-done.8.refs_4_
  40.8 3.8 %collective-permute-done.10.refs_6_ = bf16[128,512]{1,0:T(8,128)(2,1)S(1)} collective-permute-done((bf16[128,512]{1,0:T(8,128)(2,1)S(1)}, bf16[128,512]{1,0:T(8,128)(2,1)S(1)}, u32[]{:S(2)}, u32[]{:S(2)}) %collective-permute-start.10) | collective-permute-done | bytes 131104 | tf_op jit(solution)/shard_map/ppermute | solution.py:20
  44.6 0.6 shard_map.58
  45.3 1.6 %collective-permute-start.12 = (bf16[2,1,128,512]{3,2,0,1:T(8,128)(2,1)S(1)}, bf16[2,1,128,512]{3,2,0,1:T(8,128)(2,1)S(1)}, u32[]{:S(2)}, u32[]{:S(2)}) collective-permute-start(bf16[2,1,128,512]{3,2,0,1:T(8,128)(2,1)S(1)} %bitcast.26), channel_id=1, source_target_pairs={{0,16},{8,24},{16,0},{24,8},{1,17},{9,25},{17,1},{25,9},{2,18},{10... | collective-permute-start | bytes 786440 | tf_op jit(solution)/shard_map/ppermute | solution.py:20
  46.9 0.4 collective-permute-start.2
  47.4 7.2 %collective-permute-done.12 = bf16[2,1,128,512]{3,2,0,1:T(8,128)(2,1)S(1)} collective-permute-done((bf16[2,1,128,512]{3,2,0,1:T(8,128)(2,1)S(1)}, bf16[2,1,128,512]{3,2,0,1:T(8,128)(2,1)S(1)}, u32[]{:S(2)}, u32[]{:S(2)}) %collective-permute-start.12) | collective-permute-done | bytes 262176 | tf_op jit(solution)/shard_map/ppermute | solution.py:20
  54.6 0.1 maximum_bitcast_fusion
  54.7 0.1 collective-permute-start.13
  54.8 0.5 collective-permute-start.3
  55.2 2.9 %collective-permute-done.2 = bf16[2,128,512]{2,1,0:T(8,128)(2,1)S(1)} collective-permute-done((bf16[2,128,512]{2,1,0:T(8,128)(2,1)S(1)}, bf16[2,128,512]{2,1,0:T(8,128)(2,1)S(1)}, u32[]{:S(2)}, u32[]{:S(2)}) %collective-permute-start.2) | collective-permute-done | bytes 262176 | tf_op jit(solution)/shard_map/ppermute | solution.py:20
  58.1 0.0 collective-permute-start.4
  58.1 0.1 broadcast_in_dim.11
  58.3 0.0 collective-permute-done.3
  58.3 1.3 %collective-permute-done.4 = bf16[2,128,512]{2,1,0:T(8,128)(2,1)S(1)} collective-permute-done((bf16[2,128,512]{2,1,0:T(8,128)(2,1)S(1)}, bf16[2,128,512]{2,1,0:T(8,128)(2,1)S(1)}, u32[]{:S(2)}, u32[]{:S(2)}) %collective-permute-start.4) | collective-permute-done | bytes 262176 | tf_op jit(solution)/shard_map/ppermute | solution.py:20
  59.7 0.1 select_bitcast_fusion.1
  59.8 0.1 pad_maximum_fusion
  59.9 0.1 copy.6
  60.0 0.7 convolution_convert_fusion.right_prod
  60.7 9.3 %all-to-all-done.2.arrived = bf16[8,528,128]{2,1,0:T(8,128)(2,1)S(1)} async-done(((bf16[8,528,128]{2,1,0:T(8,128)(2,1)}), bf16[8,528,128]{2,1,0:T(8,128)(2,1)S(1)}, u32[]{:S(2)}, u32[]{:S(2)}) %all-to-all-start.2) | async-done | bytes 1081376 | tf_op jit(solution)/shard_map/all_to_all | solution.py:226
  69.9 0.9 %shard_map.59 = (f32[2,128,512]{2,1,0:T(8,128)S(1)}, f32[8,128]{1,0:T(8,128)S(1)}) custom-call(s32[10]{0:T(128)S(1)} %shard_map.55.plan, bf16[2,512,512]{2,1,0:T(8,128)(2,1)S(1)} %convolution_convert_fusion.right_prod, f32[2,128]{1,0:T(2,128)S(1)} %broadcast_in_dim.12.half_sq, bf16[8,528,128]{2,1,0:T(8,128)(2,1)S(1)} %all-to-all-done.2.arrived), custom_call_target="tpu_custom_call" | custom-call | tf_op jit(solution)/shard_map/pallas_call | solution.py:240
  70.9 0.1 collective-permute-start.16
  71.0 1.5 %collective-permute-start.15 = (f32[8,128]{1,0:T(8,128)S(1)}, f32[8,128]{1,0:T(8,128)S(1)}, u32[]{:S(2)}, u32[]{:S(2)}) collective-permute-start(f32[8,128]{1,0:T(8,128)S(1)} %get-tuple-element.30.refs_0_), channel_id=1, source_target_pairs={{0,16},{8,24},{16,0},{24,8},{1,17},{9,25},{17,1},{25,9},{2,18},{10... | collective-permute-start | bytes 12296 | tf_op jit(solution)/shard_map/ppermute | solution.py:20
  72.4 0.4 collective-permute-start.14
  72.8 1.2 %collective-permute-done.16.refs_3_ = f32[8,128]{1,0:T(8,128)S(1)} collective-permute-done((f32[8,128]{1,0:T(8,128)S(1)}, f32[8,128]{1,0:T(8,128)S(1)}, u32[]{:S(2)}, u32[]{:S(2)}) %collective-permute-start.16) | collective-permute-done | bytes 4128 | tf_op jit(solution)/shard_map/ppermute | solution.py:20
  74.0 0.6 collective-permute-done.15.refs_2_
  74.6 0.8 %shard_map.60 = bf16[2,128,512]{2,1,0:T(8,128)(2,1)} custom-call(f32[2,128,512]{2,1,0:T(8,128)S(1)} %get-tuple-element.29.precond, f32[8,128]{1,0:T(8,128)S(1)} %get-tuple-element.30.refs_0_, f32[8,128]{1,0:T(8,128)S(1)} %collective-permute-done.14.refs_1_, f32[8,128]{1,0:T(8,128)S(1)} %collective-permute-done.15.refs_2_, ...), custom_call_target="tpu_custom_call" | custom-call | tf_op jit(solution)/shard_map/pallas_call | solution.py:252
  (21 shorter events, 0.2 us)
Async XLA Ops:
  0.0 6.1 %copy-start.3 = (bf16[1,2,512,512]{3,2,1,0:T(8,128)(2,1)S(1)}, bf16[1,2,512,512]{3,2,1,0:T(8,128)(2,1)}, u32[]{:S(2)}) copy-start(bf16[1,2,512,512]{3,2,1,0:T(8,128)(2,1)} %param.5) | copy-start | bytes 3145732
  0.0 4.5 %copy-start.1 = (s32[9]{0:T(128)S(1)}, s32[9]{0:T(128)}, u32[]{:S(2)}) copy-start(s32[9]{0:T(128)} %offsets.1) | copy-start | bytes 112
  0.0 4.5 %copy-start = (s32[16]{0:T(128)S(1)}, s32[16]{0:T(128)}, u32[]{:S(2)}) copy-start(s32[16]{0:T(128)} %lists.1) | copy-start | bytes 196
  0.0 6.1 %collective-permute-start = (bf16[2,512,512]{2,1,0:T(8,128)(2,1)}, bf16[2,512,512]{2,1,0:T(8,128)(2,1)S(1)}, u32[]{:S(2)}, u32[]{:S(2)}) collective-permute-start(bf16[2,512,512]{2,1,0:T(8,128)(2,1)} %bitcast.29), channel_id=1, source_target_pairs={{0,8},{8,0},{16,24},{24,16},{1,9},{9,1},{17,25},{25,17},{2,10},{10... | collective-permute-start | bytes 3145736 | tf_op jit(solution)/shard_map/ppermute | solution.py:20
  0.5 13.1 %all-to-all-start = ((bf16[4,128,512]{2,1,0:T(8,128)(2,1)}), bf16[4,128,512]{2,1,0:T(8,128)(2,1)S(1)}, u32[]{:S(2)}, u32[]{:S(2)}) async-start(bf16[4,128,512]{2,1,0:T(8,128)(2,1)} %bitcast.28), calls=%async_computation | async-start | bytes 1048576 | tf_op jit(solution)/shard_map/all_to_all | solution.py:186
  13.7 16.4 %collective-permute-start.1 = (bf16[2,128,512]{2,1,0:T(8,128)(2,1)S(1)}, bf16[2,128,512]{2,1,0:T(8,128)(2,1)}, u32[]{:S(2)}, u32[]{:S(2)}) collective-permute-start(bf16[2,128,512]{2,1,0:T(8,128)(2,1)S(1)} %constant_dynamic-slice_fusion), channel_id=1, source_target_pairs={{0,16},{8,24},{16,0},{24,8},{1,17},{9,25},{17,1},{25,9},{2,18},{10... | collective-permute-start | bytes 786440 | tf_op jit(solution)/shard_map/ppermute | solution.py:20
  13.8 21.4 %all-to-all-start.1 = ((bf16[4,128,512]{2,1,0:T(8,128)(2,1)}), bf16[4,128,512]{2,1,0:T(8,128)(2,1)S(1)}, u32[]{:S(2)}, u32[]{:S(2)}) async-start(bf16[4,128,512]{2,1,0:T(8,128)(2,1)} %bitcast.3), calls=%async_computation.1 | async-start | bytes 1048576 | tf_op jit(solution)/shard_map/all_to_all | solution.py:186
  17.9 6.8 %collective-permute-start.5 = (bf16[128,512]{1,0:T(8,128)(2,1)S(1)}, bf16[128,512]{1,0:T(8,128)(2,1)S(1)}, u32[]{:S(2)}, u32[]{:S(2)}) collective-permute-start(bf16[128,512]{1,0:T(8,128)(2,1)S(1)} %get-tuple-element.22), channel_id=1, source_target_pairs={{0,1},{1,0},{2,3},{3,2},{4,5},{5,4},{6,7},{7,6},{8,9},{9,8},{10,11... | collective-permute-start | bytes 393224 | tf_op jit(solution)/shard_map/ppermute | solution.py:20
  20.1 10.0 %collective-permute-start.6 = (bf16[128,512]{1,0:T(8,128)(2,1)S(1)}, bf16[128,512]{1,0:T(8,128)(2,1)S(1)}, u32[]{:S(2)}, u32[]{:S(2)}) collective-permute-start(bf16[128,512]{1,0:T(8,128)(2,1)S(1)} %get-tuple-element.23), channel_id=1, source_target_pairs={{0,4},{1,5},{2,6},{3,7},{4,0},{5,1},{6,2},{7,3},{8,12},{9,13},{10,... | collective-permute-start | bytes 393224 | tf_op jit(solution)/shard_map/ppermute | solution.py:20
  22.7 18.1 %collective-permute-start.7 = (bf16[128,512]{1,0:T(8,128)(2,1)S(1)}, bf16[128,512]{1,0:T(8,128)(2,1)S(1)}, u32[]{:S(2)}, u32[]{:S(2)}) collective-permute-start(bf16[128,512]{1,0:T(8,128)(2,1)S(1)} %get-tuple-element.24), channel_id=1, source_target_pairs={{0,2},{1,3},{2,0},{3,1},{4,6},{5,7},{6,4},{7,5},{8,10},{9,11},{10,... | collective-permute-start | bytes 393224 | tf_op jit(solution)/shard_map/ppermute | solution.py:20
  24.2 16.5 %collective-permute-start.8 = (bf16[128,512]{1,0:T(8,128)(2,1)S(1)}, bf16[128,512]{1,0:T(8,128)(2,1)S(1)}, u32[]{:S(2)}, u32[]{:S(2)}) collective-permute-start(bf16[128,512]{1,0:T(8,128)(2,1)S(1)} %get-tuple-element.25), channel_id=1, source_target_pairs={{0,3},{1,2},{2,1},{3,0},{4,7},{5,6},{6,5},{7,4},{8,11},{9,10},{10,... | collective-permute-start | bytes 393224 | tf_op jit(solution)/shard_map/ppermute | solution.py:20
  24.7 16.1 %collective-permute-start.9 = (bf16[128,512]{1,0:T(8,128)(2,1)S(1)}, bf16[128,512]{1,0:T(8,128)(2,1)S(1)}, u32[]{:S(2)}, u32[]{:S(2)}) collective-permute-start(bf16[128,512]{1,0:T(8,128)(2,1)S(1)} %get-tuple-element.26), channel_id=1, source_target_pairs={{0,6},{1,7},{2,4},{3,5},{4,2},{5,3},{6,0},{7,1},{8,14},{9,15},{10,... | collective-permute-start | bytes 393224 | tf_op jit(solution)/shard_map/ppermute | solution.py:20
  30.1 14.5 %collective-permute-start.10 = (bf16[128,512]{1,0:T(8,128)(2,1)S(1)}, bf16[128,512]{1,0:T(8,128)(2,1)S(1)}, u32[]{:S(2)}, u32[]{:S(2)}) collective-permute-start(bf16[128,512]{1,0:T(8,128)(2,1)S(1)} %get-tuple-element.27), channel_id=1, source_target_pairs={{0,5},{1,4},{2,7},{3,6},{4,1},{5,0},{6,3},{7,2},{8,13},{9,12},{10,... | collective-permute-start | bytes 393224 | tf_op jit(solution)/shard_map/ppermute | solution.py:20
  30.1 14.5 %collective-permute-start.11 = (bf16[128,512]{1,0:T(8,128)(2,1)S(1)}, bf16[128,512]{1,0:T(8,128)(2,1)S(1)}, u32[]{:S(2)}, u32[]{:S(2)}) collective-permute-start(bf16[128,512]{1,0:T(8,128)(2,1)S(1)} %get-tuple-element.28), channel_id=1, source_target_pairs={{0,7},{1,6},{2,5},{3,4},{4,3},{5,2},{6,1},{7,0},{8,15},{9,14},{10,... | collective-permute-start | bytes 393224 | tf_op jit(solution)/shard_map/ppermute | solution.py:20
  37.0 32.9 %all-to-all-start.2 = ((bf16[8,528,128]{2,1,0:T(8,128)(2,1)}), bf16[8,528,128]{2,1,0:T(8,128)(2,1)S(1)}, u32[]{:S(2)}, u32[]{:S(2)}) async-start(bf16[8,528,128]{2,1,0:T(8,128)(2,1)} %shard_map.57.refs_8_), calls=%async_computation.2 | async-start | bytes 2162688 | tf_op jit(solution)/shard_map/all_to_all | solution.py:226
  44.6 2.3 %copy-start.2 = (bf16[2,128,512]{2,1,0:T(8,128)(2,1)S(1)}, bf16[2,128,512]{2,1,0:T(8,128)(2,1)}, u32[]{:S(2)}) copy-start(bf16[2,128,512]{2,1,0:T(8,128)(2,1)} %get-tuple-element.32) | copy-start | bytes 786436
  45.3 9.3 %collective-permute-start.12 = (bf16[2,1,128,512]{3,2,0,1:T(8,128)(2,1)S(1)}, bf16[2,1,128,512]{3,2,0,1:T(8,128)(2,1)S(1)}, u32[]{:S(2)}, u32[]{:S(2)}) collective-permute-start(bf16[2,1,128,512]{3,2,0,1:T(8,128)(2,1)S(1)} %bitcast.26), channel_id=1, source_target_pairs={{0,16},{8,24},{16,0},{24,8},{1,17},{9,25},{17,1},{25,9},{2,18},{10... | collective-permute-start | bytes 786440 | tf_op jit(solution)/shard_map/ppermute | solution.py:20
  46.9 11.2 %collective-permute-start.2 = (bf16[2,128,512]{2,1,0:T(8,128)(2,1)S(1)}, bf16[2,128,512]{2,1,0:T(8,128)(2,1)S(1)}, u32[]{:S(2)}, u32[]{:S(2)}) collective-permute-start(bf16[2,128,512]{2,1,0:T(8,128)(2,1)S(1)} %copy-done.2), channel_id=1, source_target_pairs={{0,16},{8,24},{16,0},{24,8},{1,17},{9,25},{17,1},{25,9},{2,18},{10... | collective-permute-start | bytes 786440 | tf_op jit(solution)/shard_map/ppermute | solution.py:20
  54.7 5.0 %collective-permute-start.13 = (bf16[2,2,128,512]{3,2,0,1:T(8,128)(2,1)S(1)}, bf16[2,2,128,512]{3,2,0,1:T(8,128)(2,1)S(1)}, u32[]{:S(2)}, u32[]{:S(2)}) collective-permute-start(bf16[2,2,128,512]{3,2,0,1:T(8,128)(2,1)S(1)} %maximum_bitcast_fusion), channel_id=1, source_target_pairs={{0,8},{8,0},{16,24},{24,16},{1,9},{9,1},{17,25},{25,17},{2,10},{10... | collective-permute-start | bytes 1572872 | tf_op jit(solution)/shard_map/ppermute | solution.py:20
  54.8 3.5 %collective-permute-start.3 = (bf16[2,128,512]{2,1,0:T(8,128)(2,1)S(1)}, bf16[2,128,512]{2,1,0:T(8,128)(2,1)S(1)}, u32[]{:S(2)}, u32[]{:S(2)}) collective-permute-start(bf16[2,128,512]{2,1,0:T(8,128)(2,1)S(1)} %copy-done.2), channel_id=1, source_target_pairs={{0,8},{8,0},{16,24},{24,16},{1,9},{9,1},{17,25},{25,17},{2,10},{10... | collective-permute-start | bytes 786440 | tf_op jit(solution)/shard_map/ppermute | solution.py:20
  58.1 1.5 %collective-permute-start.4 = (bf16[2,128,512]{2,1,0:T(8,128)(2,1)S(1)}, bf16[2,128,512]{2,1,0:T(8,128)(2,1)S(1)}, u32[]{:S(2)}, u32[]{:S(2)}) collective-permute-start(bf16[2,128,512]{2,1,0:T(8,128)(2,1)S(1)} %collective-permute-done.2), channel_id=1, source_target_pairs={{0,8},{8,0},{16,24},{24,16},{1,9},{9,1},{17,25},{25,17},{2,10},{10... | collective-permute-start | bytes 786440 | tf_op jit(solution)/shard_map/ppermute | solution.py:20
  70.9 3.1 %collective-permute-start.16 = (f32[8,128]{1,0:T(8,128)S(1)}, f32[8,128]{1,0:T(8,128)S(1)}, u32[]{:S(2)}, u32[]{:S(2)}) collective-permute-start(f32[8,128]{1,0:T(8,128)S(1)} %get-tuple-element.30.refs_0_), channel_id=1, source_target_pairs={{0,24},{8,16},{16,8},{24,0},{1,25},{9,17},{17,9},{25,1},{2,26},{10... | collective-permute-start | bytes 12296 | tf_op jit(solution)/shard_map/ppermute | solution.py:20
  71.0 3.7 %collective-permute-start.15 = (f32[8,128]{1,0:T(8,128)S(1)}, f32[8,128]{1,0:T(8,128)S(1)}, u32[]{:S(2)}, u32[]{:S(2)}) collective-permute-start(f32[8,128]{1,0:T(8,128)S(1)} %get-tuple-element.30.refs_0_), channel_id=1, source_target_pairs={{0,16},{8,24},{16,0},{24,8},{1,17},{9,25},{17,1},{25,9},{2,18},{10... | collective-permute-start | bytes 12296 | tf_op jit(solution)/shard_map/ppermute | solution.py:20
  72.4 2.2 %collective-permute-start.14 = (f32[8,128]{1,0:T(8,128)S(1)}, f32[8,128]{1,0:T(8,128)S(1)}, u32[]{:S(2)}, u32[]{:S(2)}) collective-permute-start(f32[8,128]{1,0:T(8,128)S(1)} %get-tuple-element.30.refs_0_), channel_id=1, source_target_pairs={{0,8},{8,0},{16,24},{24,16},{1,9},{9,1},{17,25},{25,17},{2,10},{10... | collective-permute-start | bytes 12296 | tf_op jit(solution)/shard_map/ppermute | solution.py:20

commit v13 on v10

--- a/solution.py
+++ b/solution.py
@@ -248,7 +248,7 @@
         scratch_shapes=[pltpu.VMEM((rows, width), jnp.bfloat16)],
         compiler_params=params,
     )(plan, right_prod, half_sq, left_arrived)
-    parts = [stats] + [swap(stats, "dp", d) for d in range(1, dp_count)]
+    parts = [stats] + [swap(stats, "dp", d) for d in reversed(range(1, dp_count))]
     return pl.pallas_call(
         functools.partial(finish_kernel, area, cells),
         out_shape=jax.ShapeDtypeStruct((per_shard, rows, width), jnp.bfloat16),

time: 75.6 us -> 76.4 us (1.011)
  waiting for transfers between devices: 34.4 us -> 35.2 us
    ppermute x17, waiting for transfers between devices: 25 us -> 25.8 us  [swap(): return lax.ppermute(value, axis, [(i, i ^ distance) for i in range(count)])]
where the time goes in v13:
time: 76.4 us; the launch traced here: 76.1 us
  waiting for transfers between devices  35.2 us (46%)
  starting transfers between devices  31.1 us (41%)
  Pallas kernels  6.34 us (8%)
  other arithmetic  2.19 us (3%)
    ppermute x17, waiting for transfers between devices, swap(): return lax.ppermute(value, axis, [(i, i ^ distance) for i in range(count)])  25.8 us
    ppermute x17, starting transfers between devices, swap(): return lax.ppermute(value, axis, [(i, i ^ distance) for i in range(count)])  19.9 us
    all_to_all x2, waiting for transfers between devices, over_dp(): lax.all_to_all(factor[0, 0].reshape(dp_count, rows, width), 'dp', split_a...  7.43 us
    all_to_all x2, starting transfers between devices, over_dp(): lax.all_to_all(factor[0, 0].reshape(dp_count, rows, width), 'dp', split_a...  7.42 us
    all_to_all x1, starting transfers between devices, shards(): lax.all_to_all(left_outgoing, 'mp', split_axis=0, concat_axis=0, tiled=True)  3.8 us
    all_to_all x1, waiting for transfers between devices, shards(): lax.all_to_all(left_outgoing, 'mp', split_axis=0, concat_axis=0, tiled=True)  1.97 us
    reduce_sum x1, other arithmetic, shards(): jnp.sum(total_f * total_f, axis=(1, 2)).reshape(per_shard, 1)  1.78 us
    pallas_call x1, Pallas kernels, shards(): pl.pallas_call(functools.partial(left_kernel, mp_count), out_shape=jax.Sh...  1.72 us
  transfers between devices with their start and end apart: 20, of which 9 were waited for; matrix products, arithmetic and copies ran while one was open for 4% of the time, Pallas kernels for 6%

profile of v13, /device:TPU:0, one launch (start us, length us, event | category | flops | bytes accessed | tf_op | source)
XLA Modules:
  0.0 76.1 jit_solution(14419347605989212366)
XLA Ops:
  0.0 0.5 collective-permute-start
  0.5 3.9 %all-to-all-start = ((bf16[4,128,512]{2,1,0:T(8,128)(2,1)}), bf16[4,128,512]{2,1,0:T(8,128)(2,1)S(1)}, u32[]{:S(2)}, u32[]{:S(2)}) async-start(bf16[4,128,512]{2,1,0:T(8,128)(2,1)} %bitcast.28), calls=%async_computation | async-start | bytes 1048576 | tf_op jit(solution)/shard_map/all_to_all | solution.py:186
  4.5 1.6 %shard_map.55.plan = s32[10]{0:T(128)S(1)} custom-call(s32[16]{0:T(128)S(1)} %copy-done, s32[9]{0:T(128)S(1)} %copy-done.1), custom_call_target="tpu_custom_call" | custom-call | tf_op jit(solution)/shard_map/pallas_call | solution.py:190
  6.1 0.1 fusion
  6.2 7.4 %all-to-all-done.slots = bf16[4,128,512]{2,1,0:T(8,128)(2,1)S(1)} async-done(((bf16[4,128,512]{2,1,0:T(8,128)(2,1)}), bf16[4,128,512]{2,1,0:T(8,128)(2,1)S(1)}, u32[]{:S(2)}, u32[]{:S(2)}) %all-to-all-start) | async-done | bytes 524320 | tf_op jit(solution)/shard_map/all_to_all | solution.py:186
  13.7 0.1 collective-permute-start.1
  13.8 3.5 %all-to-all-start.1 = ((bf16[4,128,512]{2,1,0:T(8,128)(2,1)}), bf16[4,128,512]{2,1,0:T(8,128)(2,1)S(1)}, u32[]{:S(2)}, u32[]{:S(2)}) async-start(bf16[4,128,512]{2,1,0:T(8,128)(2,1)} %bitcast.3), calls=%async_computation.1 | async-start | bytes 1048576 | tf_op jit(solution)/shard_map/all_to_all | solution.py:186
  17.3 0.6 shard_map.56
  17.9 2.2 %collective-permute-start.5 = (bf16[128,512]{1,0:T(8,128)(2,1)S(1)}, bf16[128,512]{1,0:T(8,128)(2,1)S(1)}, u32[]{:S(2)}, u32[]{:S(2)}) collective-permute-start(bf16[128,512]{1,0:T(8,128)(2,1)S(1)} %get-tuple-element.22), channel_id=1, source_target_pairs={{0,1},{1,0},{2,3},{3,2},{4,5},{5,4},{6,7},{7,6},{8,9},{9,8},{10,11... | collective-permute-start | bytes 393224 | tf_op jit(solution)/shard_map/ppermute | solution.py:20
  20.1 3.6 %collective-permute-start.6 = (bf16[128,512]{1,0:T(8,128)(2,1)S(1)}, bf16[128,512]{1,0:T(8,128)(2,1)S(1)}, u32[]{:S(2)}, u32[]{:S(2)}) collective-permute-start(bf16[128,512]{1,0:T(8,128)(2,1)S(1)} %get-tuple-element.23), channel_id=1, source_target_pairs={{0,6},{1,7},{2,4},{3,5},{4,2},{5,3},{6,0},{7,1},{8,14},{9,15},{10,... | collective-permute-start | bytes 393224 | tf_op jit(solution)/shard_map/ppermute | solution.py:20
  23.7 0.0 collective-permute-start.7
  23.7 2.0 %collective-permute-start.8 = (bf16[128,512]{1,0:T(8,128)(2,1)S(1)}, bf16[128,512]{1,0:T(8,128)(2,1)S(1)}, u32[]{:S(2)}, u32[]{:S(2)}) collective-permute-start(bf16[128,512]{1,0:T(8,128)(2,1)S(1)} %get-tuple-element.25), channel_id=1, source_target_pairs={{0,3},{1,2},{2,1},{3,0},{4,7},{5,6},{6,5},{7,4},{8,11},{9,10},{10,... | collective-permute-start | bytes 393224 | tf_op jit(solution)/shard_map/ppermute | solution.py:20
  25.7 1.4 %collective-permute-start.9 = (bf16[128,512]{1,0:T(8,128)(2,1)S(1)}, bf16[128,512]{1,0:T(8,128)(2,1)S(1)}, u32[]{:S(2)}, u32[]{:S(2)}) collective-permute-start(bf16[128,512]{1,0:T(8,128)(2,1)S(1)} %get-tuple-element.26), channel_id=1, source_target_pairs={{0,4},{1,5},{2,6},{3,7},{4,0},{5,1},{6,2},{7,3},{8,12},{9,13},{10,... | collective-permute-start | bytes 393224 | tf_op jit(solution)/shard_map/ppermute | solution.py:20
  27.0 1.2 %collective-permute-done.6.refs_2_ = bf16[128,512]{1,0:T(8,128)(2,1)S(1)} collective-permute-done((bf16[128,512]{1,0:T(8,128)(2,1)S(1)}, bf16[128,512]{1,0:T(8,128)(2,1)S(1)}, u32[]{:S(2)}, u32[]{:S(2)}) %collective-permute-start.6) | collective-permute-done | bytes 131104 | tf_op jit(solution)/shard_map/ppermute | solution.py:20
  28.3 3.6 %collective-permute-start.10 = (bf16[128,512]{1,0:T(8,128)(2,1)S(1)}, bf16[128,512]{1,0:T(8,128)(2,1)S(1)}, u32[]{:S(2)}, u32[]{:S(2)}) collective-permute-start(bf16[128,512]{1,0:T(8,128)(2,1)S(1)} %get-tuple-element.27), channel_id=1, source_target_pairs={{0,7},{1,6},{2,5},{3,4},{4,3},{5,2},{6,1},{7,0},{8,15},{9,14},{10,... | collective-permute-start | bytes 393224 | tf_op jit(solution)/shard_map/ppermute | solution.py:20
  31.8 0.0 collective-permute-done.1
  31.8 1.3 %collective-permute-start.11 = (bf16[128,512]{1,0:T(8,128)(2,1)S(1)}, bf16[128,512]{1,0:T(8,128)(2,1)S(1)}, u32[]{:S(2)}, u32[]{:S(2)}) collective-permute-start(bf16[128,512]{1,0:T(8,128)(2,1)S(1)} %get-tuple-element.28), channel_id=1, source_target_pairs={{0,5},{1,4},{2,7},{3,6},{4,1},{5,0},{6,3},{7,2},{8,13},{9,12},{10,... | collective-permute-start | bytes 393224 | tf_op jit(solution)/shard_map/ppermute | solution.py:20
  33.2 1.8 %multiply_reduce_fusion = (f32[2]{0:T(128)S(1)}, bf16[2,128,512]{2,1,0:T(8,128)(2,1)}) fusion(bf16[2,128,512]{2,1,0:T(8,128)(2,1)} %collective-permute-done.1, bf16[2,256,512]{2,1,0:T(8,128)(2,1)S(1)} %fusion, s32[]{:T(128)S(6)} %select_n.113), kind=kLoop, calls=%fused_computation.7 | loop fusion | flops 917502 | bytes 786444 | tf_op jit(solution)/shard_map/reduce_sum | solution.py:216
  35.0 0.1 broadcast_in_dim.12.half_sq
  35.0 1.7 %shard_map.57.refs_8_ = bf16[8,528,128]{2,1,0:T(8,128)(2,1)} custom-call(s32[10]{0:T(128)S(1)} %shard_map.55.plan, bf16[4,128,512]{2,1,0:T(8,128)(2,1)S(1)} %all-to-all-done.1.slots, f32[2,128]{1,0:T(2,128)S(1)} %broadcast_in_dim.12.half_sq), custom_call_target="tpu_custom_call" | custom-call | tf_op jit(solution)/shard_map/pallas_call | solution.py:219
  36.7 3.8 %all-to-all-start.2 = ((bf16[8,528,128]{2,1,0:T(8,128)(2,1)}), bf16[8,528,128]{2,1,0:T(8,128)(2,1)S(1)}, u32[]{:S(2)}, u32[]{:S(2)}) async-start(bf16[8,528,128]{2,1,0:T(8,128)(2,1)} %shard_map.57.refs_8_), calls=%async_computation.2 | async-start | bytes 2162688 | tf_op jit(solution)/shard_map/all_to_all | solution.py:226
  40.5 0.0 collective-permute-done.7.refs_3_
  40.6 0.0 collective-permute-done.9.refs_5_
  40.6 11.2 %collective-permute-done.11.refs_7_ = bf16[128,512]{1,0:T(8,128)(2,1)S(1)} collective-permute-done((bf16[128,512]{1,0:T(8,128)(2,1)S(1)}, bf16[128,512]{1,0:T(8,128)(2,1)S(1)}, u32[]{:S(2)}, u32[]{:S(2)}) %collective-permute-start.11) | collective-permute-done | bytes 131104 | tf_op jit(solution)/shard_map/ppermute | solution.py:20
  51.8 0.6 shard_map.58
  52.4 2.5 %collective-permute-start.12 = (bf16[2,1,128,512]{3,2,0,1:T(8,128)(2,1)S(1)}, bf16[2,1,128,512]{3,2,0,1:T(8,128)(2,1)S(1)}, u32[]{:S(2)}, u32[]{:S(2)}) collective-permute-start(bf16[2,1,128,512]{3,2,0,1:T(8,128)(2,1)S(1)} %bitcast.26), channel_id=1, source_target_pairs={{0,16},{8,24},{16,0},{24,8},{1,17},{9,25},{17,1},{25,9},{2,18},{10... | collective-permute-start | bytes 786440 | tf_op jit(solution)/shard_map/ppermute | solution.py:20
  54.9 0.2 collective-permute-start.2
  55.2 7.0 %collective-permute-done.12 = bf16[2,1,128,512]{3,2,0,1:T(8,128)(2,1)S(1)} collective-permute-done((bf16[2,1,128,512]{3,2,0,1:T(8,128)(2,1)S(1)}, bf16[2,1,128,512]{3,2,0,1:T(8,128)(2,1)S(1)}, u32[]{:S(2)}, u32[]{:S(2)}) %collective-permute-start.12) | collective-permute-done | bytes 262176 | tf_op jit(solution)/shard_map/ppermute | solution.py:20
  62.2 0.1 maximum_bitcast_fusion
  62.3 0.1 collective-permute-start.13
  62.3 0.5 collective-permute-start.3
  62.8 2.3 %collective-permute-done.2 = bf16[2,128,512]{2,1,0:T(8,128)(2,1)S(1)} collective-permute-done((bf16[2,128,512]{2,1,0:T(8,128)(2,1)S(1)}, bf16[2,128,512]{2,1,0:T(8,128)(2,1)S(1)}, u32[]{:S(2)}, u32[]{:S(2)}) %collective-permute-start.2) | collective-permute-done | bytes 262176 | tf_op jit(solution)/shard_map/ppermute | solution.py:20
  65.1 0.0 collective-permute-start.4
  65.1 0.1 broadcast_in_dim.11
  65.3 0.0 collective-permute-done.3
  65.3 1.3 %collective-permute-done.4 = bf16[2,128,512]{2,1,0:T(8,128)(2,1)S(1)} collective-permute-done((bf16[2,128,512]{2,1,0:T(8,128)(2,1)S(1)}, bf16[2,128,512]{2,1,0:T(8,128)(2,1)S(1)}, u32[]{:S(2)}, u32[]{:S(2)}) %collective-permute-start.4) | collective-permute-done | bytes 262176 | tf_op jit(solution)/shard_map/ppermute | solution.py:20
  66.7 0.1 select_bitcast_fusion.1
  66.8 0.1 pad_maximum_fusion
  66.9 0.1 copy.6
  66.9 0.7 convolution_convert_fusion.right_prod
  67.7 2.0 %all-to-all-done.2.arrived = bf16[8,528,128]{2,1,0:T(8,128)(2,1)S(1)} async-done(((bf16[8,528,128]{2,1,0:T(8,128)(2,1)}), bf16[8,528,128]{2,1,0:T(8,128)(2,1)S(1)}, u32[]{:S(2)}, u32[]{:S(2)}) %all-to-all-start.2) | async-done | bytes 1081376 | tf_op jit(solution)/shard_map/all_to_all | solution.py:226
  69.6 1.0 %shard_map.59 = (f32[2,128,512]{2,1,0:T(8,128)S(1)}, f32[8,128]{1,0:T(8,128)S(1)}) custom-call(s32[10]{0:T(128)S(1)} %shard_map.55.plan, bf16[2,512,512]{2,1,0:T(8,128)(2,1)S(1)} %convolution_convert_fusion.right_prod, f32[2,128]{1,0:T(2,128)S(1)} %broadcast_in_dim.12.half_sq, bf16[8,528,128]{2,1,0:T(8,128)(2,1)S(1)} %all-to-all-done.2.arrived), custom_call_target="tpu_custom_call" | custom-call | tf_op jit(solution)/shard_map/pallas_call | solution.py:240
  70.6 0.1 collective-permute-start.16
  70.7 1.6 %collective-permute-start.15 = (f32[8,128]{1,0:T(8,128)S(1)}, f32[8,128]{1,0:T(8,128)S(1)}, u32[]{:S(2)}, u32[]{:S(2)}) collective-permute-start(f32[8,128]{1,0:T(8,128)S(1)} %get-tuple-element.30.refs_0_), channel_id=1, source_target_pairs={{0,16},{8,24},{16,0},{24,8},{1,17},{9,25},{17,1},{25,9},{2,18},{10... | collective-permute-start | bytes 12296 | tf_op jit(solution)/shard_map/ppermute | solution.py:20
  72.3 0.2 collective-permute-start.14
  72.5 1.8 %collective-permute-done.15.refs_2_ = f32[8,128]{1,0:T(8,128)S(1)} collective-permute-done((f32[8,128]{1,0:T(8,128)S(1)}, f32[8,128]{1,0:T(8,128)S(1)}, u32[]{:S(2)}, u32[]{:S(2)}) %collective-permute-start.15) | collective-permute-done | bytes 4128 | tf_op jit(solution)/shard_map/ppermute | solution.py:20
  74.4 1.0 %collective-permute-done.14.refs_1_ = f32[8,128]{1,0:T(8,128)S(1)} collective-permute-done((f32[8,128]{1,0:T(8,128)S(1)}, f32[8,128]{1,0:T(8,128)S(1)}, u32[]{:S(2)}, u32[]{:S(2)}) %collective-permute-start.14) | collective-permute-done | bytes 4128 | tf_op jit(solution)/shard_map/ppermute | solution.py:20
  75.3 0.8 %shard_map.60 = bf16[2,128,512]{2,1,0:T(8,128)(2,1)} custom-call(f32[2,128,512]{2,1,0:T(8,128)S(1)} %get-tuple-element.29.precond, f32[8,128]{1,0:T(8,128)S(1)} %get-tuple-element.30.refs_0_, f32[8,128]{1,0:T(8,128)S(1)} %collective-permute-done.14.refs_1_, f32[8,128]{1,0:T(8,128)S(1)} %collective-permute-done.15.refs_2_, ...), custom_call_target="tpu_custom_call" | custom-call | tf_op jit(solution)/shard_map/pallas_call | solution.py:252
  (21 shorter events, 0.2 us)
Async XLA Ops:
  0.0 6.1 %copy-start.3 = (bf16[1,2,512,512]{3,2,1,0:T(8,128)(2,1)S(1)}, bf16[1,2,512,512]{3,2,1,0:T(8,128)(2,1)}, u32[]{:S(2)}) copy-start(bf16[1,2,512,512]{3,2,1,0:T(8,128)(2,1)} %param.5) | copy-start | bytes 3145732
  0.0 4.5 %copy-start.1 = (s32[9]{0:T(128)S(1)}, s32[9]{0:T(128)}, u32[]{:S(2)}) copy-start(s32[9]{0:T(128)} %offsets.1) | copy-start | bytes 112
  0.0 4.5 %copy-start = (s32[16]{0:T(128)S(1)}, s32[16]{0:T(128)}, u32[]{:S(2)}) copy-start(s32[16]{0:T(128)} %lists.1) | copy-start | bytes 196
  0.0 6.1 %collective-permute-start = (bf16[2,512,512]{2,1,0:T(8,128)(2,1)}, bf16[2,512,512]{2,1,0:T(8,128)(2,1)S(1)}, u32[]{:S(2)}, u32[]{:S(2)}) collective-permute-start(bf16[2,512,512]{2,1,0:T(8,128)(2,1)} %bitcast.29), channel_id=1, source_target_pairs={{0,8},{8,0},{16,24},{24,16},{1,9},{9,1},{17,25},{25,17},{2,10},{10... | collective-permute-start | bytes 3145736 | tf_op jit(solution)/shard_map/ppermute | solution.py:20
  0.5 13.1 %all-to-all-start = ((bf16[4,128,512]{2,1,0:T(8,128)(2,1)}), bf16[4,128,512]{2,1,0:T(8,128)(2,1)S(1)}, u32[]{:S(2)}, u32[]{:S(2)}) async-start(bf16[4,128,512]{2,1,0:T(8,128)(2,1)} %bitcast.28), calls=%async_computation | async-start | bytes 1048576 | tf_op jit(solution)/shard_map/all_to_all | solution.py:186
  13.7 18.1 %collective-permute-start.1 = (bf16[2,128,512]{2,1,0:T(8,128)(2,1)S(1)}, bf16[2,128,512]{2,1,0:T(8,128)(2,1)}, u32[]{:S(2)}, u32[]{:S(2)}) collective-permute-start(bf16[2,128,512]{2,1,0:T(8,128)(2,1)S(1)} %constant_dynamic-slice_fusion), channel_id=1, source_target_pairs={{0,16},{8,24},{16,0},{24,8},{1,17},{9,25},{17,1},{25,9},{2,18},{10... | collective-permute-start | bytes 786440 | tf_op jit(solution)/shard_map/ppermute | solution.py:20
  13.8 21.2 %all-to-all-start.1 = ((bf16[4,128,512]{2,1,0:T(8,128)(2,1)}), bf16[4,128,512]{2,1,0:T(8,128)(2,1)S(1)}, u32[]{:S(2)}, u32[]{:S(2)}) async-start(bf16[4,128,512]{2,1,0:T(8,128)(2,1)} %bitcast.3), calls=%async_computation.1 | async-start | bytes 1048576 | tf_op jit(solution)/shard_map/all_to_all | solution.py:186
  17.9 7.8 %collective-permute-start.5 = (bf16[128,512]{1,0:T(8,128)(2,1)S(1)}, bf16[128,512]{1,0:T(8,128)(2,1)S(1)}, u32[]{:S(2)}, u32[]{:S(2)}) collective-permute-start(bf16[128,512]{1,0:T(8,128)(2,1)S(1)} %get-tuple-element.22), channel_id=1, source_target_pairs={{0,1},{1,0},{2,3},{3,2},{4,5},{5,4},{6,7},{7,6},{8,9},{9,8},{10,11... | collective-permute-start | bytes 393224 | tf_op jit(solution)/shard_map/ppermute | solution.py:20
  20.1 8.2 %collective-permute-start.6 = (bf16[128,512]{1,0:T(8,128)(2,1)S(1)}, bf16[128,512]{1,0:T(8,128)(2,1)S(1)}, u32[]{:S(2)}, u32[]{:S(2)}) collective-permute-start(bf16[128,512]{1,0:T(8,128)(2,1)S(1)} %get-tuple-element.23), channel_id=1, source_target_pairs={{0,6},{1,7},{2,4},{3,5},{4,2},{5,3},{6,0},{7,1},{8,14},{9,15},{10,... | collective-permute-start | bytes 393224 | tf_op jit(solution)/shard_map/ppermute | solution.py:20
  23.7 16.9 %collective-permute-start.7 = (bf16[128,512]{1,0:T(8,128)(2,1)S(1)}, bf16[128,512]{1,0:T(8,128)(2,1)S(1)}, u32[]{:S(2)}, u32[]{:S(2)}) collective-permute-start(bf16[128,512]{1,0:T(8,128)(2,1)S(1)} %get-tuple-element.24), channel_id=1, source_target_pairs={{0,2},{1,3},{2,0},{3,1},{4,6},{5,7},{6,4},{7,5},{8,10},{9,11},{10,... | collective-permute-start | bytes 393224 | tf_op jit(solution)/shard_map/ppermute | solution.py:20
  23.7 16.9 %collective-permute-start.8 = (bf16[128,512]{1,0:T(8,128)(2,1)S(1)}, bf16[128,512]{1,0:T(8,128)(2,1)S(1)}, u32[]{:S(2)}, u32[]{:S(2)}) collective-permute-start(bf16[128,512]{1,0:T(8,128)(2,1)S(1)} %get-tuple-element.25), channel_id=1, source_target_pairs={{0,3},{1,2},{2,1},{3,0},{4,7},{5,6},{6,5},{7,4},{8,11},{9,10},{10,... | collective-permute-start | bytes 393224 | tf_op jit(solution)/shard_map/ppermute | solution.py:20
  25.7 14.9 %collective-permute-start.9 = (bf16[128,512]{1,0:T(8,128)(2,1)S(1)}, bf16[128,512]{1,0:T(8,128)(2,1)S(1)}, u32[]{:S(2)}, u32[]{:S(2)}) collective-permute-start(bf16[128,512]{1,0:T(8,128)(2,1)S(1)} %get-tuple-element.26), channel_id=1, source_target_pairs={{0,4},{1,5},{2,6},{3,7},{4,0},{5,1},{6,2},{7,3},{8,12},{9,13},{10,... | collective-permute-start | bytes 393224 | tf_op jit(solution)/shard_map/ppermute | solution.py:20
  28.3 12.3 %collective-permute-start.10 = (bf16[128,512]{1,0:T(8,128)(2,1)S(1)}, bf16[128,512]{1,0:T(8,128)(2,1)S(1)}, u32[]{:S(2)}, u32[]{:S(2)}) collective-permute-start(bf16[128,512]{1,0:T(8,128)(2,1)S(1)} %get-tuple-element.27), channel_id=1, source_target_pairs={{0,7},{1,6},{2,5},{3,4},{4,3},{5,2},{6,1},{7,0},{8,15},{9,14},{10,... | collective-permute-start | bytes 393224 | tf_op jit(solution)/shard_map/ppermute | solution.py:20
  31.8 19.9 %collective-permute-start.11 = (bf16[128,512]{1,0:T(8,128)(2,1)S(1)}, bf16[128,512]{1,0:T(8,128)(2,1)S(1)}, u32[]{:S(2)}, u32[]{:S(2)}) collective-permute-start(bf16[128,512]{1,0:T(8,128)(2,1)S(1)} %get-tuple-element.28), channel_id=1, source_target_pairs={{0,5},{1,4},{2,7},{3,6},{4,1},{5,0},{6,3},{7,2},{8,13},{9,12},{10,... | collective-permute-start | bytes 393224 | tf_op jit(solution)/shard_map/ppermute | solution.py:20
  36.7 32.9 %all-to-all-start.2 = ((bf16[8,528,128]{2,1,0:T(8,128)(2,1)}), bf16[8,528,128]{2,1,0:T(8,128)(2,1)S(1)}, u32[]{:S(2)}, u32[]{:S(2)}) async-start(bf16[8,528,128]{2,1,0:T(8,128)(2,1)} %shard_map.57.refs_8_), calls=%async_computation.2 | async-start | bytes 2162688 | tf_op jit(solution)/shard_map/all_to_all | solution.py:226
  51.8 3.2 %copy-start.2 = (bf16[2,128,512]{2,1,0:T(8,128)(2,1)S(1)}, bf16[2,128,512]{2,1,0:T(8,128)(2,1)}, u32[]{:S(2)}) copy-start(bf16[2,128,512]{2,1,0:T(8,128)(2,1)} %get-tuple-element.32) | copy-start | bytes 786436
  52.4 9.7 %collective-permute-start.12 = (bf16[2,1,128,512]{3,2,0,1:T(8,128)(2,1)S(1)}, bf16[2,1,128,512]{3,2,0,1:T(8,128)(2,1)S(1)}, u32[]{:S(2)}, u32[]{:S(2)}) collective-permute-start(bf16[2,1,128,512]{3,2,0,1:T(8,128)(2,1)S(1)} %bitcast.26), channel_id=1, source_target_pairs={{0,16},{8,24},{16,0},{24,8},{1,17},{9,25},{17,1},{25,9},{2,18},{10... | collective-permute-start | bytes 786440 | tf_op jit(solution)/shard_map/ppermute | solution.py:20
  54.9 10.2 %collective-permute-start.2 = (bf16[2,128,512]{2,1,0:T(8,128)(2,1)S(1)}, bf16[2,128,512]{2,1,0:T(8,128)(2,1)S(1)}, u32[]{:S(2)}, u32[]{:S(2)}) collective-permute-start(bf16[2,128,512]{2,1,0:T(8,128)(2,1)S(1)} %copy-done.2), channel_id=1, source_target_pairs={{0,16},{8,24},{16,0},{24,8},{1,17},{9,25},{17,1},{25,9},{2,18},{10... | collective-permute-start | bytes 786440 | tf_op jit(solution)/shard_map/ppermute | solution.py:20
  62.3 4.4 %collective-permute-start.13 = (bf16[2,2,128,512]{3,2,0,1:T(8,128)(2,1)S(1)}, bf16[2,2,128,512]{3,2,0,1:T(8,128)(2,1)S(1)}, u32[]{:S(2)}, u32[]{:S(2)}) collective-permute-start(bf16[2,2,128,512]{3,2,0,1:T(8,128)(2,1)S(1)} %maximum_bitcast_fusion), channel_id=1, source_target_pairs={{0,8},{8,0},{16,24},{24,16},{1,9},{9,1},{17,25},{25,17},{2,10},{10... | collective-permute-start | bytes 1572872 | tf_op jit(solution)/shard_map/ppermute | solution.py:20
  62.3 2.9 %collective-permute-start.3 = (bf16[2,128,512]{2,1,0:T(8,128)(2,1)S(1)}, bf16[2,128,512]{2,1,0:T(8,128)(2,1)S(1)}, u32[]{:S(2)}, u32[]{:S(2)}) collective-permute-start(bf16[2,128,512]{2,1,0:T(8,128)(2,1)S(1)} %copy-done.2), channel_id=1, source_target_pairs={{0,8},{8,0},{16,24},{24,16},{1,9},{9,1},{17,25},{25,17},{2,10},{10... | collective-permute-start | bytes 786440 | tf_op jit(solution)/shard_map/ppermute | solution.py:20
  65.1 1.5 %collective-permute-start.4 = (bf16[2,128,512]{2,1,0:T(8,128)(2,1)S(1)}, bf16[2,128,512]{2,1,0:T(8,128)(2,1)S(1)}, u32[]{:S(2)}, u32[]{:S(2)}) collective-permute-start(bf16[2,128,512]{2,1,0:T(8,128)(2,1)S(1)} %collective-permute-done.2), channel_id=1, source_target_pairs={{0,8},{8,0},{16,24},{24,16},{1,9},{9,1},{17,25},{25,17},{2,10},{10... | collective-permute-start | bytes 786440 | tf_op jit(solution)/shard_map/ppermute | solution.py:20
  70.6 1.9 %collective-permute-start.16 = (f32[8,128]{1,0:T(8,128)S(1)}, f32[8,128]{1,0:T(8,128)S(1)}, u32[]{:S(2)}, u32[]{:S(2)}) collective-permute-start(f32[8,128]{1,0:T(8,128)S(1)} %get-tuple-element.30.refs_0_), channel_id=1, source_target_pairs={{0,8},{8,0},{16,24},{24,16},{1,9},{9,1},{17,25},{25,17},{2,10},{10... | collective-permute-start | bytes 12296 | tf_op jit(solution)/shard_map/ppermute | solution.py:20
  70.7 3.7 %collective-permute-start.15 = (f32[8,128]{1,0:T(8,128)S(1)}, f32[8,128]{1,0:T(8,128)S(1)}, u32[]{:S(2)}, u32[]{:S(2)}) collective-permute-start(f32[8,128]{1,0:T(8,128)S(1)} %get-tuple-element.30.refs_0_), channel_id=1, source_target_pairs={{0,16},{8,24},{16,0},{24,8},{1,17},{9,25},{17,1},{25,9},{2,18},{10... | collective-permute-start | bytes 12296 | tf_op jit(solution)/shard_map/ppermute | solution.py:20
  72.3 3.0 %collective-permute-start.14 = (f32[8,128]{1,0:T(8,128)S(1)}, f32[8,128]{1,0:T(8,128)S(1)}, u32[]{:S(2)}, u32[]{:S(2)}) collective-permute-start(f32[8,128]{1,0:T(8,128)S(1)} %get-tuple-element.30.refs_0_), channel_id=1, source_target_pairs={{0,24},{8,16},{16,8},{24,0},{1,25},{9,17},{17,9},{25,1},{2,26},{10... | collective-permute-start | bytes 12296 | tf_op jit(solution)/shard_map/ppermute | solution.py:20
